TPU v7x, 32 devices: a whole 2x2x4 slice. The times are simulated.
32 devices in a mesh: fsdp: 2 (over x), ctx: 4 (over z), tp: 4 (over y, core).
Axes of the slice: x: 2, y: 2, z: 4, core: 2. Of those that a mesh axis runs over, the one named last changes fastest.
Arguments:
- hidden: bfloat16 [2, 3072, 2560], P('fsdp', 'ctx'), may hold values from -6 to 6
- lengths: int32 [2], replicated, may hold values from 1024 to 3072, as said below
- teacher: bfloat16 [2, 3072, 2560], P('fsdp', ('ctx', 'tp')), may hold values from -6 to 6
- attn_gain: bfloat16 [2560], P(('fsdp', 'ctx', 'tp')), may hold values from 0.5 to 1.5
- query_weight: bfloat16 [2560, 2560], P(('fsdp', 'ctx', 'tp')), may hold values from -0.125 to 0.125
- kv_weight: bfloat16 [2560, 512], P(('fsdp', 'ctx', 'tp')), may hold values from -0.125 to 0.125
- out_weight: bfloat16 [2560, 2560], P(('fsdp', 'ctx', 'tp')), may hold values from -2.5 to 2.5
- mlp_gain: bfloat16 [2560], P(('fsdp', 'ctx', 'tp')), may hold values from 0.5 to 1.5
- gate_weight: bfloat16 [2560, 7680], P(('fsdp', 'ctx'), 'tp'), may hold values from -0.125 to 0.125
- up_weight: bfloat16 [2560, 7680], P(('fsdp', 'ctx'), 'tp'), may hold values from -0.125 to 0.125
- down_weight: bfloat16 [7680, 2560], P('tp', ('fsdp', 'ctx')), may hold values from -0.0625 to 0.0625
Outputs:
- output: bfloat16 [2, 3072, 2560], P('fsdp', ('ctx', 'tp'))
- loss: float32 [], replicated
- input_grad: float32 [2, 3072, 2560], P('fsdp', ('ctx', 'tp'))
- attn_gain_grad: float32 [2560], P(('fsdp', 'ctx', 'tp'))
- query_weight_grad: float32 [2560, 2560], P(('fsdp', 'ctx', 'tp'))
- kv_weight_grad: float32 [2560, 512], P(('fsdp', 'ctx', 'tp'))
- out_weight_grad: float32 [2560, 2560], P(('fsdp', 'ctx', 'tp'))
- mlp_gain_grad: float32 [2560], P(('fsdp', 'ctx', 'tp'))
- gate_weight_grad: float32 [2560, 7680], P(('fsdp', 'ctx'), 'tp')
- up_weight_grad: float32 [2560, 7680], P(('fsdp', 'ctx'), 'tp')
- down_weight_grad: float32 [7680, 2560], P('tp', ('fsdp', 'ctx'))
Inputs may be any that keep to these rules, and one draw needn't show every extreme that they name: `lengths`: each sequence holds at least 1024 real tokens at its start; in every draw one sequence, chosen by the seed, fills all 3072 slots.
All inputs are finite; a program needn't handle non-finite values.
Results may differ from a plain program's by a relative error of at most 0.013.
Values may be sent and summed in bfloat16 or wider, within the bound.
No kernel may reach another device: no remote copies, remote signals or barrier semaphores. Data moves between devices by JAX's collectives and lax.ppermute only.
A program may use at most 320 MiB of HBM per device.

v0:
```python
import jax
import jax.numpy as jnp
from jax import lax
from jax.sharding import PartitionSpec as P

W = 2048


epsilon = 1e-06
lowest = -1e30


def shifted_2(array, axis, by):
    count = lax.axis_size(axis)
    pairs = [(i, i + by) for i in range(count) if 0 <= i + by < count]
    return lax.ppermute(array, axis, pairs)


def rms_norm(values, scaling):
    return values * lax.rsqrt(jnp.mean(values * values, axis=-1, keepdims=True) + epsilon) * scaling


def rotary_tables(positions, head_size):
    quarter = head_size // 4
    frequency = 10000.0 ** (-(jnp.arange(quarter).astype(jnp.float32) * 4.0 / head_size))
    angle = positions.astype(jnp.float32)[:, None] * frequency[None, :]
    return (jnp.cos(angle), jnp.sin(angle))


def turn(values, cosine, sine):
    quarter = cosine.shape[-1]
    first_half = values[..., :quarter]
    second_half = values[..., quarter : 2 * quarter]
    return jnp.concatenate(
        [
            first_half * cosine - second_half * sine,
            second_half * cosine + first_half * sine,
            values[..., 2 * quarter :],
        ],
        axis=-1,
    )


def gelu_tanh(values):
    return jax.nn.gelu(values, approximate=True)


def contract_last(first_op, second_op):
    return lax.dot_general(
        first_op, second_op, (((1,), (1,)), ((), ())), preferred_element_type=jnp.float32
    )


def contract_rows(first_op, second_op):
    return lax.dot_general(
        first_op, second_op, (((0,), (0,)), ((), ())), preferred_element_type=jnp.float32
    )


def masked_scores(query_part, key_rows, query_start, key_start):
    scores = jnp.einsum("qhd,kd->hqk", query_part, key_rows, preferred_element_type=jnp.float32)
    query_pos = query_start + jnp.arange(query_part.shape[0])
    key_pos = key_start + jnp.arange(key_rows.shape[0])
    allowed = (
        (key_pos[None, :] <= query_pos[:, None])
        & (key_pos[None, :] > query_pos[:, None] - W)
        & (key_pos[None, :] >= 0)
    )
    return jnp.where(allowed[None], scores, lowest)


def local(
    hidden,
    lengths,
    teacher,
    attn_gain,
    query_weight,
    kv_weight,
    out_weight,
    mlp_gain,
    gate_weight,
    up_weight,
    down_weight,
):
    tp_count = lax.axis_size("tp")
    ctx_count = lax.axis_size("ctx")
    all_count = lax.axis_size(("fsdp", "ctx", "tp"))
    tp_rank = lax.axis_index("tp")
    ctx_rank = lax.axis_index("ctx")
    fsdp_rank = lax.axis_index("fsdp")
    seq_count, span_rows, width = hidden.shape
    row_count = seq_count * span_rows
    part_rows = span_rows // tp_count
    part_count = seq_count * part_rows
    part_start = tp_rank * part_rows
    head_size = kv_weight.shape[1] // 2
    head_count = query_weight.shape[1] // head_size
    slot_count = -(-head_count // tp_count)
    fuller = head_count - (slot_count - 1) * tp_count
    first_head = tp_rank * (slot_count - 1) + jnp.minimum(tp_rank, fuller)
    slot_base = jnp.minimum(first_head, head_count - slot_count)
    slot_heads = slot_base + jnp.arange(slot_count)
    held_heads = slot_count - 1 + (tp_rank < fuller).astype(jnp.int32)
    slot_live = ((slot_heads >= first_head) & (slot_heads < first_head + held_heads)).astype(
        jnp.float32
    )
    slot_width = slot_count * head_size
    query_full, out_full, kv_full, gain_attn, gain_mlp = (
        lax.all_gather(query_weight, ("fsdp", "ctx", "tp"), axis=0, tiled=True),
        lax.all_gather(out_weight, ("fsdp", "ctx", "tp"), axis=0, tiled=True),
        lax.all_gather(kv_weight, ("fsdp", "ctx", "tp"), axis=0, tiled=True),
        lax.all_gather(attn_gain, ("fsdp", "ctx", "tp"), axis=0, tiled=True),
        lax.all_gather(mlp_gain, ("fsdp", "ctx", "tp"), axis=0, tiled=True),
    )
    query_slot = lax.dynamic_slice_in_dim(query_full, slot_base * head_size, slot_width, 1)
    out_slot = lax.dynamic_slice_in_dim(out_full, slot_base * head_size, slot_width, 1)
    gate_full, up_full, down_full = (
        lax.all_gather(gate_weight, ("fsdp", "ctx"), axis=0, tiled=True),
        lax.all_gather(up_weight, ("fsdp", "ctx"), axis=0, tiled=True),
        lax.all_gather(down_weight, ("fsdp", "ctx"), axis=1, tiled=True),
    )
    gain_attn = gain_attn.astype(jnp.float32)
    gain_mlp = gain_mlp.astype(jnp.float32)
    inputs_three = hidden.astype(jnp.float32)
    inputs = inputs_three.reshape(row_count, width)
    inputs_part = lax.dynamic_slice_in_dim(inputs_three, part_start, part_rows, 1)
    normed = rms_norm(inputs, gain_attn).astype(jnp.bfloat16)
    normed_part = lax.dynamic_slice_in_dim(
        normed.reshape(seq_count, span_rows, width), part_start, part_rows, 1
    ).reshape(part_count, width)
    query_raw = jnp.dot(normed, query_slot, preferred_element_type=jnp.float32)
    kv_raw = jnp.dot(normed, kv_full, preferred_element_type=jnp.float32)
    positions = ctx_rank * span_rows + jnp.arange(span_rows)
    cosine, sine = rotary_tables(positions, head_size)
    query_scale = head_size ** (-0.5)
    queries = (
        turn(
            query_raw.reshape(seq_count, span_rows, slot_count, head_size),
            cosine[:, None, :],
            sine[:, None, :],
        )
        * query_scale
    ).astype(jnp.bfloat16)
    kv_three = kv_raw.reshape(seq_count, span_rows, 2 * head_size)
    keys_turned = turn(kv_three[..., :head_size], cosine, sine)
    kv_local = jnp.concatenate([keys_turned, kv_three[..., head_size:]], axis=-1).astype(
        jnp.bfloat16
    )
    reach_back = min((W - 2) // span_rows + 1, ctx_count - 1)
    earlier = []
    carried_kv = kv_local
    for distance in range(1, reach_back + 1):
        carried_kv = shifted_2(kv_local, "ctx", distance)
        earlier.insert(0, carried_kv)
    keys_all = jnp.concatenate(earlier + [kv_local], axis=1)
    key_start = (ctx_rank - reach_back) * span_rows
    block_count = max(1, span_rows // 512)
    block_rows = span_rows // block_count
    item_count = seq_count * block_count

    def forward_item(item_index):
        seq_index = item_index // block_count
        query_start = ctx_rank * span_rows + item_index % block_count * block_rows
        key_values = keys_all[seq_index]
        scores = masked_scores(
            queries[item_index], key_values[:, :head_size], query_start, key_start
        )
        row_max = jnp.max(scores, axis=-1, keepdims=True)
        shifted = jnp.exp(scores - row_max)
        row_total = jnp.sum(shifted, axis=-1, keepdims=True)
        weights_soft = (shifted / row_total).astype(jnp.bfloat16)
        mixed = jnp.einsum(
            "hqk,kd->qhd",
            weights_soft,
            key_values[:, head_size:],
            preferred_element_type=jnp.float32,
        )
        return (mixed, row_max[..., 0] + jnp.log(row_total[..., 0]))

    attended, log_sums = lax.map(forward_item, jnp.arange(item_count))
    attended = attended.reshape(row_count, slot_count, head_size) * slot_live[None, :, None]
    attended_low = attended.reshape(row_count, slot_width).astype(jnp.bfloat16)
    attn_partial = contract_last(attended_low, out_slot).reshape(seq_count, span_rows, width)
    attn_part = lax.psum_scatter(
        attn_partial.astype(jnp.bfloat16), "tp", scatter_dimension=1, tiled=True
    ).astype(jnp.float32)
    residual_part = inputs_part + attn_part
    normed_two_float, norm_two_back = jax.vjp(rms_norm, residual_part, gain_mlp)
    normed_two = lax.all_gather(
        normed_two_float.astype(jnp.bfloat16), "tp", axis=1, tiled=True
    ).reshape(row_count, width)
    gate_proj = jnp.dot(normed_two, gate_full, preferred_element_type=jnp.float32)
    up_proj = jnp.dot(normed_two, up_full, preferred_element_type=jnp.float32)
    activated, gelu_back = jax.vjp(gelu_tanh, gate_proj)
    hidden_act = (activated * up_proj).astype(jnp.bfloat16)
    ffn_partial = jnp.dot(hidden_act, down_full, preferred_element_type=jnp.float32).reshape(
        seq_count, span_rows, width
    )
    ffn_part = lax.psum_scatter(
        ffn_partial.astype(jnp.bfloat16), "tp", scatter_dimension=1, tiled=True
    ).astype(jnp.float32)
    my_lengths = lax.dynamic_slice_in_dim(lengths, fsdp_rank * seq_count, seq_count, 0)
    part_positions = ctx_rank * span_rows + part_start + jnp.arange(part_rows)
    valid_part = (part_positions[None, :] < my_lengths[:, None]).astype(jnp.float32)[..., None]
    output = (residual_part + ffn_part) * valid_part
    mismatch = output - teacher.astype(jnp.float32)
    count = jnp.sum(lengths).astype(jnp.float32)
    loss_part = jnp.sum(valid_part * mismatch * mismatch)
    d_output = valid_part * mismatch * (lengths.shape[0] * ctx_count * span_rows / count)
    d_ffn = lax.all_gather(d_output.astype(jnp.bfloat16), "tp", axis=1, tiled=True).reshape(
        row_count, width
    )
    d_hidden = contract_last(d_ffn, down_full)
    grad_down = contract_rows(hidden_act, d_ffn)
    d_gate = gelu_back(d_hidden * up_proj)[0].astype(jnp.bfloat16)
    d_up = (d_hidden * activated).astype(jnp.bfloat16)
    grad_gate = contract_rows(normed_two, d_gate)
    grad_up = contract_rows(normed_two, d_up)
    grad_gate_own, grad_up_own, grad_down_own = (
        lax.psum_scatter(
            grad_gate.astype(jnp.bfloat16), ("fsdp", "ctx"), scatter_dimension=0, tiled=True
        ).astype(jnp.float32),
        lax.psum_scatter(
            grad_up.astype(jnp.bfloat16), ("fsdp", "ctx"), scatter_dimension=0, tiled=True
        ).astype(jnp.float32),
        lax.psum_scatter(
            grad_down.astype(jnp.bfloat16), ("fsdp", "ctx"), scatter_dimension=1, tiled=True
        ).astype(jnp.float32),
    )
    d_normed_partial = (contract_last(d_gate, gate_full) + contract_last(d_up, up_full)).reshape(
        seq_count, span_rows, width
    )
    d_normed_two = lax.psum_scatter(
        d_normed_partial.astype(jnp.bfloat16), "tp", scatter_dimension=1, tiled=True
    ).astype(jnp.float32)
    d_residual_norm, d_gain_mlp = norm_two_back(d_normed_two)
    d_residual = d_output + d_residual_norm
    d_attn = lax.all_gather(d_residual.astype(jnp.bfloat16), "tp", axis=1, tiled=True).reshape(
        row_count, width
    )
    grad_out_slot = contract_rows(d_attn, attended_low)
    d_attended = (
        jnp.dot(d_attn, out_slot, preferred_element_type=jnp.float32).reshape(
            row_count, slot_count, head_size
        )
        * slot_live[None, :, None]
    )
    d_attended_items = d_attended.astype(jnp.bfloat16).reshape(
        item_count, block_rows, slot_count, head_size
    )

    def backward_item(running, item_index):
        seq_index = item_index // block_count
        query_start = ctx_rank * span_rows + item_index % block_count * block_rows
        key_values = keys_all[seq_index]
        query_part = queries[item_index]
        d_att_part = d_attended_items[item_index]
        scores = masked_scores(query_part, key_values[:, :head_size], query_start, key_start)
        probs_float = jnp.exp(scores - log_sums[item_index][..., None])
        d_probs = jnp.einsum(
            "qhd,kd->hqk", d_att_part, key_values[:, head_size:], preferred_element_type=jnp.float32
        )
        row_inner = jnp.sum(probs_float * d_probs, axis=-1, keepdims=True)
        d_scores = (probs_float * (d_probs - row_inner)).astype(jnp.bfloat16)
        d_query_part = jnp.einsum(
            "hqk,kd->qhd", d_scores, key_values[:, :head_size], preferred_element_type=jnp.float32
        )
        d_key_part = jnp.einsum(
            "hqk,qhd->kd", d_scores, query_part, preferred_element_type=jnp.float32
        )
        d_value_part = jnp.einsum(
            "hqk,qhd->kd",
            probs_float.astype(jnp.bfloat16),
            d_att_part,
            preferred_element_type=jnp.float32,
        )
        running = running.at[seq_index].add(jnp.concatenate([d_key_part, d_value_part], axis=-1))
        return (running, d_query_part)

    zero_grads = jnp.zeros(keys_all.shape, jnp.float32)
    d_kv_all, d_query_items = lax.scan(backward_item, zero_grads, jnp.arange(item_count))
    d_kv_own = d_kv_all[:, reach_back * span_rows :]
    carried_grad = jnp.zeros_like(d_kv_own)
    for distance in range(reach_back, 0, -1):
        offset = (reach_back - distance) * span_rows
        piece = d_kv_all[:, offset : offset + span_rows]
        carried_grad = shifted_2(piece.astype(jnp.bfloat16), "ctx", -distance).astype(piece.dtype)
        d_kv_own = d_kv_own + carried_grad
    d_key_raw = turn(d_kv_own[..., :head_size], cosine, -sine)
    d_kv_raw = jnp.concatenate([d_key_raw, d_kv_own[..., head_size:]], axis=-1)
    d_query_raw = turn(d_query_items * query_scale, cosine[:, None, :], -sine[:, None, :])
    d_query_low = d_query_raw.reshape(row_count, slot_width).astype(jnp.bfloat16)
    grad_query_slot = contract_rows(normed, d_query_low)
    d_query_normed = contract_last(d_query_low, query_slot).reshape(seq_count, span_rows, width)
    d_normed_query, d_kv_part = (
        lax.psum_scatter(
            d_query_normed.astype(jnp.bfloat16), "tp", scatter_dimension=1, tiled=True
        ).astype(jnp.float32),
        lax.psum_scatter(
            d_kv_raw.astype(jnp.bfloat16), "tp", scatter_dimension=1, tiled=True
        ).astype(jnp.float32),
    )
    d_kv_low = d_kv_part.reshape(part_count, 2 * head_size).astype(jnp.bfloat16)
    d_normed = d_normed_query.reshape(part_count, width) + contract_last(d_kv_low, kv_full)
    grad_kv = contract_rows(normed_part, d_kv_low)
    norm_one_value, norm_one_back = jax.vjp(
        rms_norm, inputs_part.reshape(part_count, width), gain_attn
    )
    d_inputs_norm, d_gain_attn = norm_one_back(d_normed)
    input_grad = d_residual + d_inputs_norm.reshape(seq_count, part_rows, width)
    grad_query_full = lax.dynamic_update_slice_in_dim(
        jnp.zeros((width, head_count * head_size), jnp.float32),
        grad_query_slot,
        slot_base * head_size,
        1,
    )
    grad_out_full = lax.dynamic_update_slice_in_dim(
        jnp.zeros((width, head_count * head_size), jnp.float32),
        grad_out_slot,
        slot_base * head_size,
        1,
    )
    loss_terms = jnp.full((all_count,), loss_part)
    query_grad, out_grad, kv_grad, gain_attn_grad, gain_mlp_grad, loss_sums = (
        lax.psum_scatter(grad_query_full, ("fsdp", "ctx", "tp"), scatter_dimension=0, tiled=True),
        lax.psum_scatter(grad_out_full, ("fsdp", "ctx", "tp"), scatter_dimension=0, tiled=True),
        lax.psum_scatter(grad_kv, ("fsdp", "ctx", "tp"), scatter_dimension=0, tiled=True),
        lax.psum_scatter(d_gain_attn, ("fsdp", "ctx", "tp"), scatter_dimension=0, tiled=True),
        lax.psum_scatter(d_gain_mlp, ("fsdp", "ctx", "tp"), scatter_dimension=0, tiled=True),
        lax.psum_scatter(loss_terms, ("fsdp", "ctx", "tp"), scatter_dimension=0, tiled=True),
    )
    loss = loss_sums[0] / (count * width)
    output_low = output.astype(jnp.bfloat16)
    return (
        output_low,
        loss,
        input_grad,
        gain_attn_grad,
        query_grad,
        kv_grad,
        out_grad,
        gain_mlp_grad,
        grad_gate_own,
        grad_up_own,
        grad_down_own,
    )


def solution(mesh):
    in_specs = (
        P("fsdp", "ctx", None),
        P(),
        P("fsdp", ("ctx", "tp"), None),
        P(("fsdp", "ctx", "tp")),
        P(("fsdp", "ctx", "tp"), None),
        P(("fsdp", "ctx", "tp"), None),
        P(("fsdp", "ctx", "tp"), None),
        P(("fsdp", "ctx", "tp")),
        P(("fsdp", "ctx"), "tp"),
        P(("fsdp", "ctx"), "tp"),
        P("tp", ("fsdp", "ctx")),
    )
    out_specs = (
        P("fsdp", ("ctx", "tp"), None),
        P(),
        P("fsdp", ("ctx", "tp"), None),
        P(("fsdp", "ctx", "tp")),
        P(("fsdp", "ctx", "tp"), None),
        P(("fsdp", "ctx", "tp"), None),
        P(("fsdp", "ctx", "tp"), None),
        P(("fsdp", "ctx", "tp")),
        P(("fsdp", "ctx"), "tp"),
        P(("fsdp", "ctx"), "tp"),
        P("tp", ("fsdp", "ctx")),
    )
    return jax.shard_map(local, mesh=mesh, in_specs=in_specs, out_specs=out_specs, check_vma=False)
```

profile of v0, /device:TPU:0, one launch (start us, length us, event | category | flops | bytes accessed | tf_op | source)
XLA Modules:
  0.0 2461.7 jit_solution(10112349614681692047)
XLA Ops:
  12.0 42.3 %all-reduce.6 = (bf16[2560]{0:T(1024)(128)(2,1)S(1)}, bf16[2560]{0:T(1024)(128)(2,1)S(1)}) all-reduce(bf16[2560]{0:T(1024)(128)(2,1)S(1)} %dynamic-update-slice.3, bf16[2560]{0:T(1024)(128)(2,1)S(1)} %dynamic-update-slice.4), channel_id=1, replica_groups=mesh['fsdp'=2,'ctx'=4,'tp'=4] {'fsdp','ctx','tp'}, use_global_device_ids=true, to_apply=%add | all-reduce | flops 5120 | bytes 20480
  89.8 17.8 collective-permute-done.2
  107.7 33.6 %collective-permute-done.1 = bf16[1,768,512]{1,2,0:T(8,128)(2,1)S(1)} collective-permute-done((bf16[1,768,512]{1,2,0:T(8,128)(2,1)S(1)}, bf16[1,768,512]{1,2,0:T(8,128)(2,1)S(1)}, u32[]{:S(2)}, u32[]{:S(2)}) %collective-permute-start.1) | collective-permute-done | bytes 786464 | tf_op jit(solution)/shard_map/ppermute | solution.py:16
  141.2 17.0 collective-permute-done
  165.4 52.0 %all-gather.12.cloned.1.call-done = bf16[2560,2560]{1,0:T(8,128)(2,1)} async-done(((bf16[80,2560]{1,0:T(8,128)(2,1)}), bf16[2560,2560]{1,0:T(8,128)(2,1)}) %all-gather.12.cloned.1.call-update) | async-done | bytes 13107216 | tf_op jit(solution)/shard_map/all_gather | solution.py:109
  262.1 14.8 fusion.48
  278.8 38.1 %all-gather.14.cloned.1.call-done = bf16[2560,2560]{1,0:T(8,128)(2,1)} async-done(((bf16[80,2560]{1,0:T(8,128)(2,1)}), bf16[2560,2560]{1,0:T(8,128)(2,1)}) %all-gather.14.cloned.1.call-update) | async-done | bytes 13107216 | tf_op jit(solution)/shard_map/all_gather | solution.py:110
  331.7 33.5 %reduce-scatter.14.cloned.1.call-done = bf16[1,192,2560]{2,1,0:T(8,128)(2,1)} async-done(((bf16[1,768,2560]{2,1,0:T(8,128)(2,1)}), bf16[1,192,2560]{2,1,0:T(8,128)(2,1)}) %reduce-scatter.14.cloned.1.call-update) | async-done | bytes 983056 | tf_op jit(solution)/shard_map/reduce_scatter | solution.py:184
  370.0 97.4 %all-gather.18.cloned.1.call-done = bf16[2560,1920]{1,0:T(8,128)(2,1)} async-done(((bf16[320,1920]{1,0:T(8,128)(2,1)}), bf16[2560,1920]{1,0:T(8,128)(2,1)}) %all-gather.18.cloned.1.call-update) | async-done | bytes 9830416 | tf_op jit(solution)/shard_map/all_gather | solution.py:118
  467.4 33.1 %all-gather.16.cloned.1.call-done = bf16[1,768,2560]{2,1,0:T(8,128)(2,1)} async-done(((bf16[1,192,2560]{2,1,0:T(8,128)(2,1)}), bf16[1,768,2560]{2,1,0:T(8,128)(2,1)}) %all-gather.16.cloned.1.call-update) | async-done | bytes 3932176 | tf_op jit(solution)/shard_map/all_gather | solution.py:189
  514.7 130.5 %all-gather.20.cloned.1.call-done = bf16[2560,1920]{1,0:T(8,128)(2,1)} async-done(((bf16[320,1920]{1,0:T(8,128)(2,1)}), bf16[2560,1920]{1,0:T(8,128)(2,1)}) %all-gather.20.cloned.1.call-update) | async-done | bytes 9830416 | tf_op jit(solution)/shard_map/all_gather | solution.py:119
  645.2 16.0 multiply_convert_fusion.2
  661.2 126.9 %all-gather.22.cloned.1.call-done = bf16[1920,2560]{0,1:T(8,128)(2,1)} async-done(((bf16[1920,320]{0,1:T(8,128)(2,1)}), bf16[1920,2560]{0,1:T(8,128)(2,1)}) %all-gather.22.cloned.1.call-update) | async-done | bytes 9830416 | tf_op jit(solution)/shard_map/all_gather | solution.py:120
  804.5 37.8 %reduce-scatter.16.cloned.1.call-done = bf16[1,192,2560]{2,1,0:T(8,128)(2,1)} async-done(((bf16[1,768,2560]{2,1,0:T(8,128)(2,1)}), bf16[1,192,2560]{2,1,0:T(8,128)(2,1)}) %reduce-scatter.16.cloned.1.call-update) | async-done | bytes 983056 | tf_op jit(solution)/shard_map/reduce_scatter | solution.py:199
  845.1 33.1 %all-gather.24.cloned.1.call-done = bf16[1,768,2560]{2,1,0:T(8,128)(2,1)} async-done(((bf16[1,192,2560]{2,1,0:T(8,128)(2,1)}), bf16[1,768,2560]{2,1,0:T(8,128)(2,1)}) %all-gather.24.cloned.1.call-update) | async-done | bytes 3932176 | tf_op jit(solution)/shard_map/all_gather | solution.py:210
  878.2 19.7 multiply_convert_fusion.1
  898.0 14.9 fusion.109
  924.7 42.8 %reduce-scatter.18.cloned.1.call-done = bf16[1,192,2560]{2,1,0:T(8,128)(2,1)} async-done(((bf16[1,768,2560]{2,1,0:T(8,128)(2,1)}), bf16[1,192,2560]{2,1,0:T(8,128)(2,1)}) %reduce-scatter.18.cloned.1.call-update) | async-done | bytes 983056 | tf_op jit(solution)/shard_map/reduce_scatter | solution.py:233
  985.3 21.9 all-gather.26.cloned.1.call-done
  1027.9 23.6 fusion
  1051.5 23.6 fusion.2
  1088.4 16.5 collective-permute-done.5
  1105.0 51.5 %collective-permute-done.4 = bf16[1,768,512]{1,2,0:T(8,128)(2,1)S(1)} collective-permute-done((bf16[1,768,512]{1,2,0:T(8,128)(2,1)S(1)}, bf16[1,768,512]{1,2,0:T(8,128)(2,1)S(1)}, u32[]{:S(2)}, u32[]{:S(2)}) %collective-permute-start.4) | collective-permute-done | bytes 786464 | tf_op jit(solution)/shard_map/ppermute | solution.py:16
  1190.9 14.4 convolution_convert_fusion
  1273.0 81.2 %reduce-scatter.28.cloned.1.call-done = bf16[320,1920]{1,0:T(8,128)(2,1)} async-done(((bf16[2560,1920]{1,0:T(8,128)(2,1)}), bf16[320,1920]{1,0:T(8,128)(2,1)}) %reduce-scatter.28.cloned.1.call-update) | async-done | bytes 1228816 | tf_op jit(solution)/shard_map/reduce_scatter | solution.py:220
  1357.1 169.6 %reduce-scatter.30.cloned.1.call-done = bf16[320,1920]{1,0:T(8,128)(2,1)} async-done(((bf16[2560,1920]{1,0:T(8,128)(2,1)}), bf16[320,1920]{1,0:T(8,128)(2,1)}) %reduce-scatter.30.cloned.1.call-update) | async-done | bytes 1228816 | tf_op jit(solution)/shard_map/reduce_scatter | solution.py:223
  1529.5 169.7 %reduce-scatter.32.cloned.1.call-done = bf16[1920,320]{0,1:T(8,128)(2,1)} async-done(((bf16[1920,2560]{0,1:T(8,128)(2,1)}), bf16[1920,320]{0,1:T(8,128)(2,1)}) %reduce-scatter.32.cloned.1.call-update) | async-done | bytes 1228816 | tf_op jit(solution)/shard_map/reduce_scatter | solution.py:226
  1702.1 41.3 %reduce-scatter.20.cloned.1.call-done = bf16[1,192,2560]{2,1,0:T(8,128)(2,1)} async-done(((bf16[1,768,2560]{2,1,0:T(8,128)(2,1)}), bf16[1,192,2560]{2,1,0:T(8,128)(2,1)}) %reduce-scatter.20.cloned.1.call-update) | async-done | bytes 983056 | tf_op jit(solution)/shard_map/reduce_scatter | solution.py:296
  1749.1 41.0 %all-reduce.5 = (f32[32]{0:T(128)S(1)}, f32[2560]{0:T(1024)S(1)}, f32[2560]{0:T(1024)S(1)}) all-reduce(f32[32]{0:T(128)S(1)} %broadcast_in_dim.66, f32[2560]{0:T(1024)S(1)} %get-tuple-element.76, f32[2560]{0:T(1024)S(1)} %copy-done.26), channel_id=4, replica_groups=mesh['fsdp'=2,'ctx'=4,'tp'=4] {'fsdp','ctx','tp'}, use_global_device_ids=true, to_apply=%region_7.8.clone | all-reduce | flops 5152 | bytes 41216
  1796.5 93.1 %reduce-scatter.24.cloned.1.call-done = f32[80,512]{1,0:T(8,128)} async-done(((f32[2560,512]{1,0:T(8,128)}), f32[80,512]{1,0:T(8,128)}) %reduce-scatter.24.cloned.1.call-update) | async-done | bytes 163856 | tf_op jit(solution)/shard_map/reduce_scatter | solution.py:327
  1889.6 278.8 %reduce-scatter.22.cloned.1.call-done = f32[80,2560]{1,0:T(8,128)} async-done(((f32[2560,2560]{1,0:T(8,128)}), f32[80,2560]{1,0:T(8,128)}) %reduce-scatter.22.cloned.1.call-update) | async-done | bytes 819216 | tf_op jit(solution)/shard_map/reduce_scatter | solution.py:325
  2168.4 284.4 %reduce-scatter.26.cloned.1.call-done = f32[80,2560]{1,0:T(8,128)} async-done(((f32[2560,2560]{1,0:T(8,128)}), f32[80,2560]{1,0:T(8,128)}) %reduce-scatter.26.cloned.1.call-update) | async-done | bytes 819216 | tf_op jit(solution)/shard_map/reduce_scatter | solution.py:326
  (220 shorter events, 330.5 us)
Async XLA Ops:
  8.0 64.6 %all-gather.10.cloned.1.call-start = ((), (), s32[]{:S(2)}) async-start(), calls=%async_computation.11 | async-start | bytes 2703360 | tf_op jit(solution)/shard_map/all_gather | solution.py:111
  8.7 208.6 %all-gather.12.cloned.1.call-start = ((), (), s32[]{:S(2)}) async-start(), calls=%async_computation.12 | async-start | bytes 13516800 | tf_op jit(solution)/shard_map/all_gather | solution.py:109
  9.5 307.4 %all-gather.14.cloned.1.call-start = ((), (), s32[]{:S(2)}) async-start(), calls=%async_computation.13 | async-start | bytes 13516800 | tf_op jit(solution)/shard_map/all_gather | solution.py:110
  10.2 355.0 %reduce-scatter.14.cloned.1.call-start = ((), (), s32[]{:S(2)}) async-start(), calls=%async_computation.14 | async-start | bytes 4915200 | tf_op jit(solution)/shard_map/reduce_scatter | solution.py:184
  54.3 173.6 %copy-start.18 = (f32[2560]{0:T(1024)}, f32[2560]{0:T(1024)S(1)}, u32[]{:S(2)}) copy-start(f32[2560]{0:T(1024)S(1)} %convert_element_type.215) | copy-start | bytes 30724
  54.3 207.8 %copy-start.31 = (f32[3]{0:T(128)}, f32[3]{0:T(128)S(1)}, u32[]{:S(2)}) copy-start(f32[3]{0:T(128)S(1)} %and_convert_fusion) | copy-start | bytes 40
  57.8 170.2 %copy-start.27 = (f32[768]{0:T(1024)}, f32[768]{0:T(1024)S(1)}, u32[]{:S(2)}) copy-start(f32[768]{0:T(1024)S(1)} %add_rsqrt_fusion) | copy-start | bytes 9220
  59.2 175.4 %copy-start.11 = (f32[768,64]{0,1:T(8,128)}, f32[768,64]{0,1:T(8,128)S(1)}, u32[]{:S(2)}) copy-start(f32[768,64]{0,1:T(8,128)S(1)} %get-tuple-element.106) | copy-start | bytes 589828
  78.7 28.9 %collective-permute-start.2 = (bf16[1,768,512]{1,2,0:T(8,128)(2,1)S(1)}, bf16[1,768,512]{1,2,0:T(8,128)(2,1)S(1)}, u32[]{:S(2)}, u32[]{:S(2)}) collective-permute-start(bf16[1,768,512]{1,2,0:T(8,128)(2,1)S(1)} %pad_maximum_fusion), channel_id=1, source_target_pairs={{0,4},{4,8},{8,12},{1,5},{5,9},{9,13},{2,6},{6,10},{10,14},{3,7},{... | collective-permute-start | bytes 2359304 | tf_op jit(solution)/shard_map/ppermute | solution.py:16
  81.1 60.2 %collective-permute-start.1 = (bf16[1,768,512]{1,2,0:T(8,128)(2,1)S(1)}, bf16[1,768,512]{1,2,0:T(8,128)(2,1)S(1)}, u32[]{:S(2)}, u32[]{:S(2)}) collective-permute-start(bf16[1,768,512]{1,2,0:T(8,128)(2,1)S(1)} %pad_maximum_fusion), channel_id=1, source_target_pairs={{0,8},{4,12},{1,9},{5,13},{2,10},{6,14},{3,11},{7,15},{16,24},{20,... | collective-permute-start | bytes 2359304 | tf_op jit(solution)/shard_map/ppermute | solution.py:16
  85.4 72.8 %collective-permute-start = (bf16[1,768,512]{1,2,0:T(8,128)(2,1)S(1)}, bf16[1,768,512]{1,2,0:T(8,128)(2,1)S(1)}, u32[]{:S(2)}, u32[]{:S(2)}) collective-permute-start(bf16[1,768,512]{1,2,0:T(8,128)(2,1)S(1)} %pad_maximum_fusion), channel_id=1, source_target_pairs={{0,12},{1,13},{2,14},{3,15},{16,28},{17,29},{18,30},{19,31}} | collective-permute-start | bytes 2359304 | tf_op jit(solution)/shard_map/ppermute | solution.py:16
  89.8 172.3 %copy-start = (pred[768,3072]{0,1:T(8,128)(4,1)}, pred[768,3072]{0,1:T(8,128)(4,1)S(1)}, u32[]{:S(2)}) copy-start(pred[768,3072]{0,1:T(8,128)(4,1)S(1)} %and_and_fusion) | copy-start | bytes 7077892
  324.0 143.4 %all-gather.18.cloned.1.call-start = ((), (), s32[]{:S(2)}) async-start(), calls=%async_computation.16 | async-start | bytes 11059200 | tf_op jit(solution)/shard_map/all_gather | solution.py:118
  324.5 176.0 %all-gather.16.cloned.1.call-start = ((), (), s32[]{:S(2)}) async-start(), calls=%async_computation.15 | async-start | bytes 4915200 | tf_op jit(solution)/shard_map/all_gather | solution.py:189
  368.6 276.6 %all-gather.20.cloned.1.call-start = ((), (), s32[]{:S(2)}) async-start(), calls=%async_computation.17 | async-start | bytes 11059200 | tf_op jit(solution)/shard_map/all_gather | solution.py:119
  369.2 418.9 %all-gather.22.cloned.1.call-start = ((), (), s32[]{:S(2)}) async-start(), calls=%async_computation.18 | async-start | bytes 11059200 | tf_op jit(solution)/shard_map/all_gather | solution.py:120
  369.9 472.4 %reduce-scatter.16.cloned.1.call-start = ((), (), s32[]{:S(2)}) async-start(), calls=%async_computation.19 | async-start | bytes 4915200 | tf_op jit(solution)/shard_map/reduce_scatter | solution.py:199
  801.3 76.9 %all-gather.24.cloned.1.call-start = ((), (), s32[]{:S(2)}) async-start(), calls=%async_computation.20 | async-start | bytes 4915200 | tf_op jit(solution)/shard_map/all_gather | solution.py:210
  845.1 122.4 %reduce-scatter.18.cloned.1.call-start = ((), (), s32[]{:S(2)}) async-start(), calls=%async_computation.21 | async-start | bytes 4915200 | tf_op jit(solution)/shard_map/reduce_scatter | solution.py:233
  924.6 82.6 %all-gather.26.cloned.1.call-start = ((), (), s32[]{:S(2)}) async-start(), calls=%async_computation.22 | async-start | bytes 4915200 | tf_op jit(solution)/shard_map/all_gather | solution.py:238
  974.1 248.3 %reduce-scatter.34.cloned.1.call-start = ((), (), s32[]{:S(2)}) async-start(), calls=%async_computation.30 | async-start | bytes 983040
  1083.4 21.6 collective-permute-start.5
  1084.7 71.8 %collective-permute-start.4 = (bf16[1,768,512]{1,2,0:T(8,128)(2,1)S(1)}, bf16[1,768,512]{1,2,0:T(8,128)(2,1)S(1)}, u32[]{:S(2)}, u32[]{:S(2)}) collective-permute-start(bf16[1,768,512]{1,2,0:T(8,128)(2,1)S(1)} %get-tuple-element.94), channel_id=1, source_target_pairs={{8,0},{12,4},{9,1},{13,5},{10,2},{14,6},{11,3},{15,7},{24,16},{28,... | collective-permute-start | bytes 2359304 | tf_op jit(solution)/shard_map/ppermute | solution.py:16
  1086.0 70.5 %collective-permute-start.3 = (bf16[1,768,512]{1,2,0:T(8,128)(2,1)S(1)}, bf16[1,768,512]{1,2,0:T(8,128)(2,1)S(1)}, u32[]{:S(2)}, u32[]{:S(2)}) collective-permute-start(bf16[1,768,512]{1,2,0:T(8,128)(2,1)S(1)} %get-tuple-element.92), channel_id=1, source_target_pairs={{12,0},{13,1},{14,2},{15,3},{28,16},{29,17},{30,18},{31,19}} | collective-permute-start | bytes 2359304 | tf_op jit(solution)/shard_map/ppermute | solution.py:16
  1160.2 194.0 %reduce-scatter.28.cloned.1.call-start = ((), (), s32[]{:S(2)}) async-start(), calls=%async_computation.27 | async-start | bytes 11059200 | tf_op jit(solution)/shard_map/reduce_scatter | solution.py:220
  1173.4 353.2 %reduce-scatter.30.cloned.1.call-start = ((), (), s32[]{:S(2)}) async-start(), calls=%async_computation.28 | async-start | bytes 11059200 | tf_op jit(solution)/shard_map/reduce_scatter | solution.py:223
  1189.1 510.1 %reduce-scatter.32.cloned.1.call-start = ((), (), s32[]{:S(2)}) async-start(), calls=%async_computation.29 | async-start | bytes 11059200 | tf_op jit(solution)/shard_map/reduce_scatter | solution.py:226
  1205.4 538.0 %reduce-scatter.20.cloned.1.call-start = ((), (), s32[]{:S(2)}) async-start(), calls=%async_computation.23 | async-start | bytes 4915200 | tf_op jit(solution)/shard_map/reduce_scatter | solution.py:296
  1222.3 667.4 %reduce-scatter.24.cloned.1.call-start = ((), (), s32[]{:S(2)}) async-start(), calls=%async_computation.25 | async-start | bytes 5406720 | tf_op jit(solution)/shard_map/reduce_scatter | solution.py:327
  1228.4 940.0 %reduce-scatter.22.cloned.1.call-start = ((), (), s32[]{:S(2)}) async-start(), calls=%async_computation.24 | async-start | bytes 27033600 | tf_op jit(solution)/shard_map/reduce_scatter | solution.py:325
  1250.1 1202.7 %reduce-scatter.26.cloned.1.call-start = ((), (), s32[]{:S(2)}) async-start(), calls=%async_computation.26 | async-start | bytes 27033600 | tf_op jit(solution)/shard_map/reduce_scatter | solution.py:326
  1702.1 90.4 %copy-start.6 = (f32[1,192,2560]{2,1,0:T(8,128)S(1)}, f32[1,192,2560]{2,1,0:T(8,128)}, u32[]{:S(2)}) copy-start(f32[1,192,2560]{2,1,0:T(8,128)} %get-tuple-element.87) | copy-start | bytes 5898244
  (35 other events, 614.5 us)
Sparse Core Ops, SparseCore 0:
  11.7 60.7 all-gather.9
  75.4 141.8 all-gather.11
  220.2 96.7 all-gather.13
  324.1 41.0 reduce-scatter.13
  845.2 32.9 all-gather.23
  974.2 32.9 all-gather.25
Sparse Core Ops, SparseCore 1:
  326.7 140.6 all-gather.17
  469.5 31.0 all-gather.15
  502.7 142.4 all-gather.19
  647.5 140.5 all-gather.21
  801.4 40.9 reduce-scatter.15
  924.7 42.7 reduce-scatter.17
  1160.3 20.4 reduce-scatter.33
  1184.2 169.9 reduce-scatter.27
  1357.7 168.9 reduce-scatter.29
  1530.3 168.9 reduce-scatter.31
  1701.6 41.7 reduce-scatter.19
  1746.4 143.2 reduce-scatter.23
  1892.5 275.8 reduce-scatter.21
  2171.4 281.3 reduce-scatter.25
where the time goes:
time: 2470 us; the launch traced here: 2460 us
  waiting for transfers between devices  1920 us (78%)
  matrix products  271 us (11%)
  other arithmetic  94.5 us (4%)
  blocking collectives  83.2 us (3%)
  local copies, waits for them, and re-layouts  63.9 us (3%)
    reduce_scatter x1, waiting for transfers between devices, local(): lax.psum_scatter(grad_out_full, ('fsdp', 'ctx', 'tp'), scatter_dimension=...  284 us
    reduce_scatter x1, waiting for transfers between devices, local(): lax.psum_scatter(grad_query_full, ('fsdp', 'ctx', 'tp'), scatter_dimensio...  279 us
    reduce_scatter x1, waiting for transfers between devices, local(): lax.psum_scatter(grad_down.astype(jnp.bfloat16), ('fsdp', 'ctx'), scatter...  170 us
    reduce_scatter x1, waiting for transfers between devices, local(): lax.psum_scatter(grad_up.astype(jnp.bfloat16), ('fsdp', 'ctx'), scatter_d...  170 us
    ppermute x6, waiting for transfers between devices, shifted_2(): return lax.ppermute(array, axis, pairs)  136 us
    all_gather x1, waiting for transfers between devices, local(): lax.all_gather(up_weight, ('fsdp', 'ctx'), axis=0, tiled=True)  130 us
    all_gather x1, waiting for transfers between devices, local(): lax.all_gather(down_weight, ('fsdp', 'ctx'), axis=1, tiled=True)  127 us
    all_gather x1, waiting for transfers between devices, local(): lax.all_gather(gate_weight, ('fsdp', 'ctx'), axis=0, tiled=True)  97.4 us
  transfers between devices with their start and end apart: 26, of which 24 were waited for; matrix products, arithmetic and copies ran while one was open for 11% of the time, Pallas kernels for 0%

commit v1 on v0

v1 whole, which is shorter than its diff:
```python
import jax
import jax.numpy as jnp
from jax import lax
from jax.experimental import pallas as pl
from jax.experimental.pallas import tpu as pltpu
from jax.sharding import PartitionSpec as P

W = 2048

epsilon = 1e-06
lowest = -1e30
ROWS = 256
VMEM_BYTES = 40 * 1024 * 1024


def flip(array, axis, bit):
    return lax.ppermute(array, axis, [(i, i ^ bit) for i in range(lax.axis_size(axis))])


def ring(array, axis, by=1):
    count = lax.axis_size(axis)
    return lax.ppermute(array, axis, [(i, (i + by) % count) for i in range(count)])


def shifted(array, axis, by):
    count = lax.axis_size(axis)
    pairs = [(i, i + by) for i in range(count) if 0 <= i + by < count]
    return lax.ppermute(array, axis, pairs)


def low(values):
    return values.astype(jnp.bfloat16)


def wide(values):
    return values.astype(jnp.float32)


def take(array, index, axis=0):
    return lax.dynamic_index_in_dim(array, index, axis, keepdims=False)


def swapped(blocks, rank):
    if len(blocks) == 2:
        odd = rank == 1
        return [jnp.where(odd, blocks[1], blocks[0]), jnp.where(odd, blocks[0], blocks[1])]
    first = swapped(blocks[:2], rank % 2) + swapped(blocks[2:], rank % 2)
    outer = rank // 2 == 1
    return [jnp.where(outer, first[i ^ 2], first[i]) for i in range(4)]


def place(pieces, slots):
    count = len(pieces)
    shape = pieces[0].shape

    def body(slots_ref, *refs):
        out_ref, held, came, left = refs[count:]
        into = [pltpu.make_async_copy(refs[k], held.at[k], came.at[k]) for k in range(count)]
        out_of = [
            pltpu.make_async_copy(held.at[k], out_ref.at[slots_ref[k]], left.at[k])
            for k in range(count)
        ]
        for copy in into:
            copy.start()
        for first, second in zip(into, out_of):
            first.wait()
            second.start()
        for copy in out_of:
            copy.wait()

    return pl.pallas_call(
        body,
        out_shape=jax.ShapeDtypeStruct((count,) + shape, pieces[0].dtype),
        grid_spec=pltpu.PrefetchScalarGridSpec(
            num_scalar_prefetch=1,
            grid=(1,),
            in_specs=[pl.BlockSpec(memory_space=pl.ANY)] * count,
            out_specs=pl.BlockSpec(memory_space=pl.ANY),
            scratch_shapes=[
                pltpu.VMEM((count,) + shape, pieces[0].dtype),
                pltpu.SemaphoreType.DMA((count,)),
                pltpu.SemaphoreType.DMA((count,)),
            ],
        ),
        compiler_params=pltpu.CompilerParams(vmem_limit_bytes=VMEM_BYTES),
        name="place",
    )(jnp.stack(slots).astype(jnp.int32), *pieces)


def nn(first, second):
    return lax.dot_general(
        first, second, (((1,), (0,)), ((), ())), preferred_element_type=jnp.float32
    )


def nt(first, second):
    return lax.dot_general(
        first, second, (((1,), (1,)), ((), ())), preferred_element_type=jnp.float32
    )


def tn(first, second):
    return lax.dot_general(
        first, second, (((0,), (0,)), ((), ())), preferred_element_type=jnp.float32
    )


def ring_sum(block_of, axis):
    count = lax.axis_size(axis)
    rank = lax.axis_index(axis)
    moving = None
    for step in range(1, count):
        term = block_of((rank - step) % count)
        moving = low(term if moving is None else wide(moving) + wide(term))
        moving = ring(moving, axis)
    own = wide(block_of(rank))
    return own if moving is None else own + wide(moving)


def attention_forward(queries, keyvals, live, first_key, head_size):
    rows, columns = queries.shape
    heads = columns // head_size
    reach = W + ROWS
    lead = keyvals.shape[0] - rows - W

    def body(info_ref, q_ref, kv_ref, o_ref):
        head, block = pl.program_id(0), pl.program_id(1)
        start = pl.multiple_of(lead + block * ROWS, ROWS)
        keys = kv_ref[pl.ds(start, reach), :head_size]
        vals = kv_ref[pl.ds(start, reach), head_size:]
        scores = nt(q_ref[...], keys)
        row = lax.broadcasted_iota(jnp.int32, scores.shape, 0)
        column = lax.broadcasted_iota(jnp.int32, scores.shape, 1)
        ahead = column - row
        allowed = (ahead > 0) & (ahead <= W) & (column >= info_ref[0] - start)
        scores = jnp.where(allowed, scores, lowest)
        peak = jnp.max(scores, axis=1, keepdims=True)
        shares = jnp.exp(scores - peak)
        total = jnp.sum(shares, axis=1, keepdims=True)
        probs = low(shares * (1.0 / total))
        mixed = nn(probs, vals)
        o_ref[...] = low(mixed * wide(info_ref[1 + head]))

    return pl.pallas_call(
        body,
        out_shape=jax.ShapeDtypeStruct((rows, columns), jnp.bfloat16),
        grid_spec=pltpu.PrefetchScalarGridSpec(
            num_scalar_prefetch=1,
            grid=(heads, rows // ROWS),
            in_specs=[
                pl.BlockSpec((ROWS, head_size), lambda h, i, info: (i, h)),
                pl.BlockSpec(keyvals.shape, lambda h, i, info: (0, 0)),
            ],
            out_specs=pl.BlockSpec((ROWS, head_size), lambda h, i, info: (i, h)),
        ),
        compiler_params=pltpu.CompilerParams(vmem_limit_bytes=VMEM_BYTES),
        cost_estimate=pl.CostEstimate(
            flops=4 * heads * rows * reach * head_size,
            bytes_accessed=4 * rows * columns + 2 * keyvals.size,
            transcendentals=heads * rows * reach,
        ),
        name="attention_forward",
    )(jnp.concatenate([first_key[None], live]).astype(jnp.int32), queries, keyvals)


def attention_backward(queries, keyvals, d_attended, first_key, head_size):
    rows, columns = queries.shape
    heads = columns // head_size
    reach = W + ROWS
    span = keyvals.shape[0]
    lead = span - rows - W

    def body(info_ref, q_ref, kv_ref, do_ref, dq_ref, dkv_ref, sums):
        head, block = pl.program_id(0), pl.program_id(1)

        @pl.when((head == 0) & (block == 0))
        def _():
            sums[...] = jnp.zeros_like(sums)

        start = pl.multiple_of(lead + block * ROWS, ROWS)
        keys = kv_ref[pl.ds(start, reach), :head_size]
        vals = kv_ref[pl.ds(start, reach), head_size:]
        query = q_ref[...]
        d_out = do_ref[...]
        scores = nt(keys, query)
        column = lax.broadcasted_iota(jnp.int32, scores.shape, 0)
        row = lax.broadcasted_iota(jnp.int32, scores.shape, 1)
        ahead = column - row
        allowed = (ahead > 0) & (ahead <= W) & (column >= info_ref[0] - start)
        scores = jnp.where(allowed, scores, lowest)
        peak = jnp.max(scores, axis=0, keepdims=True)
        shares = jnp.exp(scores - peak)
        total = jnp.sum(shares, axis=0, keepdims=True)
        probs = shares * (1.0 / total)
        d_probs = nt(vals, d_out)
        inner = jnp.sum(probs * d_probs, axis=0, keepdims=True)
        d_scores = low(probs * (d_probs - inner))
        dq_ref[...] = tn(d_scores, keys)
        sums[pl.ds(start, reach), :head_size] += nn(d_scores, query)
        sums[pl.ds(start, reach), head_size:] += nn(low(probs), d_out)

        @pl.when((head == heads - 1) & (block == rows // ROWS - 1))
        def _():
            dkv_ref[...] = low(sums[...])

    return pl.pallas_call(
        body,
        out_shape=(
            jax.ShapeDtypeStruct((rows, columns), jnp.float32),
            jax.ShapeDtypeStruct(keyvals.shape, jnp.bfloat16),
        ),
        grid_spec=pltpu.PrefetchScalarGridSpec(
            num_scalar_prefetch=1,
            grid=(heads, rows // ROWS),
            in_specs=[
                pl.BlockSpec((ROWS, head_size), lambda h, i, info: (i, h)),
                pl.BlockSpec(keyvals.shape, lambda h, i, info: (0, 0)),
                pl.BlockSpec((ROWS, head_size), lambda h, i, info: (i, h)),
            ],
            out_specs=(
                pl.BlockSpec((ROWS, head_size), lambda h, i, info: (i, h)),
                pl.BlockSpec(keyvals.shape, lambda h, i, info: (0, 0)),
            ),
            scratch_shapes=[pltpu.VMEM(keyvals.shape, jnp.float32)],
        ),
        compiler_params=pltpu.CompilerParams(vmem_limit_bytes=VMEM_BYTES),
        cost_estimate=pl.CostEstimate(
            flops=10 * heads * rows * reach * head_size,
            bytes_accessed=8 * rows * columns + 4 * keyvals.size,
            transcendentals=heads * rows * reach,
        ),
        name="attention_backward",
    )(first_key[None].astype(jnp.int32), queries, keyvals, d_attended)


def gelu_tanh(values):
    return jax.nn.gelu(values, approximate=True)


def local(
    hidden,
    lengths,
    teacher,
    attn_gain,
    query_weight,
    kv_weight,
    out_weight,
    mlp_gain,
    gate_weight,
    up_weight,
    down_weight,
):
    tp_count = lax.axis_size("tp")
    ctx_count = lax.axis_size("ctx")
    fsdp_count = lax.axis_size("fsdp")
    tp_rank = lax.axis_index("tp")
    ctx_rank = lax.axis_index("ctx")
    fsdp_rank = lax.axis_index("fsdp")
    y_rank, core_rank = tp_rank // 2, tp_rank % 2
    hi_rank, lo_rank = ctx_rank // 2, ctx_rank % 2
    seq_count, rows, width = hidden.shape
    assert seq_count == 1 and tp_count == 4 and ctx_count == 4
    part_rows = rows // tp_count
    head_size = kv_weight.shape[1] // 2
    head_count = query_weight.shape[1] // head_size
    slot_count = -(-head_count // tp_count)
    slot_width = slot_count * head_size
    fuller = head_count - (slot_count - 1) * tp_count
    kv_width = 2 * head_size // tp_count

    def first_head_of(rank):
        return rank * (slot_count - 1) + jnp.minimum(rank, fuller)

    def slot_base_of(rank):
        return jnp.minimum(first_head_of(rank), head_count - slot_count)

    slot_heads = slot_base_of(tp_rank) + jnp.arange(slot_count)
    first_head = first_head_of(tp_rank)
    held_heads = slot_count - 1 + (tp_rank < fuller).astype(jnp.int32)
    live = ((slot_heads >= first_head) & (slot_heads < first_head + held_heads)).astype(jnp.int32)

    def over_tp(columns_of):
        blocks = [columns_of(tp_rank)]
        for bit in range(1, tp_count):
            blocks.append(flip(columns_of(tp_rank ^ bit), "tp", bit))
        return jnp.concatenate(swapped(blocks, tp_rank), axis=0)

    def over_ctx_and_fsdp(block):
        pieces, slots = [], []
        around = block
        for step in range(ctx_count):
            if step:
                around = ring(around, "ctx")
            across = around
            for turn_at in range(fsdp_count):
                if turn_at:
                    across = ring(across, "fsdp")
                pieces.append(across)
                slots.append(
                    (fsdp_rank - turn_at) % fsdp_count * ctx_count
                    + (ctx_rank - step) % ctx_count
                )
        return place(pieces, slots).reshape(width, block.shape[1])

    def head_columns(weight):
        return lambda rank: lax.dynamic_slice_in_dim(
            weight, slot_base_of(rank) * head_size, slot_width, 1
        )

    gains = jnp.pad(jnp.stack([attn_gain, mlp_gain], axis=1), ((0, 0), (0, 126)))
    kv_and_gains = over_ctx_and_fsdp(
        over_tp(
            lambda rank: jnp.concatenate(
                [lax.dynamic_slice_in_dim(kv_weight, rank * kv_width, kv_width, 1), gains], axis=1
            )
        )
    )
    kv_part = kv_and_gains[:, :kv_width]
    gain_attn = wide(kv_and_gains[:, kv_width])
    gain_mlp = wide(kv_and_gains[:, kv_width + 1])
    query_part = over_ctx_and_fsdp(over_tp(head_columns(query_weight)))
    out_part = over_ctx_and_fsdp(over_tp(head_columns(out_weight)))

    unit_count = gate_weight.shape[1]
    half = -(-unit_count // 256) * 128
    rest = unit_count - half

    def mlp_gather(block):
        near, far = block[:, :half], jnp.pad(block[:, half:], ((0, 0), (0, half - rest)))
        mine = jnp.where(lo_rank == 0, near, far)
        theirs = jnp.where(lo_rank == 0, far, near)
        got = flip(theirs, "ctx", 1)
        pair = jnp.stack(swapped([mine, got], lo_rank))
        pieces, slots = [], []
        for far_bit, around in ((0, pair), (1, flip(pair, "ctx", 2))):
            across = around
            for turn_at in range(fsdp_count):
                if turn_at:
                    across = ring(across, "fsdp")
                pieces.append(across)
                slots.append((fsdp_rank - turn_at) % fsdp_count * 2 + (hi_rank ^ far_bit))
        return place(pieces, slots).reshape(width, half)

    gate_full = mlp_gather(gate_weight)
    up_full = mlp_gather(up_weight)
    down_full = mlp_gather(down_weight.T)

    inputs_low = hidden[0]
    inputs = wide(inputs_low)
    inputs_part_low = lax.dynamic_slice_in_dim(inputs_low, tp_rank * part_rows, part_rows, 0)
    inputs_part = wide(inputs_part_low)
    scale_one = lax.rsqrt(jnp.mean(inputs * inputs, axis=-1, keepdims=True) + epsilon)
    normed = low(inputs * scale_one * gain_attn)
    positions = ctx_rank * rows + jnp.arange(rows)
    quarter = head_size // 4
    frequency = 10000.0 ** (-(jnp.arange(quarter).astype(jnp.float32) * 4.0 / head_size))
    angle = wide(positions)[:, None] * frequency[None, :]
    cosine, sine = jnp.cos(angle), jnp.sin(angle)

    def turn(values, cosine, sine):
        first, second = values[..., :quarter], values[..., quarter : 2 * quarter]
        return jnp.concatenate(
            [
                first * cosine - second * sine,
                second * cosine + first * sine,
                values[..., 2 * quarter :],
            ],
            axis=-1,
        )

    turning = tp_rank == 0
    kv_cosine, kv_sine = jnp.where(turning, cosine, 1.0), jnp.where(turning, sine, 0.0)
    kv_raw = nn(normed, kv_part)
    kv_own = low(turn(kv_raw, kv_cosine, kv_sine))
    reach_back = min((W - 2) // rows + 1, ctx_count - 1)
    chunks = [shifted(kv_own, "ctx", by) for by in range(reach_back, 0, -1)] + [kv_own]
    kv_column = jnp.concatenate(chunks, axis=0)
    kv_pair = jnp.stack([kv_column, flip(kv_column, "tp", 2)])
    kv_other = flip(kv_pair, "tp", 1)
    keyvals = jnp.concatenate(
        swapped([kv_pair[0], kv_other[0], kv_pair[1], kv_other[1]], tp_rank), axis=1
    )
    first_key = (reach_back - jnp.minimum(ctx_rank, reach_back)) * rows

    query_scale = head_size ** (-0.5)
    query_raw = nn(normed, query_part).reshape(rows, slot_count, head_size)
    queries = low(turn(query_raw, cosine[:, None, :], sine[:, None, :]) * query_scale)
    queries = queries.reshape(rows, slot_width)
    attended = attention_forward(queries, keyvals, live, first_key, head_size)

    def tp_sum(partial):
        blocks = partial.reshape(2, 2, part_rows, -1)
        got = flip(take(blocks, 1 - core_rank, 1), "tp", 1)
        summed = wide(take(blocks, core_rank, 1)) + wide(got)
        got = flip(low(take(summed, 1 - y_rank)), "tp", 2)
        return take(summed, y_rank) + wide(got)

    def tp_gather(part):
        pair = jnp.stack([part, flip(part, "tp", 2)])
        other = flip(pair, "tp", 1)
        blocks = swapped([pair[0], other[0], pair[1], other[1]], tp_rank)
        return jnp.concatenate(blocks, axis=0)

    def group_gather(part):
        middle = part_rows // 2
        over_y = flip(part, "tp", 2)
        over_z = flip(part, "ctx", 1)
        corner_top = flip(over_y[:middle], "ctx", 1)
        corner_end = flip(over_z[middle:], "tp", 2)
        near = jnp.concatenate([part, over_y, over_z, corner_top, corner_end], axis=0)
        return jnp.concatenate([near, flip(near, "tp", 1)], axis=0)

    def group_sum(partial):
        blocks = partial.reshape(2, 4, part_rows, -1)
        middle = part_rows // 2
        got = flip(blocks[1], "tp", 1)
        summed = wide(blocks[0]) + wide(got)
        own, over_y, over_z, corner = summed[0], summed[1], summed[2], summed[3]
        top = flip(low(corner[:middle]), "ctx", 1)
        end = flip(low(corner[middle:]), "tp", 2)
        over_y = jnp.concatenate([over_y[:middle] + wide(top), over_y[middle:]], axis=0)
        over_z = jnp.concatenate([over_z[:middle], over_z[middle:] + wide(end)], axis=0)
        return own + wide(flip(low(over_y), "tp", 2)) + wide(flip(low(over_z), "ctx", 1))

    attn_part = tp_sum(low(nt(attended, out_part)))
    residual = inputs_part + attn_part
    scale_two = lax.rsqrt(jnp.mean(residual * residual, axis=-1, keepdims=True) + epsilon)
    normed_two = group_gather(low(residual * scale_two * gain_mlp))
    gate_proj = nn(normed_two, gate_full)
    up_proj = nn(normed_two, up_full)
    activated, gelu_back = jax.vjp(gelu_tanh, gate_proj)
    hidden_act = low(activated * up_proj)
    ffn_part = group_sum(low(nt(hidden_act, down_full)))

    my_length = lengths[fsdp_rank]
    part_positions = ctx_rank * rows + tp_rank * part_rows + jnp.arange(part_rows)
    valid = wide(part_positions < my_length)[:, None]
    output = (residual + ffn_part) * valid
    mismatch = output - wide(teacher[0])
    count = wide(jnp.sum(lengths))
    loss_part = jnp.sum(valid * mismatch * mismatch)
    d_output = valid * mismatch * (lengths.shape[0] * ctx_count * rows / count)

    d_ffn = group_gather(low(d_output))
    d_hidden = nn(d_ffn, down_full)
    d_gate = low(gelu_back(d_hidden * up_proj)[0])
    d_up = low(d_hidden * activated)
    d_normed_two = group_sum(low(nt(d_gate, gate_full) + nt(d_up, up_full)))

    def mlp_scatter(grad):
        blocks = grad.reshape(fsdp_count, 2, 2, -1, half)
        mine = ring_sum(lambda owner: take(blocks, owner), "fsdp")
        got = flip(low(take(mine, 1 - hi_rank)), "ctx", 2)
        mine = take(mine, hi_rank) + wide(got)
        got = flip(low(take(mine, 1 - lo_rank)), "ctx", 1)
        near, far = swapped([take(mine, lo_rank), wide(got)], lo_rank)
        return jnp.concatenate([near, far[:, :rest]], axis=1)

    down_grad = mlp_scatter(tn(d_ffn, hidden_act)).T
    gate_grad = mlp_scatter(tn(normed_two, d_gate))
    up_grad = mlp_scatter(tn(normed_two, d_up))

    def vector_sum(vector):
        for axis, bit in (("tp", 1), ("tp", 2), ("ctx", 1), ("ctx", 2)):
            vector = vector + flip(vector, axis, bit)
        moving = vector
        for _ in range(1, fsdp_count):
            moving = ring(moving, "fsdp")
            vector = vector + moving
        return vector

    own_rows = attn_gain.shape[0]
    own_start = ((fsdp_rank * ctx_count + ctx_rank) * tp_count + tp_rank) * own_rows

    scaled = gain_mlp * d_normed_two
    inner_two = jnp.mean(scaled * residual, axis=-1, keepdims=True)
    d_residual = d_output + scale_two * scaled - residual * scale_two**3 * inner_two
    gain_mlp_sums = jnp.sum(d_normed_two * residual * scale_two, axis=0)
    early = vector_sum(jnp.concatenate([gain_mlp_sums, jnp.full((128,), loss_part)]))
    gain_mlp_grad = lax.dynamic_slice_in_dim(early, own_start, own_rows, 0)
    loss = early[width] / (count * width)

    d_attn = tp_gather(low(d_residual))

    def head_scatter(grad):
        blocks = grad.reshape(fsdp_count, ctx_count, tp_count, own_rows, -1)
        mine = ring_sum(lambda owner: take(blocks, owner), "fsdp")
        mine = ring_sum(lambda owner: take(mine, owner), "ctx")
        parts = [take(mine, tp_rank)]
        for bit in range(1, tp_count):
            parts.append(wide(flip(low(take(mine, tp_rank ^ bit)), "tp", bit)))
        return swapped(parts, tp_rank)

    def whole_heads(parts):
        columns = []
        for rank, part in enumerate(parts):
            first = rank * (slot_count - 1) + min(rank, fuller)
            base = min(first, head_count - slot_count)
            held = slot_count - 1 + (1 if rank < fuller else 0)
            start = (first - base) * head_size
            columns.append(part[:, start : start + held * head_size])
        return jnp.concatenate(columns, axis=1)

    out_grad = whole_heads(head_scatter(tn(d_attn, attended)))
    live_columns = jnp.repeat(live, head_size).astype(jnp.float32)
    d_attended = low(nn(d_attn, out_part) * live_columns)
    d_queries, d_keyvals = attention_backward(queries, keyvals, d_attended, first_key, head_size)
    d_query_raw = turn(
        d_queries.reshape(rows, slot_count, head_size) * query_scale,
        cosine[:, None, :],
        -sine[:, None, :],
    )
    d_query_low = low(d_query_raw.reshape(rows, slot_width))
    query_grad = whole_heads(head_scatter(tn(normed, d_query_low)))

    kv_blocks = jnp.stack(jnp.split(d_keyvals, tp_count, axis=1)).reshape(
        2, 2, -1, kv_width
    )
    got = flip(take(kv_blocks, 1 - core_rank, 1), "tp", 1)
    kv_sum = wide(take(kv_blocks, core_rank, 1)) + wide(got)
    got = flip(low(take(kv_sum, 1 - y_rank)), "tp", 2)
    kv_sum = (take(kv_sum, y_rank) + wide(got)).reshape(reach_back + 1, rows, kv_width)
    d_kv = kv_sum[reach_back]
    for by in range(1, reach_back + 1):
        d_kv = d_kv + wide(shifted(low(kv_sum[reach_back - by]), "ctx", -by))
    d_kv_low = low(turn(d_kv, kv_cosine, -kv_sine))
    kv_parts = head_scatter(tn(normed, d_kv_low))
    kv_grad = jnp.concatenate(kv_parts, axis=1)

    d_normed_partial = nt(d_query_low, query_part) + nt(d_kv_low, kv_part)
    gain_attn_sums = jnp.sum(d_normed_partial * inputs * scale_one, axis=0)
    gain_attn_grad = lax.dynamic_slice_in_dim(vector_sum(gain_attn_sums), own_start, own_rows, 0)
    d_normed = tp_sum(low(d_normed_partial))
    scale_part = lax.dynamic_slice_in_dim(scale_one, tp_rank * part_rows, part_rows, 0)
    scaled = gain_attn * d_normed
    inner_one = jnp.mean(scaled * inputs_part, axis=-1, keepdims=True)
    input_grad = d_residual + scale_part * scaled - inputs_part * scale_part**3 * inner_one
    return (
        low(output)[None],
        loss,
        input_grad[None],
        gain_attn_grad,
        query_grad,
        kv_grad,
        out_grad,
        gain_mlp_grad,
        gate_grad,
        up_grad,
        down_grad,
    )


def solution(mesh):
    in_specs = (
        P("fsdp", "ctx", None),
        P(),
        P("fsdp", ("ctx", "tp"), None),
        P(("fsdp", "ctx", "tp")),
        P(("fsdp", "ctx", "tp"), None),
        P(("fsdp", "ctx", "tp"), None),
        P(("fsdp", "ctx", "tp"), None),
        P(("fsdp", "ctx", "tp")),
        P(("fsdp", "ctx"), "tp"),
        P(("fsdp", "ctx"), "tp"),
        P("tp", ("fsdp", "ctx")),
    )
    out_specs = (
        P("fsdp", ("ctx", "tp"), None),
        P(),
        P("fsdp", ("ctx", "tp"), None),
        P(("fsdp", "ctx", "tp")),
        P(("fsdp", "ctx", "tp"), None),
        P(("fsdp", "ctx", "tp"), None),
        P(("fsdp", "ctx", "tp"), None),
        P(("fsdp", "ctx", "tp")),
        P(("fsdp", "ctx"), "tp"),
        P(("fsdp", "ctx"), "tp"),
        P("tp", ("fsdp", "ctx")),
    )
    return jax.shard_map(local, mesh=mesh, in_specs=in_specs, out_specs=out_specs, check_vma=False)
```

time: 2470 us -> 1290 us (0.52)
  waiting for transfers between devices: 1920 us -> 703 us
  starting transfers between devices: 14.1 us -> 125 us
  matrix products: 271 us -> 161 us
  blocking collectives: 83.2 us -> 0 us
  Pallas kernels: 0 us -> 67.9 us
  local copies, waits for them, and re-layouts: 63.9 us -> 122 us
    reduce_scatter x10 -> x0, waiting for transfers between devices: 1230 us -> none  [the longest x1 284 us: local(): lax.psum_scatter(grad_out_full, ('fsdp', 'ctx', 'tp'), scatter_dimension=...]
    ppermute x6 -> x118, waiting for transfers between devices: 136 us -> 703 us  [the longest x44 345 us: ring(): lax.ppermute(array, axis, [(i, (i + by) % count) for i in range(count)])]
    all_gather x9 -> x0, waiting for transfers between devices: 543 us -> none  [the longest x1 130 us: local(): lax.all_gather(up_weight, ('fsdp', 'ctx'), axis=0, tiled=True)]
    ppermute x6 -> x118, starting transfers between devices: 12.5 us -> 125 us  [the longest x68 56.8 us: flip(): lax.ppermute(array, axis, [(i, i ^ bit) for i in range(lax.axis_size(axis...]
    dot_general x24 -> x18, matrix products: 271 us -> 161 us  [the longest x6 60.3 us: nn(): lax.dot_general(first, second, (((1,), (0,)), ((), ())), preferred_elemen...]
    unnamed x2 -> x0, blocking collectives: 83.2 us -> none
    pallas_call x0 -> x8, Pallas kernels: none -> 67.9 us  [the longest x1 28.1 us: attention_backward(): pl.pallas_call(body, out_shape=(jax.ShapeDtypeStruct((rows, columns), jnp...]
    convert_element_type x16, other arithmetic: 51.8 us -> 6.71 us  [the longest x8 5.57 us: low(): return values.astype(jnp.bfloat16)]
  transfers between devices with their start and end apart: 26 -> 118, of which waited for: 24 -> 60; matrix products, arithmetic and copies ran while one was open for 11% -> 16% of each run, Pallas kernels for 0% -> 4%
where the time goes in v1:
time: 1290 us
  waiting for transfers between devices  703 us (54%)
  matrix products  161 us (12%)
  starting transfers between devices  125 us (10%)
  local copies, waits for them, and re-layouts  122 us (9%)
  other arithmetic  103 us (8%)
  Pallas kernels  67.9 us (5%)
    ppermute x44, waiting for transfers between devices, ring(): lax.ppermute(array, axis, [(i, (i + by) % count) for i in range(count)])  345 us
    ppermute x68, waiting for transfers between devices, flip(): lax.ppermute(array, axis, [(i, i ^ bit) for i in range(lax.axis_size(axis...  330 us
    dot_general x6, matrix products, nn(): lax.dot_general(first, second, (((1,), (0,)), ((), ())), preferred_elemen...  60.3 us
    ppermute x68, starting transfers between devices, flip(): lax.ppermute(array, axis, [(i, i ^ bit) for i in range(lax.axis_size(axis...  56.8 us
    ppermute x44, starting transfers between devices, ring(): lax.ppermute(array, axis, [(i, (i + by) % count) for i in range(count)])  54.5 us
    dot_general x6, matrix products, nt(): lax.dot_general(first, second, (((1,), (1,)), ((), ())), preferred_elemen...  53 us
    dot_general x6, matrix products, tn(): lax.dot_general(first, second, (((0,), (0,)), ((), ())), preferred_elemen...  47.8 us
    unnamed x208, local copies, waits for them, and re-layouts  42.9 us
  transfers between devices with their start and end apart: 118, of which 60 were waited for; matrix products, arithmetic and copies ran while one was open for 16% of the time, Pallas kernels for 4%

profile of v1, /device:TPU:0, one launch (start us, length us, event | category | flops | bytes accessed | tf_op | source)
XLA Modules:
  0.0 1287.3 jit_solution(4273355320698559954)
XLA Ops:
  191.0 18.3 %attention_forward.1 = bf16[768,768]{1,0:T(8,128)(2,1)S(1)} custom-call(s32[4]{0:T(128)S(1)} %pad_add_fusion.info_ref, bf16[768,768]{1,0:T(8,128)(2,1)S(1)} %copy.64.q_ref, bf16[3072,512]{1,0:T(8,128)(2,1)S(1)} %pad_maximum_fusion.1.kv_ref), custom_call_target="tpu_custom_call" | custom-call | flops 5435817984 | bytes 5505024 | tf_op jit(solution)/shard_map/attention_forward/pallas_call | solution.py:144
  232.8 17.9 %collective-permute-done.36 = bf16[192,2560]{1,0:T(8,128)(2,1)S(1)} collective-permute-done((bf16[192,2560]{1,0:T(8,128)(2,1)}, bf16[192,2560]{1,0:T(8,128)(2,1)S(1)}, u32[]{:S(2)}, u32[]{:S(2)}) %collective-permute-start.36) | collective-permute-done | bytes 983072 | tf_op jit(solution)/shard_map/ppermute | solution.py:17
  263.9 14.6 %collective-permute-done.37 = bf16[192,2560]{1,0:T(8,128)(2,1)} collective-permute-done((bf16[192,2560]{1,0:T(8,128)(2,1)S(1)}, bf16[192,2560]{1,0:T(8,128)(2,1)}, u32[]{:S(2)}, u32[]{:S(2)}) %collective-permute-start.37) | collective-permute-done | bytes 983072 | tf_op jit(solution)/shard_map/ppermute | solution.py:17
  282.1 27.8 %collective-permute-done.38 = bf16[192,2560]{1,0:T(8,128)(2,1)} collective-permute-done((bf16[192,2560]{1,0:T(8,128)(2,1)S(1)}, bf16[192,2560]{1,0:T(8,128)(2,1)}, u32[]{:S(2)}, u32[]{:S(2)}) %collective-permute-start.38) | collective-permute-done | bytes 983072 | tf_op jit(solution)/shard_map/ppermute | solution.py:17
  316.7 16.0 %collective-permute-done.39 = bf16[96,2560]{1,0:T(8,128)(2,1)S(1)} collective-permute-done((bf16[96,2560]{1,0:T(8,128)(2,1)S(1)}, bf16[96,2560]{1,0:T(8,128)(2,1)S(1)}, u32[]{:S(2)}, u32[]{:S(2)}) %collective-permute-start.39) | collective-permute-done | bytes 491552 | tf_op jit(solution)/shard_map/ppermute | solution.py:17
  342.4 22.6 %collective-permute-done.50 = bf16[320,1024]{1,0:T(8,128)(2,1)S(1)} collective-permute-done((bf16[320,1024]{1,0:T(8,128)(2,1)S(1)}, bf16[320,1024]{1,0:T(8,128)(2,1)S(1)}, u32[]{:S(2)}, u32[]{:S(2)}) %collective-permute-start.50) | collective-permute-done | bytes 655392 | tf_op jit(solution)/shard_map/ppermute | solution.py:17
  373.4 57.8 %collective-permute-done.48.refs_2_ = bf16[2,320,1024]{2,1,0:T(8,128)(2,1)} collective-permute-done((bf16[2,320,1024]{2,1,0:T(8,128)(2,1)S(1)}, bf16[2,320,1024]{2,1,0:T(8,128)(2,1)}, u32[]{:S(2)}, u32[]{:S(2)}) %collective-permute-start.48) | collective-permute-done | bytes 1310752 | tf_op jit(solution)/shard_map/ppermute | solution.py:17
  432.0 26.3 %collective-permute-done.52.refs_2_ = bf16[2,320,1024]{2,1,0:T(8,128)(2,1)} collective-permute-done((bf16[2,320,1024]{2,1,0:T(8,128)(2,1)}, bf16[2,320,1024]{2,1,0:T(8,128)(2,1)}, u32[]{:S(2)}, u32[]{:S(2)}) %collective-permute-start.52) | collective-permute-done | bytes 1310752 | tf_op jit(solution)/shard_map/ppermute | solution.py:17
  470.9 19.4 %collective-permute-done.51.refs_1_ = bf16[2,320,1024]{2,1,0:T(8,128)(2,1)} collective-permute-done((bf16[2,320,1024]{2,1,0:T(8,128)(2,1)}, bf16[2,320,1024]{2,1,0:T(8,128)(2,1)}, u32[]{:S(2)}, u32[]{:S(2)}) %collective-permute-start.51) | collective-permute-done | bytes 1310752 | tf_op jit(solution)/shard_map/ppermute | solution.py:22
  490.4 26.2 %collective-permute-done.53.refs_3_ = bf16[2,320,1024]{2,1,0:T(8,128)(2,1)} collective-permute-done((bf16[2,320,1024]{2,1,0:T(8,128)(2,1)}, bf16[2,320,1024]{2,1,0:T(8,128)(2,1)}, u32[]{:S(2)}, u32[]{:S(2)}) %collective-permute-start.53) | collective-permute-done | bytes 1310752 | tf_op jit(solution)/shard_map/ppermute | solution.py:22
  526.0 12.9 %fusion.109 = f32[1536,1024]{1,0:T(8,128)} fusion(bf16[1536,2560]{1,0:T(8,128)(2,1)} %constant_dynamic-update-slice_fusion.5, bf16[2560,1024]{1,0:T(8,128)(2,1)S(1)} %bitcast.450), kind=kOutput, calls=%fused_computation.380 | convolution fusion | flops 8053063680 | bytes 19398656 | tf_op jit(solution)/shard_map/dot_general | solution.py:91
  539.0 12.7 multiply_convert_fusion.1
  551.7 12.6 convolution_convert_fusion
  581.8 12.0 collective-permute-done.55
  601.5 16.8 %collective-permute-done.58 = bf16[192,2560]{1,0:T(8,128)(2,1)} collective-permute-done((bf16[192,2560]{1,0:T(8,128)(2,1)}, bf16[192,2560]{1,0:T(8,128)(2,1)}, u32[]{:S(2)}, u32[]{:S(2)}) %collective-permute-start.58) | collective-permute-done | bytes 983072 | tf_op jit(solution)/shard_map/ppermute | solution.py:17
  627.5 19.5 %collective-permute-done.59 = bf16[192,2560]{1,0:T(8,128)(2,1)S(1)} collective-permute-done((bf16[192,2560]{1,0:T(8,128)(2,1)S(1)}, bf16[192,2560]{1,0:T(8,128)(2,1)S(1)}, u32[]{:S(2)}, u32[]{:S(2)}) %collective-permute-start.59) | collective-permute-done | bytes 983072 | tf_op jit(solution)/shard_map/ppermute | solution.py:17
  674.7 19.0 %fusion.16 = (bf16[1536,1024]{1,0:T(8,128)(2,1)S(1)}, bf16[1536,1024]{1,0:T(8,128)(2,1)S(1)}) fusion(f32[1536,1024]{1,0:T(8,128)} %fusion.109, f32[1536,1024]{1,0:T(8,128)} %get-tuple-element.174, bf16[1536,2560]{1,0:T(8,128)(2,1)} %constant_dynamic-update-slice_fusion.16, bf16[2560,1024]{1,0:T(8,128)(2,1)} %bitcast.459), kind=kOutput, calls=%fused_computation.24 | convolution fusion | flops 8090812416 | bytes 31981568 | tf_op jit(solution)/shard_map/dot_general | solution.py:91
  704.9 13.3 %fusion.112 = f32[2560,1024]{1,0:T(8,128)} fusion(bf16[1536,2560]{1,0:T(8,128)(2,1)} %constant_dynamic-update-slice_fusion.5, bf16[1536,1024]{1,0:T(8,128)(2,1)S(1)} %get-tuple-element.49), kind=kOutput, calls=%fused_computation.383 | convolution fusion | flops 8053063680 | bytes 21495808 | tf_op jit(solution)/shard_map/dot_general | solution.py:103
  718.1 15.2 %add_convert_fusion = bf16[1536,2560]{1,0:T(8,128)(2,1)} fusion(f32[1536,2560]{1,0:T(8,128)} %fusion.110, bf16[1536,1024]{1,0:T(8,128)(2,1)} %copy-done.92, bf16[2560,1024]{1,0:T(8,128)(2,1)S(1)} %bitcast.453), kind=kOutput, calls=%fused_computation | convolution fusion | flops 8060928000 | bytes 31981568 | tf_op jit(solution)/shard_map/dot_general | solution.py:97
  742.0 12.0 fusion.113
  760.3 12.2 fusion.114
  777.2 24.1 %collective-permute-done.109 = bf16[2,2,320,1024]{3,2,1,0:T(8,128)(2,1)S(1)} collective-permute-done((bf16[2,2,320,1024]{3,2,1,0:T(8,128)(2,1)S(1)}, bf16[2,2,320,1024]{3,2,1,0:T(8,128)(2,1)S(1)}, u32[]{:S(2)}, u32[]{:S(2)}) %collective-permute-start.109) | collective-permute-done | bytes 2621472 | tf_op jit(solution)/shard_map/ppermute | solution.py:22
  813.0 44.5 %collective-permute-done.112 = bf16[2,2,320,1024]{3,2,1,0:T(8,128)(2,1)} collective-permute-done((bf16[2,2,320,1024]{3,2,1,0:T(8,128)(2,1)}, bf16[2,2,320,1024]{3,2,1,0:T(8,128)(2,1)}, u32[]{:S(2)}, u32[]{:S(2)}) %collective-permute-start.112) | collective-permute-done | bytes 2621472 | tf_op jit(solution)/shard_map/ppermute | solution.py:22
  866.9 46.0 %collective-permute-done.115 = bf16[2,2,320,1024]{3,2,1,0:T(8,128)(2,1)} collective-permute-done((bf16[2,2,320,1024]{3,2,1,0:T(8,128)(2,1)}, bf16[2,2,320,1024]{3,2,1,0:T(8,128)(2,1)}, u32[]{:S(2)}, u32[]{:S(2)}) %collective-permute-start.115) | collective-permute-done | bytes 2621472 | tf_op jit(solution)/shard_map/ppermute | solution.py:22
  935.0 47.2 %collective-permute-done.116 = bf16[2,320,1024]{2,1,0:T(8,128)(2,1)} collective-permute-done((bf16[2,320,1024]{2,1,0:T(8,128)(2,1)}, bf16[2,320,1024]{2,1,0:T(8,128)(2,1)}, u32[]{:S(2)}, u32[]{:S(2)}) %collective-permute-start.116) | collective-permute-done | bytes 1310752 | tf_op jit(solution)/shard_map/ppermute | solution.py:17
  987.0 13.3 %collective-permute-done.117 = bf16[320,1024]{1,0:T(8,128)(2,1)S(1)} collective-permute-done((bf16[320,1024]{1,0:T(8,128)(2,1)S(1)}, bf16[320,1024]{1,0:T(8,128)(2,1)S(1)}, u32[]{:S(2)}, u32[]{:S(2)}) %collective-permute-start.117) | collective-permute-done | bytes 655392 | tf_op jit(solution)/shard_map/ppermute | solution.py:17
  1017.6 28.1 %attention_backward.1 = (f32[768,768]{1,0:T(8,128)S(1)}, bf16[3072,512]{1,0:T(8,128)(2,1)S(1)}) custom-call(s32[1]{0:T(128)} %bitcast.1.info_ref, bf16[768,768]{1,0:T(8,128)(2,1)S(1)} %copy-done.18, bf16[3072,512]{1,0:T(8,128)(2,1)S(1)} %copy-done.10, bf16[768,768]{1,0:T(8,128)(2,1)S(1)} %multiply_convert_fusion.2.do_ref), custom_call_target="tpu_custom_call" | custom-call | flops 13589544960 | bytes 11010048 | tf_op jit(solution)/shard_map/attention_backward/pallas_call | solution.py:206
  1067.1 31.7 %collective-permute-done.102 = bf16[4,4,80,768]{3,2,1,0:T(8,128)(2,1)} collective-permute-done((bf16[4,4,80,768]{3,2,1,0:T(8,128)(2,1)}, bf16[4,4,80,768]{3,2,1,0:T(8,128)(2,1)}, u32[]{:S(2)}, u32[]{:S(2)}) %collective-permute-start.102) | collective-permute-done | bytes 1966112 | tf_op jit(solution)/shard_map/ppermute | solution.py:22
  1122.4 16.9 %collective-permute-done.79 = bf16[768,128]{1,0:T(8,128)(2,1)S(1)} collective-permute-done((bf16[768,128]{1,0:T(8,128)(2,1)S(1)}, bf16[768,128]{1,0:T(8,128)(2,1)S(1)}, u32[]{:S(2)}, u32[]{:S(2)}) %collective-permute-start.79) | collective-permute-done | bytes 196640 | tf_op jit(solution)/shard_map/ppermute | solution.py:28
  1197.8 25.6 %collective-permute-done.87 = f32[2560]{0:T(1024)S(1)} collective-permute-done((f32[2560]{0:T(1024)S(1)}, f32[2560]{0:T(1024)S(1)}, u32[]{:S(2)}, u32[]{:S(2)}) %collective-permute-start.87) | collective-permute-done | bytes 10272 | tf_op jit(solution)/shard_map/ppermute | solution.py:22
  1249.0 14.0 %collective-permute-done.90 = bf16[4,80,768]{2,1,0:T(8,128)(2,1)S(1)} collective-permute-done((bf16[4,80,768]{2,1,0:T(8,128)(2,1)S(1)}, bf16[4,80,768]{2,1,0:T(8,128)(2,1)S(1)}, u32[]{:S(2)}, u32[]{:S(2)}) %collective-permute-start.90) | collective-permute-done | bytes 491552 | tf_op jit(solution)/shard_map/ppermute | solution.py:22
  1264.6 11.9 collective-permute-done.91
  (621 shorter events, 573.2 us)
Async XLA Ops:
  12.5 47.1 %collective-permute-start.25 = (bf16[80,768]{1,0:T(8,128)(2,1)}, bf16[80,768]{1,0:T(8,128)(2,1)}, u32[]{:S(2)}, u32[]{:S(2)}) collective-permute-start(bf16[80,768]{1,0:T(8,128)(2,1)} %get-tuple-element.140), channel_id=1, source_target_pairs={{0,3},{1,2},{2,1},{3,0},{4,7},{5,6},{6,5},{7,4},{8,11},{9,10},{10,... | collective-permute-start | bytes 368648 | tf_op jit(solution)/shard_map/ppermute | solution.py:17
  123.9 63.2 %collective-permute-start.24 = (bf16[2,3072,128]{2,1,0:T(8,128)(2,1)}, bf16[2,3072,128]{2,1,0:T(8,128)(2,1)}, u32[]{:S(2)}, u32[]{:S(2)}) collective-permute-start(bf16[2,3072,128]{2,1,0:T(8,128)(2,1)} %pad_maximum_fusion.6), channel_id=1, source_target_pairs={{0,1},{1,0},{2,3},{3,2},{4,5},{5,4},{6,7},{7,6},{8,9},{9,8},{10,11... | collective-permute-start | bytes 4718600 | tf_op jit(solution)/shard_map/ppermute | solution.py:17
  256.6 53.3 %collective-permute-start.38 = (bf16[192,2560]{1,0:T(8,128)(2,1)S(1)}, bf16[192,2560]{1,0:T(8,128)(2,1)}, u32[]{:S(2)}, u32[]{:S(2)}) collective-permute-start(bf16[192,2560]{1,0:T(8,128)(2,1)S(1)} %get-tuple-element.46), channel_id=1, source_target_pairs={{0,4},{4,0},{8,12},{12,8},{1,5},{5,1},{9,13},{13,9},{2,6},{6,2},{1... | collective-permute-start | bytes 2949128 | tf_op jit(solution)/shard_map/ppermute | solution.py:17
  259.2 81.5 %collective-permute-start.46 = (bf16[320,1024]{1,0:T(8,128)(2,1)S(1)}, bf16[320,1024]{1,0:T(8,128)(2,1)}, u32[]{:S(2)}, u32[]{:S(2)}) collective-permute-start(bf16[320,1024]{1,0:T(8,128)(2,1)S(1)} %broadcast_select_fusion.19), channel_id=1, source_target_pairs={{0,4},{4,0},{8,12},{12,8},{1,5},{5,1},{9,13},{13,9},{2,6},{6,2},{1... | collective-permute-start | bytes 1966088 | tf_op jit(solution)/shard_map/ppermute | solution.py:17
  262.0 105.3 %collective-permute-start.44 = (bf16[2,320,1024]{2,1,0:T(8,128)(2,1)S(1)}, bf16[2,320,1024]{2,1,0:T(8,128)(2,1)S(1)}, u32[]{:S(2)}, u32[]{:S(2)}) collective-permute-start(bf16[2,320,1024]{2,1,0:T(8,128)(2,1)S(1)} %pad_maximum_fusion.7.refs_0_), channel_id=1, source_target_pairs={{0,8},{4,12},{8,0},{12,4},{1,9},{5,13},{9,1},{13,5},{2,10},{6,14},... | collective-permute-start | bytes 3932168 | tf_op jit(solution)/shard_map/ppermute | solution.py:17
  279.6 53.1 %collective-permute-start.39 = (bf16[96,2560]{1,0:T(8,128)(2,1)S(1)}, bf16[96,2560]{1,0:T(8,128)(2,1)S(1)}, u32[]{:S(2)}, u32[]{:S(2)}) collective-permute-start(bf16[96,2560]{1,0:T(8,128)(2,1)S(1)} %slice.312), channel_id=1, source_target_pairs={{0,4},{4,0},{8,12},{12,8},{1,5},{5,1},{9,13},{13,9},{2,6},{6,2},{1... | collective-permute-start | bytes 1474568 | tf_op jit(solution)/shard_map/ppermute | solution.py:17
  337.6 182.2 %collective-permute-start.41 = (bf16[768,2560]{1,0:T(8,128)(2,1)}, bf16[768,2560]{1,0:T(8,128)(2,1)}, u32[]{:S(2)}, u32[]{:S(2)}) collective-permute-start(bf16[768,2560]{1,0:T(8,128)(2,1)} %get-tuple-element.134), channel_id=1, source_target_pairs={{0,1},{1,0},{2,3},{3,2},{4,5},{5,4},{6,7},{7,6},{8,9},{9,8},{10,11... | collective-permute-start | bytes 11796488 | tf_op jit(solution)/shard_map/ppermute | solution.py:17
  342.3 88.9 %collective-permute-start.48 = (bf16[2,320,1024]{2,1,0:T(8,128)(2,1)S(1)}, bf16[2,320,1024]{2,1,0:T(8,128)(2,1)}, u32[]{:S(2)}, u32[]{:S(2)}) collective-permute-start(bf16[2,320,1024]{2,1,0:T(8,128)(2,1)S(1)} %pad_maximum_fusion.8.refs_0_), channel_id=1, source_target_pairs={{0,8},{4,12},{8,0},{12,4},{1,9},{5,13},{9,1},{13,5},{2,10},{6,14},... | collective-permute-start | bytes 3932168 | tf_op jit(solution)/shard_map/ppermute | solution.py:17
  366.6 91.8 %collective-permute-start.52 = (bf16[2,320,1024]{2,1,0:T(8,128)(2,1)}, bf16[2,320,1024]{2,1,0:T(8,128)(2,1)}, u32[]{:S(2)}, u32[]{:S(2)}) collective-permute-start(bf16[2,320,1024]{2,1,0:T(8,128)(2,1)} %pad_maximum_fusion.9.refs_0_), channel_id=1, source_target_pairs={{0,8},{4,12},{8,0},{12,4},{1,9},{5,13},{9,1},{13,5},{2,10},{6,14},... | collective-permute-start | bytes 3932168 | tf_op jit(solution)/shard_map/ppermute | solution.py:17
  367.3 91.9 %collective-permute-start.45 = (bf16[2,320,1024]{2,1,0:T(8,128)(2,1)S(1)}, bf16[2,320,1024]{2,1,0:T(8,128)(2,1)S(1)}, u32[]{:S(2)}, u32[]{:S(2)}) collective-permute-start(bf16[2,320,1024]{2,1,0:T(8,128)(2,1)S(1)} %collective-permute-done.44.refs_2_), channel_id=1, source_target_pairs={{0,16},{16,0},{1,17},{17,1},{2,18},{18,2},{3,19},{19,3},{4,20},{20... | collective-permute-start | bytes 3932168 | tf_op jit(solution)/shard_map/ppermute | solution.py:22
  372.2 94.6 %collective-permute-start.47 = (bf16[2,320,1024]{2,1,0:T(8,128)(2,1)S(1)}, bf16[2,320,1024]{2,1,0:T(8,128)(2,1)}, u32[]{:S(2)}, u32[]{:S(2)}) collective-permute-start(bf16[2,320,1024]{2,1,0:T(8,128)(2,1)S(1)} %pad_maximum_fusion.8.refs_0_), channel_id=1, source_target_pairs={{0,16},{16,0},{1,17},{17,1},{2,18},{18,2},{3,19},{19,3},{4,20},{20... | collective-permute-start | bytes 3932168 | tf_op jit(solution)/shard_map/ppermute | solution.py:22
  460.2 56.3 %collective-permute-start.53 = (bf16[2,320,1024]{2,1,0:T(8,128)(2,1)}, bf16[2,320,1024]{2,1,0:T(8,128)(2,1)}, u32[]{:S(2)}, u32[]{:S(2)}) collective-permute-start(bf16[2,320,1024]{2,1,0:T(8,128)(2,1)} %collective-permute-done.52.refs_2_), channel_id=1, source_target_pairs={{0,16},{16,0},{1,17},{17,1},{2,18},{18,2},{3,19},{19,3},{4,20},{20... | collective-permute-start | bytes 3932168 | tf_op jit(solution)/shard_map/ppermute | solution.py:22
  738.3 65.8 %collective-permute-start.64 = (bf16[4,192,2560]{2,1,0:T(8,128)(2,1)}, bf16[4,192,2560]{2,1,0:T(8,128)(2,1)}, u32[]{:S(2)}, u32[]{:S(2)}) collective-permute-start(bf16[4,192,2560]{2,1,0:T(8,128)(2,1)} %bitcast.57), channel_id=1, source_target_pairs={{0,1},{1,0},{2,3},{3,2},{4,5},{5,4},{6,7},{7,6},{8,9},{9,8},{10,11... | collective-permute-start | bytes 11796488 | tf_op jit(solution)/shard_map/ppermute | solution.py:17
  741.4 59.8 %collective-permute-start.109 = (bf16[2,2,320,1024]{3,2,1,0:T(8,128)(2,1)S(1)}, bf16[2,2,320,1024]{3,2,1,0:T(8,128)(2,1)S(1)}, u32[]{:S(2)}, u32[]{:S(2)}) collective-permute-start(bf16[2,2,320,1024]{3,2,1,0:T(8,128)(2,1)S(1)} %fusion.22), channel_id=1, source_target_pairs={{0,16},{16,0},{1,17},{17,1},{2,18},{18,2},{3,19},{19,3},{4,20},{20... | collective-permute-start | bytes 7864328 | tf_op jit(solution)/shard_map/ppermute | solution.py:22
  758.8 98.7 %collective-permute-start.112 = (bf16[2,2,320,1024]{3,2,1,0:T(8,128)(2,1)}, bf16[2,2,320,1024]{3,2,1,0:T(8,128)(2,1)}, u32[]{:S(2)}, u32[]{:S(2)}) collective-permute-start(bf16[2,2,320,1024]{3,2,1,0:T(8,128)(2,1)} %fusion.23), channel_id=1, source_target_pairs={{0,16},{16,0},{1,17},{17,1},{2,18},{18,2},{3,19},{19,3},{4,20},{20... | collective-permute-start | bytes 7864328 | tf_op jit(solution)/shard_map/ppermute | solution.py:22
  774.7 138.2 %collective-permute-start.115 = (bf16[2,2,320,1024]{3,2,1,0:T(8,128)(2,1)}, bf16[2,2,320,1024]{3,2,1,0:T(8,128)(2,1)}, u32[]{:S(2)}, u32[]{:S(2)}) collective-permute-start(bf16[2,2,320,1024]{3,2,1,0:T(8,128)(2,1)} %fusion.24), channel_id=1, source_target_pairs={{0,16},{16,0},{1,17},{17,1},{2,18},{18,2},{3,19},{19,3},{4,20},{20... | collective-permute-start | bytes 7864328 | tf_op jit(solution)/shard_map/ppermute | solution.py:22
  803.4 120.2 %collective-permute-start.110 = (bf16[2,320,1024]{2,1,0:T(8,128)(2,1)}, bf16[2,320,1024]{2,1,0:T(8,128)(2,1)}, u32[]{:S(2)}, u32[]{:S(2)}) collective-permute-start(bf16[2,320,1024]{2,1,0:T(8,128)(2,1)} %fusion.41), channel_id=1, source_target_pairs={{0,8},{4,12},{8,0},{12,4},{1,9},{5,13},{9,1},{13,5},{2,10},{6,14},... | collective-permute-start | bytes 3932168 | tf_op jit(solution)/shard_map/ppermute | solution.py:17
  811.0 52.6 %collective-permute-start.65 = (bf16[96,2560]{1,0:T(8,128)(2,1)S(1)}, bf16[96,2560]{1,0:T(8,128)(2,1)S(1)}, u32[]{:S(2)}, u32[]{:S(2)}) collective-permute-start(bf16[96,2560]{1,0:T(8,128)(2,1)S(1)} %get-tuple-element.70), channel_id=1, source_target_pairs={{0,4},{4,0},{8,12},{12,8},{1,5},{5,1},{9,13},{13,9},{2,6},{6,2},{1... | collective-permute-start | bytes 1474568 | tf_op jit(solution)/shard_map/ppermute | solution.py:17
  812.1 51.5 %collective-permute-start.67 = (bf16[96,2560]{1,0:T(8,128)(2,1)S(1)}, bf16[96,2560]{1,0:T(8,128)(2,1)S(1)}, u32[]{:S(2)}, u32[]{:S(2)}) collective-permute-start(bf16[96,2560]{1,0:T(8,128)(2,1)S(1)} %get-tuple-element.71), channel_id=1, source_target_pairs={{0,2},{1,3},{2,0},{3,1},{4,6},{5,7},{6,4},{7,5},{8,10},{9,11},{10,... | collective-permute-start | bytes 1474568 | tf_op jit(solution)/shard_map/ppermute | solution.py:17
  863.0 68.9 %collective-permute-start.113 = (bf16[2,320,1024]{2,1,0:T(8,128)(2,1)}, bf16[2,320,1024]{2,1,0:T(8,128)(2,1)}, u32[]{:S(2)}, u32[]{:S(2)}) collective-permute-start(bf16[2,320,1024]{2,1,0:T(8,128)(2,1)} %fusion.42), channel_id=1, source_target_pairs={{0,8},{4,12},{8,0},{12,4},{1,9},{5,13},{9,1},{13,5},{2,10},{6,14},... | collective-permute-start | bytes 3932168 | tf_op jit(solution)/shard_map/ppermute | solution.py:17
  864.9 62.6 %collective-permute-start.68 = (bf16[192,2560]{1,0:T(8,128)(2,1)}, bf16[192,2560]{1,0:T(8,128)(2,1)S(1)}, u32[]{:S(2)}, u32[]{:S(2)}) collective-permute-start(bf16[192,2560]{1,0:T(8,128)(2,1)} %pad_maximum_fusion.14), channel_id=1, source_target_pairs={{0,4},{4,0},{8,12},{12,8},{1,5},{5,1},{9,13},{13,9},{2,6},{6,2},{1... | collective-permute-start | bytes 2949128 | tf_op jit(solution)/shard_map/ppermute | solution.py:17
  866.0 61.5 %collective-permute-start.66 = (bf16[192,2560]{1,0:T(8,128)(2,1)S(1)}, bf16[192,2560]{1,0:T(8,128)(2,1)S(1)}, u32[]{:S(2)}, u32[]{:S(2)}) collective-permute-start(bf16[192,2560]{1,0:T(8,128)(2,1)S(1)} %pad_maximum_fusion.13), channel_id=1, source_target_pairs={{0,2},{1,3},{2,0},{3,1},{4,6},{5,7},{6,4},{7,5},{8,10},{9,11},{10,... | collective-permute-start | bytes 2949128 | tf_op jit(solution)/shard_map/ppermute | solution.py:17
  922.8 59.4 %collective-permute-start.116 = (bf16[2,320,1024]{2,1,0:T(8,128)(2,1)}, bf16[2,320,1024]{2,1,0:T(8,128)(2,1)}, u32[]{:S(2)}, u32[]{:S(2)}) collective-permute-start(bf16[2,320,1024]{2,1,0:T(8,128)(2,1)} %fusion.43), channel_id=1, source_target_pairs={{0,8},{4,12},{8,0},{12,4},{1,9},{5,13},{9,1},{13,5},{2,10},{6,14},... | collective-permute-start | bytes 3932168 | tf_op jit(solution)/shard_map/ppermute | solution.py:17
  926.4 57.7 %collective-permute-start.111 = (bf16[320,1024]{1,0:T(8,128)(2,1)}, bf16[320,1024]{1,0:T(8,128)(2,1)S(1)}, u32[]{:S(2)}, u32[]{:S(2)}) collective-permute-start(bf16[320,1024]{1,0:T(8,128)(2,1)} %fusion.63), channel_id=1, source_target_pairs={{0,4},{4,0},{8,12},{12,8},{1,5},{5,1},{9,13},{13,9},{2,6},{6,2},{1... | collective-permute-start | bytes 1966088 | tf_op jit(solution)/shard_map/ppermute | solution.py:17
  931.0 53.5 %collective-permute-start.74 = (bf16[192,2560]{1,0:T(8,128)(2,1)S(1)}, bf16[192,2560]{1,0:T(8,128)(2,1)S(1)}, u32[]{:S(2)}, u32[]{:S(2)}) collective-permute-start(bf16[192,2560]{1,0:T(8,128)(2,1)S(1)} %get-tuple-element.37), channel_id=1, source_target_pairs={{0,2},{1,3},{2,0},{3,1},{4,6},{5,7},{6,4},{7,5},{8,10},{9,11},{10,... | collective-permute-start | bytes 2949128 | tf_op jit(solution)/shard_map/ppermute | solution.py:17
  933.9 50.9 %collective-permute-start.114 = (bf16[320,1024]{1,0:T(8,128)(2,1)S(1)}, bf16[320,1024]{1,0:T(8,128)(2,1)S(1)}, u32[]{:S(2)}, u32[]{:S(2)}) collective-permute-start(bf16[320,1024]{1,0:T(8,128)(2,1)S(1)} %fusion.64), channel_id=1, source_target_pairs={{0,4},{4,0},{8,12},{12,8},{1,5},{5,1},{9,13},{13,9},{2,6},{6,2},{1... | collective-permute-start | bytes 1966088 | tf_op jit(solution)/shard_map/ppermute | solution.py:17
  1009.9 46.7 %collective-permute-start.72 = (f32[2688]{0:T(1024)S(1)}, f32[2688]{0:T(1024)S(1)}, u32[]{:S(2)}, u32[]{:S(2)}) collective-permute-start(f32[2688]{0:T(1024)S(1)} %add.677), channel_id=1, source_target_pairs={{0,8},{4,12},{8,0},{12,4},{1,9},{5,13},{9,1},{13,5},{2,10},{6,14},... | collective-permute-start | bytes 32264 | tf_op jit(solution)/shard_map/ppermute | solution.py:17
  1053.7 45.1 %collective-permute-start.102 = (bf16[4,4,80,768]{3,2,1,0:T(8,128)(2,1)}, bf16[4,4,80,768]{3,2,1,0:T(8,128)(2,1)}, u32[]{:S(2)}, u32[]{:S(2)}) collective-permute-start(bf16[4,4,80,768]{3,2,1,0:T(8,128)(2,1)} %fusion.32), channel_id=1, source_target_pairs={{0,16},{16,0},{1,17},{17,1},{2,18},{18,2},{3,19},{19,3},{4,20},{20... | collective-permute-start | bytes 5898248 | tf_op jit(solution)/shard_map/ppermute | solution.py:22
  1056.5 136.9 %collective-permute-start.73 = (f32[2688]{0:T(1024)S(1)}, f32[2688]{0:T(1024)S(1)}, u32[]{:S(2)}, u32[]{:S(2)}) collective-permute-start(f32[2688]{0:T(1024)S(1)} %add.678), channel_id=1, source_target_pairs={{0,16},{16,0},{1,17},{17,1},{2,18},{18,2},{3,19},{19,3},{4,20},{20... | collective-permute-start | bytes 32264 | tf_op jit(solution)/shard_map/ppermute | solution.py:22
  1118.3 68.8 %collective-permute-start.104 = (bf16[4,80,768]{2,1,0:T(8,128)(2,1)S(1)}, bf16[4,80,768]{2,1,0:T(8,128)(2,1)S(1)}, u32[]{:S(2)}, u32[]{:S(2)}) collective-permute-start(bf16[4,80,768]{2,1,0:T(8,128)(2,1)S(1)} %fusion.58), channel_id=1, source_target_pairs={{0,4},{4,8},{8,12},{12,0},{1,5},{5,9},{9,13},{13,1},{2,6},{6,10},{... | collective-permute-start | bytes 1474568 | tf_op jit(solution)/shard_map/ppermute | solution.py:22
  1178.7 51.8 %collective-permute-start.88 = (bf16[4,4,80,768]{3,2,1,0:T(8,128)(2,1)}, bf16[4,4,80,768]{3,2,1,0:T(8,128)(2,1)S(1)}, u32[]{:S(2)}, u32[]{:S(2)}) collective-permute-start(bf16[4,4,80,768]{3,2,1,0:T(8,128)(2,1)} %fusion.31), channel_id=1, source_target_pairs={{0,16},{16,0},{1,17},{17,1},{2,18},{18,2},{3,19},{19,3},{4,20},{20... | collective-permute-start | bytes 5898248 | tf_op jit(solution)/shard_map/ppermute | solution.py:22
  1184.1 49.7 %collective-permute-start.81 = (bf16[2,192,2560]{2,1,0:T(8,128)(2,1)}, bf16[2,192,2560]{2,1,0:T(8,128)(2,1)}, u32[]{:S(2)}, u32[]{:S(2)}) collective-permute-start(bf16[2,192,2560]{2,1,0:T(8,128)(2,1)} %dynamic-slice_bitcast_fusion), channel_id=1, source_target_pairs={{0,1},{1,0},{2,3},{3,2},{4,5},{5,4},{6,7},{7,6},{8,9},{9,8},{10,11... | collective-permute-start | bytes 5898248 | tf_op jit(solution)/shard_map/ppermute | solution.py:17
  (185 other events, 3786.7 us)

commit v2 on v1

--- a/solution.py
+++ b/solution.py
@@ -14,18 +14,68 @@
 
 
 def flip(array, axis, bit):
-    return lax.ppermute(array, axis, [(i, i ^ bit) for i in range(lax.axis_size(axis))])
+    link = Chain.link(axis, bit)
+    array = Chain.before(array, link)
+    got = lax.ppermute(array, axis, [(i, i ^ bit) for i in range(lax.axis_size(axis))])
+    return Chain.done(got, link)
 
 
 def ring(array, axis, by=1):
     count = lax.axis_size(axis)
-    return lax.ppermute(array, axis, [(i, (i + by) % count) for i in range(count)])
+    link = Chain.link(axis, 2)
+    array = Chain.before(array, link)
+    got = lax.ppermute(array, axis, [(i, (i + by) % count) for i in range(count)])
+    return Chain.done(got, link)
 
 
 def shifted(array, axis, by):
     count = lax.axis_size(axis)
     pairs = [(i, i + by) for i in range(count) if 0 <= i + by < count]
     return lax.ppermute(array, axis, pairs)
+
+
+class Chain:
+    on = ()
+    sent = {}
+
+    @staticmethod
+    def link(axis, bit=1):
+        if axis == "fsdp":
+            return "x"
+        if axis == "tp":
+            return "y" if bit > 1 else None
+        return "z" if bit != 1 else "zl"
+
+    @staticmethod
+    def before(array, link):
+        if link in Chain.on and len(Chain.sent.setdefault(link, [])) >= 1:
+            array = after(array, Chain.sent[link][-1])
+        return array
+
+    @staticmethod
+    def done(got, link):
+        Chain.sent.setdefault(link, []).append(got)
+        return got
+
+
+class Steps:
+    on = True
+
+    def next(self):
+        if not Steps.on:
+            return
+        self.__dict__.update(lax.optimization_barrier(dict(self.__dict__)))
+
+    def drop(self, *names):
+        return [self.__dict__.pop(name) for name in names]
+
+
+def sync(*trees):
+    return lax.optimization_barrier(trees)
+
+
+def after(array, *others):
+    return lax.optimization_barrier((array, others))[0]
 
 
 def low(values):
@@ -83,6 +133,9 @@
             ],
         ),
         compiler_params=pltpu.CompilerParams(vmem_limit_bytes=VMEM_BYTES),
+        cost_estimate=pl.CostEstimate(
+            flops=0, bytes_accessed=4 * count * pieces[0].size, transcendentals=0
+        ),
         name="place",
     )(jnp.stack(slots).astype(jnp.int32), *pieces)
 
@@ -285,72 +338,63 @@
             blocks.append(flip(columns_of(tp_rank ^ bit), "tp", bit))
         return jnp.concatenate(swapped(blocks, tp_rank), axis=0)
 
-    def over_ctx_and_fsdp(block):
+    def over_fsdp(block):
+        blocks = [block]
+        for _ in range(1, fsdp_count):
+            blocks.append(ring(blocks[-1], "fsdp"))
+        return blocks
+
+    def placed(by_ctx):
         pieces, slots = [], []
-        around = block
-        for step in range(ctx_count):
-            if step:
-                around = ring(around, "ctx")
-            across = around
-            for turn_at in range(fsdp_count):
-                if turn_at:
-                    across = ring(across, "fsdp")
-                pieces.append(across)
+        for step, blocks in enumerate(by_ctx):
+            for turn_at, block in enumerate(blocks):
+                pieces.append(block)
                 slots.append(
                     (fsdp_rank - turn_at) % fsdp_count * ctx_count
                     + (ctx_rank - step) % ctx_count
                 )
-        return place(pieces, slots).reshape(width, block.shape[1])
+        return place(pieces, slots).reshape(width, pieces[0].shape[1])
 
     def head_columns(weight):
         return lambda rank: lax.dynamic_slice_in_dim(
             weight, slot_base_of(rank) * head_size, slot_width, 1
         )
 
-    gains = jnp.pad(jnp.stack([attn_gain, mlp_gain], axis=1), ((0, 0), (0, 126)))
-    kv_and_gains = over_ctx_and_fsdp(
-        over_tp(
-            lambda rank: jnp.concatenate(
-                [lax.dynamic_slice_in_dim(kv_weight, rank * kv_width, kv_width, 1), gains], axis=1
-            )
-        )
-    )
-    kv_part = kv_and_gains[:, :kv_width]
-    gain_attn = wide(kv_and_gains[:, kv_width])
-    gain_mlp = wide(kv_and_gains[:, kv_width + 1])
-    query_part = over_ctx_and_fsdp(over_tp(head_columns(query_weight)))
-    out_part = over_ctx_and_fsdp(over_tp(head_columns(out_weight)))
-
     unit_count = gate_weight.shape[1]
     half = -(-unit_count // 256) * 128
     rest = unit_count - half
 
-    def mlp_gather(block):
+    def near_halves(block):
         near, far = block[:, :half], jnp.pad(block[:, half:], ((0, 0), (0, half - rest)))
         mine = jnp.where(lo_rank == 0, near, far)
         theirs = jnp.where(lo_rank == 0, far, near)
-        got = flip(theirs, "ctx", 1)
-        pair = jnp.stack(swapped([mine, got], lo_rank))
+        return mine, theirs
+
+    def near_pair(halves):
+        mine, theirs = halves
+        return jnp.stack(swapped([mine, flip(theirs, "ctx", 1)], lo_rank))
+
+    def quarters(pair):
+        return jnp.split(pair.reshape(-1, half), 4)
+
+    def far(pieces):
+        if len(pieces) == 1:
+            return [flip(pieces[0], "ctx", 2)]
+        return jnp.split(flip(jnp.concatenate(pieces, axis=0), "ctx", 2), len(pieces))
+
+    def mlp_placed(own, other):
         pieces, slots = [], []
-        for far_bit, around in ((0, pair), (1, flip(pair, "ctx", 2))):
-            across = around
-            for turn_at in range(fsdp_count):
-                if turn_at:
-                    across = ring(across, "fsdp")
-                pieces.append(across)
+        for far_bit, blocks in enumerate((own, other)):
+            for turn_at, block in enumerate(blocks):
+                pieces.append(block.reshape(-1, half))
                 slots.append((fsdp_rank - turn_at) % fsdp_count * 2 + (hi_rank ^ far_bit))
         return place(pieces, slots).reshape(width, half)
-
-    gate_full = mlp_gather(gate_weight)
-    up_full = mlp_gather(up_weight)
-    down_full = mlp_gather(down_weight.T)
 
     inputs_low = hidden[0]
     inputs = wide(inputs_low)
     inputs_part_low = lax.dynamic_slice_in_dim(inputs_low, tp_rank * part_rows, part_rows, 0)
     inputs_part = wide(inputs_part_low)
     scale_one = lax.rsqrt(jnp.mean(inputs * inputs, axis=-1, keepdims=True) + epsilon)
-    normed = low(inputs * scale_one * gain_attn)
     positions = ctx_rank * rows + jnp.arange(rows)
     quarter = head_size // 4
     frequency = 10000.0 ** (-(jnp.arange(quarter).astype(jnp.float32) * 4.0 / head_size))
@@ -370,67 +414,253 @@
 
     turning = tp_rank == 0
     kv_cosine, kv_sine = jnp.where(turning, cosine, 1.0), jnp.where(turning, sine, 0.0)
-    kv_raw = nn(normed, kv_part)
-    kv_own = low(turn(kv_raw, kv_cosine, kv_sine))
+    query_scale = head_size ** (-0.5)
     reach_back = min((W - 2) // rows + 1, ctx_count - 1)
-    chunks = [shifted(kv_own, "ctx", by) for by in range(reach_back, 0, -1)] + [kv_own]
-    kv_column = jnp.concatenate(chunks, axis=0)
-    kv_pair = jnp.stack([kv_column, flip(kv_column, "tp", 2)])
-    kv_other = flip(kv_pair, "tp", 1)
-    keyvals = jnp.concatenate(
+    first_key = (reach_back - jnp.minimum(ctx_rank, reach_back)) * rows
+
+    at = Steps()
+    Steps.on = True
+    Chain.on = ()
+    Chain.sent = {}
+    gains = jnp.pad(jnp.stack([attn_gain, mlp_gain], axis=1), ((0, 0), (0, 126)))
+
+    def qkv_columns(rank):
+        kv = lax.dynamic_slice_in_dim(kv_weight, rank * kv_width, kv_width, 1)
+        return jnp.concatenate([head_columns(query_weight)(rank), kv, gains], axis=1)
+
+    def to_tp(columns_of):
+        return [columns_of(tp_rank ^ bit) for bit in range(tp_count)]
+
+    def flip_tp(blocks):
+        return blocks[:1] + [flip(blocks[bit], "tp", bit) for bit in range(1, tp_count)]
+
+    def from_tp(blocks):
+        return jnp.concatenate(swapped(blocks, tp_rank), axis=0)
+
+    def paired(mine, got):
+        return jnp.stack(swapped([mine, got], lo_rank))
+
+    at.qkv = to_tp(qkv_columns)
+    at.gate_mine, at.gate_sent = near_halves(gate_weight)
+    at.out = to_tp(head_columns(out_weight))
+    at.up_mine, at.up_sent = near_halves(up_weight)
+    at.down_mine, at.down_sent = near_halves(down_weight.T)
+    at.next()
+    at.qkv = flip_tp(at.qkv)
+    at.gate_got = flip(at.gate_sent, "ctx", 1)
+    at.next()
+    at.qkv_0 = from_tp(at.drop("qkv")[0])
+    at.gate_pair = paired(*at.drop("gate_mine", "gate_got"))
+    at.next()
+    at.qkv_x = [over_fsdp(at.qkv_0)]
+    at.qkv_1 = ring(at.qkv_0, "ctx")
+    at.next()
+    at.qkv_x.append(over_fsdp(at.qkv_1))
+    at.qkv_2 = ring(at.qkv_1, "ctx")
+    at.next()
+    at.qkv_x.append(over_fsdp(at.qkv_2))
+    at.qkv_3 = ring(at.qkv_2, "ctx")
+    at.out = flip_tp(at.out)
+    at.next()
+    at.out_0 = from_tp(at.drop("out")[0])
+    at.drop("qkv_0", "qkv_1", "qkv_2", "gate_sent")
+    at.next()
+    at.qkv_x.append(over_fsdp(at.qkv_3))
+    at.out_1 = ring(at.out_0, "ctx")
+    at.next()
+
+    qkv_part = placed(at.drop("qkv_x")[0])
+    query_part = qkv_part[:, :slot_width]
+    kv_part = qkv_part[:, slot_width : slot_width + kv_width]
+    gain_attn = wide(qkv_part[:, slot_width + kv_width])
+    gain_mlp = wide(qkv_part[:, slot_width + kv_width + 1])
+    at.normed = low(inputs * scale_one * gain_attn)
+    at.kv_own = low(turn(nn(at.normed, kv_part), kv_cosine, kv_sine))
+    query_raw = nn(at.normed, query_part).reshape(rows, slot_count, head_size)
+    queries = low(turn(query_raw, cosine[:, None, :], sine[:, None, :]) * query_scale)
+    at.queries = queries.reshape(rows, slot_width)
+    at.gate_x = over_fsdp(at.gate_pair)
+    at.out_2 = ring(at.out_1, "ctx")
+    at.up_got = flip(at.up_sent, "ctx", 1)
+    at.far_1 = far(quarters(at.gate_pair)[:1])
+    at.next()
+    normed = at.normed
+    at.up_pair = paired(*at.drop("up_mine", "up_got"))
+    at.out_near = jnp.stack([at.out_0, at.out_1, at.out_2])
+    at.next()
+    out_x = over_fsdp(at.out_near)
+    at.chunks = [shifted(at.kv_own, "ctx", by) for by in range(reach_back, 0, -1)]
+    at.out_3 = ring(at.out_2, "ctx")
+    at.next()
+    at.kv_column = jnp.concatenate(at.drop("chunks")[0] + [at.kv_own], axis=0)
+    at.gate_far = jnp.concatenate(quarters(at.gate_pair)[1:3], axis=0)
+    at.drop("out_0", "out_1", "out_2", "kv_own", "qkv_3")
+    at.next()
+    at.kv_over_y = flip(at.kv_column, "tp", 2)
+    at.down_got = flip(at.down_sent, "ctx", 1)
+    at.far_2 = flip(at.gate_far, "ctx", 2)
+    at.out_x = out_x
+    at.next()
+    at.kv_pair = jnp.stack(at.drop("kv_column", "kv_over_y"))
+    at.down_pair = paired(*at.drop("down_mine", "down_got"))
+    at.next()
+    at.kv_other = flip(at.kv_pair, "tp", 1)
+    at.out_y = over_fsdp(at.out_3)
+    at.next()
+    kv_pair, kv_other = at.drop("kv_pair", "kv_other")
+    at.keyvals = jnp.concatenate(
         swapped([kv_pair[0], kv_other[0], kv_pair[1], kv_other[1]], tp_rank), axis=1
     )
-    first_key = (reach_back - jnp.minimum(ctx_rank, reach_back)) * rows
-
-    query_scale = head_size ** (-0.5)
-    query_raw = nn(normed, query_part).reshape(rows, slot_count, head_size)
-    queries = low(turn(query_raw, cosine[:, None, :], sine[:, None, :]) * query_scale)
-    queries = queries.reshape(rows, slot_width)
-    attended = attention_forward(queries, keyvals, live, first_key, head_size)
-
-    def tp_sum(partial):
-        blocks = partial.reshape(2, 2, part_rows, -1)
-        got = flip(take(blocks, 1 - core_rank, 1), "tp", 1)
-        summed = wide(take(blocks, core_rank, 1)) + wide(got)
-        got = flip(low(take(summed, 1 - y_rank)), "tp", 2)
-        return take(summed, y_rank) + wide(got)
-
-    def tp_gather(part):
-        pair = jnp.stack([part, flip(part, "tp", 2)])
-        other = flip(pair, "tp", 1)
-        blocks = swapped([pair[0], other[0], pair[1], other[1]], tp_rank)
-        return jnp.concatenate(blocks, axis=0)
-
-    def group_gather(part):
-        middle = part_rows // 2
-        over_y = flip(part, "tp", 2)
-        over_z = flip(part, "ctx", 1)
-        corner_top = flip(over_y[:middle], "ctx", 1)
-        corner_end = flip(over_z[middle:], "tp", 2)
-        near = jnp.concatenate([part, over_y, over_z, corner_top, corner_end], axis=0)
-        return jnp.concatenate([near, flip(near, "tp", 1)], axis=0)
-
-    def group_sum(partial):
-        blocks = partial.reshape(2, 4, part_rows, -1)
-        middle = part_rows // 2
-        got = flip(blocks[1], "tp", 1)
-        summed = wide(blocks[0]) + wide(got)
-        own, over_y, over_z, corner = summed[0], summed[1], summed[2], summed[3]
-        top = flip(low(corner[:middle]), "ctx", 1)
-        end = flip(low(corner[middle:]), "tp", 2)
-        over_y = jnp.concatenate([over_y[:middle] + wide(top), over_y[middle:]], axis=0)
-        over_z = jnp.concatenate([over_z[:middle], over_z[middle:] + wide(end)], axis=0)
-        return own + wide(flip(low(over_y), "tp", 2)) + wide(flip(low(over_z), "ctx", 1))
-
-    attn_part = tp_sum(low(nt(attended, out_part)))
-    residual = inputs_part + attn_part
+    at.mixed_far = jnp.concatenate(quarters(at.gate_pair)[3:] + quarters(at.up_pair)[:1], axis=0)
+    at.drop("up_sent", "down_sent", "gate_far", "out_near")
+    at.next()
+
+    queries, keyvals = at.queries, at.keyvals
+    at.attended = attention_forward(queries, keyvals, live, first_key, head_size)
+    out_x, out_y = at.drop("out_x", "out_y")
+    at.out_part = placed([[block[i] for block in out_x] for i in range(3)] + [out_y])
+    blocks = low(nt(at.attended, at.out_part)).reshape(2, 2, part_rows, -1)
+    at.kept, at.sent = take(blocks, core_rank, 1), take(blocks, 1 - core_rank, 1)
+    at.up_x = over_fsdp(at.up_pair)
+    at.far_3 = flip(at.mixed_far, "ctx", 2)
+    at.next()
+
+    out_part = at.out_part
+    quarter_rows = at.far_1[0].shape[0]
+    at.gate_other = jnp.concatenate(
+        at.far_1 + [at.far_2, at.far_3[:quarter_rows]], axis=0
+    ).reshape(at.gate_pair.shape)
+    at.up_far = jnp.concatenate(quarters(at.up_pair)[1:3], axis=0)
+    at.next()
+    at.got = flip(at.sent, "tp", 1)
+    at.next()
+    summed = wide(at.kept) + wide(at.got)
+    at.kept, at.sent = take(summed, y_rank), low(take(summed, 1 - y_rank))
+    at.next()
+    at.got = flip(at.sent, "tp", 2)
+    at.gate_z = over_fsdp(at.gate_other)
+    at.far_4 = flip(at.up_far, "ctx", 2)
+    at.next()
+
+    middle = part_rows // 2
+
+    def gather_sides():
+        at.over_y, at.over_z = flip(at.part, "tp", 2), flip(at.part, "ctx", 1)
+        at.core_own = flip(at.part, "tp", 1)
+
+    def between_sides_and_corners():
+        at.to_z, at.to_y = at.over_y[:middle], at.over_z[middle:]
+        at.sides = jnp.concatenate([at.over_y, at.over_z], axis=0)
+
+    def gather_corners():
+        at.corner_top = flip(at.to_z, "ctx", 1)
+        at.corner_end = flip(at.to_y, "tp", 2)
+        at.core_sides = flip(at.sides, "tp", 1)
+
+    def between_corners_and_core():
+        at.corner = jnp.concatenate(at.drop("corner_top", "corner_end"), axis=0)
+        at.drop("to_z", "to_y", "over_y", "over_z")
+
+    def gathered():
+        return jnp.concatenate(
+            at.drop("part", "sides", "corner", "core_own", "core_sides", "core_corner"), axis=0
+        )
+
+    def before_sum(partial):
+        mine, theirs = partial.reshape(2, 4, part_rows, -1)
+        at.mine, at.mine_corner = mine[:3], mine[3]
+        at.theirs, at.theirs_corner = theirs[:3], theirs[3]
+
+    def between_core_and_corners():
+        corner = wide(at.drop("mine_corner")[0]) + wide(at.drop("got_corner")[0])
+        at.to_z, at.to_y = low(corner[:middle]), low(corner[middle:])
+
+    def sum_corners():
+        at.corner_top = flip(at.to_z, "ctx", 1)
+        at.corner_end = flip(at.to_y, "tp", 2)
+
+    def between_corners_and_sides():
+        mine, got, top, end = at.drop("mine", "got", "corner_top", "corner_end")
+        own, over_y, over_z = wide(mine) + wide(got)
+        at.over_y = low(jnp.concatenate([over_y[:middle] + wide(top), over_y[middle:]], axis=0))
+        at.over_z = low(jnp.concatenate([over_z[:middle], over_z[middle:] + wide(end)], axis=0))
+        at.part = own
+        at.drop("theirs", "theirs_corner", "to_z", "to_y")
+
+    def sum_sides():
+        at.got_y, at.got_z = flip(at.over_y, "tp", 2), flip(at.over_z, "ctx", 1)
+
+    def summed():
+        own, got_y, got_z = at.drop("part", "got_y", "got_z")
+        at.drop("over_y", "over_z")
+        return own + wide(got_y) + wide(got_z)
+
+    residual = inputs_part + (at.kept + wide(at.got))
+    at.drop("kept", "got", "sent")
     scale_two = lax.rsqrt(jnp.mean(residual * residual, axis=-1, keepdims=True) + epsilon)
-    normed_two = group_gather(low(residual * scale_two * gain_mlp))
-    gate_proj = nn(normed_two, gate_full)
-    up_proj = nn(normed_two, up_full)
+    at.residual = residual
+    at.part = low(residual * scale_two * gain_mlp)
+    at.mixed_far = jnp.concatenate(quarters(at.up_pair)[3:] + quarters(at.down_pair)[:1], axis=0)
+    at.next()
+    residual = at.residual
+    gather_sides()
+    at.down_x = over_fsdp(at.down_pair)
+    at.far_5 = flip(at.mixed_far, "ctx", 2)
+    at.next()
+    between_sides_and_corners()
+    at.up_a = jnp.concatenate([at.far_3[quarter_rows:], at.far_4[:quarter_rows]], axis=0)
+    at.up_b = jnp.concatenate([at.far_4[quarter_rows:], at.far_5[:quarter_rows]], axis=0)
+    at.down_quarters = quarters(at.down_pair)[1:]
+    at.next()
+    gather_corners()
+    at.up_a = over_fsdp(at.up_a)
+    at.far_6 = flip(at.down_quarters[0], "ctx", 2)
+    at.next()
+    between_corners_and_core()
+    at.down_a = jnp.concatenate([at.far_5[quarter_rows:], at.far_6], axis=0)
+    at.next()
+    at.core_corner = flip(at.corner, "tp", 1)
+    at.next()
+    at.normed_two = gathered()
+    gate_full = mlp_placed(*at.drop("gate_x", "gate_z"))
+    at.gate_proj = nn(at.normed_two, gate_full)
+    at.up_b = over_fsdp(at.up_b)
+    at.far_7 = flip(at.down_quarters[1], "ctx", 2)
+    at.next()
+    up_a, up_b = at.drop("up_a", "up_b")
+    up_z = [jnp.stack(pair) for pair in zip(up_a, up_b)]
+    up_full = mlp_placed(at.drop("up_x")[0], up_z)
+    at.up_proj = nn(at.normed_two, up_full)
+    at.down_a = over_fsdp(at.down_a)
+    at.far_8 = flip(at.down_quarters[2], "ctx", 2)
+    at.next()
+    at.down_b = jnp.concatenate([at.far_7, at.far_8], axis=0)
+    at.next()
+    gate_proj, up_proj = at.gate_proj, at.up_proj
     activated, gelu_back = jax.vjp(gelu_tanh, gate_proj)
-    hidden_act = low(activated * up_proj)
-    ffn_part = group_sum(low(nt(hidden_act, down_full)))
+    at.hidden_act = low(activated * up_proj)
+    at.down_b = over_fsdp(at.down_b)
+    at.next()
+    at.drop("far_1", "far_2", "far_3", "far_4", "far_5", "far_6", "far_7", "gate_pair", "up_pair")
+    at.drop("far_8", "gate_other", "up_far", "down_quarters", "mixed_far")
+    at.drop("gate_proj", "up_proj", "down_pair")
+    down_x, down_a, down_b = at.drop("down_x", "down_a", "down_b")
+    down_z = [jnp.stack(pair) for pair in zip(down_a, down_b)]
+    down_full = mlp_placed(down_x, down_z)
+    before_sum(low(nt(at.hidden_act, down_full)))
+    at.next()
+    at.got = flip(at.theirs, "tp", 1)
+    at.got_corner = flip(at.theirs_corner, "tp", 1)
+    at.next()
+    between_core_and_corners()
+    at.next()
+    sum_corners()
+    at.next()
+    between_corners_and_sides()
+    at.next()
+    sum_sides()
+    at.next()
+    ffn_part = summed()
 
     my_length = lengths[fsdp_rank]
     part_positions = ctx_rank * rows + tp_rank * part_rows + jnp.arange(part_rows)
@@ -439,57 +669,241 @@
     mismatch = output - wide(teacher[0])
     count = wide(jnp.sum(lengths))
     loss_part = jnp.sum(valid * mismatch * mismatch)
-    d_output = valid * mismatch * (lengths.shape[0] * ctx_count * rows / count)
-
-    d_ffn = group_gather(low(d_output))
-    d_hidden = nn(d_ffn, down_full)
-    d_gate = low(gelu_back(d_hidden * up_proj)[0])
-    d_up = low(d_hidden * activated)
-    d_normed_two = group_sum(low(nt(d_gate, gate_full) + nt(d_up, up_full)))
-
-    def mlp_scatter(grad):
+    at.d_output = valid * mismatch * (lengths.shape[0] * ctx_count * rows / count)
+    at.part = low(at.d_output)
+    at.next()
+    gather_sides()
+    at.next()
+    between_sides_and_corners()
+    at.next()
+    gather_corners()
+    at.next()
+    between_corners_and_core()
+    at.next()
+    at.core_corner = flip(at.corner, "tp", 1)
+    at.next()
+
+    def terms(blocks_of, axis):
+        count, rank = lax.axis_size(axis), lax.axis_index(axis)
+        return [blocks_of((rank - step) % count) for step in range(1, count + 1)]
+
+    def around(sent, axis):
+        moving = ring(sent[0], axis)
+        for term in sent[1:-1]:
+            moving = ring(low(wide(moving) + wide(term)), axis)
+        return moving
+
+    def with_own(sent, arrived):
+        return wide(sent[-1]) + wide(arrived)
+
+    def far_and_own(grad):
         blocks = grad.reshape(fsdp_count, 2, 2, -1, half)
-        mine = ring_sum(lambda owner: take(blocks, owner), "fsdp")
-        got = flip(low(take(mine, 1 - hi_rank)), "ctx", 2)
-        mine = take(mine, hi_rank) + wide(got)
-        got = flip(low(take(mine, 1 - lo_rank)), "ctx", 1)
-        near, far = swapped([take(mine, lo_rank), wide(got)], lo_rank)
-        return jnp.concatenate([near, far[:, :rest]], axis=1)
-
-    down_grad = mlp_scatter(tn(d_ffn, hidden_act)).T
-    gate_grad = mlp_scatter(tn(normed_two, d_gate))
-    up_grad = mlp_scatter(tn(normed_two, d_up))
-
-    def vector_sum(vector):
-        for axis, bit in (("tp", 1), ("tp", 2), ("ctx", 1), ("ctx", 2)):
-            vector = vector + flip(vector, axis, bit)
-        moving = vector
-        for _ in range(1, fsdp_count):
-            moving = ring(moving, "fsdp")
-            vector = vector + moving
-        return vector
+        return [
+            terms(lambda owner: take(take(blocks, owner), high), "fsdp")
+            for high in (1 - hi_rank, hi_rank)
+        ]
+
+    def near_split(mine):
+        return wide(take(mine, lo_rank)), low(take(mine, 1 - lo_rank))
+
+    def near_joined(kept, got):
+        near, rest_of = swapped([kept, wide(got)], lo_rank)
+        return jnp.concatenate([near, rest_of[:, :rest]], axis=1)
+
+    at.d_ffn = gathered()
+    at.down_far, at.down_own = far_and_own(low(tn(at.d_ffn, at.hidden_act)))
+    at.next()
+    Steps.on = False
+    Chain.on = ('x',)
+    Chain.sent = {}
+    at.down_far_got = around(at.down_far, "fsdp")
+    d_hidden = nn(at.d_ffn, down_full)
+    at.d_gate = low(gelu_back(d_hidden * up_proj)[0])
+    at.d_up = low(d_hidden * activated)
+    at.next()
+    at.drop("d_ffn", "hidden_act")
+    at.down_far = low(with_own(*at.drop("down_far", "down_far_got")))
+    at.next()
+    at.down_own_got = around(at.down_own, "fsdp")
+    at.down_got_0 = flip(at.down_far[0], "ctx", 2)
+    before_sum(low(nt(at.d_gate, gate_full) + nt(at.d_up, up_full)))
+    at.next()
+    at.got = flip(at.theirs, "tp", 1)
+    at.got_corner = flip(at.theirs_corner, "tp", 1)
+    at.next()
+    between_core_and_corners()
+    at.next()
+    sum_corners()
+    at.down_got_1 = flip(at.down_far[1], "ctx", 2)
+    at.gate_far, at.gate_own = far_and_own(low(tn(at.normed_two, at.d_gate)))
+    at.next()
+    at.drop("d_gate")
+    between_corners_and_sides()
+    at.down_own = low(with_own(*at.drop("down_own", "down_own_got")))
+    at.next()
+    sum_sides()
+    at.gate_far_got = around(at.gate_far, "fsdp")
+    at.up_far, at.up_own = far_and_own(low(tn(at.normed_two, at.d_up)))
+    at.next()
+    at.drop("normed_two", "d_up")
+    at.gate_far = low(with_own(*at.drop("gate_far", "gate_far_got")))
+    d_normed_two = summed()
+    scaled = gain_mlp * d_normed_two
+    inner_two = jnp.mean(scaled * residual, axis=-1, keepdims=True)
+    at.d_residual = at.d_output + scale_two * scaled - residual * scale_two**3 * inner_two
+    gain_mlp_sums = jnp.sum(d_normed_two * residual * scale_two, axis=0)
+    at.vector = jnp.concatenate([gain_mlp_sums, jnp.full((128,), loss_part)])
+    at.part = low(at.d_residual)
+    at.next()
+    at.over_y = flip(at.part, "tp", 2)
+    at.gate_own_got = around(at.gate_own, "fsdp")
+    at.gate_got_0 = flip(at.gate_far[0], "ctx", 2)
+    at.next()
+    at.pair = jnp.stack(at.drop("part", "over_y"))
+    at.next()
+    at.other = flip(at.pair, "tp", 1)
+    at.got_vector = flip(at.vector, "tp", 1)
+    at.next()
+    pair, other = at.drop("pair", "other")
+    d_attn = swapped([pair[0], other[0], pair[1], other[1]], tp_rank)
+    at.d_attn = jnp.concatenate(d_attn, axis=0)
+    down_got = jnp.stack(at.drop("down_got_0", "down_got_1"))
+    at.down_kept, at.down_sent = near_split(wide(at.down_own) + wide(down_got))
+    at.vector = at.vector + at.drop("got_vector")[0]
+    at.next()
+    at.drop("down_own", "down_far")
+    at.got_vector = flip(at.vector, "tp", 2)
+    at.down_got = flip(at.down_sent, "ctx", 1)
+    live_columns = jnp.repeat(live, head_size).astype(jnp.float32)
+    at.d_attended = low(nn(at.d_attn, out_part) * live_columns)
+    out_grad = low(tn(at.d_attn, at.attended))
 
     own_rows = attn_gain.shape[0]
     own_start = ((fsdp_rank * ctx_count + ctx_rank) * tp_count + tp_rank) * own_rows
 
-    scaled = gain_mlp * d_normed_two
-    inner_two = jnp.mean(scaled * residual, axis=-1, keepdims=True)
-    d_residual = d_output + scale_two * scaled - residual * scale_two**3 * inner_two
-    gain_mlp_sums = jnp.sum(d_normed_two * residual * scale_two, axis=0)
-    early = vector_sum(jnp.concatenate([gain_mlp_sums, jnp.full((128,), loss_part)]))
-    gain_mlp_grad = lax.dynamic_slice_in_dim(early, own_start, own_rows, 0)
-    loss = early[width] / (count * width)
-
-    d_attn = tp_gather(low(d_residual))
-
-    def head_scatter(grad):
-        blocks = grad.reshape(fsdp_count, ctx_count, tp_count, own_rows, -1)
-        mine = ring_sum(lambda owner: take(blocks, owner), "fsdp")
-        mine = ring_sum(lambda owner: take(mine, owner), "ctx")
-        parts = [take(mine, tp_rank)]
-        for bit in range(1, tp_count):
-            parts.append(wide(flip(low(take(mine, tp_rank ^ bit)), "tp", bit)))
-        return swapped(parts, tp_rank)
+    def by_rows(grad):
+        return grad.reshape(fsdp_count, ctx_count, tp_count * own_rows, -1)
+
+    at.out_terms = terms(lambda owner: take(by_rows(out_grad), owner), "fsdp")
+    at.gate_own = low(with_own(*at.drop("gate_own", "gate_own_got")))
+    at.next()
+    at.drop("attended", "d_attn", "down_sent")
+    at.vector = at.vector + at.drop("got_vector")[0]
+    at.next()
+    at.got_vector = flip(at.vector, "ctx", 1)
+    at.gate_got_1 = flip(at.gate_far[1], "ctx", 2)
+    at.up_far_got = around(at.up_far, "fsdp")
+    at.d_queries, at.d_keyvals = attention_backward(
+        queries, keyvals, at.d_attended, first_key, head_size
+    )
+    kv_blocks = jnp.stack(jnp.split(at.d_keyvals, tp_count, axis=1)).reshape(2, 2, -1, kv_width)
+    at.kv_kept, at.kv_sent = take(kv_blocks, core_rank, 1), take(kv_blocks, 1 - core_rank, 1)
+    at.next()
+    at.drop("d_attended", "d_keyvals")
+    at.kv_got = flip(at.kv_sent, "tp", 1)
+    at.next()
+    at.vector = at.vector + at.drop("got_vector")[0]
+    kv_sum = wide(at.kv_kept) + wide(at.kv_got)
+    at.kv_kept, at.kv_sent = take(kv_sum, y_rank), low(take(kv_sum, 1 - y_rank))
+    at.up_far = low(with_own(*at.drop("up_far", "up_far_got")))
+    at.next()
+    at.kv_got = flip(at.kv_sent, "tp", 2)
+    at.got_vector = flip(at.vector, "ctx", 2)
+    at.up_got_0 = flip(at.up_far[0], "ctx", 2)
+    at.out_got = around(at.out_terms, "fsdp")
+    d_query_raw = turn(
+        at.d_queries.reshape(rows, slot_count, head_size) * query_scale,
+        cosine[:, None, :],
+        -sine[:, None, :],
+    )
+    at.d_query_low = low(d_query_raw.reshape(rows, slot_width))
+    query_grad = by_rows(low(tn(normed, at.d_query_low)))
+    turned = [take(query_grad, (ctx_rank - by) % ctx_count, 1) for by in range(1, ctx_count + 1)]
+    first_half, second_half = jnp.stack(turned[:2], axis=1), jnp.stack(turned[2:], axis=1)
+    at.query_1 = terms(lambda owner: take(first_half, owner), "fsdp")
+    at.query_2 = terms(lambda owner: take(second_half, owner), "fsdp")
+    at.next()
+    at.drop("d_queries", "kv_sent", "gate_far")
+    at.vector = at.vector + at.drop("got_vector")[0]
+    kv_sum = (at.drop("kv_kept")[0] + wide(at.drop("kv_got")[0])).reshape(reach_back + 1, rows, -1)
+    at.kv_low = [low(kv_sum[reach_back - by]) for by in range(1, reach_back + 1)]
+    at.d_kv = kv_sum[reach_back]
+    out_mine = low(with_own(*at.drop("out_terms", "out_got")))
+    at.out_terms = terms(lambda owner: take(out_mine, owner), "ctx")
+    at.next()
+    at.kv_got = [shifted(at.kv_low[by - 1], "ctx", -by) for by in range(1, reach_back + 1)]
+    at.up_own_got = around(at.up_own, "fsdp")
+    at.out_z = ring(at.out_terms[0], "ctx")
+    gate_got = jnp.stack(at.drop("gate_got_0", "gate_got_1"))
+    at.gate_kept, at.gate_sent = near_split(wide(at.gate_own) + wide(gate_got))
+    at.next()
+    at.drop("gate_own")
+    d_kv = at.d_kv
+    for got in at.drop("kv_got")[0]:
+        d_kv = d_kv + wide(got)
+    d_kv_low = low(turn(d_kv, kv_cosine, -kv_sine))
+    partial = low(nt(at.d_query_low, query_part) + nt(d_kv_low, kv_part))
+    gain_attn_sums = jnp.sum(wide(partial) * inputs * scale_one, axis=0)
+    gain_column = jnp.pad(gain_attn_sums[:, None], ((0, 0), (0, 127)))
+    kv_grad = low(jnp.concatenate([tn(normed, d_kv_low), gain_column], axis=1))
+    at.kv_terms = terms(lambda owner: take(by_rows(kv_grad), owner), "fsdp")
+    blocks = partial.reshape(2, 2, part_rows, -1)
+    at.kept, at.sent = take(blocks, core_rank, 1), take(blocks, 1 - core_rank, 1)
+    at.query_1_got = around(at.query_1, "fsdp")
+    at.up_got_1 = flip(at.up_far[1], "ctx", 2)
+    at.gate_got = flip(at.gate_sent, "ctx", 1)
+    at.up_own = low(with_own(*at.drop("up_own", "up_own_got")))
+    at.out_z = low(wide(at.out_z) + wide(at.out_terms[1]))
+    at.next()
+    at.drop("d_query_low", "kv_low", "d_kv", "gate_sent")
+    at.query_1 = low(with_own(*at.drop("query_1", "query_1_got")))
+    at.got = flip(at.sent, "tp", 1)
+    at.next()
+    summed_rows = wide(at.kept) + wide(at.got)
+    at.kept, at.sent = take(summed_rows, y_rank), low(take(summed_rows, 1 - y_rank))
+    at.next()
+    at.got = flip(at.sent, "tp", 2)
+    at.query_2_got = around(at.query_2, "fsdp")
+    at.query_z = ring(at.query_1[0], "ctx")
+    at.out_z = ring(at.out_z, "ctx")
+    at.next()
+    at.query_z = low(wide(at.query_z) + wide(at.query_1[1]))
+    at.out_z = low(wide(at.out_z) + wide(at.out_terms[2]))
+    at.query_2 = with_own(*at.drop("query_2", "query_2_got"))
+    at.d_normed = at.kept + wide(at.got)
+    up_got = jnp.stack(at.drop("up_got_0", "up_got_1"))
+    at.up_kept, at.up_sent = near_split(wide(at.up_own) + wide(up_got))
+    at.next()
+    at.drop("query_1", "kept", "sent", "got")
+    at.query_z = ring(at.query_z, "ctx")
+    at.out_z = ring(at.out_z, "ctx")
+    at.kv_got = around(at.kv_terms, "fsdp")
+    at.up_got = flip(at.up_sent, "ctx", 1)
+    moving = ring(at.vector, "fsdp")
+    at.vector = at.vector + moving
+    for _ in range(2, fsdp_count):
+        moving = ring(moving, "fsdp")
+        at.vector = at.vector + moving
+    at.next()
+    at.query_z = low(wide(at.query_z) + at.query_2[0])
+    kv_mine = low(with_own(*at.drop("kv_terms", "kv_got")))
+    at.kv_own = take(kv_mine, ctx_rank)
+    at.kv_sent = [take(kv_mine, (ctx_rank + by) % ctx_count) for by in range(1, ctx_count)]
+
+    def to_tp_back(mine):
+        blocks = low(mine).reshape(tp_count, own_rows, -1)
+        return [take(blocks, tp_rank ^ bit) for bit in range(tp_count)]
+
+    at.out_back = to_tp_back(wide(at.out_z) + wide(at.out_terms[3]))
+    at.next()
+    at.drop("up_far", "up_own", "out_z", "out_terms")
+    at.query_z = ring(at.query_z, "ctx")
+    at.kv_got = [ring(at.kv_sent[by - 1], "ctx", by) for by in range(1, ctx_count)]
+    at.next()
+    at.query_back = to_tp_back(wide(at.query_z) + at.query_2[1])
+    at.kv_back = to_tp_back(sum([wide(got) for got in at.kv_got], wide(at.kv_own)))
+    at.next()
+    at.drop("query_z", "query_2", "kv_got", "kv_own", "kv_sent", "up_sent")
 
     def whole_heads(parts):
         columns = []
@@ -498,39 +912,20 @@
             base = min(first, head_count - slot_count)
             held = slot_count - 1 + (1 if rank < fuller else 0)
             start = (first - base) * head_size
-            columns.append(part[:, start : start + held * head_size])
+            columns.append(wide(part[:, start : start + held * head_size]))
         return jnp.concatenate(columns, axis=1)
 
-    out_grad = whole_heads(head_scatter(tn(d_attn, attended)))
-    live_columns = jnp.repeat(live, head_size).astype(jnp.float32)
-    d_attended = low(nn(d_attn, out_part) * live_columns)
-    d_queries, d_keyvals = attention_backward(queries, keyvals, d_attended, first_key, head_size)
-    d_query_raw = turn(
-        d_queries.reshape(rows, slot_count, head_size) * query_scale,
-        cosine[:, None, :],
-        -sine[:, None, :],
-    )
-    d_query_low = low(d_query_raw.reshape(rows, slot_width))
-    query_grad = whole_heads(head_scatter(tn(normed, d_query_low)))
-
-    kv_blocks = jnp.stack(jnp.split(d_keyvals, tp_count, axis=1)).reshape(
-        2, 2, -1, kv_width
-    )
-    got = flip(take(kv_blocks, 1 - core_rank, 1), "tp", 1)
-    kv_sum = wide(take(kv_blocks, core_rank, 1)) + wide(got)
-    got = flip(low(take(kv_sum, 1 - y_rank)), "tp", 2)
-    kv_sum = (take(kv_sum, y_rank) + wide(got)).reshape(reach_back + 1, rows, kv_width)
-    d_kv = kv_sum[reach_back]
-    for by in range(1, reach_back + 1):
-        d_kv = d_kv + wide(shifted(low(kv_sum[reach_back - by]), "ctx", -by))
-    d_kv_low = low(turn(d_kv, kv_cosine, -kv_sine))
-    kv_parts = head_scatter(tn(normed, d_kv_low))
-    kv_grad = jnp.concatenate(kv_parts, axis=1)
-
-    d_normed_partial = nt(d_query_low, query_part) + nt(d_kv_low, kv_part)
-    gain_attn_sums = jnp.sum(d_normed_partial * inputs * scale_one, axis=0)
-    gain_attn_grad = lax.dynamic_slice_in_dim(vector_sum(gain_attn_sums), own_start, own_rows, 0)
-    d_normed = tp_sum(low(d_normed_partial))
+    query_grad = whole_heads(swapped(flip_tp(at.query_back), tp_rank))
+    out_grad = whole_heads(swapped(flip_tp(at.out_back), tp_rank))
+    kv_parts = [wide(part) for part in swapped(flip_tp(at.kv_back), tp_rank)]
+    kv_grad = jnp.concatenate([part[:, :kv_width] for part in kv_parts], axis=1)
+    gain_attn_grad = sum(part[:, kv_width] for part in kv_parts)
+    down_grad = near_joined(at.down_kept, at.down_got).T
+    gate_grad = near_joined(at.gate_kept, at.gate_got)
+    up_grad = near_joined(at.up_kept, at.up_got)
+    gain_mlp_grad = lax.dynamic_slice_in_dim(at.vector, own_start, own_rows, 0)
+    loss = at.vector[width] / (count * width)
+    d_normed, d_residual = at.d_normed, at.d_residual
     scale_part = lax.dynamic_slice_in_dim(scale_one, tp_rank * part_rows, part_rows, 0)
     scaled = gain_attn * d_normed
     inner_one = jnp.mean(scaled * inputs_part, axis=-1, keepdims=True)

time: 1290 us -> 1080 us (0.84)
  waiting for transfers between devices: 703 us -> 547 us
  local copies, waits for them, and re-layouts: 122 us -> 91.6 us
    ppermute x44 -> x40, waiting for transfers between devices: 345 us -> 211 us  [ring(): lax.ppermute(array, axis, [(i, (i + by) % count) for i in range(count)])]
    ppermute x68 -> x75, waiting for transfers between devices: 330 us -> 301 us  [flip(): lax.ppermute(array, axis, [(i, i ^ bit) for i in range(lax.axis_size(axis...]
    ppermute x44 -> x40, starting transfers between devices: 54.5 us -> 32.3 us  [ring(): lax.ppermute(array, axis, [(i, (i + by) % count) for i in range(count)])]
    add x26 -> x15, other arithmetic: 33 us -> 13 us  [the longest x1 2.7 us: local(): summed = wide(at.kept) + wide(at.got)]
    convert_element_type x24 -> x6, local copies, waits for them, and re-layouts: 19.6 us -> 1.53 us  [low(): return values.astype(jnp.bfloat16)]
    unnamed x208 -> x234, local copies, waits for them, and re-layouts: 42.9 us -> 28.5 us
    ppermute x68 -> x75, starting transfers between devices: 56.8 us -> 68 us  [flip(): lax.ppermute(array, axis, [(i, i ^ bit) for i in range(lax.axis_size(axis...]
  transfers between devices with their start and end apart: 118 -> 121, of which waited for: 60 -> 68; matrix products, arithmetic and copies ran while one was open for 16% -> 17% of each run, Pallas kernels for 4% -> 5%
where the time goes in v2:
time: 1080 us; the launch traced here: 1070 us
  waiting for transfers between devices  547 us (51%)
  matrix products  151 us (14%)
  starting transfers between devices  114 us (11%)
  other arithmetic  96.3 us (9%)
  local copies, waits for them, and re-layouts  91.6 us (8%)
  Pallas kernels  60.5 us (6%)
    ppermute x75, waiting for transfers between devices, flip(): lax.ppermute(array, axis, [(i, i ^ bit) for i in range(lax.axis_size(axis...  301 us
    ppermute x40, waiting for transfers between devices, ring(): lax.ppermute(array, axis, [(i, (i + by) % count) for i in range(count)])  211 us
    ppermute x75, starting transfers between devices, flip(): lax.ppermute(array, axis, [(i, i ^ bit) for i in range(lax.axis_size(axis...  68 us
    dot_general x6, matrix products, nn(): lax.dot_general(first, second, (((1,), (0,)), ((), ())), preferred_elemen...  58.9 us
    dot_general x6, matrix products, nt(): lax.dot_general(first, second, (((1,), (1,)), ((), ())), preferred_elemen...  51 us
    dot_general x6, matrix products, tn(): lax.dot_general(first, second, (((0,), (0,)), ((), ())), preferred_elemen...  40.6 us
    ppermute x6, waiting for transfers between devices, shifted(): return lax.ppermute(array, axis, pairs)  34.3 us
    ppermute x40, starting transfers between devices, ring(): lax.ppermute(array, axis, [(i, (i + by) % count) for i in range(count)])  32.3 us
  transfers between devices with their start and end apart: 121, of which 68 were waited for; matrix products, arithmetic and copies ran while one was open for 17% of the time, Pallas kernels for 5%

profile of v2, /device:TPU:0, one launch (start us, length us, event | category | flops | bytes accessed | tf_op | source)
XLA Modules:
  0.0 1066.1 jit_solution(6655386530228177468)
XLA Ops:
  29.8 12.7 %collective-permute-done.5.refs_1_ = bf16[320,1024]{1,0:T(8,128)(2,1)S(1)} collective-permute-done((bf16[320,1024]{1,0:T(8,128)(2,1)S(1)}, bf16[320,1024]{1,0:T(8,128)(2,1)S(1)}, u32[]{:S(2)}, u32[]{:S(2)}) %collective-permute-start.5) | collective-permute-done | bytes 655392 | tf_op jit(solution)/shard_map/ppermute | solution.py:27
  46.0 13.8 %collective-permute-done.7.refs_3_ = bf16[320,1024]{1,0:T(8,128)(2,1)S(1)} collective-permute-done((bf16[320,1024]{1,0:T(8,128)(2,1)S(1)}, bf16[320,1024]{1,0:T(8,128)(2,1)S(1)}, u32[]{:S(2)}, u32[]{:S(2)}) %collective-permute-start.7) | collective-permute-done | bytes 655392 | tf_op jit(solution)/shard_map/ppermute | solution.py:27
  167.8 21.9 %collective-permute-done.23 = bf16[320,1024]{1,0:T(8,128)(2,1)S(1)} collective-permute-done((bf16[320,1024]{1,0:T(8,128)(2,1)S(1)}, bf16[320,1024]{1,0:T(8,128)(2,1)S(1)}, u32[]{:S(2)}, u32[]{:S(2)}) %collective-permute-start.23) | collective-permute-done | bytes 655392 | tf_op jit(solution)/shard_map/ppermute | solution.py:19
  197.6 12.3 %collective-permute-done.28.refs_7_ = bf16[320,768]{1,0:T(8,128)(2,1)} collective-permute-done((bf16[320,768]{1,0:T(8,128)(2,1)S(1)}, bf16[320,768]{1,0:T(8,128)(2,1)}, u32[]{:S(2)}, u32[]{:S(2)}) %collective-permute-start.28) | collective-permute-done | bytes 491552 | tf_op jit(solution)/shard_map/ppermute | solution.py:27
  221.9 18.3 %attention_forward.1 = bf16[768,768]{1,0:T(8,128)(2,1)S(1)} custom-call(s32[4]{0:T(128)S(1)} %pad_add_fusion.info_ref, bf16[768,768]{1,0:T(8,128)(2,1)S(1)} %copy-done.16, bf16[3072,512]{1,0:T(8,128)(2,1)S(1)} %copy-done.8), custom_call_target="tpu_custom_call" | custom-call | flops 5435817984 | bytes 5505024 | tf_op jit(solution)/shard_map/attention_forward/pallas_call | solution.py:197
  272.1 28.5 %collective-permute-done.32 = bf16[320,1024]{1,0:T(8,128)(2,1)} collective-permute-done((bf16[320,1024]{1,0:T(8,128)(2,1)}, bf16[320,1024]{1,0:T(8,128)(2,1)}, u32[]{:S(2)}, u32[]{:S(2)}) %collective-permute-start.32) | collective-permute-done | bytes 655392 | tf_op jit(solution)/shard_map/ppermute | solution.py:19
  312.2 30.2 %collective-permute-done.37 = bf16[320,1024]{1,0:T(8,128)(2,1)S(1)} collective-permute-done((bf16[320,1024]{1,0:T(8,128)(2,1)S(1)}, bf16[320,1024]{1,0:T(8,128)(2,1)S(1)}, u32[]{:S(2)}, u32[]{:S(2)}) %collective-permute-start.37) | collective-permute-done | bytes 655392 | tf_op jit(solution)/shard_map/ppermute | solution.py:19
  354.4 15.8 %collective-permute-done.43 = bf16[160,1024]{1,0:T(8,128)(2,1)S(1)} collective-permute-done((bf16[160,1024]{1,0:T(8,128)(2,1)S(1)}, bf16[160,1024]{1,0:T(8,128)(2,1)S(1)}, u32[]{:S(2)}, u32[]{:S(2)}) %collective-permute-start.43) | collective-permute-done | bytes 327712 | tf_op jit(solution)/shard_map/ppermute | solution.py:19
  392.6 12.8 %fusion.108 = f32[1536,1024]{1,0:T(8,128)S(1)} fusion(bf16[1536,2560]{1,0:T(8,128)(2,1)} %copy-done.85, bf16[2560,1024]{1,0:T(8,128)(2,1)S(1)} %bitcast.487), kind=kOutput, calls=%fused_computation.421 | convolution fusion | flops 8053063680 | bytes 19398656 | tf_op jit(solution)/shard_map/dot_general | solution.py:144
  410.5 12.6 %fusion.109 = f32[1536,1024]{1,0:T(8,128)S(1)} fusion(bf16[1536,2560]{1,0:T(8,128)(2,1)} %copy-done.85, bf16[2560,1024]{1,0:T(8,128)(2,1)S(1)} %bitcast.491), kind=kOutput, calls=%fused_computation.422 | convolution fusion | flops 8053063680 | bytes 19398656 | tf_op jit(solution)/shard_map/dot_general | solution.py:144
  426.2 13.1 %collective-permute-done.50 = bf16[320,1024]{1,0:T(8,128)(2,1)S(1)} collective-permute-done((bf16[320,1024]{1,0:T(8,128)(2,1)S(1)}, bf16[320,1024]{1,0:T(8,128)(2,1)S(1)}, u32[]{:S(2)}, u32[]{:S(2)}) %collective-permute-start.50) | collective-permute-done | bytes 655392 | tf_op jit(solution)/shard_map/ppermute | solution.py:27
  461.1 11.4 %collective-permute-done.53 = bf16[96,2560]{1,0:T(8,128)(2,1)S(1)} collective-permute-done((bf16[96,2560]{1,0:T(8,128)(2,1)S(1)}, bf16[96,2560]{1,0:T(8,128)(2,1)S(1)}, u32[]{:S(2)}, u32[]{:S(2)}) %collective-permute-start.53) | collective-permute-done | bytes 491552 | tf_op jit(solution)/shard_map/ppermute | solution.py:19
  482.7 17.9 %collective-permute-done.55 = bf16[192,2560]{1,0:T(8,128)(2,1)} collective-permute-done((bf16[192,2560]{1,0:T(8,128)(2,1)}, bf16[192,2560]{1,0:T(8,128)(2,1)}, u32[]{:S(2)}, u32[]{:S(2)}) %collective-permute-start.55) | collective-permute-done | bytes 983072 | tf_op jit(solution)/shard_map/ppermute | solution.py:19
  509.1 19.6 %collective-permute-done.59 = bf16[192,2560]{1,0:T(8,128)(2,1)S(1)} collective-permute-done((bf16[192,2560]{1,0:T(8,128)(2,1)S(1)}, bf16[192,2560]{1,0:T(8,128)(2,1)S(1)}, u32[]{:S(2)}, u32[]{:S(2)}) %collective-permute-start.59) | collective-permute-done | bytes 983072 | tf_op jit(solution)/shard_map/ppermute | solution.py:19
  531.5 11.9 %collective-permute-done.61 = bf16[96,2560]{1,0:T(8,128)(2,1)S(1)} collective-permute-done((bf16[96,2560]{1,0:T(8,128)(2,1)S(1)}, bf16[96,2560]{1,0:T(8,128)(2,1)S(1)}, u32[]{:S(2)}, u32[]{:S(2)}) %collective-permute-start.61) | collective-permute-done | bytes 491552 | tf_op jit(solution)/shard_map/ppermute | solution.py:19
  565.0 20.7 %multiply_convert_fusion = (bf16[1536,1024]{1,0:T(8,128)(2,1)}, bf16[1536,1024]{1,0:T(8,128)(2,1)}) fusion(f32[1536,1024]{1,0:T(8,128)} %copy-done.33, f32[1536,1024]{1,0:T(8,128)} %copy-done.34, bf16[1536,2560]{1,0:T(8,128)(2,1)} %copy-done.86, bf16[2560,1024]{1,0:T(8,128)(2,1)S(1)} %bitcast.498), kind=kOutput, calls=%fused_computation.24 | convolution fusion | flops 8090812416 | bytes 31981568 | tf_op jit(solution)/shard_map/dot_general | solution.py:144
  585.7 13.0 %fusion.110 = f32[1536,2560]{1,0:T(8,128)} fusion(bf16[1536,1024]{1,0:T(8,128)(2,1)} %get-tuple-element.1282, bf16[2560,1024]{1,0:T(8,128)(2,1)S(1)} %bitcast.490), kind=kOutput, calls=%fused_computation.423 | convolution fusion | flops 8053063680 | bytes 24117248 | tf_op jit(solution)/shard_map/dot_general | solution.py:150
  598.8 15.0 %add_convert_fusion = bf16[1536,2560]{1,0:T(8,128)(2,1)} fusion(f32[1536,2560]{1,0:T(8,128)} %fusion.110, bf16[1536,1024]{1,0:T(8,128)(2,1)} %get-tuple-element.1281, bf16[2560,1024]{1,0:T(8,128)(2,1)S(1)} %bitcast.494), kind=kOutput, calls=%fused_computation | convolution fusion | flops 8060928000 | bytes 31981568 | tf_op jit(solution)/shard_map/dot_general | solution.py:150
  619.1 10.9 %convolution_convert_fusion.2 = bf16[2560,1024]{1,0:T(8,128)(2,1)S(1)} fusion(bf16[1536,2560]{1,0:T(8,128)(2,1)} %copy-done.85, bf16[1536,1024]{1,0:T(8,128)(2,1)S(1)} %copy-done.102), kind=kOutput, calls=%fused_computation.30 | convolution fusion | flops 8055685120 | bytes 16252928 | tf_op jit(solution)/shard_map/dot_general | solution.py:156
  630.6 12.5 %convolution_convert_fusion.1 = bf16[2560,1024]{1,0:T(8,128)(2,1)S(1)} fusion(bf16[1536,2560]{1,0:T(8,128)(2,1)} %copy-done.85, bf16[1536,1024]{1,0:T(8,128)(2,1)S(1)} %copy-done.101), kind=kOutput, calls=%fused_computation.29 | convolution fusion | flops 8055685120 | bytes 16252928 | tf_op jit(solution)/shard_map/dot_general | solution.py:156
  656.5 22.7 %collective-permute-done.82 = bf16[2,320,1024]{2,1,0:T(8,128)(2,1)S(1)} collective-permute-done((bf16[2,320,1024]{2,1,0:T(8,128)(2,1)S(1)}, bf16[2,320,1024]{2,1,0:T(8,128)(2,1)S(1)}, u32[]{:S(2)}, u32[]{:S(2)}) %collective-permute-start.82) | collective-permute-done | bytes 1310752 | tf_op jit(solution)/shard_map/ppermute | solution.py:27
  686.5 15.6 %collective-permute-done.118 = bf16[320,1024]{1,0:T(8,128)(2,1)} collective-permute-done((bf16[320,1024]{1,0:T(8,128)(2,1)}, bf16[320,1024]{1,0:T(8,128)(2,1)}, u32[]{:S(2)}, u32[]{:S(2)}) %collective-permute-start.118) | collective-permute-done | bytes 655392 | tf_op jit(solution)/shard_map/ppermute | solution.py:19
  702.1 11.5 %collective-permute-done.119 = bf16[320,1024]{1,0:T(8,128)(2,1)} collective-permute-done((bf16[320,1024]{1,0:T(8,128)(2,1)}, bf16[320,1024]{1,0:T(8,128)(2,1)}, u32[]{:S(2)}, u32[]{:S(2)}) %collective-permute-start.119) | collective-permute-done | bytes 655392 | tf_op jit(solution)/shard_map/ppermute | solution.py:19
  721.1 17.7 %collective-permute-done.69 = bf16[192,2560]{1,0:T(8,128)(2,1)S(1)} collective-permute-done((bf16[192,2560]{1,0:T(8,128)(2,1)S(1)}, bf16[192,2560]{1,0:T(8,128)(2,1)S(1)}, u32[]{:S(2)}, u32[]{:S(2)}) %collective-permute-start.69) | collective-permute-done | bytes 983072 | tf_op jit(solution)/shard_map/ppermute | solution.py:19
  750.8 16.9 %collective-permute-done.71 = f32[2688]{0:T(1024)S(1)} collective-permute-done((f32[2688]{0:T(1024)S(1)}, f32[2688]{0:T(1024)S(1)}, u32[]{:S(2)}, u32[]{:S(2)}) %collective-permute-start.71) | collective-permute-done | bytes 10784 | tf_op jit(solution)/shard_map/ppermute | solution.py:19
  792.1 15.8 %collective-permute-done.85 = bf16[2,320,1024]{2,1,0:T(8,128)(2,1)S(1)} collective-permute-done((bf16[2,320,1024]{2,1,0:T(8,128)(2,1)S(1)}, bf16[2,320,1024]{2,1,0:T(8,128)(2,1)S(1)}, u32[]{:S(2)}, u32[]{:S(2)}) %collective-permute-start.85) | collective-permute-done | bytes 1310752 | tf_op jit(solution)/shard_map/ppermute | solution.py:27
  823.6 28.1 %attention_backward.1 = (f32[768,768]{1,0:T(8,128)S(1)}, bf16[3072,512]{1,0:T(8,128)(2,1)S(1)}) custom-call(s32[1]{0:T(128)} %bitcast.info_ref, bf16[768,768]{1,0:T(8,128)(2,1)S(1)} %copy-done.17, bf16[3072,512]{1,0:T(8,128)(2,1)S(1)} %copy-done.9, bf16[768,768]{1,0:T(8,128)(2,1)S(1)} %multiply_convert_fusion.2.do_ref), custom_call_target="tpu_custom_call" | custom-call | flops 13589544960 | bytes 11010048 | tf_op jit(solution)/shard_map/attention_backward/pallas_call | solution.py:259
  877.8 23.2 %collective-permute-done.86 = bf16[4,320,768]{2,1,0:T(8,128)(2,1)} collective-permute-done((bf16[4,320,768]{2,1,0:T(8,128)(2,1)}, bf16[4,320,768]{2,1,0:T(8,128)(2,1)}, u32[]{:S(2)}, u32[]{:S(2)}) %collective-permute-start.86) | collective-permute-done | bytes 1966112 | tf_op jit(solution)/shard_map/ppermute | solution.py:27
  907.1 12.0 %collective-permute-done.106 = bf16[320,768]{1,0:T(8,128)(2,1)S(1)} collective-permute-done((bf16[320,768]{1,0:T(8,128)(2,1)S(1)}, bf16[320,768]{1,0:T(8,128)(2,1)S(1)}, u32[]{:S(2)}, u32[]{:S(2)}) %collective-permute-start.106) | collective-permute-done | bytes 491552 | tf_op jit(solution)/shard_map/ppermute | solution.py:27
  927.6 17.5 %collective-permute-done.79 = bf16[768,128]{1,0:T(8,128)(2,1)S(1)} collective-permute-done((bf16[768,128]{1,0:T(8,128)(2,1)S(1)}, bf16[768,128]{1,0:T(8,128)(2,1)S(1)}, u32[]{:S(2)}, u32[]{:S(2)}) %collective-permute-start.79) | collective-permute-done | bytes 196640 | tf_op jit(solution)/shard_map/ppermute | solution.py:34
  956.6 10.2 collective-permute-done.108
  998.7 12.0 %collective-permute-done.100 = bf16[320,768]{1,0:T(8,128)(2,1)S(1)} collective-permute-done((bf16[320,768]{1,0:T(8,128)(2,1)S(1)}, bf16[320,768]{1,0:T(8,128)(2,1)S(1)}, u32[]{:S(2)}, u32[]{:S(2)}) %collective-permute-start.100) | collective-permute-done | bytes 491552 | tf_op jit(solution)/shard_map/ppermute | solution.py:27
  (695 shorter events, 531.5 us)
Async XLA Ops:
  99.4 33.8 %collective-permute-start.16 = (bf16[2,320,1024]{2,1,0:T(8,128)(2,1)S(1)}, bf16[2,320,1024]{2,1,0:T(8,128)(2,1)S(1)}, u32[]{:S(2)}, u32[]{:S(2)}) collective-permute-start(bf16[2,320,1024]{2,1,0:T(8,128)(2,1)S(1)} %pad_maximum_fusion.10), channel_id=1, source_target_pairs={{0,16},{16,0},{1,17},{17,1},{2,18},{18,2},{3,19},{19,3},{4,20},{20... | collective-permute-start | bytes 3932168 | tf_op jit(solution)/shard_map/ppermute | solution.py:27
  136.7 56.9 %collective-permute-start.26 = (bf16[3,320,768]{2,1,0:T(8,128)(2,1)S(1)}, bf16[3,320,768]{2,1,0:T(8,128)(2,1)}, u32[]{:S(2)}, u32[]{:S(2)}) collective-permute-start(bf16[3,320,768]{2,1,0:T(8,128)(2,1)S(1)} %pad_maximum_fusion.9), channel_id=1, source_target_pairs={{0,16},{16,0},{1,17},{17,1},{2,18},{18,2},{3,19},{19,3},{4,20},{20... | collective-permute-start | bytes 4423688 | tf_op jit(solution)/shard_map/ppermute | solution.py:27
  157.6 35.2 %collective-permute-start.25 = (bf16[3072,128]{1,0:T(8,128)(2,1)S(1)}, bf16[3072,128]{1,0:T(8,128)(2,1)S(1)}, u32[]{:S(2)}, u32[]{:S(2)}) collective-permute-start(bf16[3072,128]{1,0:T(8,128)(2,1)S(1)} %pad_maximum_fusion.25), channel_id=1, source_target_pairs={{0,2},{1,3},{2,0},{3,1},{4,6},{5,7},{6,4},{7,5},{8,10},{9,11},{10,... | collective-permute-start | bytes 2359304 | tf_op jit(solution)/shard_map/ppermute | solution.py:19
  157.9 31.7 %collective-permute-start.23 = (bf16[320,1024]{1,0:T(8,128)(2,1)S(1)}, bf16[320,1024]{1,0:T(8,128)(2,1)S(1)}, u32[]{:S(2)}, u32[]{:S(2)}) collective-permute-start(bf16[320,1024]{1,0:T(8,128)(2,1)S(1)} %copy-done.77), channel_id=1, source_target_pairs={{0,4},{4,0},{8,12},{12,8},{1,5},{5,1},{9,13},{13,9},{2,6},{6,2},{1... | collective-permute-start | bytes 1966088 | tf_op jit(solution)/shard_map/ppermute | solution.py:19
  214.8 38.4 %collective-permute-start.29 = (bf16[320,1024]{1,0:T(8,128)(2,1)}, bf16[320,1024]{1,0:T(8,128)(2,1)}, u32[]{:S(2)}, u32[]{:S(2)}) collective-permute-start(bf16[320,1024]{1,0:T(8,128)(2,1)} %pad_maximum_fusion.29), channel_id=1, source_target_pairs={{0,8},{4,12},{8,0},{12,4},{1,9},{5,13},{9,1},{13,5},{2,10},{6,14},... | collective-permute-start | bytes 1966088 | tf_op jit(solution)/shard_map/ppermute | solution.py:19
  217.2 36.0 %collective-permute-start.30 = (bf16[2,320,1024]{2,1,0:T(8,128)(2,1)S(1)}, bf16[2,320,1024]{2,1,0:T(8,128)(2,1)S(1)}, u32[]{:S(2)}, u32[]{:S(2)}) collective-permute-start(bf16[2,320,1024]{2,1,0:T(8,128)(2,1)S(1)} %pad_maximum_fusion.11), channel_id=1, source_target_pairs={{0,16},{16,0},{1,17},{17,1},{2,18},{18,2},{3,19},{19,3},{4,20},{20... | collective-permute-start | bytes 3932168 | tf_op jit(solution)/shard_map/ppermute | solution.py:27
  267.8 32.8 %collective-permute-start.33 = (bf16[2,320,1024]{2,1,0:T(8,128)(2,1)}, bf16[2,320,1024]{2,1,0:T(8,128)(2,1)}, u32[]{:S(2)}, u32[]{:S(2)}) collective-permute-start(bf16[2,320,1024]{2,1,0:T(8,128)(2,1)} %bitcast.48), channel_id=1, source_target_pairs={{0,16},{16,0},{1,17},{17,1},{2,18},{18,2},{3,19},{19,3},{4,20},{20... | collective-permute-start | bytes 3932168 | tf_op jit(solution)/shard_map/ppermute | solution.py:27
  268.5 32.1 %collective-permute-start.34 = (bf16[192,2560]{1,0:T(8,128)(2,1)}, bf16[192,2560]{1,0:T(8,128)(2,1)}, u32[]{:S(2)}, u32[]{:S(2)}) collective-permute-start(bf16[192,2560]{1,0:T(8,128)(2,1)} %fusion.40), channel_id=1, source_target_pairs={{0,2},{1,3},{2,0},{3,1},{4,6},{5,7},{6,4},{7,5},{8,10},{9,11},{10,... | collective-permute-start | bytes 2949128 | tf_op jit(solution)/shard_map/ppermute | solution.py:19
  268.8 31.8 %collective-permute-start.32 = (bf16[320,1024]{1,0:T(8,128)(2,1)}, bf16[320,1024]{1,0:T(8,128)(2,1)}, u32[]{:S(2)}, u32[]{:S(2)}) collective-permute-start(bf16[320,1024]{1,0:T(8,128)(2,1)} %concatenate.188), channel_id=1, source_target_pairs={{0,8},{4,12},{8,0},{12,4},{1,9},{5,13},{9,1},{13,5},{2,10},{6,14},... | collective-permute-start | bytes 1966088 | tf_op jit(solution)/shard_map/ppermute | solution.py:19
  306.2 38.0 %collective-permute-start.36 = (bf16[2,320,1024]{2,1,0:T(8,128)(2,1)S(1)}, bf16[2,320,1024]{2,1,0:T(8,128)(2,1)S(1)}, u32[]{:S(2)}, u32[]{:S(2)}) collective-permute-start(bf16[2,320,1024]{2,1,0:T(8,128)(2,1)S(1)} %copy-done.1), channel_id=1, source_target_pairs={{0,16},{16,0},{1,17},{17,1},{2,18},{18,2},{3,19},{19,3},{4,20},{20... | collective-permute-start | bytes 3932168 | tf_op jit(solution)/shard_map/ppermute | solution.py:27
  307.9 36.4 %collective-permute-start.39 = (bf16[192,2560]{1,0:T(8,128)(2,1)S(1)}, bf16[192,2560]{1,0:T(8,128)(2,1)S(1)}, u32[]{:S(2)}, u32[]{:S(2)}) collective-permute-start(bf16[192,2560]{1,0:T(8,128)(2,1)S(1)} %multiply_convert_fusion.3), channel_id=1, source_target_pairs={{0,4},{4,0},{8,12},{12,8},{1,5},{5,1},{9,13},{13,9},{2,6},{6,2},{1... | collective-permute-start | bytes 2949128 | tf_op jit(solution)/shard_map/ppermute | solution.py:19
  308.2 36.1 %collective-permute-start.38 = (bf16[192,2560]{1,0:T(8,128)(2,1)S(1)}, bf16[192,2560]{1,0:T(8,128)(2,1)S(1)}, u32[]{:S(2)}, u32[]{:S(2)}) collective-permute-start(bf16[192,2560]{1,0:T(8,128)(2,1)S(1)} %multiply_convert_fusion.3), channel_id=1, source_target_pairs={{0,2},{1,3},{2,0},{3,1},{4,6},{5,7},{6,4},{7,5},{8,10},{9,11},{10,... | collective-permute-start | bytes 2949128 | tf_op jit(solution)/shard_map/ppermute | solution.py:19
  309.2 35.0 %collective-permute-start.35 = (bf16[192,2560]{1,0:T(8,128)(2,1)S(1)}, bf16[192,2560]{1,0:T(8,128)(2,1)S(1)}, u32[]{:S(2)}, u32[]{:S(2)}) collective-permute-start(bf16[192,2560]{1,0:T(8,128)(2,1)S(1)} %multiply_convert_fusion.3), channel_id=1, source_target_pairs={{0,1},{1,0},{2,3},{3,2},{4,5},{5,4},{6,7},{7,6},{8,9},{9,8},{10,11... | collective-permute-start | bytes 2949128 | tf_op jit(solution)/shard_map/ppermute | solution.py:19
  309.3 33.2 %collective-permute-start.37 = (bf16[320,1024]{1,0:T(8,128)(2,1)S(1)}, bf16[320,1024]{1,0:T(8,128)(2,1)S(1)}, u32[]{:S(2)}, u32[]{:S(2)}) collective-permute-start(bf16[320,1024]{1,0:T(8,128)(2,1)S(1)} %pad_maximum_fusion.30), channel_id=1, source_target_pairs={{0,8},{4,12},{8,0},{12,4},{1,9},{5,13},{9,1},{13,5},{2,10},{6,14},... | collective-permute-start | bytes 1966088 | tf_op jit(solution)/shard_map/ppermute | solution.py:19
  630.2 50.6 %collective-permute-start.64 = (bf16[3,192,2560]{2,1,0:T(8,128)(2,1)S(1)}, bf16[3,192,2560]{2,1,0:T(8,128)(2,1)S(1)}, u32[]{:S(2)}, u32[]{:S(2)}) collective-permute-start(bf16[3,192,2560]{2,1,0:T(8,128)(2,1)S(1)} %bitcast.536), channel_id=1, source_target_pairs={{0,1},{1,0},{2,3},{3,2},{4,5},{5,4},{6,7},{7,6},{8,9},{9,8},{10,11... | collective-permute-start | bytes 8847368 | tf_op jit(solution)/shard_map/ppermute | solution.py:19
  651.0 32.3 %collective-permute-start.66 = (bf16[96,2560]{1,0:T(8,128)(2,1)}, bf16[96,2560]{1,0:T(8,128)(2,1)S(1)}, u32[]{:S(2)}, u32[]{:S(2)}) collective-permute-start(bf16[96,2560]{1,0:T(8,128)(2,1)} %get-tuple-element.1361), channel_id=1, source_target_pairs={{0,4},{4,0},{8,12},{12,8},{1,5},{5,1},{9,13},{13,9},{2,6},{6,2},{1... | collective-permute-start | bytes 1474568 | tf_op jit(solution)/shard_map/ppermute | solution.py:19
  652.2 31.0 %collective-permute-start.68 = (bf16[96,2560]{1,0:T(8,128)(2,1)}, bf16[96,2560]{1,0:T(8,128)(2,1)}, u32[]{:S(2)}, u32[]{:S(2)}) collective-permute-start(bf16[96,2560]{1,0:T(8,128)(2,1)} %get-tuple-element.1362), channel_id=1, source_target_pairs={{0,2},{1,3},{2,0},{3,1},{4,6},{5,7},{6,4},{7,5},{8,10},{9,11},{10,... | collective-permute-start | bytes 1474568 | tf_op jit(solution)/shard_map/ppermute | solution.py:19
  655.1 47.1 %collective-permute-start.118 = (bf16[320,1024]{1,0:T(8,128)(2,1)}, bf16[320,1024]{1,0:T(8,128)(2,1)}, u32[]{:S(2)}, u32[]{:S(2)}) collective-permute-start(bf16[320,1024]{1,0:T(8,128)(2,1)} %get-tuple-element.1346), channel_id=1, source_target_pairs={{0,8},{4,12},{8,0},{12,4},{1,9},{5,13},{9,1},{13,5},{2,10},{6,14},... | collective-permute-start | bytes 1966088 | tf_op jit(solution)/shard_map/ppermute | solution.py:19
  679.3 34.4 %collective-permute-start.119 = (bf16[320,1024]{1,0:T(8,128)(2,1)}, bf16[320,1024]{1,0:T(8,128)(2,1)}, u32[]{:S(2)}, u32[]{:S(2)}) collective-permute-start(bf16[320,1024]{1,0:T(8,128)(2,1)} %get-tuple-element.1347), channel_id=1, source_target_pairs={{0,8},{4,12},{8,0},{12,4},{1,9},{5,13},{9,1},{13,5},{2,10},{6,14},... | collective-permute-start | bytes 1966088 | tf_op jit(solution)/shard_map/ppermute | solution.py:19
  680.8 35.1 %collective-permute-start.83 = (bf16[2,320,1024]{2,1,0:T(8,128)(2,1)}, bf16[2,320,1024]{2,1,0:T(8,128)(2,1)}, u32[]{:S(2)}, u32[]{:S(2)}) collective-permute-start(bf16[2,320,1024]{2,1,0:T(8,128)(2,1)} %get-tuple-element.1238), channel_id=1, source_target_pairs={{0,16},{16,0},{1,17},{17,1},{2,18},{18,2},{3,19},{19,3},{4,20},{20... | collective-permute-start | bytes 3932168 | tf_op jit(solution)/shard_map/ppermute | solution.py:27
  684.6 54.1 %collective-permute-start.69 = (bf16[192,2560]{1,0:T(8,128)(2,1)S(1)}, bf16[192,2560]{1,0:T(8,128)(2,1)S(1)}, u32[]{:S(2)}, u32[]{:S(2)}) collective-permute-start(bf16[192,2560]{1,0:T(8,128)(2,1)S(1)} %pad_maximum_fusion.24), channel_id=1, source_target_pairs={{0,4},{4,0},{8,12},{12,8},{1,5},{5,1},{9,13},{13,9},{2,6},{6,2},{1... | collective-permute-start | bytes 2949128 | tf_op jit(solution)/shard_map/ppermute | solution.py:19
  685.0 54.4 %collective-permute-start.67 = (bf16[192,2560]{1,0:T(8,128)(2,1)S(1)}, bf16[192,2560]{1,0:T(8,128)(2,1)S(1)}, u32[]{:S(2)}, u32[]{:S(2)}) collective-permute-start(bf16[192,2560]{1,0:T(8,128)(2,1)S(1)} %pad_maximum_fusion.23), channel_id=1, source_target_pairs={{0,2},{1,3},{2,0},{3,1},{4,6},{5,7},{6,4},{7,5},{8,10},{9,11},{10,... | collective-permute-start | bytes 2949128 | tf_op jit(solution)/shard_map/ppermute | solution.py:19
  715.8 33.8 %collective-permute-start.120 = (bf16[320,1024]{1,0:T(8,128)(2,1)S(1)}, bf16[320,1024]{1,0:T(8,128)(2,1)S(1)}, u32[]{:S(2)}, u32[]{:S(2)}) collective-permute-start(bf16[320,1024]{1,0:T(8,128)(2,1)S(1)} %fusion.69), channel_id=1, source_target_pairs={{0,4},{4,0},{8,12},{12,8},{1,5},{5,1},{9,13},{13,9},{2,6},{6,2},{1... | collective-permute-start | bytes 1966088 | tf_op jit(solution)/shard_map/ppermute | solution.py:19
  718.1 49.6 %collective-permute-start.112 = (bf16[320,1024]{1,0:T(8,128)(2,1)S(1)}, bf16[320,1024]{1,0:T(8,128)(2,1)S(1)}, u32[]{:S(2)}, u32[]{:S(2)}) collective-permute-start(bf16[320,1024]{1,0:T(8,128)(2,1)S(1)} %get-tuple-element.1350), channel_id=1, source_target_pairs={{0,8},{4,12},{8,0},{12,4},{1,9},{5,13},{9,1},{13,5},{2,10},{6,14},... | collective-permute-start | bytes 1966088 | tf_op jit(solution)/shard_map/ppermute | solution.py:19
  720.5 54.9 %collective-permute-start.113 = (bf16[320,1024]{1,0:T(8,128)(2,1)S(1)}, bf16[320,1024]{1,0:T(8,128)(2,1)S(1)}, u32[]{:S(2)}, u32[]{:S(2)}) collective-permute-start(bf16[320,1024]{1,0:T(8,128)(2,1)S(1)} %get-tuple-element.1351), channel_id=1, source_target_pairs={{0,8},{4,12},{8,0},{12,4},{1,9},{5,13},{9,1},{13,5},{2,10},{6,14},... | collective-permute-start | bytes 1966088 | tf_op jit(solution)/shard_map/ppermute | solution.py:19
  738.7 36.8 %collective-permute-start.84 = (bf16[2,320,1024]{2,1,0:T(8,128)(2,1)S(1)}, bf16[2,320,1024]{2,1,0:T(8,128)(2,1)S(1)}, u32[]{:S(2)}, u32[]{:S(2)}) collective-permute-start(bf16[2,320,1024]{2,1,0:T(8,128)(2,1)S(1)} %copy-done.64), channel_id=1, source_target_pairs={{0,16},{16,0},{1,17},{17,1},{2,18},{18,2},{3,19},{19,3},{4,20},{20... | collective-permute-start | bytes 3932168 | tf_op jit(solution)/shard_map/ppermute | solution.py:27
  743.3 33.2 %collective-permute-start.74 = (bf16[192,2560]{1,0:T(8,128)(2,1)S(1)}, bf16[192,2560]{1,0:T(8,128)(2,1)S(1)}, u32[]{:S(2)}, u32[]{:S(2)}) collective-permute-start(bf16[192,2560]{1,0:T(8,128)(2,1)S(1)} %get-tuple-element.1271), channel_id=1, source_target_pairs={{0,2},{1,3},{2,0},{3,1},{4,6},{5,7},{6,4},{7,5},{8,10},{9,11},{10,... | collective-permute-start | bytes 2949128 | tf_op jit(solution)/shard_map/ppermute | solution.py:19
  776.7 35.9 %collective-permute-start.75 = (bf16[2,192,2560]{2,1,0:T(8,128)(2,1)S(1)}, bf16[2,192,2560]{2,1,0:T(8,128)(2,1)S(1)}, u32[]{:S(2)}, u32[]{:S(2)}) collective-permute-start(bf16[2,192,2560]{2,1,0:T(8,128)(2,1)S(1)} %pad_maximum_fusion.7), channel_id=1, source_target_pairs={{0,1},{1,0},{2,3},{3,2},{4,5},{5,4},{6,7},{7,6},{8,9},{9,8},{10,11... | collective-permute-start | bytes 5898248 | tf_op jit(solution)/shard_map/ppermute | solution.py:19
  809.6 144.4 %collective-permute-start.115 = (bf16[320,1024]{1,0:T(8,128)(2,1)}, bf16[320,1024]{1,0:T(8,128)(2,1)}, u32[]{:S(2)}, u32[]{:S(2)}) collective-permute-start(bf16[320,1024]{1,0:T(8,128)(2,1)} %get-tuple-element.1348), channel_id=1, source_target_pairs={{0,8},{4,12},{8,0},{12,4},{1,9},{5,13},{9,1},{13,5},{2,10},{6,14},... | collective-permute-start | bytes 1966088 | tf_op jit(solution)/shard_map/ppermute | solution.py:19
  812.1 142.0 %collective-permute-start.116 = (bf16[320,1024]{1,0:T(8,128)(2,1)}, bf16[320,1024]{1,0:T(8,128)(2,1)}, u32[]{:S(2)}, u32[]{:S(2)}) collective-permute-start(bf16[320,1024]{1,0:T(8,128)(2,1)} %get-tuple-element.1349), channel_id=1, source_target_pairs={{0,8},{4,12},{8,0},{12,4},{1,9},{5,13},{9,1},{13,5},{2,10},{6,14},... | collective-permute-start | bytes 1966088 | tf_op jit(solution)/shard_map/ppermute | solution.py:19
  855.4 45.5 %collective-permute-start.86 = (bf16[4,320,768]{2,1,0:T(8,128)(2,1)}, bf16[4,320,768]{2,1,0:T(8,128)(2,1)}, u32[]{:S(2)}, u32[]{:S(2)}) collective-permute-start(bf16[4,320,768]{2,1,0:T(8,128)(2,1)} %dynamic-slice_bitcast_fusion.1), channel_id=1, source_target_pairs={{0,16},{16,0},{1,17},{17,1},{2,18},{18,2},{3,19},{19,3},{4,20},{20... | collective-permute-start | bytes 5898248 | tf_op jit(solution)/shard_map/ppermute | solution.py:27
  953.7 43.7 %collective-permute-start.92 = (bf16[2,192,2560]{2,1,0:T(8,128)(2,1)S(1)}, bf16[2,192,2560]{2,1,0:T(8,128)(2,1)S(1)}, u32[]{:S(2)}, u32[]{:S(2)}) collective-permute-start(bf16[2,192,2560]{2,1,0:T(8,128)(2,1)S(1)} %dynamic-slice_bitcast_fusion), channel_id=1, source_target_pairs={{0,1},{1,0},{2,3},{3,2},{4,5},{5,4},{6,7},{7,6},{8,9},{9,8},{10,11... | collective-permute-start | bytes 5898248 | tf_op jit(solution)/shard_map/ppermute | solution.py:19
  (203 other events, 3481.0 us)

commit v3 on v2

--- a/solution.py
+++ b/solution.py
@@ -14,18 +14,12 @@
 
 
 def flip(array, axis, bit):
-    link = Chain.link(axis, bit)
-    array = Chain.before(array, link)
-    got = lax.ppermute(array, axis, [(i, i ^ bit) for i in range(lax.axis_size(axis))])
-    return Chain.done(got, link)
+    return lax.ppermute(array, axis, [(i, i ^ bit) for i in range(lax.axis_size(axis))])
 
 
 def ring(array, axis, by=1):
     count = lax.axis_size(axis)
-    link = Chain.link(axis, 2)
-    array = Chain.before(array, link)
-    got = lax.ppermute(array, axis, [(i, (i + by) % count) for i in range(count)])
-    return Chain.done(got, link)
+    return lax.ppermute(array, axis, [(i, (i + by) % count) for i in range(count)])
 
 
 def shifted(array, axis, by):
@@ -34,36 +28,8 @@
     return lax.ppermute(array, axis, pairs)
 
 
-class Chain:
-    on = ()
-    sent = {}
-
-    @staticmethod
-    def link(axis, bit=1):
-        if axis == "fsdp":
-            return "x"
-        if axis == "tp":
-            return "y" if bit > 1 else None
-        return "z" if bit != 1 else "zl"
-
-    @staticmethod
-    def before(array, link):
-        if link in Chain.on and len(Chain.sent.setdefault(link, [])) >= 1:
-            array = after(array, Chain.sent[link][-1])
-        return array
-
-    @staticmethod
-    def done(got, link):
-        Chain.sent.setdefault(link, []).append(got)
-        return got
-
-
 class Steps:
-    on = True
-
     def next(self):
-        if not Steps.on:
-            return
         self.__dict__.update(lax.optimization_barrier(dict(self.__dict__)))
 
     def drop(self, *names):
@@ -419,9 +385,6 @@
     first_key = (reach_back - jnp.minimum(ctx_rank, reach_back)) * rows
 
     at = Steps()
-    Steps.on = True
-    Chain.on = ()
-    Chain.sent = {}
     gains = jnp.pad(jnp.stack([attn_gain, mlp_gain], axis=1), ((0, 0), (0, 126)))
 
     def qkv_columns(rank):
@@ -470,30 +433,32 @@
     at.next()
 
     qkv_part = placed(at.drop("qkv_x")[0])
-    query_part = qkv_part[:, :slot_width]
-    kv_part = qkv_part[:, slot_width : slot_width + kv_width]
     gain_attn = wide(qkv_part[:, slot_width + kv_width])
     gain_mlp = wide(qkv_part[:, slot_width + kv_width + 1])
     at.normed = low(inputs * scale_one * gain_attn)
-    at.kv_own = low(turn(nn(at.normed, kv_part), kv_cosine, kv_sine))
-    query_raw = nn(at.normed, query_part).reshape(rows, slot_count, head_size)
+    at.qkv_raw = nn(at.normed, qkv_part)
+    at.gate_a = over_fsdp(at.gate_pair[0])
+    at.out_2 = ring(at.out_1, "ctx")
+    at.up_got = flip(at.up_sent, "ctx", 1)
+    at.next()
+    (qkv_raw,) = at.drop("qkv_raw")
+    kv_raw = qkv_raw[:, slot_width : slot_width + kv_width]
+    at.kv_own = low(turn(kv_raw, kv_cosine, kv_sine))
+    query_raw = qkv_raw[:, :slot_width].reshape(rows, slot_count, head_size)
     queries = low(turn(query_raw, cosine[:, None, :], sine[:, None, :]) * query_scale)
     at.queries = queries.reshape(rows, slot_width)
-    at.gate_x = over_fsdp(at.gate_pair)
-    at.out_2 = ring(at.out_1, "ctx")
-    at.up_got = flip(at.up_sent, "ctx", 1)
-    at.far_1 = far(quarters(at.gate_pair)[:1])
+    at.gate_b = over_fsdp(at.gate_pair[1])
+    at.out_3 = ring(at.out_2, "ctx")
     at.next()
     normed = at.normed
     at.up_pair = paired(*at.drop("up_mine", "up_got"))
-    at.out_near = jnp.stack([at.out_0, at.out_1, at.out_2])
+    at.out_near = jnp.stack([at.out_0, at.out_1, at.out_2, at.out_3])
     at.next()
     out_x = over_fsdp(at.out_near)
     at.chunks = [shifted(at.kv_own, "ctx", by) for by in range(reach_back, 0, -1)]
-    at.out_3 = ring(at.out_2, "ctx")
     at.next()
     at.kv_column = jnp.concatenate(at.drop("chunks")[0] + [at.kv_own], axis=0)
-    at.gate_far = jnp.concatenate(quarters(at.gate_pair)[1:3], axis=0)
+    at.gate_far = jnp.concatenate(quarters(at.gate_pair)[:2], axis=0)
     at.drop("out_0", "out_1", "out_2", "kv_own", "qkv_3")
     at.next()
     at.kv_over_y = flip(at.kv_column, "tp", 2)
@@ -505,20 +470,20 @@
     at.down_pair = paired(*at.drop("down_mine", "down_got"))
     at.next()
     at.kv_other = flip(at.kv_pair, "tp", 1)
-    at.out_y = over_fsdp(at.out_3)
+    at.far_1 = far(quarters(at.gate_pair)[2:3])
+    (out_x,) = at.drop("out_x")
+    at.out_part = placed([[block[i] for block in out_x] for i in range(ctx_count)])
     at.next()
     kv_pair, kv_other = at.drop("kv_pair", "kv_other")
     at.keyvals = jnp.concatenate(
         swapped([kv_pair[0], kv_other[0], kv_pair[1], kv_other[1]], tp_rank), axis=1
     )
-    at.mixed_far = jnp.concatenate(quarters(at.gate_pair)[3:] + quarters(at.up_pair)[:1], axis=0)
+    at.mixed_far = jnp.concatenate(quarters(at.gate_pair)[3:] + quarters(at.up_pair)[:2], axis=0)
     at.drop("up_sent", "down_sent", "gate_far", "out_near")
     at.next()
 
     queries, keyvals = at.queries, at.keyvals
     at.attended = attention_forward(queries, keyvals, live, first_key, head_size)
-    out_x, out_y = at.drop("out_x", "out_y")
-    at.out_part = placed([[block[i] for block in out_x] for i in range(3)] + [out_y])
     blocks = low(nt(at.attended, at.out_part)).reshape(2, 2, part_rows, -1)
     at.kept, at.sent = take(blocks, core_rank, 1), take(blocks, 1 - core_rank, 1)
     at.up_x = over_fsdp(at.up_pair)
@@ -527,12 +492,11 @@
 
     out_part = at.out_part
     quarter_rows = at.far_1[0].shape[0]
+    at.got = flip(at.sent, "tp", 1)
     at.gate_other = jnp.concatenate(
-        at.far_1 + [at.far_2, at.far_3[:quarter_rows]], axis=0
+        [at.far_2] + at.far_1 + [at.far_3[:quarter_rows]], axis=0
     ).reshape(at.gate_pair.shape)
-    at.up_far = jnp.concatenate(quarters(at.up_pair)[1:3], axis=0)
-    at.next()
-    at.got = flip(at.sent, "tp", 1)
+    at.up_far = jnp.concatenate(quarters(at.up_pair)[2:], axis=0)
     at.next()
     summed = wide(at.kept) + wide(at.got)
     at.kept, at.sent = take(summed, y_rank), low(take(summed, 1 - y_rank))
@@ -600,39 +564,39 @@
     scale_two = lax.rsqrt(jnp.mean(residual * residual, axis=-1, keepdims=True) + epsilon)
     at.residual = residual
     at.part = low(residual * scale_two * gain_mlp)
-    at.mixed_far = jnp.concatenate(quarters(at.up_pair)[3:] + quarters(at.down_pair)[:1], axis=0)
+    at.down_quarters = quarters(at.down_pair)
     at.next()
     residual = at.residual
     gather_sides()
     at.down_x = over_fsdp(at.down_pair)
-    at.far_5 = flip(at.mixed_far, "ctx", 2)
+    at.far_5 = flip(at.down_quarters[0], "ctx", 2)
+    at.up_a, at.up_b = at.far_3[quarter_rows:], at.far_4
+    gate_a, gate_b, gate_z = at.drop("gate_a", "gate_b", "gate_z")
+    at.gate_full = mlp_placed([jnp.stack(pair) for pair in zip(gate_a, gate_b)], gate_z)
     at.next()
     between_sides_and_corners()
-    at.up_a = jnp.concatenate([at.far_3[quarter_rows:], at.far_4[:quarter_rows]], axis=0)
-    at.up_b = jnp.concatenate([at.far_4[quarter_rows:], at.far_5[:quarter_rows]], axis=0)
-    at.down_quarters = quarters(at.down_pair)[1:]
     at.next()
     gather_corners()
     at.up_a = over_fsdp(at.up_a)
-    at.far_6 = flip(at.down_quarters[0], "ctx", 2)
+    at.far_6 = flip(at.down_quarters[1], "ctx", 2)
     at.next()
     between_corners_and_core()
-    at.down_a = jnp.concatenate([at.far_5[quarter_rows:], at.far_6], axis=0)
     at.next()
     at.core_corner = flip(at.corner, "tp", 1)
     at.next()
     at.normed_two = gathered()
-    gate_full = mlp_placed(*at.drop("gate_x", "gate_z"))
-    at.gate_proj = nn(at.normed_two, gate_full)
+    at.gate_proj = nn(at.normed_two, at.gate_full)
     at.up_b = over_fsdp(at.up_b)
-    at.far_7 = flip(at.down_quarters[1], "ctx", 2)
-    at.next()
+    at.far_7 = flip(at.down_quarters[2], "ctx", 2)
+    at.down_a = jnp.concatenate([at.far_5, at.far_6], axis=0)
+    at.next()
+    gate_full = at.gate_full
     up_a, up_b = at.drop("up_a", "up_b")
     up_z = [jnp.stack(pair) for pair in zip(up_a, up_b)]
     up_full = mlp_placed(at.drop("up_x")[0], up_z)
     at.up_proj = nn(at.normed_two, up_full)
     at.down_a = over_fsdp(at.down_a)
-    at.far_8 = flip(at.down_quarters[2], "ctx", 2)
+    at.far_8 = flip(at.down_quarters[3], "ctx", 2)
     at.next()
     at.down_b = jnp.concatenate([at.far_7, at.far_8], axis=0)
     at.next()
@@ -649,12 +613,12 @@
     down_full = mlp_placed(down_x, down_z)
     before_sum(low(nt(at.hidden_act, down_full)))
     at.next()
+    at.got_corner = flip(at.theirs_corner, "tp", 1)
+    at.next()
+    between_core_and_corners()
+    at.next()
+    sum_corners()
     at.got = flip(at.theirs, "tp", 1)
-    at.got_corner = flip(at.theirs_corner, "tp", 1)
-    at.next()
-    between_core_and_corners()
-    at.next()
-    sum_corners()
     at.next()
     between_corners_and_sides()
     at.next()
@@ -703,6 +667,14 @@
             for high in (1 - hi_rank, hi_rank)
         ]
 
+    def blocks_of(grad):
+        blocks = grad.reshape(fsdp_count, 2, 2, -1, half)
+        return [
+            terms(lambda owner: take(take(blocks, owner), high)[lo], "fsdp")
+            for high in (1 - hi_rank, hi_rank)
+            for lo in range(2)
+        ]
+
     def near_split(mine):
         return wide(take(mine, lo_rank)), low(take(mine, 1 - lo_rank))
 
@@ -711,182 +683,194 @@
         return jnp.concatenate([near, rest_of[:, :rest]], axis=1)
 
     at.d_ffn = gathered()
-    at.down_far, at.down_own = far_and_own(low(tn(at.d_ffn, at.hidden_act)))
-    at.next()
-    Steps.on = False
-    Chain.on = ('x',)
-    Chain.sent = {}
-    at.down_far_got = around(at.down_far, "fsdp")
+    at.down_terms = blocks_of(low(tn(at.d_ffn, at.hidden_act)))
+    at.next()
+    at.down_x = [around(at.down_terms[0], "fsdp")]
     d_hidden = nn(at.d_ffn, down_full)
     at.d_gate = low(gelu_back(d_hidden * up_proj)[0])
     at.d_up = low(d_hidden * activated)
     at.next()
     at.drop("d_ffn", "hidden_act")
-    at.down_far = low(with_own(*at.drop("down_far", "down_far_got")))
-    at.next()
-    at.down_own_got = around(at.down_own, "fsdp")
+    at.down_x += [around(at.down_terms[1], "fsdp")]
+    at.gate_terms = blocks_of(low(tn(at.normed_two, at.d_gate)))
+    at.next()
+    at.down_far = [low(with_own(at.down_terms[i], at.down_x[i])) for i in range(2)]
+    at.next()
+    at.down_x += [around(at.down_terms[2], "fsdp"), around(at.down_terms[3], "fsdp")]
     at.down_got_0 = flip(at.down_far[0], "ctx", 2)
     before_sum(low(nt(at.d_gate, gate_full) + nt(at.d_up, up_full)))
     at.next()
+    at.got_corner = flip(at.theirs_corner, "tp", 1)
+    at.next()
+    between_core_and_corners()
+    at.drop("d_gate")
+    at.down_rest = jnp.split(at.down_far[1], 2)
+    at.next()
+    sum_corners()
     at.got = flip(at.theirs, "tp", 1)
-    at.got_corner = flip(at.theirs_corner, "tp", 1)
-    at.next()
-    between_core_and_corners()
-    at.next()
-    sum_corners()
-    at.down_got_1 = flip(at.down_far[1], "ctx", 2)
-    at.gate_far, at.gate_own = far_and_own(low(tn(at.normed_two, at.d_gate)))
-    at.next()
-    at.drop("d_gate")
+    at.gate_got = [around(at.gate_terms[0], "fsdp")]
+    at.down_got_1 = flip(at.down_rest[0], "ctx", 2)
+    at.next()
     between_corners_and_sides()
-    at.down_own = low(with_own(*at.drop("down_own", "down_own_got")))
     at.next()
     sum_sides()
-    at.gate_far_got = around(at.gate_far, "fsdp")
-    at.up_far, at.up_own = far_and_own(low(tn(at.normed_two, at.d_up)))
-    at.next()
-    at.drop("normed_two", "d_up")
-    at.gate_far = low(with_own(*at.drop("gate_far", "gate_far_got")))
+    down_terms, down_x = at.drop("down_terms", "down_x")
+    at.down_own = jnp.stack([low(with_own(down_terms[i], down_x[i])) for i in (2, 3)])
+    at.gate_got += [around(at.gate_terms[1], "fsdp"), around(at.gate_terms[2], "fsdp")]
+    at.down_got_2 = flip(at.down_rest[1], "ctx", 2)
+    at.up_terms = blocks_of(low(tn(at.normed_two, at.d_up)))
+    at.next()
+    at.drop("normed_two", "d_up", "down_far", "down_rest")
+    at.gate_far = [low(with_own(at.gate_terms[i], at.gate_got[i])) for i in range(2)]
     d_normed_two = summed()
     scaled = gain_mlp * d_normed_two
     inner_two = jnp.mean(scaled * residual, axis=-1, keepdims=True)
     at.d_residual = at.d_output + scale_two * scaled - residual * scale_two**3 * inner_two
-    gain_mlp_sums = jnp.sum(d_normed_two * residual * scale_two, axis=0)
-    at.vector = jnp.concatenate([gain_mlp_sums, jnp.full((128,), loss_part)])
+    at.gain_mlp_sums = jnp.sum(d_normed_two * residual * scale_two, axis=0)
     at.part = low(at.d_residual)
     at.next()
     at.over_y = flip(at.part, "tp", 2)
-    at.gate_own_got = around(at.gate_own, "fsdp")
-    at.gate_got_0 = flip(at.gate_far[0], "ctx", 2)
+    got_0, got_1, got_2 = at.drop("down_got_0", "down_got_1", "down_got_2")
+    down_got = jnp.stack([got_0, jnp.concatenate([got_1, got_2], axis=0)])
+    at.down_kept, at.down_sent = near_split(wide(at.drop("down_own")[0]) + wide(down_got))
+    at.gate_got += [around(at.gate_terms[3], "fsdp")]
+    at.up_got = [around(at.up_terms[0], "fsdp")]
+    at.gate_far_0 = flip(at.gate_far[0], "ctx", 2)
     at.next()
     at.pair = jnp.stack(at.drop("part", "over_y"))
     at.next()
     at.other = flip(at.pair, "tp", 1)
-    at.got_vector = flip(at.vector, "tp", 1)
     at.next()
     pair, other = at.drop("pair", "other")
     d_attn = swapped([pair[0], other[0], pair[1], other[1]], tp_rank)
     at.d_attn = jnp.concatenate(d_attn, axis=0)
-    down_got = jnp.stack(at.drop("down_got_0", "down_got_1"))
-    at.down_kept, at.down_sent = near_split(wide(at.down_own) + wide(down_got))
-    at.vector = at.vector + at.drop("got_vector")[0]
-    at.next()
-    at.drop("down_own", "down_far")
-    at.got_vector = flip(at.vector, "tp", 2)
+    at.next()
     at.down_got = flip(at.down_sent, "ctx", 1)
+    at.up_got += [around(at.up_terms[1], "fsdp")]
     live_columns = jnp.repeat(live, head_size).astype(jnp.float32)
     at.d_attended = low(nn(at.d_attn, out_part) * live_columns)
     out_grad = low(tn(at.d_attn, at.attended))
 
     own_rows = attn_gain.shape[0]
-    own_start = ((fsdp_rank * ctx_count + ctx_rank) * tp_count + tp_rank) * own_rows
+
+    def split_sums(columns):
+        rounded = low(columns)
+        return jnp.concatenate([rounded, low(columns - wide(rounded))], axis=-1)
+
+    def joined_sums(columns):
+        return columns[..., :64] + columns[..., 64:]
 
     def by_rows(grad):
         return grad.reshape(fsdp_count, ctx_count, tp_count * own_rows, -1)
 
-    at.out_terms = terms(lambda owner: take(by_rows(out_grad), owner), "fsdp")
-    at.gate_own = low(with_own(*at.drop("gate_own", "gate_own_got")))
+    def halves_of(grad):
+        grad = by_rows(grad)
+        turned = [take(grad, (ctx_rank - by) % ctx_count, 1) for by in range(1, ctx_count + 1)]
+        pairs = [jnp.stack(turned[:2], axis=1), jnp.stack(turned[2:], axis=1)]
+        return [terms(lambda owner: take(pair, owner), "fsdp") for pair in pairs]
+
+    at.out_terms = halves_of(out_grad)
     at.next()
     at.drop("attended", "d_attn", "down_sent")
-    at.vector = at.vector + at.drop("got_vector")[0]
-    at.next()
-    at.got_vector = flip(at.vector, "ctx", 1)
-    at.gate_got_1 = flip(at.gate_far[1], "ctx", 2)
-    at.up_far_got = around(at.up_far, "fsdp")
     at.d_queries, at.d_keyvals = attention_backward(
         queries, keyvals, at.d_attended, first_key, head_size
     )
+    at.up_got += [around(at.up_terms[2], "fsdp"), around(at.up_terms[3], "fsdp")]
+    at.gate_far_1 = flip(at.gate_far[1], "ctx", 2)
+    at.next()
     kv_blocks = jnp.stack(jnp.split(at.d_keyvals, tp_count, axis=1)).reshape(2, 2, -1, kv_width)
     at.kv_kept, at.kv_sent = take(kv_blocks, core_rank, 1), take(kv_blocks, 1 - core_rank, 1)
-    at.next()
     at.drop("d_attended", "d_keyvals")
+    at.next()
     at.kv_got = flip(at.kv_sent, "tp", 1)
     at.next()
-    at.vector = at.vector + at.drop("got_vector")[0]
     kv_sum = wide(at.kv_kept) + wide(at.kv_got)
     at.kv_kept, at.kv_sent = take(kv_sum, y_rank), low(take(kv_sum, 1 - y_rank))
-    at.up_far = low(with_own(*at.drop("up_far", "up_far_got")))
+    at.up_far = [low(with_own(at.up_terms[i], at.up_got[i])) for i in range(2)]
     at.next()
     at.kv_got = flip(at.kv_sent, "tp", 2)
-    at.got_vector = flip(at.vector, "ctx", 2)
-    at.up_got_0 = flip(at.up_far[0], "ctx", 2)
-    at.out_got = around(at.out_terms, "fsdp")
+    at.up_far_0 = flip(at.up_far[0], "ctx", 2)
+    at.out_got = [around(at.out_terms[0], "fsdp")]
     d_query_raw = turn(
         at.d_queries.reshape(rows, slot_count, head_size) * query_scale,
         cosine[:, None, :],
         -sine[:, None, :],
     )
     at.d_query_low = low(d_query_raw.reshape(rows, slot_width))
-    query_grad = by_rows(low(tn(normed, at.d_query_low)))
-    turned = [take(query_grad, (ctx_rank - by) % ctx_count, 1) for by in range(1, ctx_count + 1)]
-    first_half, second_half = jnp.stack(turned[:2], axis=1), jnp.stack(turned[2:], axis=1)
-    at.query_1 = terms(lambda owner: take(first_half, owner), "fsdp")
-    at.query_2 = terms(lambda owner: take(second_half, owner), "fsdp")
-    at.next()
-    at.drop("d_queries", "kv_sent", "gate_far")
-    at.vector = at.vector + at.drop("got_vector")[0]
+    at.query_terms = halves_of(low(tn(normed, at.d_query_low)))
+    at.next()
+    at.drop("d_queries", "kv_sent")
     kv_sum = (at.drop("kv_kept")[0] + wide(at.drop("kv_got")[0])).reshape(reach_back + 1, rows, -1)
     at.kv_low = [low(kv_sum[reach_back - by]) for by in range(1, reach_back + 1)]
     at.d_kv = kv_sum[reach_back]
-    out_mine = low(with_own(*at.drop("out_terms", "out_got")))
-    at.out_terms = terms(lambda owner: take(out_mine, owner), "ctx")
-    at.next()
+    at.out_1 = low(with_own(at.out_terms[0], at.out_got[0]))
+    at.next()
+    gate_terms, gate_got = at.drop("gate_terms", "gate_got")
+    gate_far_got = jnp.stack(at.drop("gate_far_0", "gate_far_1"))
+    gate_own = jnp.stack([with_own(gate_terms[i], gate_got[i]) for i in (2, 3)])
+    at.gate_kept, at.gate_sent = near_split(gate_own + wide(gate_far_got))
+    at.drop("gate_far")
     at.kv_got = [shifted(at.kv_low[by - 1], "ctx", -by) for by in range(1, reach_back + 1)]
-    at.up_own_got = around(at.up_own, "fsdp")
-    at.out_z = ring(at.out_terms[0], "ctx")
-    gate_got = jnp.stack(at.drop("gate_got_0", "gate_got_1"))
-    at.gate_kept, at.gate_sent = near_split(wide(at.gate_own) + wide(gate_got))
-    at.next()
-    at.drop("gate_own")
+    at.out_got += [around(at.out_terms[1], "fsdp")]
+    at.out_z = ring(at.out_1[0], "ctx")
+    at.next()
     d_kv = at.d_kv
     for got in at.drop("kv_got")[0]:
         d_kv = d_kv + wide(got)
     d_kv_low = low(turn(d_kv, kv_cosine, -kv_sine))
-    partial = low(nt(at.d_query_low, query_part) + nt(d_kv_low, kv_part))
+    at.d_qkv = jnp.concatenate(
+        [at.d_query_low, jnp.pad(d_kv_low, ((0, 0), (0, kv_width)))], axis=1
+    )
+    at.out_z = low(wide(at.out_z) + wide(at.out_1[1]))
+    at.next()
+    at.query_got = [around(at.query_terms[0], "fsdp")]
+    at.up_far_1 = flip(at.up_far[1], "ctx", 2)
+    at.gate_near = flip(at.gate_sent, "ctx", 1)
+    at.partial = low(nt(at.d_qkv, qkv_part))
+    at.next()
+    (partial,) = at.drop("partial")
+    d_kv_low = at.d_qkv[:, slot_width : slot_width + kv_width]
     gain_attn_sums = jnp.sum(wide(partial) * inputs * scale_one, axis=0)
-    gain_column = jnp.pad(gain_attn_sums[:, None], ((0, 0), (0, 127)))
-    kv_grad = low(jnp.concatenate([tn(normed, d_kv_low), gain_column], axis=1))
+    sums = [gain_attn_sums, at.gain_mlp_sums, jnp.full(gain_attn_sums.shape, loss_part)]
+    columns = jnp.pad(jnp.stack(sums, axis=1), ((0, 0), (0, 61)))
+    kv_grad = jnp.concatenate([low(tn(normed, d_kv_low)), split_sums(columns)], axis=1)
     at.kv_terms = terms(lambda owner: take(by_rows(kv_grad), owner), "fsdp")
     blocks = partial.reshape(2, 2, part_rows, -1)
     at.kept, at.sent = take(blocks, core_rank, 1), take(blocks, 1 - core_rank, 1)
-    at.query_1_got = around(at.query_1, "fsdp")
-    at.up_got_1 = flip(at.up_far[1], "ctx", 2)
-    at.gate_got = flip(at.gate_sent, "ctx", 1)
-    at.up_own = low(with_own(*at.drop("up_own", "up_own_got")))
-    at.out_z = low(wide(at.out_z) + wide(at.out_terms[1]))
-    at.next()
-    at.drop("d_query_low", "kv_low", "d_kv", "gate_sent")
-    at.query_1 = low(with_own(*at.drop("query_1", "query_1_got")))
+    at.next()
+    at.drop("d_query_low", "kv_low", "d_kv", "gate_sent", "d_qkv")
+    at.query_1 = low(with_own(at.query_terms[0], at.query_got[0]))
     at.got = flip(at.sent, "tp", 1)
     at.next()
     summed_rows = wide(at.kept) + wide(at.got)
     at.kept, at.sent = take(summed_rows, y_rank), low(take(summed_rows, 1 - y_rank))
+    at.out_2 = with_own(at.out_terms[1], at.out_got[1])
     at.next()
     at.got = flip(at.sent, "tp", 2)
-    at.query_2_got = around(at.query_2, "fsdp")
+    at.query_got += [around(at.query_terms[1], "fsdp")]
     at.query_z = ring(at.query_1[0], "ctx")
     at.out_z = ring(at.out_z, "ctx")
     at.next()
     at.query_z = low(wide(at.query_z) + wide(at.query_1[1]))
-    at.out_z = low(wide(at.out_z) + wide(at.out_terms[2]))
-    at.query_2 = with_own(*at.drop("query_2", "query_2_got"))
+    at.out_z = low(wide(at.out_z) + at.out_2[0])
+    at.query_2 = with_own(at.query_terms[1], at.query_got[1])
     at.d_normed = at.kept + wide(at.got)
-    up_got = jnp.stack(at.drop("up_got_0", "up_got_1"))
-    at.up_kept, at.up_sent = near_split(wide(at.up_own) + wide(up_got))
-    at.next()
-    at.drop("query_1", "kept", "sent", "got")
+    at.next()
+    up_terms, up_got = at.drop("up_terms", "up_got")
+    up_far_got = jnp.stack(at.drop("up_far_0", "up_far_1"))
+    up_own = jnp.stack([with_own(up_terms[i], up_got[i]) for i in (2, 3)])
+    at.up_kept, at.up_sent = near_split(up_own + wide(up_far_got))
+    at.drop("query_1", "kept", "sent", "got", "up_far", "query_terms", "query_got")
+    at.drop("out_terms", "out_got")
     at.query_z = ring(at.query_z, "ctx")
     at.out_z = ring(at.out_z, "ctx")
     at.kv_got = around(at.kv_terms, "fsdp")
-    at.up_got = flip(at.up_sent, "ctx", 1)
-    moving = ring(at.vector, "fsdp")
-    at.vector = at.vector + moving
-    for _ in range(2, fsdp_count):
-        moving = ring(moving, "fsdp")
-        at.vector = at.vector + moving
     at.next()
     at.query_z = low(wide(at.query_z) + at.query_2[0])
-    kv_mine = low(with_own(*at.drop("kv_terms", "kv_got")))
+    kv_mine = with_own(*at.drop("kv_terms", "kv_got"))
+    kv_mine = jnp.concatenate(
+        [low(kv_mine[..., :kv_width]), split_sums(joined_sums(kv_mine[..., kv_width:]))], axis=-1
+    )
     at.kv_own = take(kv_mine, ctx_rank)
     at.kv_sent = [take(kv_mine, (ctx_rank + by) % ctx_count) for by in range(1, ctx_count)]
 
@@ -894,15 +878,21 @@
         blocks = low(mine).reshape(tp_count, own_rows, -1)
         return [take(blocks, tp_rank ^ bit) for bit in range(tp_count)]
 
-    at.out_back = to_tp_back(wide(at.out_z) + wide(at.out_terms[3]))
-    at.next()
-    at.drop("up_far", "up_own", "out_z", "out_terms")
+    at.out_back = to_tp_back(wide(at.out_z) + at.out_2[1])
+    at.next()
+    at.drop("out_z", "out_2")
+    at.out_back = flip_tp(at.out_back)
     at.query_z = ring(at.query_z, "ctx")
     at.kv_got = [ring(at.kv_sent[by - 1], "ctx", by) for by in range(1, ctx_count)]
     at.next()
-    at.query_back = to_tp_back(wide(at.query_z) + at.query_2[1])
-    at.kv_back = to_tp_back(sum([wide(got) for got in at.kv_got], wide(at.kv_own)))
-    at.next()
+    query_mine = low(wide(at.query_z) + at.query_2[1])
+    kv_mine = sum([wide(got) for got in at.kv_got], wide(at.kv_own))
+    kv_mine = jnp.concatenate(
+        [low(kv_mine[:, :kv_width]), split_sums(joined_sums(kv_mine[:, kv_width:]))], axis=1
+    )
+    at.back = to_tp_back(jnp.concatenate([query_mine, kv_mine], axis=1))
+    at.next()
+    up_near = flip(at.up_sent, "ctx", 1)
     at.drop("query_z", "query_2", "kv_got", "kv_own", "kv_sent", "up_sent")
 
     def whole_heads(parts):
@@ -915,16 +905,17 @@
             columns.append(wide(part[:, start : start + held * head_size]))
         return jnp.concatenate(columns, axis=1)
 
-    query_grad = whole_heads(swapped(flip_tp(at.query_back), tp_rank))
-    out_grad = whole_heads(swapped(flip_tp(at.out_back), tp_rank))
-    kv_parts = [wide(part) for part in swapped(flip_tp(at.kv_back), tp_rank)]
+    parts = swapped(flip_tp(at.back), tp_rank)
+    query_grad = whole_heads([part[:, :slot_width] for part in parts])
+    out_grad = whole_heads(swapped(at.out_back, tp_rank))
+    kv_parts = [wide(part[:, slot_width:]) for part in parts]
     kv_grad = jnp.concatenate([part[:, :kv_width] for part in kv_parts], axis=1)
-    gain_attn_grad = sum(part[:, kv_width] for part in kv_parts)
+    sums = joined_sums(sum(part[:, kv_width:] for part in kv_parts))
+    gain_attn_grad, gain_mlp_grad, loss_sum = sums[:, 0], sums[:, 1], sums[0, 2]
     down_grad = near_joined(at.down_kept, at.down_got).T
-    gate_grad = near_joined(at.gate_kept, at.gate_got)
-    up_grad = near_joined(at.up_kept, at.up_got)
-    gain_mlp_grad = lax.dynamic_slice_in_dim(at.vector, own_start, own_rows, 0)
-    loss = at.vector[width] / (count * width)
+    gate_grad = near_joined(at.gate_kept, at.gate_near)
+    up_grad = near_joined(at.up_kept, up_near)
+    loss = loss_sum / (count * width)
     d_normed, d_residual = at.d_normed, at.d_residual
     scale_part = lax.dynamic_slice_in_dim(scale_one, tp_rank * part_rows, part_rows, 0)
     scaled = gain_attn * d_normed

time: 1080 us -> 1030 us (0.954)
  waiting for transfers between devices: 547 us -> 456 us
  other arithmetic: 96.3 us -> 129 us
  matrix products: 151 us -> 133 us
  starting transfers between devices: 114 us -> 127 us
  local copies, waits for them, and re-layouts: 91.6 us -> 103 us
    ppermute x40 -> x46, waiting for transfers between devices: 211 us -> 129 us  [ring(): lax.ppermute(array, axis, [(i, (i + by) % count) for i in range(count)])]
    ppermute x40 -> x46, starting transfers between devices: 32.3 us -> 46.7 us  [ring(): lax.ppermute(array, axis, [(i, (i + by) % count) for i in range(count)])]
    convert_element_type x19 -> x23, other arithmetic: 17.5 us -> 29.2 us  [low(): return values.astype(jnp.bfloat16)]
    dot_general x6 -> x5, matrix products: 58.9 us -> 49.7 us  [nn(): lax.dot_general(first, second, (((1,), (0,)), ((), ())), preferred_elemen...]
    dot_general x6 -> x5, matrix products: 51 us -> 45.4 us  [nt(): lax.dot_general(first, second, (((1,), (1,)), ((), ())), preferred_elemen...]
    unnamed x234 -> x335, local copies, waits for them, and re-layouts: 28.5 us -> 32.6 us
    ppermute x75 -> x69, starting transfers between devices: 68 us -> 66.3 us  [flip(): lax.ppermute(array, axis, [(i, i ^ bit) for i in range(lax.axis_size(axis...]
    ppermute x75 -> x69, waiting for transfers between devices: 301 us -> 301 us  [flip(): lax.ppermute(array, axis, [(i, i ^ bit) for i in range(lax.axis_size(axis...]
  transfers between devices with their start and end apart: 121 -> 121, of which waited for: 68 -> 67; matrix products, arithmetic and copies ran while one was open for 17% -> 21% of each run, Pallas kernels for 5% -> 6%
where the time goes in v3:
time: 1030 us; the launch traced here: 1020 us
  waiting for transfers between devices  456 us (44%)
  matrix products  133 us (13%)
  other arithmetic  129 us (13%)
  starting transfers between devices  127 us (12%)
  local copies, waits for them, and re-layouts  103 us (10%)
  Pallas kernels  62.5 us (6%)
    ppermute x69, waiting for transfers between devices, flip(): lax.ppermute(array, axis, [(i, i ^ bit) for i in range(lax.axis_size(axis...  301 us
    ppermute x46, waiting for transfers between devices, ring(): lax.ppermute(array, axis, [(i, (i + by) % count) for i in range(count)])  129 us
    ppermute x69, starting transfers between devices, flip(): lax.ppermute(array, axis, [(i, i ^ bit) for i in range(lax.axis_size(axis...  66.3 us
    dot_general x5, matrix products, nn(): lax.dot_general(first, second, (((1,), (0,)), ((), ())), preferred_elemen...  49.7 us
    ppermute x46, starting transfers between devices, ring(): lax.ppermute(array, axis, [(i, (i + by) % count) for i in range(count)])  46.7 us
    dot_general x5, matrix products, nt(): lax.dot_general(first, second, (((1,), (1,)), ((), ())), preferred_elemen...  45.4 us
    dot_general x6, matrix products, tn(): lax.dot_general(first, second, (((0,), (0,)), ((), ())), preferred_elemen...  38.2 us
    unnamed x335, local copies, waits for them, and re-layouts  32.6 us
  transfers between devices with their start and end apart: 121, of which 67 were waited for; matrix products, arithmetic and copies ran while one was open for 21% of the time, Pallas kernels for 6%

profile of v3, /device:TPU:0, one launch (start us, length us, event | category | flops | bytes accessed | tf_op | source)
XLA Modules:
  0.0 1018.0 jit_solution(14523468785283307017)
XLA Ops:
  30.9 12.7 %collective-permute-done.5.refs_1_ = bf16[320,1024]{1,0:T(8,128)(2,1)S(1)} collective-permute-done((bf16[320,1024]{1,0:T(8,128)(2,1)S(1)}, bf16[320,1024]{1,0:T(8,128)(2,1)S(1)}, u32[]{:S(2)}, u32[]{:S(2)}) %collective-permute-start.5) | collective-permute-done | bytes 655392 | tf_op jit(solution)/shard_map/ppermute | solution.py:22
  47.1 13.8 %collective-permute-done.7.refs_3_ = bf16[320,1024]{1,0:T(8,128)(2,1)S(1)} collective-permute-done((bf16[320,1024]{1,0:T(8,128)(2,1)S(1)}, bf16[320,1024]{1,0:T(8,128)(2,1)S(1)}, u32[]{:S(2)}, u32[]{:S(2)}) %collective-permute-start.7) | collective-permute-done | bytes 655392 | tf_op jit(solution)/shard_map/ppermute | solution.py:22
  161.8 16.4 %collective-permute-done.23 = bf16[320,1024]{1,0:T(8,128)(2,1)S(1)} collective-permute-done((bf16[320,1024]{1,0:T(8,128)(2,1)S(1)}, bf16[320,1024]{1,0:T(8,128)(2,1)S(1)}, u32[]{:S(2)}, u32[]{:S(2)}) %collective-permute-start.23) | collective-permute-done | bytes 655392 | tf_op jit(solution)/shard_map/ppermute | solution.py:17
  193.7 9.9 collective-permute-done.27
  217.8 18.3 %attention_forward.1 = bf16[768,768]{1,0:T(8,128)(2,1)S(1)} custom-call(s32[4]{0:T(128)S(1)} %pad_add_fusion.info_ref, bf16[768,768]{1,0:T(8,128)(2,1)S(1)} %copy-done.11, bf16[3072,512]{1,0:T(8,128)(2,1)S(1)} %copy-done.7), custom_call_target="tpu_custom_call" | custom-call | flops 5435817984 | bytes 5505024 | tf_op jit(solution)/shard_map/attention_forward/pallas_call | solution.py:163
  241.9 13.4 %collective-permute-done.29 = bf16[480,1024]{1,0:T(8,128)(2,1)} collective-permute-done((bf16[480,1024]{1,0:T(8,128)(2,1)}, bf16[480,1024]{1,0:T(8,128)(2,1)}, u32[]{:S(2)}, u32[]{:S(2)}) %collective-permute-start.29) | collective-permute-done | bytes 983072 | tf_op jit(solution)/shard_map/ppermute | solution.py:17
  268.1 30.3 %collective-permute-done.32 = bf16[320,1024]{1,0:T(8,128)(2,1)} collective-permute-done((bf16[320,1024]{1,0:T(8,128)(2,1)}, bf16[320,1024]{1,0:T(8,128)(2,1)}, u32[]{:S(2)}, u32[]{:S(2)}) %collective-permute-start.32) | collective-permute-done | bytes 655392 | tf_op jit(solution)/shard_map/ppermute | solution.py:17
  314.2 18.1 %collective-permute-done.37 = bf16[160,1024]{1,0:T(8,128)(2,1)S(1)} collective-permute-done((bf16[160,1024]{1,0:T(8,128)(2,1)}, bf16[160,1024]{1,0:T(8,128)(2,1)S(1)}, u32[]{:S(2)}, u32[]{:S(2)}) %collective-permute-start.37) | collective-permute-done | bytes 327712 | tf_op jit(solution)/shard_map/ppermute | solution.py:17
  343.9 15.7 %collective-permute-done.43 = bf16[160,1024]{1,0:T(8,128)(2,1)S(1)} collective-permute-done((bf16[160,1024]{1,0:T(8,128)(2,1)S(1)}, bf16[160,1024]{1,0:T(8,128)(2,1)S(1)}, u32[]{:S(2)}, u32[]{:S(2)}) %collective-permute-start.43) | collective-permute-done | bytes 327712 | tf_op jit(solution)/shard_map/ppermute | solution.py:17
  388.4 12.6 %fusion.98 = f32[1536,1024]{1,0:T(8,128)S(1)} fusion(bf16[1536,2560]{1,0:T(8,128)(2,1)} %copy-done.135, bf16[2560,1024]{1,0:T(8,128)(2,1)S(1)} %bitcast.438), kind=kOutput, calls=%fused_computation.456 | convolution fusion | flops 8053063680 | bytes 19398656 | tf_op jit(solution)/shard_map/dot_general | solution.py:110
  407.9 9.6 collective-permute-done.50
  436.1 11.4 %collective-permute-done.52 = bf16[96,2560]{1,0:T(8,128)(2,1)S(1)} collective-permute-done((bf16[96,2560]{1,0:T(8,128)(2,1)S(1)}, bf16[96,2560]{1,0:T(8,128)(2,1)S(1)}, u32[]{:S(2)}, u32[]{:S(2)}) %collective-permute-start.52) | collective-permute-done | bytes 491552 | tf_op jit(solution)/shard_map/ppermute | solution.py:17
  457.6 18.2 %collective-permute-done.55 = bf16[192,2560]{1,0:T(8,128)(2,1)} collective-permute-done((bf16[192,2560]{1,0:T(8,128)(2,1)}, bf16[192,2560]{1,0:T(8,128)(2,1)}, u32[]{:S(2)}, u32[]{:S(2)}) %collective-permute-start.55) | collective-permute-done | bytes 983072 | tf_op jit(solution)/shard_map/ppermute | solution.py:17
  484.6 19.6 %collective-permute-done.59 = bf16[192,2560]{1,0:T(8,128)(2,1)S(1)} collective-permute-done((bf16[192,2560]{1,0:T(8,128)(2,1)S(1)}, bf16[192,2560]{1,0:T(8,128)(2,1)S(1)}, u32[]{:S(2)}, u32[]{:S(2)}) %collective-permute-start.59) | collective-permute-done | bytes 983072 | tf_op jit(solution)/shard_map/ppermute | solution.py:17
  507.1 11.8 %collective-permute-done.61 = bf16[96,2560]{1,0:T(8,128)(2,1)S(1)} collective-permute-done((bf16[96,2560]{1,0:T(8,128)(2,1)S(1)}, bf16[96,2560]{1,0:T(8,128)(2,1)S(1)}, u32[]{:S(2)}, u32[]{:S(2)}) %collective-permute-start.61) | collective-permute-done | bytes 491552 | tf_op jit(solution)/shard_map/ppermute | solution.py:17
  529.8 9.0 convolution_convert_fusion.3
  542.2 18.0 %multiply_convert_fusion = (bf16[1536,1024]{1,0:T(8,128)(2,1)}, bf16[1536,1024]{1,0:T(8,128)(2,1)}) fusion(f32[1536,1024]{1,0:T(8,128)S(1)} %bitcast.466, f32[1536,1024]{1,0:T(8,128)} %copy-done.39, bf16[1536,2560]{1,0:T(8,128)(2,1)} %copy-done.136, bf16[2560,1024]{1,0:T(8,128)(2,1)S(1)} %bitcast.445), kind=kOutput, calls=%fused_computation.23 | convolution fusion | flops 8090812416 | bytes 31981568 | tf_op jit(solution)/shard_map/dot_general | solution.py:110
  561.1 11.9 %convolution_convert_fusion.2 = bf16[2560,1024]{1,0:T(8,128)(2,1)S(1)} fusion(bf16[1536,2560]{1,0:T(8,128)(2,1)} %copy-done.135, bf16[1536,1024]{1,0:T(8,128)(2,1)} %get-tuple-element.2336), kind=kOutput, calls=%fused_computation.29 | convolution fusion | flops 8055685120 | bytes 16252928 | tf_op jit(solution)/shard_map/dot_general | solution.py:122
  582.6 11.1 %fusion.99 = f32[1536,2560]{1,0:T(8,128)} fusion(bf16[1536,1024]{1,0:T(8,128)(2,1)S(1)} %copy-done.149, bf16[2560,1024]{1,0:T(8,128)(2,1)S(1)} %bitcast.441), kind=kOutput, calls=%fused_computation.457 | convolution fusion | flops 8053063680 | bytes 24117248 | tf_op jit(solution)/shard_map/dot_general | solution.py:116
  593.8 14.8 %add_convert_fusion = bf16[1536,2560]{1,0:T(8,128)(2,1)} fusion(f32[1536,2560]{1,0:T(8,128)} %fusion.99, bf16[1536,1024]{1,0:T(8,128)(2,1)} %get-tuple-element.2336, bf16[2560,1024]{1,0:T(8,128)(2,1)S(1)} %bitcast.437), kind=kOutput, calls=%fused_computation | convolution fusion | flops 8060928000 | bytes 31981568 | tf_op jit(solution)/shard_map/dot_general | solution.py:116
  622.2 15.7 %collective-permute-done.72 = bf16[160,1024]{1,0:T(8,128)(2,1)S(1)} collective-permute-done((bf16[160,1024]{1,0:T(8,128)(2,1)S(1)}, bf16[160,1024]{1,0:T(8,128)(2,1)S(1)}, u32[]{:S(2)}, u32[]{:S(2)}) %collective-permute-start.72) | collective-permute-done | bytes 327712 | tf_op jit(solution)/shard_map/ppermute | solution.py:17
  647.2 9.2 convolution_convert_fusion.1
  661.8 11.0 %collective-permute-done.77 = bf16[320,1024]{1,0:T(8,128)(2,1)S(1)} collective-permute-done((bf16[320,1024]{1,0:T(8,128)(2,1)S(1)}, bf16[320,1024]{1,0:T(8,128)(2,1)S(1)}, u32[]{:S(2)}, u32[]{:S(2)}) %collective-permute-start.77) | collective-permute-done | bytes 655392 | tf_op jit(solution)/shard_map/ppermute | solution.py:22
  687.0 21.2 %collective-permute-done.80 = bf16[320,1024]{1,0:T(8,128)(2,1)S(1)} collective-permute-done((bf16[320,1024]{1,0:T(8,128)(2,1)}, bf16[320,1024]{1,0:T(8,128)(2,1)S(1)}, u32[]{:S(2)}, u32[]{:S(2)}) %collective-permute-start.80) | collective-permute-done | bytes 655392 | tf_op jit(solution)/shard_map/ppermute | solution.py:17
  739.2 28.1 %attention_backward.1 = (f32[768,768]{1,0:T(8,128)S(1)}, bf16[3072,512]{1,0:T(8,128)(2,1)S(1)}) custom-call(s32[1]{0:T(128)} %bitcast.info_ref, bf16[768,768]{1,0:T(8,128)(2,1)S(1)} %copy-done.12, bf16[3072,512]{1,0:T(8,128)(2,1)S(1)} %copy-done.8, bf16[768,768]{1,0:T(8,128)(2,1)S(1)} %multiply_convert_fusion.2.do_ref), custom_call_target="tpu_custom_call" | custom-call | flops 13589544960 | bytes 11010048 | tf_op jit(solution)/shard_map/attention_backward/pallas_call | solution.py:225
  798.3 15.8 %collective-permute-done.93 = bf16[320,1024]{1,0:T(8,128)(2,1)} collective-permute-done((bf16[320,1024]{1,0:T(8,128)(2,1)}, bf16[320,1024]{1,0:T(8,128)(2,1)}, u32[]{:S(2)}, u32[]{:S(2)}) %collective-permute-start.93) | collective-permute-done | bytes 655392 | tf_op jit(solution)/shard_map/ppermute | solution.py:17
  827.8 19.7 %collective-permute-done.95 = bf16[768,128]{1,0:T(8,128)(2,1)S(1)} collective-permute-done((bf16[768,128]{1,0:T(8,128)(2,1)S(1)}, bf16[768,128]{1,0:T(8,128)(2,1)S(1)}, u32[]{:S(2)}, u32[]{:S(2)}) %collective-permute-start.95) | collective-permute-done | bytes 196640 | tf_op jit(solution)/shard_map/ppermute | solution.py:28
  864.5 19.3 %collective-permute-done.99 = bf16[320,1024]{1,0:T(8,128)(2,1)S(1)} collective-permute-done((bf16[320,1024]{1,0:T(8,128)(2,1)S(1)}, bf16[320,1024]{1,0:T(8,128)(2,1)S(1)}, u32[]{:S(2)}, u32[]{:S(2)}) %collective-permute-start.99) | collective-permute-done | bytes 655392 | tf_op jit(solution)/shard_map/ppermute | solution.py:17
  905.6 14.6 %collective-permute-done.106 = bf16[320,768]{1,0:T(8,128)(2,1)} collective-permute-done((bf16[320,768]{1,0:T(8,128)(2,1)}, bf16[320,768]{1,0:T(8,128)(2,1)}, u32[]{:S(2)}, u32[]{:S(2)}) %collective-permute-start.106) | collective-permute-done | bytes 491552 | tf_op jit(solution)/shard_map/ppermute | solution.py:22
  920.2 9.4 collective-permute-done.104
  942.2 9.0 collective-permute-done.108
  973.9 9.5 collective-permute-done.110
  (821 shorter events, 532.2 us)
Async XLA Ops:
  135.7 45.4 %collective-permute-start.26 = (bf16[4,320,768]{2,1,0:T(8,128)(2,1)S(1)}, bf16[4,320,768]{2,1,0:T(8,128)(2,1)S(1)}, u32[]{:S(2)}, u32[]{:S(2)}) collective-permute-start(bf16[4,320,768]{2,1,0:T(8,128)(2,1)S(1)} %pad_maximum_fusion.5), channel_id=1, source_target_pairs={{0,16},{16,0},{1,17},{17,1},{2,18},{18,2},{3,19},{19,3},{4,20},{20... | collective-permute-start | bytes 5898248 | tf_op jit(solution)/shard_map/ppermute | solution.py:22
  152.2 28.9 %collective-permute-start.25 = (bf16[3072,128]{1,0:T(8,128)(2,1)S(1)}, bf16[3072,128]{1,0:T(8,128)(2,1)S(1)}, u32[]{:S(2)}, u32[]{:S(2)}) collective-permute-start(bf16[3072,128]{1,0:T(8,128)(2,1)S(1)} %pad_maximum_fusion.30), channel_id=1, source_target_pairs={{0,2},{1,3},{2,0},{3,1},{4,6},{5,7},{6,4},{7,5},{8,10},{9,11},{10,... | collective-permute-start | bytes 2359304 | tf_op jit(solution)/shard_map/ppermute | solution.py:17
  210.3 44.9 %collective-permute-start.29 = (bf16[480,1024]{1,0:T(8,128)(2,1)}, bf16[480,1024]{1,0:T(8,128)(2,1)}, u32[]{:S(2)}, u32[]{:S(2)}) collective-permute-start(bf16[480,1024]{1,0:T(8,128)(2,1)} %pad_maximum_fusion.23), channel_id=1, source_target_pairs={{0,8},{4,12},{8,0},{12,4},{1,9},{5,13},{9,1},{13,5},{2,10},{6,14},... | collective-permute-start | bytes 2949128 | tf_op jit(solution)/shard_map/ppermute | solution.py:17
  212.7 42.6 %collective-permute-start.30 = (bf16[2,320,1024]{2,1,0:T(8,128)(2,1)S(1)}, bf16[2,320,1024]{2,1,0:T(8,128)(2,1)S(1)}, u32[]{:S(2)}, u32[]{:S(2)}) collective-permute-start(bf16[2,320,1024]{2,1,0:T(8,128)(2,1)S(1)} %pad_maximum_fusion.11), channel_id=1, source_target_pairs={{0,16},{16,0},{1,17},{17,1},{2,18},{18,2},{3,19},{19,3},{4,20},{20... | collective-permute-start | bytes 3932168 | tf_op jit(solution)/shard_map/ppermute | solution.py:22
  265.1 33.3 %collective-permute-start.33 = (bf16[2,320,1024]{2,1,0:T(8,128)(2,1)}, bf16[2,320,1024]{2,1,0:T(8,128)(2,1)}, u32[]{:S(2)}, u32[]{:S(2)}) collective-permute-start(bf16[2,320,1024]{2,1,0:T(8,128)(2,1)} %bitcast.51), channel_id=1, source_target_pairs={{0,16},{16,0},{1,17},{17,1},{2,18},{18,2},{3,19},{19,3},{4,20},{20... | collective-permute-start | bytes 3932168 | tf_op jit(solution)/shard_map/ppermute | solution.py:22
  266.7 31.7 %collective-permute-start.34 = (bf16[192,2560]{1,0:T(8,128)(2,1)}, bf16[192,2560]{1,0:T(8,128)(2,1)}, u32[]{:S(2)}, u32[]{:S(2)}) collective-permute-start(bf16[192,2560]{1,0:T(8,128)(2,1)} %fusion.30), channel_id=1, source_target_pairs={{0,2},{1,3},{2,0},{3,1},{4,6},{5,7},{6,4},{7,5},{8,10},{9,11},{10,... | collective-permute-start | bytes 2949128 | tf_op jit(solution)/shard_map/ppermute | solution.py:17
  267.8 30.6 %collective-permute-start.32 = (bf16[320,1024]{1,0:T(8,128)(2,1)}, bf16[320,1024]{1,0:T(8,128)(2,1)}, u32[]{:S(2)}, u32[]{:S(2)}) collective-permute-start(bf16[320,1024]{1,0:T(8,128)(2,1)} %slice_bitcast_fusion.10), channel_id=1, source_target_pairs={{0,8},{4,12},{8,0},{12,4},{1,9},{5,13},{9,1},{13,5},{2,10},{6,14},... | collective-permute-start | bytes 1966088 | tf_op jit(solution)/shard_map/ppermute | solution.py:17
  303.4 31.2 %collective-permute-start.36 = (bf16[2,320,1024]{2,1,0:T(8,128)(2,1)S(1)}, bf16[2,320,1024]{2,1,0:T(8,128)(2,1)}, u32[]{:S(2)}, u32[]{:S(2)}) collective-permute-start(bf16[2,320,1024]{2,1,0:T(8,128)(2,1)S(1)} %pad_maximum_fusion.12), channel_id=1, source_target_pairs={{0,16},{16,0},{1,17},{17,1},{2,18},{18,2},{3,19},{19,3},{4,20},{20... | collective-permute-start | bytes 3932168 | tf_op jit(solution)/shard_map/ppermute | solution.py:22
  303.8 30.7 %collective-permute-start.39 = (bf16[192,2560]{1,0:T(8,128)(2,1)}, bf16[192,2560]{1,0:T(8,128)(2,1)}, u32[]{:S(2)}, u32[]{:S(2)}) collective-permute-start(bf16[192,2560]{1,0:T(8,128)(2,1)} %multiply_convert_fusion.3), channel_id=1, source_target_pairs={{0,4},{4,0},{8,12},{12,8},{1,5},{5,1},{9,13},{13,9},{2,6},{6,2},{1... | collective-permute-start | bytes 2949128 | tf_op jit(solution)/shard_map/ppermute | solution.py:17
  303.8 30.7 %collective-permute-start.38 = (bf16[192,2560]{1,0:T(8,128)(2,1)}, bf16[192,2560]{1,0:T(8,128)(2,1)}, u32[]{:S(2)}, u32[]{:S(2)}) collective-permute-start(bf16[192,2560]{1,0:T(8,128)(2,1)} %multiply_convert_fusion.3), channel_id=1, source_target_pairs={{0,2},{1,3},{2,0},{3,1},{4,6},{5,7},{6,4},{7,5},{8,10},{9,11},{10,... | collective-permute-start | bytes 2949128 | tf_op jit(solution)/shard_map/ppermute | solution.py:17
  305.3 29.2 %collective-permute-start.35 = (bf16[192,2560]{1,0:T(8,128)(2,1)}, bf16[192,2560]{1,0:T(8,128)(2,1)}, u32[]{:S(2)}, u32[]{:S(2)}) collective-permute-start(bf16[192,2560]{1,0:T(8,128)(2,1)} %multiply_convert_fusion.3), channel_id=1, source_target_pairs={{0,1},{1,0},{2,3},{3,2},{4,5},{5,4},{6,7},{7,6},{8,9},{9,8},{10,11... | collective-permute-start | bytes 2949128 | tf_op jit(solution)/shard_map/ppermute | solution.py:17
  579.2 34.4 %collective-permute-start.66 = (bf16[320,1024]{1,0:T(8,128)(2,1)}, bf16[320,1024]{1,0:T(8,128)(2,1)}, u32[]{:S(2)}, u32[]{:S(2)}) collective-permute-start(bf16[320,1024]{1,0:T(8,128)(2,1)} %add_convert_fusion.12), channel_id=1, source_target_pairs={{0,8},{4,12},{8,0},{12,4},{1,9},{5,13},{9,1},{13,5},{2,10},{6,14},... | collective-permute-start | bytes 1966088 | tf_op jit(solution)/shard_map/ppermute | solution.py:17
  580.6 32.9 %collective-permute-start.67 = (bf16[320,1024]{1,0:T(8,128)(2,1)}, bf16[320,1024]{1,0:T(8,128)(2,1)}, u32[]{:S(2)}, u32[]{:S(2)}) collective-permute-start(bf16[320,1024]{1,0:T(8,128)(2,1)} %get-tuple-element.2341), channel_id=1, source_target_pairs={{0,16},{16,0},{1,17},{17,1},{2,18},{18,2},{3,19},{19,3},{4,20},{20... | collective-permute-start | bytes 1966088 | tf_op jit(solution)/shard_map/ppermute | solution.py:22
  581.7 31.8 %collective-permute-start.68 = (bf16[320,1024]{1,0:T(8,128)(2,1)}, bf16[320,1024]{1,0:T(8,128)(2,1)}, u32[]{:S(2)}, u32[]{:S(2)}) collective-permute-start(bf16[320,1024]{1,0:T(8,128)(2,1)} %get-tuple-element.2343), channel_id=1, source_target_pairs={{0,16},{16,0},{1,17},{17,1},{2,18},{18,2},{3,19},{19,3},{4,20},{20... | collective-permute-start | bytes 1966088 | tf_op jit(solution)/shard_map/ppermute | solution.py:22
  644.8 28.0 %collective-permute-start.77 = (bf16[320,1024]{1,0:T(8,128)(2,1)S(1)}, bf16[320,1024]{1,0:T(8,128)(2,1)S(1)}, u32[]{:S(2)}, u32[]{:S(2)}) collective-permute-start(bf16[320,1024]{1,0:T(8,128)(2,1)S(1)} %copy-done.88), channel_id=1, source_target_pairs={{0,16},{16,0},{1,17},{17,1},{2,18},{18,2},{3,19},{19,3},{4,20},{20... | collective-permute-start | bytes 1966088 | tf_op jit(solution)/shard_map/ppermute | solution.py:22
  645.8 27.0 %collective-permute-start.78 = (bf16[192,2560]{1,0:T(8,128)(2,1)S(1)}, bf16[192,2560]{1,0:T(8,128)(2,1)S(1)}, u32[]{:S(2)}, u32[]{:S(2)}) collective-permute-start(bf16[192,2560]{1,0:T(8,128)(2,1)S(1)} %pad_maximum_fusion.28), channel_id=1, source_target_pairs={{0,2},{1,3},{2,0},{3,1},{4,6},{5,7},{6,4},{7,5},{8,10},{9,11},{10,... | collective-permute-start | bytes 2949128 | tf_op jit(solution)/shard_map/ppermute | solution.py:17
  678.3 30.0 %collective-permute-start.82 = (bf16[192,2560]{1,0:T(8,128)(2,1)S(1)}, bf16[192,2560]{1,0:T(8,128)(2,1)}, u32[]{:S(2)}, u32[]{:S(2)}) collective-permute-start(bf16[192,2560]{1,0:T(8,128)(2,1)S(1)} %get-tuple-element.2587), channel_id=1, source_target_pairs={{0,2},{1,3},{2,0},{3,1},{4,6},{5,7},{6,4},{7,5},{8,10},{9,11},{10,... | collective-permute-start | bytes 2949128 | tf_op jit(solution)/shard_map/ppermute | solution.py:17
  679.6 28.5 %collective-permute-start.80 = (bf16[320,1024]{1,0:T(8,128)(2,1)}, bf16[320,1024]{1,0:T(8,128)(2,1)S(1)}, u32[]{:S(2)}, u32[]{:S(2)}) collective-permute-start(bf16[320,1024]{1,0:T(8,128)(2,1)} %add_convert_fusion.8), channel_id=1, source_target_pairs={{0,8},{4,12},{8,0},{12,4},{1,9},{5,13},{9,1},{13,5},{2,10},{6,14},... | collective-permute-start | bytes 1966088 | tf_op jit(solution)/shard_map/ppermute | solution.py:17
  680.2 27.9 %collective-permute-start.81 = (bf16[320,1024]{1,0:T(8,128)(2,1)}, bf16[320,1024]{1,0:T(8,128)(2,1)S(1)}, u32[]{:S(2)}, u32[]{:S(2)}) collective-permute-start(bf16[320,1024]{1,0:T(8,128)(2,1)} %get-tuple-element.2552), channel_id=1, source_target_pairs={{0,16},{16,0},{1,17},{17,1},{2,18},{18,2},{3,19},{19,3},{4,20},{20... | collective-permute-start | bytes 1966088 | tf_op jit(solution)/shard_map/ppermute | solution.py:22
  681.1 27.2 %collective-permute-start.83 = (bf16[320,1024]{1,0:T(8,128)(2,1)}, bf16[320,1024]{1,0:T(8,128)(2,1)S(1)}, u32[]{:S(2)}, u32[]{:S(2)}) collective-permute-start(bf16[320,1024]{1,0:T(8,128)(2,1)} %get-tuple-element.2562), channel_id=1, source_target_pairs={{0,16},{16,0},{1,17},{17,1},{2,18},{18,2},{3,19},{19,3},{4,20},{20... | collective-permute-start | bytes 1966088 | tf_op jit(solution)/shard_map/ppermute | solution.py:22
  735.5 31.8 %collective-permute-start.87 = (bf16[320,1024]{1,0:T(8,128)(2,1)S(1)}, bf16[320,1024]{1,0:T(8,128)(2,1)S(1)}, u32[]{:S(2)}, u32[]{:S(2)}) collective-permute-start(bf16[320,1024]{1,0:T(8,128)(2,1)S(1)} %copy-done.113), channel_id=1, source_target_pairs={{0,8},{4,12},{8,0},{12,4},{1,9},{5,13},{9,1},{13,5},{2,10},{6,14},... | collective-permute-start | bytes 1966088 | tf_op jit(solution)/shard_map/ppermute | solution.py:17
  737.2 30.2 %collective-permute-start.89 = (bf16[320,1024]{1,0:T(8,128)(2,1)S(1)}, bf16[320,1024]{1,0:T(8,128)(2,1)S(1)}, u32[]{:S(2)}, u32[]{:S(2)}) collective-permute-start(bf16[320,1024]{1,0:T(8,128)(2,1)S(1)} %copy-done.86), channel_id=1, source_target_pairs={{0,16},{16,0},{1,17},{17,1},{2,18},{18,2},{3,19},{19,3},{4,20},{20... | collective-permute-start | bytes 1966088 | tf_op jit(solution)/shard_map/ppermute | solution.py:22
  738.4 29.0 %collective-permute-start.88 = (bf16[320,1024]{1,0:T(8,128)(2,1)S(1)}, bf16[320,1024]{1,0:T(8,128)(2,1)S(1)}, u32[]{:S(2)}, u32[]{:S(2)}) collective-permute-start(bf16[320,1024]{1,0:T(8,128)(2,1)S(1)} %copy-done.85), channel_id=1, source_target_pairs={{0,16},{16,0},{1,17},{17,1},{2,18},{18,2},{3,19},{19,3},{4,20},{20... | collective-permute-start | bytes 1966088 | tf_op jit(solution)/shard_map/ppermute | solution.py:22
  782.1 32.0 %collective-permute-start.93 = (bf16[320,1024]{1,0:T(8,128)(2,1)}, bf16[320,1024]{1,0:T(8,128)(2,1)}, u32[]{:S(2)}, u32[]{:S(2)}) collective-permute-start(bf16[320,1024]{1,0:T(8,128)(2,1)} %add_convert_fusion.6), channel_id=1, source_target_pairs={{0,8},{4,12},{8,0},{12,4},{1,9},{5,13},{9,1},{13,5},{2,10},{6,14},... | collective-permute-start | bytes 1966088 | tf_op jit(solution)/shard_map/ppermute | solution.py:17
  783.4 30.8 %collective-permute-start.91 = (bf16[3072,128]{1,0:T(8,128)(2,1)}, bf16[3072,128]{1,0:T(8,128)(2,1)}, u32[]{:S(2)}, u32[]{:S(2)}) collective-permute-start(bf16[3072,128]{1,0:T(8,128)(2,1)} %fusion.62), channel_id=1, source_target_pairs={{0,2},{1,3},{2,0},{3,1},{4,6},{5,7},{6,4},{7,5},{8,10},{9,11},{10,... | collective-permute-start | bytes 2359304 | tf_op jit(solution)/shard_map/ppermute | solution.py:17
  784.4 29.7 %collective-permute-start.92 = (bf16[2,320,768]{2,1,0:T(8,128)(2,1)}, bf16[2,320,768]{2,1,0:T(8,128)(2,1)}, u32[]{:S(2)}, u32[]{:S(2)}) collective-permute-start(bf16[2,320,768]{2,1,0:T(8,128)(2,1)} %get-tuple-element.2832), channel_id=1, source_target_pairs={{0,16},{16,0},{1,17},{17,1},{2,18},{18,2},{3,19},{19,3},{4,20},{20... | collective-permute-start | bytes 2949128 | tf_op jit(solution)/shard_map/ppermute | solution.py:22
  818.7 28.9 %collective-permute-start.95 = (bf16[768,128]{1,0:T(8,128)(2,1)S(1)}, bf16[768,128]{1,0:T(8,128)(2,1)S(1)}, u32[]{:S(2)}, u32[]{:S(2)}) collective-permute-start(bf16[768,128]{1,0:T(8,128)(2,1)S(1)} %get-tuple-element.2882), channel_id=1, source_target_pairs={{8,0},{12,4},{9,1},{13,5},{10,2},{14,6},{11,3},{15,7},{24,16},{28,... | collective-permute-start | bytes 589832 | tf_op jit(solution)/shard_map/ppermute | solution.py:28
  820.0 27.6 %collective-permute-start.96 = (bf16[768,128]{1,0:T(8,128)(2,1)S(1)}, bf16[768,128]{1,0:T(8,128)(2,1)S(1)}, u32[]{:S(2)}, u32[]{:S(2)}) collective-permute-start(bf16[768,128]{1,0:T(8,128)(2,1)S(1)} %get-tuple-element.2883), channel_id=1, source_target_pairs={{12,0},{13,1},{14,2},{15,3},{28,16},{29,17},{30,18},{31,19}} | collective-permute-start | bytes 589832 | tf_op jit(solution)/shard_map/ppermute | solution.py:28
  852.3 32.7 %collective-permute-start.100 = (bf16[2,320,768]{2,1,0:T(8,128)(2,1)S(1)}, bf16[2,320,768]{2,1,0:T(8,128)(2,1)S(1)}, u32[]{:S(2)}, u32[]{:S(2)}) collective-permute-start(bf16[2,320,768]{2,1,0:T(8,128)(2,1)S(1)} %copy-done.80), channel_id=1, source_target_pairs={{0,16},{16,0},{1,17},{17,1},{2,18},{18,2},{3,19},{19,3},{4,20},{20... | collective-permute-start | bytes 2949128 | tf_op jit(solution)/shard_map/ppermute | solution.py:22
  854.2 29.6 %collective-permute-start.99 = (bf16[320,1024]{1,0:T(8,128)(2,1)S(1)}, bf16[320,1024]{1,0:T(8,128)(2,1)S(1)}, u32[]{:S(2)}, u32[]{:S(2)}) collective-permute-start(bf16[320,1024]{1,0:T(8,128)(2,1)S(1)} %copy-done.108), channel_id=1, source_target_pairs={{0,4},{4,0},{8,12},{12,8},{1,5},{5,1},{9,13},{13,9},{2,6},{6,2},{1... | collective-permute-start | bytes 1966088 | tf_op jit(solution)/shard_map/ppermute | solution.py:17
  854.4 30.6 %collective-permute-start.101 = (bf16[320,1024]{1,0:T(8,128)(2,1)S(1)}, bf16[320,1024]{1,0:T(8,128)(2,1)S(1)}, u32[]{:S(2)}, u32[]{:S(2)}) collective-permute-start(bf16[320,1024]{1,0:T(8,128)(2,1)S(1)} %copy-done.114), channel_id=1, source_target_pairs={{0,8},{4,12},{8,0},{12,4},{1,9},{5,13},{9,1},{13,5},{2,10},{6,14},... | collective-permute-start | bytes 1966088 | tf_op jit(solution)/shard_map/ppermute | solution.py:17
  902.0 27.6 %collective-permute-start.103 = (bf16[192,2560]{1,0:T(8,128)(2,1)}, bf16[192,2560]{1,0:T(8,128)(2,1)}, u32[]{:S(2)}, u32[]{:S(2)}) collective-permute-start(bf16[192,2560]{1,0:T(8,128)(2,1)} %fusion.31), channel_id=1, source_target_pairs={{0,2},{1,3},{2,0},{3,1},{4,6},{5,7},{6,4},{7,5},{8,10},{9,11},{10,... | collective-permute-start | bytes 2949128 | tf_op jit(solution)/shard_map/ppermute | solution.py:17
  (252 other events, 2977.5 us)

commit v4 on v3

--- a/solution.py
+++ b/solution.py
@@ -601,13 +601,12 @@
     at.down_b = jnp.concatenate([at.far_7, at.far_8], axis=0)
     at.next()
     gate_proj, up_proj = at.gate_proj, at.up_proj
-    activated, gelu_back = jax.vjp(gelu_tanh, gate_proj)
-    at.hidden_act = low(activated * up_proj)
+    at.hidden_act = low(gelu_tanh(gate_proj) * up_proj)
     at.down_b = over_fsdp(at.down_b)
     at.next()
     at.drop("far_1", "far_2", "far_3", "far_4", "far_5", "far_6", "far_7", "gate_pair", "up_pair")
     at.drop("far_8", "gate_other", "up_far", "down_quarters", "mixed_far")
-    at.drop("gate_proj", "up_proj", "down_pair")
+    at.drop("down_pair")
     down_x, down_a, down_b = at.drop("down_x", "down_a", "down_b")
     down_z = [jnp.stack(pair) for pair in zip(down_a, down_b)]
     down_full = mlp_placed(down_x, down_z)
@@ -623,19 +622,29 @@
     between_corners_and_sides()
     at.next()
     sum_sides()
-    at.next()
-    ffn_part = summed()
-
+    gate_proj, up_proj = at.drop("gate_proj", "up_proj")
+    at.activated, gelu_back = jax.vjp(gelu_tanh, gate_proj)
+    at.slope = gelu_back(up_proj)[0]
+    at.next()
+    at.ffn_parts = at.drop("part", "got_y", "got_z")
+    at.drop("over_y", "over_z")
     my_length = lengths[fsdp_rank]
     part_positions = ctx_rank * rows + tp_rank * part_rows + jnp.arange(part_rows)
     valid = wide(part_positions < my_length)[:, None]
-    output = (residual + ffn_part) * valid
-    mismatch = output - wide(teacher[0])
     count = wide(jnp.sum(lengths))
+    d_scale = lengths.shape[0] * ctx_count * rows / count
+
+    def outputs_of(residual, ffn_parts):
+        own, got_y, got_z = ffn_parts
+        output = (residual + (own + wide(got_y) + wide(got_z))) * valid
+        return output, output - wide(teacher[0])
+
+    at.part = low(valid * outputs_of(residual, at.ffn_parts)[1] * d_scale)
+    at.next()
+    output, mismatch = outputs_of(at.residual, at.drop("ffn_parts")[0])
     loss_part = jnp.sum(valid * mismatch * mismatch)
-    at.d_output = valid * mismatch * (lengths.shape[0] * ctx_count * rows / count)
-    at.part = low(at.d_output)
-    at.next()
+    at.d_output = valid * mismatch * d_scale
+    at.output_low = low(output)
     gather_sides()
     at.next()
     between_sides_and_corners()
@@ -687,10 +696,10 @@
     at.next()
     at.down_x = [around(at.down_terms[0], "fsdp")]
     d_hidden = nn(at.d_ffn, down_full)
-    at.d_gate = low(gelu_back(d_hidden * up_proj)[0])
-    at.d_up = low(d_hidden * activated)
-    at.next()
-    at.drop("d_ffn", "hidden_act")
+    at.d_gate = low(d_hidden * at.slope)
+    at.d_up = low(d_hidden * at.activated)
+    at.next()
+    at.drop("d_ffn", "hidden_act", "slope", "activated")
     at.down_x += [around(at.down_terms[1], "fsdp")]
     at.gate_terms = blocks_of(low(tn(at.normed_two, at.d_gate)))
     at.next()
@@ -718,7 +727,14 @@
     at.down_own = jnp.stack([low(with_own(down_terms[i], down_x[i])) for i in (2, 3)])
     at.gate_got += [around(at.gate_terms[1], "fsdp"), around(at.gate_terms[2], "fsdp")]
     at.down_got_2 = flip(at.down_rest[1], "ctx", 2)
-    at.up_terms = blocks_of(low(tn(at.normed_two, at.d_up)))
+    up_blocks = low(tn(at.normed_two, at.d_up)).reshape(fsdp_count, 2, 2, -1, half)
+    at.up_first = terms(lambda owner: take(take(up_blocks, owner), 1 - hi_rank)[0], "fsdp")
+    at.up_others = terms(
+        lambda owner: jnp.concatenate(
+            [take(take(up_blocks, owner), 1 - hi_rank)[1:], take(take(up_blocks, owner), hi_rank)]
+        ),
+        "fsdp",
+    )
     at.next()
     at.drop("normed_two", "d_up", "down_far", "down_rest")
     at.gate_far = [low(with_own(at.gate_terms[i], at.gate_got[i])) for i in range(2)]
@@ -734,21 +750,23 @@
     down_got = jnp.stack([got_0, jnp.concatenate([got_1, got_2], axis=0)])
     at.down_kept, at.down_sent = near_split(wide(at.drop("down_own")[0]) + wide(down_got))
     at.gate_got += [around(at.gate_terms[3], "fsdp")]
-    at.up_got = [around(at.up_terms[0], "fsdp")]
+    at.up_first_got = around(at.up_first, "fsdp")
     at.gate_far_0 = flip(at.gate_far[0], "ctx", 2)
     at.next()
     at.pair = jnp.stack(at.drop("part", "over_y"))
     at.next()
     at.other = flip(at.pair, "tp", 1)
+    at.up_far = jnp.split(low(with_own(*at.drop("up_first", "up_first_got"))), 2)
+    gate_terms, gate_got = at.drop("gate_terms", "gate_got")
+    at.gate_own = jnp.stack([low(with_own(gate_terms[i], gate_got[i])) for i in (2, 3)])
     at.next()
     pair, other = at.drop("pair", "other")
     d_attn = swapped([pair[0], other[0], pair[1], other[1]], tp_rank)
     at.d_attn = jnp.concatenate(d_attn, axis=0)
     at.next()
     at.down_got = flip(at.down_sent, "ctx", 1)
-    at.up_got += [around(at.up_terms[1], "fsdp")]
     live_columns = jnp.repeat(live, head_size).astype(jnp.float32)
-    at.d_attended = low(nn(at.d_attn, out_part) * live_columns)
+    d_attended = low(nn(at.d_attn, out_part) * live_columns)
     out_grad = low(tn(at.d_attn, at.attended))
 
     own_rows = attn_gain.shape[0]
@@ -759,6 +777,10 @@
 
     def joined_sums(columns):
         return columns[..., :64] + columns[..., 64:]
+
+    def to_tp_back(mine):
+        blocks = low(mine).reshape(tp_count, own_rows, -1)
+        return [take(blocks, tp_rank ^ bit) for bit in range(tp_count)]
 
     def by_rows(grad):
         return grad.reshape(fsdp_count, ctx_count, tp_count * own_rows, -1)
@@ -770,26 +792,35 @@
         return [terms(lambda owner: take(pair, owner), "fsdp") for pair in pairs]
 
     at.out_terms = halves_of(out_grad)
+    at.d_queries, at.d_keyvals = attention_backward(
+        queries, keyvals, d_attended, first_key, head_size
+    )
+    at.up_others_got = around(at.up_others, "fsdp")
+    at.gate_far_1 = flip(at.gate_far[1], "ctx", 2)
+    at.up_far_0 = flip(at.up_far[0], "ctx", 2)
     at.next()
     at.drop("attended", "d_attn", "down_sent")
-    at.d_queries, at.d_keyvals = attention_backward(
-        queries, keyvals, at.d_attended, first_key, head_size
-    )
-    at.up_got += [around(at.up_terms[2], "fsdp"), around(at.up_terms[3], "fsdp")]
-    at.gate_far_1 = flip(at.gate_far[1], "ctx", 2)
-    at.next()
     kv_blocks = jnp.stack(jnp.split(at.d_keyvals, tp_count, axis=1)).reshape(2, 2, -1, kv_width)
     at.kv_kept, at.kv_sent = take(kv_blocks, core_rank, 1), take(kv_blocks, 1 - core_rank, 1)
-    at.drop("d_attended", "d_keyvals")
+    at.drop("d_keyvals")
     at.next()
     at.kv_got = flip(at.kv_sent, "tp", 1)
+    up_others, up_others_got = at.drop("up_others", "up_others_got")
+    up_rest = jnp.split(low(wide(up_others[-1][0]) + wide(up_others_got[0])), 2)
+    at.up_mixed = jnp.concatenate([at.up_far[1], up_rest[0]], axis=0)
+    at.up_last = up_rest[1]
+    at.up_own, at.up_own_got = up_others[-1][1:], up_others_got[1:]
+    gate_far_got = jnp.stack(at.drop("gate_far_0", "gate_far_1"))
+    at.gate_kept, at.gate_sent = near_split(wide(at.drop("gate_own")[0]) + wide(gate_far_got))
+    at.drop("gate_far")
     at.next()
     kv_sum = wide(at.kv_kept) + wide(at.kv_got)
     at.kv_kept, at.kv_sent = take(kv_sum, y_rank), low(take(kv_sum, 1 - y_rank))
-    at.up_far = [low(with_own(at.up_terms[i], at.up_got[i])) for i in range(2)]
     at.next()
     at.kv_got = flip(at.kv_sent, "tp", 2)
-    at.up_far_0 = flip(at.up_far[0], "ctx", 2)
+    at.up_far_1 = flip(at.up_mixed, "ctx", 2)
+    at.gate_near = flip(at.gate_sent, "ctx", 1)
+    at.up_own = low(wide(at.up_own) + wide(at.drop("up_own_got")[0]))
     at.out_got = [around(at.out_terms[0], "fsdp")]
     d_query_raw = turn(
         at.d_queries.reshape(rows, slot_count, head_size) * query_scale,
@@ -805,11 +836,6 @@
     at.d_kv = kv_sum[reach_back]
     at.out_1 = low(with_own(at.out_terms[0], at.out_got[0]))
     at.next()
-    gate_terms, gate_got = at.drop("gate_terms", "gate_got")
-    gate_far_got = jnp.stack(at.drop("gate_far_0", "gate_far_1"))
-    gate_own = jnp.stack([with_own(gate_terms[i], gate_got[i]) for i in (2, 3)])
-    at.gate_kept, at.gate_sent = near_split(gate_own + wide(gate_far_got))
-    at.drop("gate_far")
     at.kv_got = [shifted(at.kv_low[by - 1], "ctx", -by) for by in range(1, reach_back + 1)]
     at.out_got += [around(at.out_terms[1], "fsdp")]
     at.out_z = ring(at.out_1[0], "ctx")
@@ -824,47 +850,47 @@
     at.out_z = low(wide(at.out_z) + wide(at.out_1[1]))
     at.next()
     at.query_got = [around(at.query_terms[0], "fsdp")]
-    at.up_far_1 = flip(at.up_far[1], "ctx", 2)
-    at.gate_near = flip(at.gate_sent, "ctx", 1)
+    at.up_far_2 = flip(at.up_last, "ctx", 2)
+    at.out_z = ring(at.out_z, "ctx")
     at.partial = low(nt(at.d_qkv, qkv_part))
     at.next()
-    (partial,) = at.drop("partial")
-    d_kv_low = at.d_qkv[:, slot_width : slot_width + kv_width]
-    gain_attn_sums = jnp.sum(wide(partial) * inputs * scale_one, axis=0)
+    partial = at.partial
+    blocks = partial.reshape(2, 2, part_rows, -1)
+    at.kept, at.sent = take(blocks, core_rank, 1), take(blocks, 1 - core_rank, 1)
+    at.next()
+    at.drop("d_query_low", "kv_low", "d_kv", "gate_sent")
+    at.query_1 = low(with_own(at.query_terms[0], at.query_got[0]))
+    at.out_2 = with_own(at.out_terms[1], at.out_got[1])
+    at.out_z = low(wide(at.out_z) + at.out_2[0])
+    at.got = flip(at.sent, "tp", 1)
+    at.next()
+    summed_rows = wide(at.kept) + wide(at.got)
+    at.kept, at.sent = take(summed_rows, y_rank), low(take(summed_rows, 1 - y_rank))
+    at.next()
+    at.got = flip(at.sent, "tp", 2)
+    gain_attn_sums = jnp.sum(wide(at.partial) * inputs * scale_one, axis=0)
     sums = [gain_attn_sums, at.gain_mlp_sums, jnp.full(gain_attn_sums.shape, loss_part)]
     columns = jnp.pad(jnp.stack(sums, axis=1), ((0, 0), (0, 61)))
-    kv_grad = jnp.concatenate([low(tn(normed, d_kv_low)), split_sums(columns)], axis=1)
+    kv_grad = jnp.concatenate([low(tn(normed, at.d_qkv[:, slot_width : slot_width + kv_width])), split_sums(columns)], axis=1)
     at.kv_terms = terms(lambda owner: take(by_rows(kv_grad), owner), "fsdp")
-    blocks = partial.reshape(2, 2, part_rows, -1)
-    at.kept, at.sent = take(blocks, core_rank, 1), take(blocks, 1 - core_rank, 1)
-    at.next()
-    at.drop("d_query_low", "kv_low", "d_kv", "gate_sent", "d_qkv")
-    at.query_1 = low(with_own(at.query_terms[0], at.query_got[0]))
-    at.got = flip(at.sent, "tp", 1)
-    at.next()
-    summed_rows = wide(at.kept) + wide(at.got)
-    at.kept, at.sent = take(summed_rows, y_rank), low(take(summed_rows, 1 - y_rank))
-    at.out_2 = with_own(at.out_terms[1], at.out_got[1])
-    at.next()
-    at.got = flip(at.sent, "tp", 2)
     at.query_got += [around(at.query_terms[1], "fsdp")]
     at.query_z = ring(at.query_1[0], "ctx")
     at.out_z = ring(at.out_z, "ctx")
     at.next()
     at.query_z = low(wide(at.query_z) + wide(at.query_1[1]))
-    at.out_z = low(wide(at.out_z) + at.out_2[0])
+    at.next()
     at.query_2 = with_own(at.query_terms[1], at.query_got[1])
     at.d_normed = at.kept + wide(at.got)
-    at.next()
-    up_terms, up_got = at.drop("up_terms", "up_got")
-    up_far_got = jnp.stack(at.drop("up_far_0", "up_far_1"))
-    up_own = jnp.stack([with_own(up_terms[i], up_got[i]) for i in (2, 3)])
-    at.up_kept, at.up_sent = near_split(up_own + wide(up_far_got))
-    at.drop("query_1", "kept", "sent", "got", "up_far", "query_terms", "query_got")
+    got = at.drop("up_far_0", "up_far_1", "up_far_2")
+    up_far_got = jnp.concatenate(got, axis=0).reshape(2, -1, half)
+    at.up_kept, at.up_sent = near_split(wide(at.up_own) + wide(up_far_got))
+    at.drop("partial", "d_qkv")
+    at.drop("query_1", "kept", "sent", "got", "up_far", "up_mixed", "up_last", "up_own")
+    at.drop("query_terms", "query_got")
     at.drop("out_terms", "out_got")
     at.query_z = ring(at.query_z, "ctx")
-    at.out_z = ring(at.out_z, "ctx")
     at.kv_got = around(at.kv_terms, "fsdp")
+    at.out_back = to_tp_back(wide(at.out_z) + at.out_2[1])
     at.next()
     at.query_z = low(wide(at.query_z) + at.query_2[0])
     kv_mine = with_own(*at.drop("kv_terms", "kv_got"))
@@ -874,11 +900,6 @@
     at.kv_own = take(kv_mine, ctx_rank)
     at.kv_sent = [take(kv_mine, (ctx_rank + by) % ctx_count) for by in range(1, ctx_count)]
 
-    def to_tp_back(mine):
-        blocks = low(mine).reshape(tp_count, own_rows, -1)
-        return [take(blocks, tp_rank ^ bit) for bit in range(tp_count)]
-
-    at.out_back = to_tp_back(wide(at.out_z) + at.out_2[1])
     at.next()
     at.drop("out_z", "out_2")
     at.out_back = flip_tp(at.out_back)
@@ -922,7 +943,7 @@
     inner_one = jnp.mean(scaled * inputs_part, axis=-1, keepdims=True)
     input_grad = d_residual + scale_part * scaled - inputs_part * scale_part**3 * inner_one
     return (
-        low(output)[None],
+        at.output_low[None],
         loss,
         input_grad[None],
         gain_attn_grad,

time: 1030 us -> 1000 us (0.971)
  waiting for transfers between devices: 456 us -> 430 us
  other arithmetic: 129 us -> 140 us
    ppermute x69 -> x70, waiting for transfers between devices: 301 us -> 272 us  [flip(): lax.ppermute(array, axis, [(i, i ^ bit) for i in range(lax.axis_size(axis...]
    ppermute x46 -> x44, waiting for transfers between devices: 129 us -> 121 us  [ring(): lax.ppermute(array, axis, [(i, (i + by) % count) for i in range(count)])]
    ppermute x46 -> x44, starting transfers between devices: 46.7 us -> 39.9 us  [ring(): lax.ppermute(array, axis, [(i, (i + by) % count) for i in range(count)])]
    convert_element_type x23 -> x25, other arithmetic: 29.2 us -> 26.2 us  [low(): return values.astype(jnp.bfloat16)]
    unnamed x335 -> x325, local copies, waits for them, and re-layouts: 32.6 us -> 34 us
    ppermute x69 -> x70, starting transfers between devices: 66.3 us -> 65.3 us  [flip(): lax.ppermute(array, axis, [(i, i ^ bit) for i in range(lax.axis_size(axis...]
  transfers between devices with their start and end apart: 121 -> 120, of which waited for: 67 -> 68; matrix products, arithmetic and copies ran while one was open for 21% -> 23% of each run, Pallas kernels for 6% -> 6%
where the time goes in v4:
time: 1000 us; the launch traced here: 992 us
  waiting for transfers between devices  430 us (43%)
  other arithmetic  140 us (14%)
  matrix products  130 us (13%)
  starting transfers between devices  119 us (12%)
  local copies, waits for them, and re-layouts  104 us (10%)
  Pallas kernels  62.3 us (6%)
    ppermute x70, waiting for transfers between devices, flip(): lax.ppermute(array, axis, [(i, i ^ bit) for i in range(lax.axis_size(axis...  272 us
    ppermute x44, waiting for transfers between devices, ring(): lax.ppermute(array, axis, [(i, (i + by) % count) for i in range(count)])  121 us
    ppermute x70, starting transfers between devices, flip(): lax.ppermute(array, axis, [(i, i ^ bit) for i in range(lax.axis_size(axis...  65.3 us
    dot_general x5, matrix products, nn(): lax.dot_general(first, second, (((1,), (0,)), ((), ())), preferred_elemen...  45.9 us
    dot_general x5, matrix products, nt(): lax.dot_general(first, second, (((1,), (1,)), ((), ())), preferred_elemen...  45.5 us
    ppermute x44, starting transfers between devices, ring(): lax.ppermute(array, axis, [(i, (i + by) % count) for i in range(count)])  39.9 us
    dot_general x6, matrix products, tn(): lax.dot_general(first, second, (((0,), (0,)), ((), ())), preferred_elemen...  39 us
    ppermute x6, waiting for transfers between devices, shifted(): return lax.ppermute(array, axis, pairs)  36.1 us
  transfers between devices with their start and end apart: 120, of which 68 were waited for; matrix products, arithmetic and copies ran while one was open for 23% of the time, Pallas kernels for 6%

profile of v4, /device:TPU:0, one launch (start us, length us, event | category | flops | bytes accessed | tf_op | source)
XLA Modules:
  0.0 992.1 jit_solution(229483669103945686)
XLA Ops:
  30.8 12.7 %collective-permute-done.5.refs_1_ = bf16[320,1024]{1,0:T(8,128)(2,1)S(1)} collective-permute-done((bf16[320,1024]{1,0:T(8,128)(2,1)S(1)}, bf16[320,1024]{1,0:T(8,128)(2,1)S(1)}, u32[]{:S(2)}, u32[]{:S(2)}) %collective-permute-start.5) | collective-permute-done | bytes 655392 | tf_op jit(solution)/shard_map/ppermute | solution.py:22
  47.1 13.8 %collective-permute-done.7.refs_3_ = bf16[320,1024]{1,0:T(8,128)(2,1)S(1)} collective-permute-done((bf16[320,1024]{1,0:T(8,128)(2,1)S(1)}, bf16[320,1024]{1,0:T(8,128)(2,1)S(1)}, u32[]{:S(2)}, u32[]{:S(2)}) %collective-permute-start.7) | collective-permute-done | bytes 655392 | tf_op jit(solution)/shard_map/ppermute | solution.py:22
  161.8 16.4 %collective-permute-done.23 = bf16[320,1024]{1,0:T(8,128)(2,1)S(1)} collective-permute-done((bf16[320,1024]{1,0:T(8,128)(2,1)S(1)}, bf16[320,1024]{1,0:T(8,128)(2,1)S(1)}, u32[]{:S(2)}, u32[]{:S(2)}) %collective-permute-start.23) | collective-permute-done | bytes 655392 | tf_op jit(solution)/shard_map/ppermute | solution.py:17
  193.6 9.9 collective-permute-done.27
  217.8 18.3 %attention_forward.1 = bf16[768,768]{1,0:T(8,128)(2,1)S(1)} custom-call(s32[4]{0:T(128)S(1)} %pad_add_fusion.info_ref, bf16[768,768]{1,0:T(8,128)(2,1)S(1)} %copy-done.11, bf16[3072,512]{1,0:T(8,128)(2,1)S(1)} %copy-done.7), custom_call_target="tpu_custom_call" | custom-call | flops 5435817984 | bytes 5505024 | tf_op jit(solution)/shard_map/attention_forward/pallas_call | solution.py:163
  241.9 13.3 %collective-permute-done.29 = bf16[480,1024]{1,0:T(8,128)(2,1)} collective-permute-done((bf16[480,1024]{1,0:T(8,128)(2,1)}, bf16[480,1024]{1,0:T(8,128)(2,1)}, u32[]{:S(2)}, u32[]{:S(2)}) %collective-permute-start.29) | collective-permute-done | bytes 983072 | tf_op jit(solution)/shard_map/ppermute | solution.py:17
  268.2 30.3 %collective-permute-done.32 = bf16[320,1024]{1,0:T(8,128)(2,1)} collective-permute-done((bf16[320,1024]{1,0:T(8,128)(2,1)}, bf16[320,1024]{1,0:T(8,128)(2,1)}, u32[]{:S(2)}, u32[]{:S(2)}) %collective-permute-start.32) | collective-permute-done | bytes 655392 | tf_op jit(solution)/shard_map/ppermute | solution.py:17
  314.2 18.1 %collective-permute-done.37 = bf16[160,1024]{1,0:T(8,128)(2,1)S(1)} collective-permute-done((bf16[160,1024]{1,0:T(8,128)(2,1)}, bf16[160,1024]{1,0:T(8,128)(2,1)S(1)}, u32[]{:S(2)}, u32[]{:S(2)}) %collective-permute-start.37) | collective-permute-done | bytes 327712 | tf_op jit(solution)/shard_map/ppermute | solution.py:17
  343.9 15.7 %collective-permute-done.43 = bf16[160,1024]{1,0:T(8,128)(2,1)S(1)} collective-permute-done((bf16[160,1024]{1,0:T(8,128)(2,1)S(1)}, bf16[160,1024]{1,0:T(8,128)(2,1)S(1)}, u32[]{:S(2)}, u32[]{:S(2)}) %collective-permute-start.43) | collective-permute-done | bytes 327712 | tf_op jit(solution)/shard_map/ppermute | solution.py:17
  388.4 12.6 %fusion.113 = f32[1536,1024]{1,0:T(8,128)S(1)} fusion(bf16[1536,2560]{1,0:T(8,128)(2,1)} %copy-done.126, bf16[2560,1024]{1,0:T(8,128)(2,1)S(1)} %bitcast.435), kind=kOutput, calls=%fused_computation.476 | convolution fusion | flops 8053063680 | bytes 19398656 | tf_op jit(solution)/shard_map/dot_general | solution.py:110
  405.3 10.9 %collective-permute-done.50 = bf16[320,1024]{1,0:T(8,128)(2,1)S(1)} collective-permute-done((bf16[320,1024]{1,0:T(8,128)(2,1)S(1)}, bf16[320,1024]{1,0:T(8,128)(2,1)S(1)}, u32[]{:S(2)}, u32[]{:S(2)}) %collective-permute-start.50) | collective-permute-done | bytes 655392 | tf_op jit(solution)/shard_map/ppermute | solution.py:22
  439.4 9.0 collective-permute-done.52
  463.1 13.0 %collective-permute-done.55 = bf16[192,2560]{1,0:T(8,128)(2,1)S(1)} collective-permute-done((bf16[192,2560]{1,0:T(8,128)(2,1)S(1)}, bf16[192,2560]{1,0:T(8,128)(2,1)S(1)}, u32[]{:S(2)}, u32[]{:S(2)}) %collective-permute-start.55) | collective-permute-done | bytes 983072 | tf_op jit(solution)/shard_map/ppermute | solution.py:17
  483.9 15.9 %collective-permute-done.59 = bf16[192,2560]{1,0:T(8,128)(2,1)S(1)} collective-permute-done((bf16[192,2560]{1,0:T(8,128)(2,1)S(1)}, bf16[192,2560]{1,0:T(8,128)(2,1)S(1)}, u32[]{:S(2)}, u32[]{:S(2)}) %collective-permute-start.59) | collective-permute-done | bytes 983072 | tf_op jit(solution)/shard_map/ppermute | solution.py:17
  503.3 11.9 %collective-permute-done.61 = bf16[96,2560]{1,0:T(8,128)(2,1)S(1)} collective-permute-done((bf16[96,2560]{1,0:T(8,128)(2,1)S(1)}, bf16[96,2560]{1,0:T(8,128)(2,1)S(1)}, u32[]{:S(2)}, u32[]{:S(2)}) %collective-permute-start.61) | collective-permute-done | bytes 491552 | tf_op jit(solution)/shard_map/ppermute | solution.py:17
  524.8 8.9 convolution_convert_fusion.3
  537.0 14.3 %multiply_convert_fusion = (bf16[1536,1024]{1,0:T(8,128)(2,1)}, bf16[1536,1024]{1,0:T(8,128)(2,1)}) fusion(f32[1536,1024]{1,0:T(8,128)} %get-tuple-element.2256, f32[1536,1024]{1,0:T(8,128)S(1)} %bitcast.467, bf16[1536,2560]{1,0:T(8,128)(2,1)} %copy-done.127, bf16[2560,1024]{1,0:T(8,128)(2,1)S(1)} %bitcast.442), kind=kOutput, calls=%fused_computation.32 | convolution fusion | flops 8059355136 | bytes 31981568 | tf_op jit(solution)/shard_map/dot_general | solution.py:110
  554.6 11.8 %convolution_convert_fusion.2 = bf16[2560,1024]{1,0:T(8,128)(2,1)S(1)} fusion(bf16[1536,2560]{1,0:T(8,128)(2,1)} %copy-done.126, bf16[1536,1024]{1,0:T(8,128)(2,1)} %get-tuple-element.2329), kind=kOutput, calls=%fused_computation.38 | convolution fusion | flops 8055685120 | bytes 16252928 | tf_op jit(solution)/shard_map/dot_general | solution.py:122
  575.0 11.1 %fusion.114 = f32[1536,2560]{1,0:T(8,128)} fusion(bf16[1536,1024]{1,0:T(8,128)(2,1)S(1)} %copy-done.140, bf16[2560,1024]{1,0:T(8,128)(2,1)S(1)} %bitcast.438), kind=kOutput, calls=%fused_computation.477 | convolution fusion | flops 8053063680 | bytes 24117248 | tf_op jit(solution)/shard_map/dot_general | solution.py:116
  586.1 14.9 %add_convert_fusion = bf16[1536,2560]{1,0:T(8,128)(2,1)} fusion(f32[1536,2560]{1,0:T(8,128)} %fusion.114, bf16[1536,1024]{1,0:T(8,128)(2,1)} %get-tuple-element.2329, bf16[2560,1024]{1,0:T(8,128)(2,1)S(1)} %bitcast.434), kind=kOutput, calls=%fused_computation | convolution fusion | flops 8060928000 | bytes 31981568 | tf_op jit(solution)/shard_map/dot_general | solution.py:116
  614.7 15.8 %collective-permute-done.72 = bf16[160,1024]{1,0:T(8,128)(2,1)S(1)} collective-permute-done((bf16[160,1024]{1,0:T(8,128)(2,1)S(1)}, bf16[160,1024]{1,0:T(8,128)(2,1)S(1)}, u32[]{:S(2)}, u32[]{:S(2)}) %collective-permute-start.72) | collective-permute-done | bytes 327712 | tf_op jit(solution)/shard_map/ppermute | solution.py:17
  641.2 9.3 convolution_convert_fusion.1
  656.5 8.9 collective-permute-done.77
  679.6 21.1 %collective-permute-done.80 = bf16[320,1024]{1,0:T(8,128)(2,1)S(1)} collective-permute-done((bf16[320,1024]{1,0:T(8,128)(2,1)}, bf16[320,1024]{1,0:T(8,128)(2,1)S(1)}, u32[]{:S(2)}, u32[]{:S(2)}) %collective-permute-start.80) | collective-permute-done | bytes 655392 | tf_op jit(solution)/shard_map/ppermute | solution.py:17
  716.7 28.3 %attention_backward.1 = (f32[768,768]{1,0:T(8,128)S(1)}, bf16[3072,512]{1,0:T(8,128)(2,1)S(1)}) custom-call(s32[1]{0:T(128)} %bitcast.info_ref, bf16[768,768]{1,0:T(8,128)(2,1)S(1)} %copy-done.12, bf16[3072,512]{1,0:T(8,128)(2,1)S(1)} %copy-done.8, bf16[768,768]{1,0:T(8,128)(2,1)S(1)} %multiply_convert_fusion.2.do_ref), custom_call_target="tpu_custom_call" | custom-call | flops 13589544960 | bytes 11010048 | tf_op jit(solution)/shard_map/attention_backward/pallas_call | solution.py:225
  790.3 12.8 %collective-permute-done.90 = bf16[320,1024]{1,0:T(8,128)(2,1)} collective-permute-done((bf16[320,1024]{1,0:T(8,128)(2,1)}, bf16[320,1024]{1,0:T(8,128)(2,1)}, u32[]{:S(2)}, u32[]{:S(2)}) %collective-permute-start.90) | collective-permute-done | bytes 655392 | tf_op jit(solution)/shard_map/ppermute | solution.py:17
  814.6 14.0 %collective-permute-done.94 = bf16[768,128]{1,0:T(8,128)(2,1)S(1)} collective-permute-done((bf16[768,128]{1,0:T(8,128)(2,1)S(1)}, bf16[768,128]{1,0:T(8,128)(2,1)S(1)}, u32[]{:S(2)}, u32[]{:S(2)}) %collective-permute-start.94) | collective-permute-done | bytes 196640 | tf_op jit(solution)/shard_map/ppermute | solution.py:28
  828.5 16.1 %collective-permute-done.95 = bf16[768,128]{1,0:T(8,128)(2,1)S(1)} collective-permute-done((bf16[768,128]{1,0:T(8,128)(2,1)S(1)}, bf16[768,128]{1,0:T(8,128)(2,1)S(1)}, u32[]{:S(2)}, u32[]{:S(2)}) %collective-permute-start.95) | collective-permute-done | bytes 196640 | tf_op jit(solution)/shard_map/ppermute | solution.py:28
  857.7 13.6 %collective-permute-done.101 = bf16[160,1024]{1,0:T(8,128)(2,1)S(1)} collective-permute-done((bf16[160,1024]{1,0:T(8,128)(2,1)S(1)}, bf16[160,1024]{1,0:T(8,128)(2,1)S(1)}, u32[]{:S(2)}, u32[]{:S(2)}) %collective-permute-start.101) | collective-permute-done | bytes 327712 | tf_op jit(solution)/shard_map/ppermute | solution.py:17
  894.1 13.2 %collective-permute-done.106 = bf16[320,768]{1,0:T(8,128)(2,1)S(1)} collective-permute-done((bf16[320,768]{1,0:T(8,128)(2,1)}, bf16[320,768]{1,0:T(8,128)(2,1)S(1)}, u32[]{:S(2)}, u32[]{:S(2)}) %collective-permute-start.106) | collective-permute-done | bytes 491552 | tf_op jit(solution)/shard_map/ppermute | solution.py:22
  907.3 9.9 collective-permute-done.104
  946.3 9.5 collective-permute-done.109
  (824 shorter events, 530.1 us)
Async XLA Ops:
  135.7 45.4 %collective-permute-start.26 = (bf16[4,320,768]{2,1,0:T(8,128)(2,1)S(1)}, bf16[4,320,768]{2,1,0:T(8,128)(2,1)S(1)}, u32[]{:S(2)}, u32[]{:S(2)}) collective-permute-start(bf16[4,320,768]{2,1,0:T(8,128)(2,1)S(1)} %pad_maximum_fusion.5), channel_id=1, source_target_pairs={{0,16},{16,0},{1,17},{17,1},{2,18},{18,2},{3,19},{19,3},{4,20},{20... | collective-permute-start | bytes 5898248 | tf_op jit(solution)/shard_map/ppermute | solution.py:22
  152.1 28.9 %collective-permute-start.25 = (bf16[3072,128]{1,0:T(8,128)(2,1)S(1)}, bf16[3072,128]{1,0:T(8,128)(2,1)S(1)}, u32[]{:S(2)}, u32[]{:S(2)}) collective-permute-start(bf16[3072,128]{1,0:T(8,128)(2,1)S(1)} %pad_maximum_fusion.34), channel_id=1, source_target_pairs={{0,2},{1,3},{2,0},{3,1},{4,6},{5,7},{6,4},{7,5},{8,10},{9,11},{10,... | collective-permute-start | bytes 2359304 | tf_op jit(solution)/shard_map/ppermute | solution.py:17
  210.3 44.9 %collective-permute-start.29 = (bf16[480,1024]{1,0:T(8,128)(2,1)}, bf16[480,1024]{1,0:T(8,128)(2,1)}, u32[]{:S(2)}, u32[]{:S(2)}) collective-permute-start(bf16[480,1024]{1,0:T(8,128)(2,1)} %pad_maximum_fusion.27), channel_id=1, source_target_pairs={{0,8},{4,12},{8,0},{12,4},{1,9},{5,13},{9,1},{13,5},{2,10},{6,14},... | collective-permute-start | bytes 2949128 | tf_op jit(solution)/shard_map/ppermute | solution.py:17
  212.7 42.5 %collective-permute-start.30 = (bf16[2,320,1024]{2,1,0:T(8,128)(2,1)S(1)}, bf16[2,320,1024]{2,1,0:T(8,128)(2,1)S(1)}, u32[]{:S(2)}, u32[]{:S(2)}) collective-permute-start(bf16[2,320,1024]{2,1,0:T(8,128)(2,1)S(1)} %pad_maximum_fusion.13), channel_id=1, source_target_pairs={{0,16},{16,0},{1,17},{17,1},{2,18},{18,2},{3,19},{19,3},{4,20},{20... | collective-permute-start | bytes 3932168 | tf_op jit(solution)/shard_map/ppermute | solution.py:22
  265.2 33.3 %collective-permute-start.33 = (bf16[2,320,1024]{2,1,0:T(8,128)(2,1)}, bf16[2,320,1024]{2,1,0:T(8,128)(2,1)}, u32[]{:S(2)}, u32[]{:S(2)}) collective-permute-start(bf16[2,320,1024]{2,1,0:T(8,128)(2,1)} %bitcast.51), channel_id=1, source_target_pairs={{0,16},{16,0},{1,17},{17,1},{2,18},{18,2},{3,19},{19,3},{4,20},{20... | collective-permute-start | bytes 3932168 | tf_op jit(solution)/shard_map/ppermute | solution.py:22
  266.8 31.7 %collective-permute-start.34 = (bf16[192,2560]{1,0:T(8,128)(2,1)}, bf16[192,2560]{1,0:T(8,128)(2,1)}, u32[]{:S(2)}, u32[]{:S(2)}) collective-permute-start(bf16[192,2560]{1,0:T(8,128)(2,1)} %fusion.41), channel_id=1, source_target_pairs={{0,2},{1,3},{2,0},{3,1},{4,6},{5,7},{6,4},{7,5},{8,10},{9,11},{10,... | collective-permute-start | bytes 2949128 | tf_op jit(solution)/shard_map/ppermute | solution.py:17
  267.8 30.6 %collective-permute-start.32 = (bf16[320,1024]{1,0:T(8,128)(2,1)}, bf16[320,1024]{1,0:T(8,128)(2,1)}, u32[]{:S(2)}, u32[]{:S(2)}) collective-permute-start(bf16[320,1024]{1,0:T(8,128)(2,1)} %slice_bitcast_fusion.11), channel_id=1, source_target_pairs={{0,8},{4,12},{8,0},{12,4},{1,9},{5,13},{9,1},{13,5},{2,10},{6,14},... | collective-permute-start | bytes 1966088 | tf_op jit(solution)/shard_map/ppermute | solution.py:17
  303.4 31.1 %collective-permute-start.36 = (bf16[2,320,1024]{2,1,0:T(8,128)(2,1)S(1)}, bf16[2,320,1024]{2,1,0:T(8,128)(2,1)}, u32[]{:S(2)}, u32[]{:S(2)}) collective-permute-start(bf16[2,320,1024]{2,1,0:T(8,128)(2,1)S(1)} %pad_maximum_fusion.14), channel_id=1, source_target_pairs={{0,16},{16,0},{1,17},{17,1},{2,18},{18,2},{3,19},{19,3},{4,20},{20... | collective-permute-start | bytes 3932168 | tf_op jit(solution)/shard_map/ppermute | solution.py:22
  303.8 30.7 %collective-permute-start.39 = (bf16[192,2560]{1,0:T(8,128)(2,1)}, bf16[192,2560]{1,0:T(8,128)(2,1)}, u32[]{:S(2)}, u32[]{:S(2)}) collective-permute-start(bf16[192,2560]{1,0:T(8,128)(2,1)} %multiply_convert_fusion.3), channel_id=1, source_target_pairs={{0,4},{4,0},{8,12},{12,8},{1,5},{5,1},{9,13},{13,9},{2,6},{6,2},{1... | collective-permute-start | bytes 2949128 | tf_op jit(solution)/shard_map/ppermute | solution.py:17
  303.8 30.7 %collective-permute-start.38 = (bf16[192,2560]{1,0:T(8,128)(2,1)}, bf16[192,2560]{1,0:T(8,128)(2,1)}, u32[]{:S(2)}, u32[]{:S(2)}) collective-permute-start(bf16[192,2560]{1,0:T(8,128)(2,1)} %multiply_convert_fusion.3), channel_id=1, source_target_pairs={{0,2},{1,3},{2,0},{3,1},{4,6},{5,7},{6,4},{7,5},{8,10},{9,11},{10,... | collective-permute-start | bytes 2949128 | tf_op jit(solution)/shard_map/ppermute | solution.py:17
  305.3 29.2 %collective-permute-start.35 = (bf16[192,2560]{1,0:T(8,128)(2,1)}, bf16[192,2560]{1,0:T(8,128)(2,1)}, u32[]{:S(2)}, u32[]{:S(2)}) collective-permute-start(bf16[192,2560]{1,0:T(8,128)(2,1)} %multiply_convert_fusion.3), channel_id=1, source_target_pairs={{0,1},{1,0},{2,3},{3,2},{4,5},{5,4},{6,7},{7,6},{8,9},{9,8},{10,11... | collective-permute-start | bytes 2949128 | tf_op jit(solution)/shard_map/ppermute | solution.py:17
  571.5 34.4 %collective-permute-start.66 = (bf16[320,1024]{1,0:T(8,128)(2,1)}, bf16[320,1024]{1,0:T(8,128)(2,1)}, u32[]{:S(2)}, u32[]{:S(2)}) collective-permute-start(bf16[320,1024]{1,0:T(8,128)(2,1)} %add_convert_fusion.15), channel_id=1, source_target_pairs={{0,8},{4,12},{8,0},{12,4},{1,9},{5,13},{9,1},{13,5},{2,10},{6,14},... | collective-permute-start | bytes 1966088 | tf_op jit(solution)/shard_map/ppermute | solution.py:17
  572.9 32.9 %collective-permute-start.67 = (bf16[320,1024]{1,0:T(8,128)(2,1)}, bf16[320,1024]{1,0:T(8,128)(2,1)}, u32[]{:S(2)}, u32[]{:S(2)}) collective-permute-start(bf16[320,1024]{1,0:T(8,128)(2,1)} %get-tuple-element.2334), channel_id=1, source_target_pairs={{0,16},{16,0},{1,17},{17,1},{2,18},{18,2},{3,19},{19,3},{4,20},{20... | collective-permute-start | bytes 1966088 | tf_op jit(solution)/shard_map/ppermute | solution.py:22
  574.2 31.7 %collective-permute-start.68 = (bf16[320,1024]{1,0:T(8,128)(2,1)}, bf16[320,1024]{1,0:T(8,128)(2,1)}, u32[]{:S(2)}, u32[]{:S(2)}) collective-permute-start(bf16[320,1024]{1,0:T(8,128)(2,1)} %get-tuple-element.2336), channel_id=1, source_target_pairs={{0,16},{16,0},{1,17},{17,1},{2,18},{18,2},{3,19},{19,3},{4,20},{20... | collective-permute-start | bytes 1966088 | tf_op jit(solution)/shard_map/ppermute | solution.py:22
  636.8 28.7 %collective-permute-start.77 = (bf16[320,1024]{1,0:T(8,128)(2,1)S(1)}, bf16[320,1024]{1,0:T(8,128)(2,1)S(1)}, u32[]{:S(2)}, u32[]{:S(2)}) collective-permute-start(bf16[320,1024]{1,0:T(8,128)(2,1)S(1)} %copy-done.85), channel_id=1, source_target_pairs={{0,16},{16,0},{1,17},{17,1},{2,18},{18,2},{3,19},{19,3},{4,20},{20... | collective-permute-start | bytes 1966088 | tf_op jit(solution)/shard_map/ppermute | solution.py:22
  670.7 30.2 %collective-permute-start.82 = (bf16[192,2560]{1,0:T(8,128)(2,1)S(1)}, bf16[192,2560]{1,0:T(8,128)(2,1)}, u32[]{:S(2)}, u32[]{:S(2)}) collective-permute-start(bf16[192,2560]{1,0:T(8,128)(2,1)S(1)} %get-tuple-element.2581), channel_id=1, source_target_pairs={{0,2},{1,3},{2,0},{3,1},{4,6},{5,7},{6,4},{7,5},{8,10},{9,11},{10,... | collective-permute-start | bytes 2949128 | tf_op jit(solution)/shard_map/ppermute | solution.py:17
  672.2 28.6 %collective-permute-start.80 = (bf16[320,1024]{1,0:T(8,128)(2,1)}, bf16[320,1024]{1,0:T(8,128)(2,1)S(1)}, u32[]{:S(2)}, u32[]{:S(2)}) collective-permute-start(bf16[320,1024]{1,0:T(8,128)(2,1)} %add_convert_fusion.11), channel_id=1, source_target_pairs={{0,8},{4,12},{8,0},{12,4},{1,9},{5,13},{9,1},{13,5},{2,10},{6,14},... | collective-permute-start | bytes 1966088 | tf_op jit(solution)/shard_map/ppermute | solution.py:17
  672.8 27.9 %collective-permute-start.81 = (bf16[320,1024]{1,0:T(8,128)(2,1)}, bf16[320,1024]{1,0:T(8,128)(2,1)S(1)}, u32[]{:S(2)}, u32[]{:S(2)}) collective-permute-start(bf16[320,1024]{1,0:T(8,128)(2,1)} %get-tuple-element.2548), channel_id=1, source_target_pairs={{0,16},{16,0},{1,17},{17,1},{2,18},{18,2},{3,19},{19,3},{4,20},{20... | collective-permute-start | bytes 1966088 | tf_op jit(solution)/shard_map/ppermute | solution.py:22
  709.3 42.5 %collective-permute-start.87 = (bf16[160,1024]{1,0:T(8,128)(2,1)S(1)}, bf16[160,1024]{1,0:T(8,128)(2,1)S(1)}, u32[]{:S(2)}, u32[]{:S(2)}) collective-permute-start(bf16[160,1024]{1,0:T(8,128)(2,1)S(1)} %get-tuple-element.2657), channel_id=1, source_target_pairs={{0,8},{4,12},{8,0},{12,4},{1,9},{5,13},{9,1},{13,5},{2,10},{6,14},... | collective-permute-start | bytes 983048 | tf_op jit(solution)/shard_map/ppermute | solution.py:17
  710.6 41.1 %collective-permute-start.85 = (bf16[320,1024]{1,0:T(8,128)(2,1)S(1)}, bf16[320,1024]{1,0:T(8,128)(2,1)S(1)}, u32[]{:S(2)}, u32[]{:S(2)}) collective-permute-start(bf16[320,1024]{1,0:T(8,128)(2,1)S(1)} %copy-done.94), channel_id=1, source_target_pairs={{0,4},{4,0},{8,12},{12,8},{1,5},{5,1},{9,13},{13,9},{2,6},{6,2},{1... | collective-permute-start | bytes 1966088 | tf_op jit(solution)/shard_map/ppermute | solution.py:17
  711.9 43.3 %collective-permute-start.86 = (bf16[320,1024]{1,0:T(8,128)(2,1)S(1)}, bf16[320,1024]{1,0:T(8,128)(2,1)S(1)}, u32[]{:S(2)}, u32[]{:S(2)}) collective-permute-start(bf16[320,1024]{1,0:T(8,128)(2,1)S(1)} %copy-done.96), channel_id=1, source_target_pairs={{0,8},{4,12},{8,0},{12,4},{1,9},{5,13},{9,1},{13,5},{2,10},{6,14},... | collective-permute-start | bytes 1966088 | tf_op jit(solution)/shard_map/ppermute | solution.py:17
  713.1 44.2 %collective-permute-start.88 = (bf16[3,320,1024]{2,1,0:T(8,128)(2,1)}, bf16[3,320,1024]{2,1,0:T(8,128)(2,1)S(1)}, u32[]{:S(2)}, u32[]{:S(2)}) collective-permute-start(bf16[3,320,1024]{2,1,0:T(8,128)(2,1)} %pad_maximum_fusion.8), channel_id=1, source_target_pairs={{0,16},{16,0},{1,17},{17,1},{2,18},{18,2},{3,19},{19,3},{4,20},{20... | collective-permute-start | bytes 5898248 | tf_op jit(solution)/shard_map/ppermute | solution.py:22
  772.3 30.9 %collective-permute-start.90 = (bf16[320,1024]{1,0:T(8,128)(2,1)}, bf16[320,1024]{1,0:T(8,128)(2,1)}, u32[]{:S(2)}, u32[]{:S(2)}) collective-permute-start(bf16[320,1024]{1,0:T(8,128)(2,1)} %fusion.81), channel_id=1, source_target_pairs={{0,4},{4,0},{8,12},{12,8},{1,5},{5,1},{9,13},{13,9},{2,6},{6,2},{1... | collective-permute-start | bytes 1966088 | tf_op jit(solution)/shard_map/ppermute | solution.py:17
  773.4 32.2 %collective-permute-start.93 = (bf16[320,1024]{1,0:T(8,128)(2,1)}, bf16[320,1024]{1,0:T(8,128)(2,1)}, u32[]{:S(2)}, u32[]{:S(2)}) collective-permute-start(bf16[320,1024]{1,0:T(8,128)(2,1)} %pad_maximum_fusion.38), channel_id=1, source_target_pairs={{0,8},{4,12},{8,0},{12,4},{1,9},{5,13},{9,1},{13,5},{2,10},{6,14},... | collective-permute-start | bytes 1966088 | tf_op jit(solution)/shard_map/ppermute | solution.py:17
  774.7 30.9 %collective-permute-start.91 = (bf16[3072,128]{1,0:T(8,128)(2,1)}, bf16[3072,128]{1,0:T(8,128)(2,1)}, u32[]{:S(2)}, u32[]{:S(2)}) collective-permute-start(bf16[3072,128]{1,0:T(8,128)(2,1)} %fusion.74), channel_id=1, source_target_pairs={{0,2},{1,3},{2,0},{3,1},{4,6},{5,7},{6,4},{7,5},{8,10},{9,11},{10,... | collective-permute-start | bytes 2359304 | tf_op jit(solution)/shard_map/ppermute | solution.py:17
  775.6 30.0 %collective-permute-start.92 = (bf16[2,320,768]{2,1,0:T(8,128)(2,1)}, bf16[2,320,768]{2,1,0:T(8,128)(2,1)}, u32[]{:S(2)}, u32[]{:S(2)}) collective-permute-start(bf16[2,320,768]{2,1,0:T(8,128)(2,1)} %get-tuple-element.2750), channel_id=1, source_target_pairs={{0,16},{16,0},{1,17},{17,1},{2,18},{18,2},{3,19},{19,3},{4,20},{20... | collective-permute-start | bytes 2949128 | tf_op jit(solution)/shard_map/ppermute | solution.py:22
  809.7 35.8 %collective-permute-start.97 = (bf16[2,320,768]{2,1,0:T(8,128)(2,1)S(1)}, bf16[2,320,768]{2,1,0:T(8,128)(2,1)S(1)}, u32[]{:S(2)}, u32[]{:S(2)}) collective-permute-start(bf16[2,320,768]{2,1,0:T(8,128)(2,1)S(1)} %copy-done.78), channel_id=1, source_target_pairs={{0,16},{16,0},{1,17},{17,1},{2,18},{18,2},{3,19},{19,3},{4,20},{20... | collective-permute-start | bytes 2949128 | tf_op jit(solution)/shard_map/ppermute | solution.py:22
  810.6 34.1 %collective-permute-start.98 = (bf16[320,768]{1,0:T(8,128)(2,1)S(1)}, bf16[320,768]{1,0:T(8,128)(2,1)S(1)}, u32[]{:S(2)}, u32[]{:S(2)}) collective-permute-start(bf16[320,768]{1,0:T(8,128)(2,1)S(1)} %slice_bitcast_fusion.21), channel_id=1, source_target_pairs={{0,4},{4,8},{8,12},{12,0},{1,5},{5,9},{9,13},{13,1},{2,6},{6,10},{... | collective-permute-start | bytes 1474568 | tf_op jit(solution)/shard_map/ppermute | solution.py:22
  812.0 32.7 %collective-permute-start.95 = (bf16[768,128]{1,0:T(8,128)(2,1)S(1)}, bf16[768,128]{1,0:T(8,128)(2,1)S(1)}, u32[]{:S(2)}, u32[]{:S(2)}) collective-permute-start(bf16[768,128]{1,0:T(8,128)(2,1)S(1)} %get-tuple-element.2791), channel_id=1, source_target_pairs={{8,0},{12,4},{9,1},{13,5},{10,2},{14,6},{11,3},{15,7},{24,16},{28,... | collective-permute-start | bytes 589832 | tf_op jit(solution)/shard_map/ppermute | solution.py:28
  813.3 31.4 %collective-permute-start.96 = (bf16[768,128]{1,0:T(8,128)(2,1)S(1)}, bf16[768,128]{1,0:T(8,128)(2,1)S(1)}, u32[]{:S(2)}, u32[]{:S(2)}) collective-permute-start(bf16[768,128]{1,0:T(8,128)(2,1)S(1)} %get-tuple-element.2792), channel_id=1, source_target_pairs={{12,0},{13,1},{14,2},{15,3},{28,16},{29,17},{30,18},{31,19}} | collective-permute-start | bytes 589832 | tf_op jit(solution)/shard_map/ppermute | solution.py:28
  889.1 28.0 %collective-permute-start.103 = (bf16[192,2560]{1,0:T(8,128)(2,1)}, bf16[192,2560]{1,0:T(8,128)(2,1)}, u32[]{:S(2)}, u32[]{:S(2)}) collective-permute-start(bf16[192,2560]{1,0:T(8,128)(2,1)} %fusion.42), channel_id=1, source_target_pairs={{0,2},{1,3},{2,0},{3,1},{4,6},{5,7},{6,4},{7,5},{8,10},{9,11},{10,... | collective-permute-start | bytes 2949128 | tf_op jit(solution)/shard_map/ppermute | solution.py:17
  889.2 27.9 %collective-permute-start.105 = (bf16[2,320,768]{2,1,0:T(8,128)(2,1)}, bf16[2,320,768]{2,1,0:T(8,128)(2,1)}, u32[]{:S(2)}, u32[]{:S(2)}) collective-permute-start(bf16[2,320,768]{2,1,0:T(8,128)(2,1)} %get-tuple-element.2924), channel_id=1, source_target_pairs={{0,16},{16,0},{1,17},{17,1},{2,18},{18,2},{3,19},{19,3},{4,20},{20... | collective-permute-start | bytes 2949128 | tf_op jit(solution)/shard_map/ppermute | solution.py:22
  (248 other events, 2743.3 us)

commit v5 on v4

--- a/solution.py
+++ b/solution.py
@@ -451,11 +451,11 @@
     at.out_3 = ring(at.out_2, "ctx")
     at.next()
     normed = at.normed
-    at.up_pair = paired(*at.drop("up_mine", "up_got"))
     at.out_near = jnp.stack([at.out_0, at.out_1, at.out_2, at.out_3])
     at.next()
     out_x = over_fsdp(at.out_near)
     at.chunks = [shifted(at.kv_own, "ctx", by) for by in range(reach_back, 0, -1)]
+    at.up_pair = paired(*at.drop("up_mine", "up_got"))
     at.next()
     at.kv_column = jnp.concatenate(at.drop("chunks")[0] + [at.kv_own], axis=0)
     at.gate_far = jnp.concatenate(quarters(at.gate_pair)[:2], axis=0)
@@ -467,9 +467,10 @@
     at.out_x = out_x
     at.next()
     at.kv_pair = jnp.stack(at.drop("kv_column", "kv_over_y"))
+    at.next()
+    at.kv_other = flip(at.kv_pair, "tp", 1)
     at.down_pair = paired(*at.drop("down_mine", "down_got"))
-    at.next()
-    at.kv_other = flip(at.kv_pair, "tp", 1)
+    at.mixed_far = jnp.concatenate(quarters(at.gate_pair)[3:] + quarters(at.up_pair)[:2], axis=0)
     at.far_1 = far(quarters(at.gate_pair)[2:3])
     (out_x,) = at.drop("out_x")
     at.out_part = placed([[block[i] for block in out_x] for i in range(ctx_count)])
@@ -478,7 +479,6 @@
     at.keyvals = jnp.concatenate(
         swapped([kv_pair[0], kv_other[0], kv_pair[1], kv_other[1]], tp_rank), axis=1
     )
-    at.mixed_far = jnp.concatenate(quarters(at.gate_pair)[3:] + quarters(at.up_pair)[:2], axis=0)
     at.drop("up_sent", "down_sent", "gate_far", "out_near")
     at.next()
 
@@ -623,8 +623,8 @@
     at.next()
     sum_sides()
     gate_proj, up_proj = at.drop("gate_proj", "up_proj")
-    at.activated, gelu_back = jax.vjp(gelu_tanh, gate_proj)
-    at.slope = gelu_back(up_proj)[0]
+    activated, gelu_back = jax.vjp(gelu_tanh, gate_proj)
+    at.activated, at.slope = low(activated), low(gelu_back(up_proj)[0])
     at.next()
     at.ffn_parts = at.drop("part", "got_y", "got_z")
     at.drop("over_y", "over_z")
@@ -696,8 +696,8 @@
     at.next()
     at.down_x = [around(at.down_terms[0], "fsdp")]
     d_hidden = nn(at.d_ffn, down_full)
-    at.d_gate = low(d_hidden * at.slope)
-    at.d_up = low(d_hidden * at.activated)
+    at.d_gate = low(d_hidden * wide(at.slope))
+    at.d_up = low(d_hidden * wide(at.activated))
     at.next()
     at.drop("d_ffn", "hidden_act", "slope", "activated")
     at.down_x += [around(at.down_terms[1], "fsdp")]
@@ -820,6 +820,7 @@
     at.kv_got = flip(at.kv_sent, "tp", 2)
     at.up_far_1 = flip(at.up_mixed, "ctx", 2)
     at.gate_near = flip(at.gate_sent, "ctx", 1)
+    at.down_out = near_joined(*at.drop("down_kept", "down_got")).T
     at.up_own = low(wide(at.up_own) + wide(at.drop("up_own_got")[0]))
     at.out_got = [around(at.out_terms[0], "fsdp")]
     d_query_raw = turn(
@@ -838,7 +839,6 @@
     at.next()
     at.kv_got = [shifted(at.kv_low[by - 1], "ctx", -by) for by in range(1, reach_back + 1)]
     at.out_got += [around(at.out_terms[1], "fsdp")]
-    at.out_z = ring(at.out_1[0], "ctx")
     at.next()
     d_kv = at.d_kv
     for got in at.drop("kv_got")[0]:
@@ -847,11 +847,10 @@
     at.d_qkv = jnp.concatenate(
         [at.d_query_low, jnp.pad(d_kv_low, ((0, 0), (0, kv_width)))], axis=1
     )
-    at.out_z = low(wide(at.out_z) + wide(at.out_1[1]))
     at.next()
     at.query_got = [around(at.query_terms[0], "fsdp")]
     at.up_far_2 = flip(at.up_last, "ctx", 2)
-    at.out_z = ring(at.out_z, "ctx")
+    at.out_z = ring(at.out_1[0], "ctx")
     at.partial = low(nt(at.d_qkv, qkv_part))
     at.next()
     partial = at.partial
@@ -861,19 +860,26 @@
     at.drop("d_query_low", "kv_low", "d_kv", "gate_sent")
     at.query_1 = low(with_own(at.query_terms[0], at.query_got[0]))
     at.out_2 = with_own(at.out_terms[1], at.out_got[1])
-    at.out_z = low(wide(at.out_z) + at.out_2[0])
+    at.out_z = low(wide(at.out_z) + wide(at.out_1[1]))
     at.got = flip(at.sent, "tp", 1)
-    at.next()
-    summed_rows = wide(at.kept) + wide(at.got)
-    at.kept, at.sent = take(summed_rows, y_rank), low(take(summed_rows, 1 - y_rank))
-    at.next()
-    at.got = flip(at.sent, "tp", 2)
+    at.out_z = ring(at.out_z, "ctx")
     gain_attn_sums = jnp.sum(wide(at.partial) * inputs * scale_one, axis=0)
     sums = [gain_attn_sums, at.gain_mlp_sums, jnp.full(gain_attn_sums.shape, loss_part)]
     columns = jnp.pad(jnp.stack(sums, axis=1), ((0, 0), (0, 61)))
     kv_grad = jnp.concatenate([low(tn(normed, at.d_qkv[:, slot_width : slot_width + kv_width])), split_sums(columns)], axis=1)
     at.kv_terms = terms(lambda owner: take(by_rows(kv_grad), owner), "fsdp")
+    at.next()
+    summed_rows = wide(at.kept) + wide(at.got)
+    at.kept, at.sent = take(summed_rows, y_rank), low(take(summed_rows, 1 - y_rank))
+    at.out_z = low(wide(at.out_z) + at.out_2[0])
+    at.next()
+    at.got = flip(at.sent, "tp", 2)
     at.query_got += [around(at.query_terms[1], "fsdp")]
+    got = at.drop("up_far_0", "up_far_1", "up_far_2")
+    up_far_got = jnp.concatenate(got, axis=0).reshape(2, -1, half)
+    at.up_kept, up_sent = near_split(wide(at.up_own) + wide(up_far_got))
+    at.up_sent = jnp.split(up_sent, 2)
+    at.gate_out = near_joined(*at.drop("gate_kept", "gate_near"))
     at.query_z = ring(at.query_1[0], "ctx")
     at.out_z = ring(at.out_z, "ctx")
     at.next()
@@ -881,15 +887,13 @@
     at.next()
     at.query_2 = with_own(at.query_terms[1], at.query_got[1])
     at.d_normed = at.kept + wide(at.got)
-    got = at.drop("up_far_0", "up_far_1", "up_far_2")
-    up_far_got = jnp.concatenate(got, axis=0).reshape(2, -1, half)
-    at.up_kept, at.up_sent = near_split(wide(at.up_own) + wide(up_far_got))
     at.drop("partial", "d_qkv")
     at.drop("query_1", "kept", "sent", "got", "up_far", "up_mixed", "up_last", "up_own")
     at.drop("query_terms", "query_got")
     at.drop("out_terms", "out_got")
     at.query_z = ring(at.query_z, "ctx")
     at.kv_got = around(at.kv_terms, "fsdp")
+    at.up_near = flip(at.up_sent[0], "ctx", 1)
     at.out_back = to_tp_back(wide(at.out_z) + at.out_2[1])
     at.next()
     at.query_z = low(wide(at.query_z) + at.query_2[0])
@@ -913,7 +917,7 @@
     )
     at.back = to_tp_back(jnp.concatenate([query_mine, kv_mine], axis=1))
     at.next()
-    up_near = flip(at.up_sent, "ctx", 1)
+    up_near = jnp.concatenate([at.up_near, flip(at.up_sent[1], "ctx", 1)], axis=0)
     at.drop("query_z", "query_2", "kv_got", "kv_own", "kv_sent", "up_sent")
 
     def whole_heads(parts):
@@ -933,8 +937,7 @@
     kv_grad = jnp.concatenate([part[:, :kv_width] for part in kv_parts], axis=1)
     sums = joined_sums(sum(part[:, kv_width:] for part in kv_parts))
     gain_attn_grad, gain_mlp_grad, loss_sum = sums[:, 0], sums[:, 1], sums[0, 2]
-    down_grad = near_joined(at.down_kept, at.down_got).T
-    gate_grad = near_joined(at.gate_kept, at.gate_near)
+    down_grad, gate_grad = at.down_out, at.gate_out
     up_grad = near_joined(at.up_kept, up_near)
     loss = loss_sum / (count * width)
     d_normed, d_residual = at.d_normed, at.d_residual

time: 1000 us -> 984 us (0.984)
  waiting for transfers between devices: 430 us -> 407 us
    ppermute x6, waiting for transfers between devices: 36.1 us -> 18.6 us  [shifted(): return lax.ppermute(array, axis, pairs)]
    convert_element_type x25 -> x26, other arithmetic: 26.2 us -> 33.4 us  [low(): return values.astype(jnp.bfloat16)]
    unnamed x325 -> x293, local copies, waits for them, and re-layouts: 34 us -> 29.2 us
    ppermute x70 -> x71, waiting for transfers between devices: 272 us -> 276 us  [flip(): lax.ppermute(array, axis, [(i, i ^ bit) for i in range(lax.axis_size(axis...]
    ppermute x70 -> x71, starting transfers between devices: 65.3 us -> 68 us  [flip(): lax.ppermute(array, axis, [(i, i ^ bit) for i in range(lax.axis_size(axis...]
  transfers between devices with their start and end apart: 120 -> 121, of which waited for: 68 -> 70; matrix products, arithmetic and copies ran while one was open for 23% -> 24% of each run, Pallas kernels for 6% -> 6%
where the time goes in v5:
time: 984 us; the launch traced here: 973 us
  waiting for transfers between devices  407 us (41%)
  other arithmetic  142 us (14%)
  starting transfers between devices  127 us (13%)
  matrix products  126 us (13%)
  local copies, waits for them, and re-layouts  102 us (10%)
  Pallas kernels  62.3 us (6%)
    ppermute x71, waiting for transfers between devices, flip(): lax.ppermute(array, axis, [(i, i ^ bit) for i in range(lax.axis_size(axis...  276 us
    ppermute x44, waiting for transfers between devices, ring(): lax.ppermute(array, axis, [(i, (i + by) % count) for i in range(count)])  113 us
    ppermute x71, starting transfers between devices, flip(): lax.ppermute(array, axis, [(i, i ^ bit) for i in range(lax.axis_size(axis...  68 us
    ppermute x44, starting transfers between devices, ring(): lax.ppermute(array, axis, [(i, (i + by) % count) for i in range(count)])  45.9 us
    dot_general x5, matrix products, nt(): lax.dot_general(first, second, (((1,), (1,)), ((), ())), preferred_elemen...  45.4 us
    dot_general x5, matrix products, nn(): lax.dot_general(first, second, (((1,), (0,)), ((), ())), preferred_elemen...  43.8 us
    dot_general x6, matrix products, tn(): lax.dot_general(first, second, (((0,), (0,)), ((), ())), preferred_elemen...  37 us
    convert_element_type x26, other arithmetic, low(): return values.astype(jnp.bfloat16)  33.4 us
  transfers between devices with their start and end apart: 121, of which 70 were waited for; matrix products, arithmetic and copies ran while one was open for 24% of the time, Pallas kernels for 6%

profile of v5, /device:TPU:0, one launch (start us, length us, event | category | flops | bytes accessed | tf_op | source)
XLA Modules:
  0.0 973.4 jit_solution(8128026424427534329)
XLA Ops:
  30.8 12.7 %collective-permute-done.5.refs_1_ = bf16[320,1024]{1,0:T(8,128)(2,1)S(1)} collective-permute-done((bf16[320,1024]{1,0:T(8,128)(2,1)S(1)}, bf16[320,1024]{1,0:T(8,128)(2,1)S(1)}, u32[]{:S(2)}, u32[]{:S(2)}) %collective-permute-start.5) | collective-permute-done | bytes 655392 | tf_op jit(solution)/shard_map/ppermute | solution.py:22
  47.1 13.8 %collective-permute-done.7.refs_3_ = bf16[320,1024]{1,0:T(8,128)(2,1)S(1)} collective-permute-done((bf16[320,1024]{1,0:T(8,128)(2,1)S(1)}, bf16[320,1024]{1,0:T(8,128)(2,1)S(1)}, u32[]{:S(2)}, u32[]{:S(2)}) %collective-permute-start.7) | collective-permute-done | bytes 655392 | tf_op jit(solution)/shard_map/ppermute | solution.py:22
  84.8 7.6 collective-permute-done.13
  162.6 16.2 %collective-permute-done.23 = bf16[320,1024]{1,0:T(8,128)(2,1)} collective-permute-done((bf16[320,1024]{1,0:T(8,128)(2,1)}, bf16[320,1024]{1,0:T(8,128)(2,1)}, u32[]{:S(2)}, u32[]{:S(2)}) %collective-permute-start.23) | collective-permute-done | bytes 655392 | tf_op jit(solution)/shard_map/ppermute | solution.py:17
  211.7 18.3 %attention_forward.1 = bf16[768,768]{1,0:T(8,128)(2,1)S(1)} custom-call(s32[4]{0:T(128)S(1)} %pad_add_fusion.info_ref, bf16[768,768]{1,0:T(8,128)(2,1)S(1)} %copy-done.11, bf16[3072,512]{1,0:T(8,128)(2,1)S(1)} %copy-done.7), custom_call_target="tpu_custom_call" | custom-call | flops 5435817984 | bytes 5505024 | tf_op jit(solution)/shard_map/attention_forward/pallas_call | solution.py:163
  235.7 13.1 %collective-permute-done.29 = bf16[480,1024]{1,0:T(8,128)(2,1)} collective-permute-done((bf16[480,1024]{1,0:T(8,128)(2,1)}, bf16[480,1024]{1,0:T(8,128)(2,1)}, u32[]{:S(2)}, u32[]{:S(2)}) %collective-permute-start.29) | collective-permute-done | bytes 983072 | tf_op jit(solution)/shard_map/ppermute | solution.py:17
  261.5 31.4 %collective-permute-done.32 = bf16[320,1024]{1,0:T(8,128)(2,1)} collective-permute-done((bf16[320,1024]{1,0:T(8,128)(2,1)}, bf16[320,1024]{1,0:T(8,128)(2,1)}, u32[]{:S(2)}, u32[]{:S(2)}) %collective-permute-start.32) | collective-permute-done | bytes 655392 | tf_op jit(solution)/shard_map/ppermute | solution.py:17
  308.2 18.4 %collective-permute-done.37 = bf16[160,1024]{1,0:T(8,128)(2,1)S(1)} collective-permute-done((bf16[160,1024]{1,0:T(8,128)(2,1)}, bf16[160,1024]{1,0:T(8,128)(2,1)S(1)}, u32[]{:S(2)}, u32[]{:S(2)}) %collective-permute-start.37) | collective-permute-done | bytes 327712 | tf_op jit(solution)/shard_map/ppermute | solution.py:17
  338.1 15.8 %collective-permute-done.43 = bf16[160,1024]{1,0:T(8,128)(2,1)S(1)} collective-permute-done((bf16[160,1024]{1,0:T(8,128)(2,1)S(1)}, bf16[160,1024]{1,0:T(8,128)(2,1)S(1)}, u32[]{:S(2)}, u32[]{:S(2)}) %collective-permute-start.43) | collective-permute-done | bytes 327712 | tf_op jit(solution)/shard_map/ppermute | solution.py:17
  363.3 8.3 fusion.112
  382.7 12.6 %fusion.113 = f32[1536,1024]{1,0:T(8,128)S(1)} fusion(bf16[1536,2560]{1,0:T(8,128)(2,1)} %copy-done.111, bf16[2560,1024]{1,0:T(8,128)(2,1)S(1)} %bitcast.434), kind=kOutput, calls=%fused_computation.479 | convolution fusion | flops 8053063680 | bytes 19398656 | tf_op jit(solution)/shard_map/dot_general | solution.py:110
  399.5 10.9 %collective-permute-done.50 = bf16[320,1024]{1,0:T(8,128)(2,1)S(1)} collective-permute-done((bf16[320,1024]{1,0:T(8,128)(2,1)S(1)}, bf16[320,1024]{1,0:T(8,128)(2,1)S(1)}, u32[]{:S(2)}, u32[]{:S(2)}) %collective-permute-start.50) | collective-permute-done | bytes 655392 | tf_op jit(solution)/shard_map/ppermute | solution.py:22
  413.0 8.8 convolution_convert_fusion
  433.0 9.5 collective-permute-done.52
  456.5 13.7 %collective-permute-done.55 = bf16[192,2560]{1,0:T(8,128)(2,1)S(1)} collective-permute-done((bf16[192,2560]{1,0:T(8,128)(2,1)S(1)}, bf16[192,2560]{1,0:T(8,128)(2,1)S(1)}, u32[]{:S(2)}, u32[]{:S(2)}) %collective-permute-start.55) | collective-permute-done | bytes 983072 | tf_op jit(solution)/shard_map/ppermute | solution.py:17
  477.7 16.3 %collective-permute-done.59 = bf16[192,2560]{1,0:T(8,128)(2,1)S(1)} collective-permute-done((bf16[192,2560]{1,0:T(8,128)(2,1)S(1)}, bf16[192,2560]{1,0:T(8,128)(2,1)S(1)}, u32[]{:S(2)}, u32[]{:S(2)}) %collective-permute-start.59) | collective-permute-done | bytes 983072 | tf_op jit(solution)/shard_map/ppermute | solution.py:17
  497.4 12.0 %collective-permute-done.61 = bf16[96,2560]{1,0:T(8,128)(2,1)S(1)} collective-permute-done((bf16[96,2560]{1,0:T(8,128)(2,1)S(1)}, bf16[96,2560]{1,0:T(8,128)(2,1)S(1)}, u32[]{:S(2)}, u32[]{:S(2)}) %collective-permute-start.61) | collective-permute-done | bytes 491552 | tf_op jit(solution)/shard_map/ppermute | solution.py:17
  518.7 8.9 convolution_convert_fusion.3
  531.4 12.2 %multiply_convert_fusion = (bf16[1536,1024]{1,0:T(8,128)(2,1)}, bf16[1536,1024]{1,0:T(8,128)(2,1)S(1)}) fusion(bf16[1536,1024]{1,0:T(8,128)(2,1)S(1)} %copy-done.50, bf16[1536,1024]{1,0:T(8,128)(2,1)S(1)} %copy-done.49, bf16[1536,2560]{1,0:T(8,128)(2,1)} %copy-done.112, bf16[2560,1024]{1,0:T(8,128)(2,1)S(1)} %bitcast.441), kind=kOutput, calls=%fused_computation.33 | convolution fusion | flops 8062500864 | bytes 25690112 | tf_op jit(solution)/shard_map/dot_general | solution.py:110
  548.0 11.0 %convolution_convert_fusion.2 = bf16[2560,1024]{1,0:T(8,128)(2,1)S(1)} fusion(bf16[1536,2560]{1,0:T(8,128)(2,1)} %copy-done.111, bf16[1536,1024]{1,0:T(8,128)(2,1)S(1)} %get-tuple-element.2316), kind=kOutput, calls=%fused_computation.39 | convolution fusion | flops 8055685120 | bytes 16252928 | tf_op jit(solution)/shard_map/dot_general | solution.py:122
  567.5 11.0 %fusion.114 = f32[1536,2560]{1,0:T(8,128)} fusion(bf16[1536,1024]{1,0:T(8,128)(2,1)S(1)} %copy-done.125, bf16[2560,1024]{1,0:T(8,128)(2,1)S(1)} %bitcast.437), kind=kOutput, calls=%fused_computation.480 | convolution fusion | flops 8053063680 | bytes 24117248 | tf_op jit(solution)/shard_map/dot_general | solution.py:116
  578.6 15.0 %add_convert_fusion = bf16[1536,2560]{1,0:T(8,128)(2,1)} fusion(f32[1536,2560]{1,0:T(8,128)} %fusion.114, bf16[1536,1024]{1,0:T(8,128)(2,1)} %copy-done.127, bf16[2560,1024]{1,0:T(8,128)(2,1)S(1)} %bitcast.433), kind=kOutput, calls=%fused_computation | convolution fusion | flops 8060928000 | bytes 31981568 | tf_op jit(solution)/shard_map/dot_general | solution.py:116
  607.9 15.8 %collective-permute-done.72 = bf16[160,1024]{1,0:T(8,128)(2,1)S(1)} collective-permute-done((bf16[160,1024]{1,0:T(8,128)(2,1)S(1)}, bf16[160,1024]{1,0:T(8,128)(2,1)S(1)}, u32[]{:S(2)}, u32[]{:S(2)}) %collective-permute-start.72) | collective-permute-done | bytes 327712 | tf_op jit(solution)/shard_map/ppermute | solution.py:17
  634.5 9.3 convolution_convert_fusion.1
  649.8 8.8 collective-permute-done.77
  672.8 20.9 %collective-permute-done.80 = bf16[320,1024]{1,0:T(8,128)(2,1)S(1)} collective-permute-done((bf16[320,1024]{1,0:T(8,128)(2,1)}, bf16[320,1024]{1,0:T(8,128)(2,1)S(1)}, u32[]{:S(2)}, u32[]{:S(2)}) %collective-permute-start.80) | collective-permute-done | bytes 655392 | tf_op jit(solution)/shard_map/ppermute | solution.py:17
  710.2 28.3 %attention_backward.1 = (f32[768,768]{1,0:T(8,128)S(1)}, bf16[3072,512]{1,0:T(8,128)(2,1)S(1)}) custom-call(s32[1]{0:T(128)} %bitcast.info_ref, bf16[768,768]{1,0:T(8,128)(2,1)S(1)} %copy-done.12, bf16[3072,512]{1,0:T(8,128)(2,1)S(1)} %copy-done.8, bf16[768,768]{1,0:T(8,128)(2,1)S(1)} %multiply_convert_fusion.3.do_ref), custom_call_target="tpu_custom_call" | custom-call | flops 13589544960 | bytes 11010048 | tf_op jit(solution)/shard_map/attention_backward/pallas_call | solution.py:225
  788.3 9.5 collective-permute-done.90
  813.6 12.1 %collective-permute-done.95 = bf16[768,128]{1,0:T(8,128)(2,1)S(1)} collective-permute-done((bf16[768,128]{1,0:T(8,128)(2,1)}, bf16[768,128]{1,0:T(8,128)(2,1)S(1)}, u32[]{:S(2)}, u32[]{:S(2)}) %collective-permute-start.95) | collective-permute-done | bytes 196640 | tf_op jit(solution)/shard_map/ppermute | solution.py:28
  843.7 13.4 %collective-permute-done.100 = bf16[160,1024]{1,0:T(8,128)(2,1)S(1)} collective-permute-done((bf16[160,1024]{1,0:T(8,128)(2,1)S(1)}, bf16[160,1024]{1,0:T(8,128)(2,1)S(1)}, u32[]{:S(2)}, u32[]{:S(2)}) %collective-permute-start.100) | collective-permute-done | bytes 327712 | tf_op jit(solution)/shard_map/ppermute | solution.py:17
  897.5 8.0 collective-permute-done.104
  938.7 7.8 collective-permute-done.110
  (793 shorter events, 535.4 us)
Async XLA Ops:
  134.6 47.1 %collective-permute-start.26 = (bf16[4,320,768]{2,1,0:T(8,128)(2,1)}, bf16[4,320,768]{2,1,0:T(8,128)(2,1)}, u32[]{:S(2)}, u32[]{:S(2)}) collective-permute-start(bf16[4,320,768]{2,1,0:T(8,128)(2,1)} %pad_maximum_fusion.5), channel_id=1, source_target_pairs={{0,16},{16,0},{1,17},{17,1},{2,18},{18,2},{3,19},{19,3},{4,20},{20... | collective-permute-start | bytes 5898248 | tf_op jit(solution)/shard_map/ppermute | solution.py:22
  150.8 30.9 %collective-permute-start.25 = (bf16[3072,128]{1,0:T(8,128)(2,1)}, bf16[3072,128]{1,0:T(8,128)(2,1)}, u32[]{:S(2)}, u32[]{:S(2)}) collective-permute-start(bf16[3072,128]{1,0:T(8,128)(2,1)} %pad_maximum_fusion.34), channel_id=1, source_target_pairs={{0,2},{1,3},{2,0},{3,1},{4,6},{5,7},{6,4},{7,5},{8,10},{9,11},{10,... | collective-permute-start | bytes 2359304 | tf_op jit(solution)/shard_map/ppermute | solution.py:17
  153.2 25.6 %collective-permute-start.23 = (bf16[320,1024]{1,0:T(8,128)(2,1)}, bf16[320,1024]{1,0:T(8,128)(2,1)}, u32[]{:S(2)}, u32[]{:S(2)}) collective-permute-start(bf16[320,1024]{1,0:T(8,128)(2,1)} %get-tuple-element.1675), channel_id=1, source_target_pairs={{0,4},{4,0},{8,12},{12,8},{1,5},{5,1},{9,13},{13,9},{2,6},{6,2},{1... | collective-permute-start | bytes 1966088 | tf_op jit(solution)/shard_map/ppermute | solution.py:17
  204.2 44.6 %collective-permute-start.29 = (bf16[480,1024]{1,0:T(8,128)(2,1)}, bf16[480,1024]{1,0:T(8,128)(2,1)}, u32[]{:S(2)}, u32[]{:S(2)}) collective-permute-start(bf16[480,1024]{1,0:T(8,128)(2,1)} %pad_maximum_fusion.27), channel_id=1, source_target_pairs={{0,8},{4,12},{8,0},{12,4},{1,9},{5,13},{9,1},{13,5},{2,10},{6,14},... | collective-permute-start | bytes 2949128 | tf_op jit(solution)/shard_map/ppermute | solution.py:17
  206.6 42.2 %collective-permute-start.30 = (bf16[2,320,1024]{2,1,0:T(8,128)(2,1)S(1)}, bf16[2,320,1024]{2,1,0:T(8,128)(2,1)S(1)}, u32[]{:S(2)}, u32[]{:S(2)}) collective-permute-start(bf16[2,320,1024]{2,1,0:T(8,128)(2,1)S(1)} %pad_maximum_fusion.13), channel_id=1, source_target_pairs={{0,16},{16,0},{1,17},{17,1},{2,18},{18,2},{3,19},{19,3},{4,20},{20... | collective-permute-start | bytes 3932168 | tf_op jit(solution)/shard_map/ppermute | solution.py:22
  258.7 34.2 %collective-permute-start.33 = (bf16[2,320,1024]{2,1,0:T(8,128)(2,1)}, bf16[2,320,1024]{2,1,0:T(8,128)(2,1)}, u32[]{:S(2)}, u32[]{:S(2)}) collective-permute-start(bf16[2,320,1024]{2,1,0:T(8,128)(2,1)} %bitcast.50), channel_id=1, source_target_pairs={{0,16},{16,0},{1,17},{17,1},{2,18},{18,2},{3,19},{19,3},{4,20},{20... | collective-permute-start | bytes 3932168 | tf_op jit(solution)/shard_map/ppermute | solution.py:22
  260.9 32.0 %collective-permute-start.34 = (bf16[192,2560]{1,0:T(8,128)(2,1)}, bf16[192,2560]{1,0:T(8,128)(2,1)}, u32[]{:S(2)}, u32[]{:S(2)}) collective-permute-start(bf16[192,2560]{1,0:T(8,128)(2,1)} %fusion.42), channel_id=1, source_target_pairs={{0,2},{1,3},{2,0},{3,1},{4,6},{5,7},{6,4},{7,5},{8,10},{9,11},{10,... | collective-permute-start | bytes 2949128 | tf_op jit(solution)/shard_map/ppermute | solution.py:17
  261.2 31.7 %collective-permute-start.32 = (bf16[320,1024]{1,0:T(8,128)(2,1)}, bf16[320,1024]{1,0:T(8,128)(2,1)}, u32[]{:S(2)}, u32[]{:S(2)}) collective-permute-start(bf16[320,1024]{1,0:T(8,128)(2,1)} %slice_bitcast_fusion.10), channel_id=1, source_target_pairs={{0,8},{4,12},{8,0},{12,4},{1,9},{5,13},{9,1},{13,5},{2,10},{6,14},... | collective-permute-start | bytes 1966088 | tf_op jit(solution)/shard_map/ppermute | solution.py:17
  297.8 31.1 %collective-permute-start.36 = (bf16[2,320,1024]{2,1,0:T(8,128)(2,1)S(1)}, bf16[2,320,1024]{2,1,0:T(8,128)(2,1)}, u32[]{:S(2)}, u32[]{:S(2)}) collective-permute-start(bf16[2,320,1024]{2,1,0:T(8,128)(2,1)S(1)} %pad_maximum_fusion.14), channel_id=1, source_target_pairs={{0,16},{16,0},{1,17},{17,1},{2,18},{18,2},{3,19},{19,3},{4,20},{20... | collective-permute-start | bytes 3932168 | tf_op jit(solution)/shard_map/ppermute | solution.py:22
  298.0 30.8 %collective-permute-start.39 = (bf16[192,2560]{1,0:T(8,128)(2,1)}, bf16[192,2560]{1,0:T(8,128)(2,1)}, u32[]{:S(2)}, u32[]{:S(2)}) collective-permute-start(bf16[192,2560]{1,0:T(8,128)(2,1)} %multiply_convert_fusion.4), channel_id=1, source_target_pairs={{0,4},{4,0},{8,12},{12,8},{1,5},{5,1},{9,13},{13,9},{2,6},{6,2},{1... | collective-permute-start | bytes 2949128 | tf_op jit(solution)/shard_map/ppermute | solution.py:17
  298.0 30.8 %collective-permute-start.38 = (bf16[192,2560]{1,0:T(8,128)(2,1)}, bf16[192,2560]{1,0:T(8,128)(2,1)}, u32[]{:S(2)}, u32[]{:S(2)}) collective-permute-start(bf16[192,2560]{1,0:T(8,128)(2,1)} %multiply_convert_fusion.4), channel_id=1, source_target_pairs={{0,2},{1,3},{2,0},{3,1},{4,6},{5,7},{6,4},{7,5},{8,10},{9,11},{10,... | collective-permute-start | bytes 2949128 | tf_op jit(solution)/shard_map/ppermute | solution.py:17
  299.6 29.2 %collective-permute-start.35 = (bf16[192,2560]{1,0:T(8,128)(2,1)}, bf16[192,2560]{1,0:T(8,128)(2,1)}, u32[]{:S(2)}, u32[]{:S(2)}) collective-permute-start(bf16[192,2560]{1,0:T(8,128)(2,1)} %multiply_convert_fusion.4), channel_id=1, source_target_pairs={{0,1},{1,0},{2,3},{3,2},{4,5},{5,4},{6,7},{7,6},{8,9},{9,8},{10,11... | collective-permute-start | bytes 2949128 | tf_op jit(solution)/shard_map/ppermute | solution.py:17
  299.6 27.0 %collective-permute-start.37 = (bf16[160,1024]{1,0:T(8,128)(2,1)}, bf16[160,1024]{1,0:T(8,128)(2,1)S(1)}, u32[]{:S(2)}, u32[]{:S(2)}) collective-permute-start(bf16[160,1024]{1,0:T(8,128)(2,1)} %get-tuple-element.1826), channel_id=1, source_target_pairs={{0,8},{4,12},{8,0},{12,4},{1,9},{5,13},{9,1},{13,5},{2,10},{6,14},... | collective-permute-start | bytes 983048 | tf_op jit(solution)/shard_map/ppermute | solution.py:17
  564.4 33.9 %collective-permute-start.66 = (bf16[320,1024]{1,0:T(8,128)(2,1)}, bf16[320,1024]{1,0:T(8,128)(2,1)}, u32[]{:S(2)}, u32[]{:S(2)}) collective-permute-start(bf16[320,1024]{1,0:T(8,128)(2,1)} %add_convert_fusion.15), channel_id=1, source_target_pairs={{0,8},{4,12},{8,0},{12,4},{1,9},{5,13},{9,1},{13,5},{2,10},{6,14},... | collective-permute-start | bytes 1966088 | tf_op jit(solution)/shard_map/ppermute | solution.py:17
  565.5 32.9 %collective-permute-start.67 = (bf16[320,1024]{1,0:T(8,128)(2,1)}, bf16[320,1024]{1,0:T(8,128)(2,1)}, u32[]{:S(2)}, u32[]{:S(2)}) collective-permute-start(bf16[320,1024]{1,0:T(8,128)(2,1)} %get-tuple-element.2321), channel_id=1, source_target_pairs={{0,16},{16,0},{1,17},{17,1},{2,18},{18,2},{3,19},{19,3},{4,20},{20... | collective-permute-start | bytes 1966088 | tf_op jit(solution)/shard_map/ppermute | solution.py:22
  567.2 31.2 %collective-permute-start.68 = (bf16[320,1024]{1,0:T(8,128)(2,1)}, bf16[320,1024]{1,0:T(8,128)(2,1)}, u32[]{:S(2)}, u32[]{:S(2)}) collective-permute-start(bf16[320,1024]{1,0:T(8,128)(2,1)} %get-tuple-element.2323), channel_id=1, source_target_pairs={{0,16},{16,0},{1,17},{17,1},{2,18},{18,2},{3,19},{19,3},{4,20},{20... | collective-permute-start | bytes 1966088 | tf_op jit(solution)/shard_map/ppermute | solution.py:22
  630.0 28.7 %collective-permute-start.77 = (bf16[320,1024]{1,0:T(8,128)(2,1)S(1)}, bf16[320,1024]{1,0:T(8,128)(2,1)S(1)}, u32[]{:S(2)}, u32[]{:S(2)}) collective-permute-start(bf16[320,1024]{1,0:T(8,128)(2,1)S(1)} %copy-done.75), channel_id=1, source_target_pairs={{0,16},{16,0},{1,17},{17,1},{2,18},{18,2},{3,19},{19,3},{4,20},{20... | collective-permute-start | bytes 1966088 | tf_op jit(solution)/shard_map/ppermute | solution.py:22
  631.6 27.0 %collective-permute-start.78 = (bf16[192,2560]{1,0:T(8,128)(2,1)S(1)}, bf16[192,2560]{1,0:T(8,128)(2,1)S(1)}, u32[]{:S(2)}, u32[]{:S(2)}) collective-permute-start(bf16[192,2560]{1,0:T(8,128)(2,1)S(1)} %pad_maximum_fusion.32), channel_id=1, source_target_pairs={{0,2},{1,3},{2,0},{3,1},{4,6},{5,7},{6,4},{7,5},{8,10},{9,11},{10,... | collective-permute-start | bytes 2949128 | tf_op jit(solution)/shard_map/ppermute | solution.py:17
  632.3 26.4 %collective-permute-start.79 = (bf16[192,2560]{1,0:T(8,128)(2,1)S(1)}, bf16[192,2560]{1,0:T(8,128)(2,1)S(1)}, u32[]{:S(2)}, u32[]{:S(2)}) collective-permute-start(bf16[192,2560]{1,0:T(8,128)(2,1)S(1)} %pad_maximum_fusion.33), channel_id=1, source_target_pairs={{0,4},{4,0},{8,12},{12,8},{1,5},{5,1},{9,13},{13,9},{2,6},{6,2},{1... | collective-permute-start | bytes 2949128 | tf_op jit(solution)/shard_map/ppermute | solution.py:17
  663.9 30.2 %collective-permute-start.82 = (bf16[192,2560]{1,0:T(8,128)(2,1)S(1)}, bf16[192,2560]{1,0:T(8,128)(2,1)}, u32[]{:S(2)}, u32[]{:S(2)}) collective-permute-start(bf16[192,2560]{1,0:T(8,128)(2,1)S(1)} %get-tuple-element.2568), channel_id=1, source_target_pairs={{0,2},{1,3},{2,0},{3,1},{4,6},{5,7},{6,4},{7,5},{8,10},{9,11},{10,... | collective-permute-start | bytes 2949128 | tf_op jit(solution)/shard_map/ppermute | solution.py:17
  665.2 28.5 %collective-permute-start.80 = (bf16[320,1024]{1,0:T(8,128)(2,1)}, bf16[320,1024]{1,0:T(8,128)(2,1)S(1)}, u32[]{:S(2)}, u32[]{:S(2)}) collective-permute-start(bf16[320,1024]{1,0:T(8,128)(2,1)} %add_convert_fusion.11), channel_id=1, source_target_pairs={{0,8},{4,12},{8,0},{12,4},{1,9},{5,13},{9,1},{13,5},{2,10},{6,14},... | collective-permute-start | bytes 1966088 | tf_op jit(solution)/shard_map/ppermute | solution.py:17
  666.0 27.7 %collective-permute-start.81 = (bf16[320,1024]{1,0:T(8,128)(2,1)}, bf16[320,1024]{1,0:T(8,128)(2,1)S(1)}, u32[]{:S(2)}, u32[]{:S(2)}) collective-permute-start(bf16[320,1024]{1,0:T(8,128)(2,1)} %get-tuple-element.2535), channel_id=1, source_target_pairs={{0,16},{16,0},{1,17},{17,1},{2,18},{18,2},{3,19},{19,3},{4,20},{20... | collective-permute-start | bytes 1966088 | tf_op jit(solution)/shard_map/ppermute | solution.py:22
  666.4 27.7 %collective-permute-start.83 = (bf16[320,1024]{1,0:T(8,128)(2,1)}, bf16[320,1024]{1,0:T(8,128)(2,1)S(1)}, u32[]{:S(2)}, u32[]{:S(2)}) collective-permute-start(bf16[320,1024]{1,0:T(8,128)(2,1)} %get-tuple-element.2546), channel_id=1, source_target_pairs={{0,16},{16,0},{1,17},{17,1},{2,18},{18,2},{3,19},{19,3},{4,20},{20... | collective-permute-start | bytes 1966088 | tf_op jit(solution)/shard_map/ppermute | solution.py:22
  702.4 42.8 %collective-permute-start.87 = (bf16[160,1024]{1,0:T(8,128)(2,1)S(1)}, bf16[160,1024]{1,0:T(8,128)(2,1)S(1)}, u32[]{:S(2)}, u32[]{:S(2)}) collective-permute-start(bf16[160,1024]{1,0:T(8,128)(2,1)S(1)} %get-tuple-element.2644), channel_id=1, source_target_pairs={{0,8},{4,12},{8,0},{12,4},{1,9},{5,13},{9,1},{13,5},{2,10},{6,14},... | collective-permute-start | bytes 983048 | tf_op jit(solution)/shard_map/ppermute | solution.py:17
  703.8 41.5 %collective-permute-start.85 = (bf16[320,1024]{1,0:T(8,128)(2,1)S(1)}, bf16[320,1024]{1,0:T(8,128)(2,1)S(1)}, u32[]{:S(2)}, u32[]{:S(2)}) collective-permute-start(bf16[320,1024]{1,0:T(8,128)(2,1)S(1)} %copy-done.82), channel_id=1, source_target_pairs={{0,4},{4,0},{8,12},{12,8},{1,5},{5,1},{9,13},{13,9},{2,6},{6,2},{1... | collective-permute-start | bytes 1966088 | tf_op jit(solution)/shard_map/ppermute | solution.py:17
  705.4 43.2 %collective-permute-start.86 = (bf16[320,1024]{1,0:T(8,128)(2,1)S(1)}, bf16[320,1024]{1,0:T(8,128)(2,1)S(1)}, u32[]{:S(2)}, u32[]{:S(2)}) collective-permute-start(bf16[320,1024]{1,0:T(8,128)(2,1)S(1)} %copy-done.83), channel_id=1, source_target_pairs={{0,8},{4,12},{8,0},{12,4},{1,9},{5,13},{9,1},{13,5},{2,10},{6,14},... | collective-permute-start | bytes 1966088 | tf_op jit(solution)/shard_map/ppermute | solution.py:17
  706.6 44.5 %collective-permute-start.88 = (bf16[3,320,1024]{2,1,0:T(8,128)(2,1)}, bf16[3,320,1024]{2,1,0:T(8,128)(2,1)S(1)}, u32[]{:S(2)}, u32[]{:S(2)}) collective-permute-start(bf16[3,320,1024]{2,1,0:T(8,128)(2,1)} %pad_maximum_fusion.8), channel_id=1, source_target_pairs={{0,16},{16,0},{1,17},{17,1},{2,18},{18,2},{3,19},{19,3},{4,20},{20... | collective-permute-start | bytes 5898248 | tf_op jit(solution)/shard_map/ppermute | solution.py:22
  766.6 31.2 %collective-permute-start.90 = (bf16[320,1024]{1,0:T(8,128)(2,1)}, bf16[320,1024]{1,0:T(8,128)(2,1)}, u32[]{:S(2)}, u32[]{:S(2)}) collective-permute-start(bf16[320,1024]{1,0:T(8,128)(2,1)} %fusion.81), channel_id=1, source_target_pairs={{0,4},{4,0},{8,12},{12,8},{1,5},{5,1},{9,13},{13,9},{2,6},{6,2},{1... | collective-permute-start | bytes 1966088 | tf_op jit(solution)/shard_map/ppermute | solution.py:17
  767.5 32.2 %collective-permute-start.93 = (bf16[320,1024]{1,0:T(8,128)(2,1)}, bf16[320,1024]{1,0:T(8,128)(2,1)}, u32[]{:S(2)}, u32[]{:S(2)}) collective-permute-start(bf16[320,1024]{1,0:T(8,128)(2,1)} %pad_maximum_fusion.38), channel_id=1, source_target_pairs={{0,8},{4,12},{8,0},{12,4},{1,9},{5,13},{9,1},{13,5},{2,10},{6,14},... | collective-permute-start | bytes 1966088 | tf_op jit(solution)/shard_map/ppermute | solution.py:17
  768.8 30.9 %collective-permute-start.91 = (bf16[3072,128]{1,0:T(8,128)(2,1)}, bf16[3072,128]{1,0:T(8,128)(2,1)}, u32[]{:S(2)}, u32[]{:S(2)}) collective-permute-start(bf16[3072,128]{1,0:T(8,128)(2,1)} %fusion.74), channel_id=1, source_target_pairs={{0,2},{1,3},{2,0},{3,1},{4,6},{5,7},{6,4},{7,5},{8,10},{9,11},{10,... | collective-permute-start | bytes 2359304 | tf_op jit(solution)/shard_map/ppermute | solution.py:17
  769.8 29.8 %collective-permute-start.92 = (bf16[2,320,768]{2,1,0:T(8,128)(2,1)}, bf16[2,320,768]{2,1,0:T(8,128)(2,1)}, u32[]{:S(2)}, u32[]{:S(2)}) collective-permute-start(bf16[2,320,768]{2,1,0:T(8,128)(2,1)} %get-tuple-element.2737), channel_id=1, source_target_pairs={{0,16},{16,0},{1,17},{17,1},{2,18},{18,2},{3,19},{19,3},{4,20},{20... | collective-permute-start | bytes 2949128 | tf_op jit(solution)/shard_map/ppermute | solution.py:22
  830.9 26.3 %collective-permute-start.100 = (bf16[160,1024]{1,0:T(8,128)(2,1)S(1)}, bf16[160,1024]{1,0:T(8,128)(2,1)S(1)}, u32[]{:S(2)}, u32[]{:S(2)}) collective-permute-start(bf16[160,1024]{1,0:T(8,128)(2,1)S(1)} %copy-done.94), channel_id=1, source_target_pairs={{0,8},{4,12},{8,0},{12,4},{1,9},{5,13},{9,1},{13,5},{2,10},{6,14},... | collective-permute-start | bytes 983048 | tf_op jit(solution)/shard_map/ppermute | solution.py:17
  (233 other events, 2455.8 us)

commit v6 on v5

--- a/solution.py
+++ b/solution.py
@@ -405,9 +405,7 @@
 
     at.qkv = to_tp(qkv_columns)
     at.gate_mine, at.gate_sent = near_halves(gate_weight)
-    at.out = to_tp(head_columns(out_weight))
-    at.up_mine, at.up_sent = near_halves(up_weight)
-    at.down_mine, at.down_sent = near_halves(down_weight.T)
+    at.out_weight, at.up_weight, at.down_weight = out_weight, up_weight, down_weight
     at.next()
     at.qkv = flip_tp(at.qkv)
     at.gate_got = flip(at.gate_sent, "ctx", 1)
@@ -417,9 +415,12 @@
     at.next()
     at.qkv_x = [over_fsdp(at.qkv_0)]
     at.qkv_1 = ring(at.qkv_0, "ctx")
+    at.out = to_tp(head_columns(at.drop("out_weight")[0]))
     at.next()
     at.qkv_x.append(over_fsdp(at.qkv_1))
     at.qkv_2 = ring(at.qkv_1, "ctx")
+    at.up_mine, at.up_sent = near_halves(at.drop("up_weight")[0])
+    at.down_mine, at.down_sent = near_halves(at.drop("down_weight")[0].T)
     at.next()
     at.qkv_x.append(over_fsdp(at.qkv_2))
     at.qkv_3 = ring(at.qkv_2, "ctx")
@@ -544,8 +545,8 @@
         at.corner_end = flip(at.to_y, "tp", 2)
 
     def between_corners_and_sides():
-        mine, got, top, end = at.drop("mine", "got", "corner_top", "corner_end")
-        own, over_y, over_z = wide(mine) + wide(got)
+        sums, top, end = at.drop("sums", "corner_top", "corner_end")
+        own, over_y, over_z = sums
         at.over_y = low(jnp.concatenate([over_y[:middle] + wide(top), over_y[middle:]], axis=0))
         at.over_z = low(jnp.concatenate([over_z[:middle], over_z[middle:] + wide(end)], axis=0))
         at.part = own
@@ -617,7 +618,7 @@
     between_core_and_corners()
     at.next()
     sum_corners()
-    at.got = flip(at.theirs, "tp", 1)
+    at.sums = wide(at.drop("mine")[0]) + wide(flip(at.theirs, "tp", 1))
     at.next()
     between_corners_and_sides()
     at.next()
@@ -716,7 +717,7 @@
     at.down_rest = jnp.split(at.down_far[1], 2)
     at.next()
     sum_corners()
-    at.got = flip(at.theirs, "tp", 1)
+    at.sums = wide(at.drop("mine")[0]) + wide(flip(at.theirs, "tp", 1))
     at.gate_got = [around(at.gate_terms[0], "fsdp")]
     at.down_got_1 = flip(at.down_rest[0], "ctx", 2)
     at.next()

time: 984 us -> 977 us (level)
  transfers between devices with their start and end apart: 121 -> 121, of which waited for: 70 -> 67; matrix products, arithmetic and copies ran while one was open for 24% -> 25% of each run, Pallas kernels for 6% -> 6%
where the time goes in v6:
time: 977 us; the launch traced here: 966 us
  waiting for transfers between devices  400 us (41%)
  other arithmetic  140 us (14%)
  starting transfers between devices  129 us (13%)
  matrix products  126 us (13%)
  local copies, waits for them, and re-layouts  102 us (10%)
  Pallas kernels  62.3 us (6%)
    ppermute x71, waiting for transfers between devices, flip(): lax.ppermute(array, axis, [(i, i ^ bit) for i in range(lax.axis_size(axis...  269 us
    ppermute x44, waiting for transfers between devices, ring(): lax.ppermute(array, axis, [(i, (i + by) % count) for i in range(count)])  113 us
    ppermute x71, starting transfers between devices, flip(): lax.ppermute(array, axis, [(i, i ^ bit) for i in range(lax.axis_size(axis...  67.2 us
    ppermute x44, starting transfers between devices, ring(): lax.ppermute(array, axis, [(i, (i + by) % count) for i in range(count)])  48.1 us
    dot_general x5, matrix products, nt(): lax.dot_general(first, second, (((1,), (1,)), ((), ())), preferred_elemen...  45.4 us
    dot_general x5, matrix products, nn(): lax.dot_general(first, second, (((1,), (0,)), ((), ())), preferred_elemen...  43.8 us
    dot_general x6, matrix products, tn(): lax.dot_general(first, second, (((0,), (0,)), ((), ())), preferred_elemen...  37 us
    convert_element_type x26, other arithmetic, low(): return values.astype(jnp.bfloat16)  33.4 us
  transfers between devices with their start and end apart: 121, of which 67 were waited for; matrix products, arithmetic and copies ran while one was open for 25% of the time, Pallas kernels for 6%

profile of v6, /device:TPU:0, one launch (start us, length us, event | category | flops | bytes accessed | tf_op | source)
XLA Modules:
  0.0 966.0 jit_solution(7093697884155342227)
XLA Ops:
  27.5 12.0 %collective-permute-done.5.refs_1_ = bf16[320,1024]{1,0:T(8,128)(2,1)S(1)} collective-permute-done((bf16[320,1024]{1,0:T(8,128)(2,1)S(1)}, bf16[320,1024]{1,0:T(8,128)(2,1)S(1)}, u32[]{:S(2)}, u32[]{:S(2)}) %collective-permute-start.5) | collective-permute-done | bytes 655392 | tf_op jit(solution)/shard_map/ppermute | solution.py:22
  45.2 11.7 %collective-permute-done.7.refs_3_ = bf16[320,1024]{1,0:T(8,128)(2,1)S(1)} collective-permute-done((bf16[320,1024]{1,0:T(8,128)(2,1)S(1)}, bf16[320,1024]{1,0:T(8,128)(2,1)S(1)}, u32[]{:S(2)}, u32[]{:S(2)}) %collective-permute-start.7) | collective-permute-done | bytes 655392 | tf_op jit(solution)/shard_map/ppermute | solution.py:22
  158.6 16.2 %collective-permute-done.23 = bf16[320,1024]{1,0:T(8,128)(2,1)} collective-permute-done((bf16[320,1024]{1,0:T(8,128)(2,1)}, bf16[320,1024]{1,0:T(8,128)(2,1)}, u32[]{:S(2)}, u32[]{:S(2)}) %collective-permute-start.23) | collective-permute-done | bytes 655392 | tf_op jit(solution)/shard_map/ppermute | solution.py:17
  207.6 18.3 %attention_forward.1 = bf16[768,768]{1,0:T(8,128)(2,1)S(1)} custom-call(s32[4]{0:T(128)S(1)} %pad_add_fusion.info_ref, bf16[768,768]{1,0:T(8,128)(2,1)S(1)} %copy-done.11, bf16[3072,512]{1,0:T(8,128)(2,1)S(1)} %copy-done.7), custom_call_target="tpu_custom_call" | custom-call | flops 5435817984 | bytes 5505024 | tf_op jit(solution)/shard_map/attention_forward/pallas_call | solution.py:163
  231.7 13.1 %collective-permute-done.29 = bf16[480,1024]{1,0:T(8,128)(2,1)} collective-permute-done((bf16[480,1024]{1,0:T(8,128)(2,1)}, bf16[480,1024]{1,0:T(8,128)(2,1)}, u32[]{:S(2)}, u32[]{:S(2)}) %collective-permute-start.29) | collective-permute-done | bytes 983072 | tf_op jit(solution)/shard_map/ppermute | solution.py:17
  257.5 31.4 %collective-permute-done.32 = bf16[320,1024]{1,0:T(8,128)(2,1)} collective-permute-done((bf16[320,1024]{1,0:T(8,128)(2,1)}, bf16[320,1024]{1,0:T(8,128)(2,1)}, u32[]{:S(2)}, u32[]{:S(2)}) %collective-permute-start.32) | collective-permute-done | bytes 655392 | tf_op jit(solution)/shard_map/ppermute | solution.py:17
  304.3 18.4 %collective-permute-done.37 = bf16[160,1024]{1,0:T(8,128)(2,1)S(1)} collective-permute-done((bf16[160,1024]{1,0:T(8,128)(2,1)}, bf16[160,1024]{1,0:T(8,128)(2,1)S(1)}, u32[]{:S(2)}, u32[]{:S(2)}) %collective-permute-start.37) | collective-permute-done | bytes 327712 | tf_op jit(solution)/shard_map/ppermute | solution.py:17
  334.1 15.8 %collective-permute-done.43 = bf16[160,1024]{1,0:T(8,128)(2,1)S(1)} collective-permute-done((bf16[160,1024]{1,0:T(8,128)(2,1)S(1)}, bf16[160,1024]{1,0:T(8,128)(2,1)S(1)}, u32[]{:S(2)}, u32[]{:S(2)}) %collective-permute-start.43) | collective-permute-done | bytes 327712 | tf_op jit(solution)/shard_map/ppermute | solution.py:17
  359.4 8.3 fusion.106
  378.7 12.6 %fusion.107 = f32[1536,1024]{1,0:T(8,128)S(1)} fusion(bf16[1536,2560]{1,0:T(8,128)(2,1)} %copy-done.111, bf16[2560,1024]{1,0:T(8,128)(2,1)S(1)} %bitcast.426), kind=kOutput, calls=%fused_computation.473 | convolution fusion | flops 8053063680 | bytes 19398656 | tf_op jit(solution)/shard_map/dot_general | solution.py:110
  395.5 10.9 %collective-permute-done.50 = bf16[320,1024]{1,0:T(8,128)(2,1)S(1)} collective-permute-done((bf16[320,1024]{1,0:T(8,128)(2,1)S(1)}, bf16[320,1024]{1,0:T(8,128)(2,1)S(1)}, u32[]{:S(2)}, u32[]{:S(2)}) %collective-permute-start.50) | collective-permute-done | bytes 655392 | tf_op jit(solution)/shard_map/ppermute | solution.py:22
  409.0 8.8 convolution_convert_fusion
  432.0 8.1 collective-permute-done.52
  451.6 12.8 %collective-permute-done.55 = bf16[192,2560]{1,0:T(8,128)(2,1)S(1)} collective-permute-done((bf16[192,2560]{1,0:T(8,128)(2,1)S(1)}, bf16[192,2560]{1,0:T(8,128)(2,1)S(1)}, u32[]{:S(2)}, u32[]{:S(2)}) %collective-permute-start.55) | collective-permute-done | bytes 983072 | tf_op jit(solution)/shard_map/ppermute | solution.py:17
  471.8 16.1 %collective-permute-done.59 = bf16[192,2560]{1,0:T(8,128)(2,1)S(1)} collective-permute-done((bf16[192,2560]{1,0:T(8,128)(2,1)S(1)}, bf16[192,2560]{1,0:T(8,128)(2,1)S(1)}, u32[]{:S(2)}, u32[]{:S(2)}) %collective-permute-start.59) | collective-permute-done | bytes 983072 | tf_op jit(solution)/shard_map/ppermute | solution.py:17
  491.7 11.6 %collective-permute-done.61 = bf16[96,2560]{1,0:T(8,128)(2,1)S(1)} collective-permute-done((bf16[96,2560]{1,0:T(8,128)(2,1)S(1)}, bf16[96,2560]{1,0:T(8,128)(2,1)S(1)}, u32[]{:S(2)}, u32[]{:S(2)}) %collective-permute-start.61) | collective-permute-done | bytes 491552 | tf_op jit(solution)/shard_map/ppermute | solution.py:17
  513.0 8.9 convolution_convert_fusion.3
  525.7 12.2 %multiply_convert_fusion = (bf16[1536,1024]{1,0:T(8,128)(2,1)}, bf16[1536,1024]{1,0:T(8,128)(2,1)S(1)}) fusion(bf16[1536,1024]{1,0:T(8,128)(2,1)S(1)} %copy-done.50, bf16[1536,1024]{1,0:T(8,128)(2,1)S(1)} %copy-done.49, bf16[1536,2560]{1,0:T(8,128)(2,1)} %copy-done.112, bf16[2560,1024]{1,0:T(8,128)(2,1)S(1)} %bitcast.433), kind=kOutput, calls=%fused_computation.33 | convolution fusion | flops 8062500864 | bytes 25690112 | tf_op jit(solution)/shard_map/dot_general | solution.py:110
  542.3 10.9 %convolution_convert_fusion.2 = bf16[2560,1024]{1,0:T(8,128)(2,1)S(1)} fusion(bf16[1536,2560]{1,0:T(8,128)(2,1)} %copy-done.111, bf16[1536,1024]{1,0:T(8,128)(2,1)S(1)} %get-tuple-element.2279), kind=kOutput, calls=%fused_computation.39 | convolution fusion | flops 8055685120 | bytes 16252928 | tf_op jit(solution)/shard_map/dot_general | solution.py:122
  561.7 11.0 %fusion.108 = f32[1536,2560]{1,0:T(8,128)} fusion(bf16[1536,1024]{1,0:T(8,128)(2,1)S(1)} %copy-done.125, bf16[2560,1024]{1,0:T(8,128)(2,1)S(1)} %bitcast.429), kind=kOutput, calls=%fused_computation.474 | convolution fusion | flops 8053063680 | bytes 24117248 | tf_op jit(solution)/shard_map/dot_general | solution.py:116
  572.8 15.0 %add_convert_fusion = bf16[1536,2560]{1,0:T(8,128)(2,1)} fusion(f32[1536,2560]{1,0:T(8,128)} %fusion.108, bf16[1536,1024]{1,0:T(8,128)(2,1)} %copy-done.127, bf16[2560,1024]{1,0:T(8,128)(2,1)S(1)} %bitcast.425), kind=kOutput, calls=%fused_computation | convolution fusion | flops 8060928000 | bytes 31981568 | tf_op jit(solution)/shard_map/dot_general | solution.py:116
  602.2 11.6 %collective-permute-done.72 = bf16[160,1024]{1,0:T(8,128)(2,1)S(1)} collective-permute-done((bf16[160,1024]{1,0:T(8,128)(2,1)S(1)}, bf16[160,1024]{1,0:T(8,128)(2,1)S(1)}, u32[]{:S(2)}, u32[]{:S(2)}) %collective-permute-start.72) | collective-permute-done | bytes 327712 | tf_op jit(solution)/shard_map/ppermute | solution.py:17
  626.0 9.2 convolution_convert_fusion.1
  641.2 8.6 collective-permute-done.77
  664.7 21.3 %collective-permute-done.80 = bf16[320,1024]{1,0:T(8,128)(2,1)S(1)} collective-permute-done((bf16[320,1024]{1,0:T(8,128)(2,1)}, bf16[320,1024]{1,0:T(8,128)(2,1)S(1)}, u32[]{:S(2)}, u32[]{:S(2)}) %collective-permute-start.80) | collective-permute-done | bytes 655392 | tf_op jit(solution)/shard_map/ppermute | solution.py:17
  704.1 28.3 %attention_backward.1 = (f32[768,768]{1,0:T(8,128)S(1)}, bf16[3072,512]{1,0:T(8,128)(2,1)S(1)}) custom-call(s32[1]{0:T(128)} %bitcast.info_ref, bf16[768,768]{1,0:T(8,128)(2,1)S(1)} %copy-done.12, bf16[3072,512]{1,0:T(8,128)(2,1)S(1)} %copy-done.8, bf16[768,768]{1,0:T(8,128)(2,1)S(1)} %multiply_convert_fusion.3.do_ref), custom_call_target="tpu_custom_call" | custom-call | flops 13589544960 | bytes 11010048 | tf_op jit(solution)/shard_map/attention_backward/pallas_call | solution.py:225
  781.6 8.5 collective-permute-done.90
  807.1 11.7 %collective-permute-done.95 = bf16[768,128]{1,0:T(8,128)(2,1)S(1)} collective-permute-done((bf16[768,128]{1,0:T(8,128)(2,1)}, bf16[768,128]{1,0:T(8,128)(2,1)S(1)}, u32[]{:S(2)}, u32[]{:S(2)}) %collective-permute-start.95) | collective-permute-done | bytes 196640 | tf_op jit(solution)/shard_map/ppermute | solution.py:28
  835.2 15.1 %collective-permute-done.100 = bf16[160,1024]{1,0:T(8,128)(2,1)S(1)} collective-permute-done((bf16[160,1024]{1,0:T(8,128)(2,1)S(1)}, bf16[160,1024]{1,0:T(8,128)(2,1)S(1)}, u32[]{:S(2)}, u32[]{:S(2)}) %collective-permute-start.100) | collective-permute-done | bytes 327712 | tf_op jit(solution)/shard_map/ppermute | solution.py:17
  891.9 7.8 collective-permute-done.104
  910.8 8.1 collective-permute-done.108
  931.5 7.7 collective-permute-done.110
  (795 shorter events, 537.7 us)
Async XLA Ops:
  130.6 47.1 %collective-permute-start.26 = (bf16[4,320,768]{2,1,0:T(8,128)(2,1)}, bf16[4,320,768]{2,1,0:T(8,128)(2,1)}, u32[]{:S(2)}, u32[]{:S(2)}) collective-permute-start(bf16[4,320,768]{2,1,0:T(8,128)(2,1)} %pad_maximum_fusion.5), channel_id=1, source_target_pairs={{0,16},{16,0},{1,17},{17,1},{2,18},{18,2},{3,19},{19,3},{4,20},{20... | collective-permute-start | bytes 5898248 | tf_op jit(solution)/shard_map/ppermute | solution.py:22
  146.7 30.9 %collective-permute-start.25 = (bf16[3072,128]{1,0:T(8,128)(2,1)}, bf16[3072,128]{1,0:T(8,128)(2,1)}, u32[]{:S(2)}, u32[]{:S(2)}) collective-permute-start(bf16[3072,128]{1,0:T(8,128)(2,1)} %pad_maximum_fusion.34), channel_id=1, source_target_pairs={{0,2},{1,3},{2,0},{3,1},{4,6},{5,7},{6,4},{7,5},{8,10},{9,11},{10,... | collective-permute-start | bytes 2359304 | tf_op jit(solution)/shard_map/ppermute | solution.py:17
  149.2 25.6 %collective-permute-start.23 = (bf16[320,1024]{1,0:T(8,128)(2,1)}, bf16[320,1024]{1,0:T(8,128)(2,1)}, u32[]{:S(2)}, u32[]{:S(2)}) collective-permute-start(bf16[320,1024]{1,0:T(8,128)(2,1)} %get-tuple-element.1639), channel_id=1, source_target_pairs={{0,4},{4,0},{8,12},{12,8},{1,5},{5,1},{9,13},{13,9},{2,6},{6,2},{1... | collective-permute-start | bytes 1966088 | tf_op jit(solution)/shard_map/ppermute | solution.py:17
  200.2 44.6 %collective-permute-start.29 = (bf16[480,1024]{1,0:T(8,128)(2,1)}, bf16[480,1024]{1,0:T(8,128)(2,1)}, u32[]{:S(2)}, u32[]{:S(2)}) collective-permute-start(bf16[480,1024]{1,0:T(8,128)(2,1)} %pad_maximum_fusion.27), channel_id=1, source_target_pairs={{0,8},{4,12},{8,0},{12,4},{1,9},{5,13},{9,1},{13,5},{2,10},{6,14},... | collective-permute-start | bytes 2949128 | tf_op jit(solution)/shard_map/ppermute | solution.py:17
  202.6 42.2 %collective-permute-start.30 = (bf16[2,320,1024]{2,1,0:T(8,128)(2,1)S(1)}, bf16[2,320,1024]{2,1,0:T(8,128)(2,1)S(1)}, u32[]{:S(2)}, u32[]{:S(2)}) collective-permute-start(bf16[2,320,1024]{2,1,0:T(8,128)(2,1)S(1)} %pad_maximum_fusion.13), channel_id=1, source_target_pairs={{0,16},{16,0},{1,17},{17,1},{2,18},{18,2},{3,19},{19,3},{4,20},{20... | collective-permute-start | bytes 3932168 | tf_op jit(solution)/shard_map/ppermute | solution.py:22
  254.7 34.2 %collective-permute-start.33 = (bf16[2,320,1024]{2,1,0:T(8,128)(2,1)}, bf16[2,320,1024]{2,1,0:T(8,128)(2,1)}, u32[]{:S(2)}, u32[]{:S(2)}) collective-permute-start(bf16[2,320,1024]{2,1,0:T(8,128)(2,1)} %bitcast.50), channel_id=1, source_target_pairs={{0,16},{16,0},{1,17},{17,1},{2,18},{18,2},{3,19},{19,3},{4,20},{20... | collective-permute-start | bytes 3932168 | tf_op jit(solution)/shard_map/ppermute | solution.py:22
  256.8 32.0 %collective-permute-start.34 = (bf16[192,2560]{1,0:T(8,128)(2,1)}, bf16[192,2560]{1,0:T(8,128)(2,1)}, u32[]{:S(2)}, u32[]{:S(2)}) collective-permute-start(bf16[192,2560]{1,0:T(8,128)(2,1)} %fusion.42), channel_id=1, source_target_pairs={{0,2},{1,3},{2,0},{3,1},{4,6},{5,7},{6,4},{7,5},{8,10},{9,11},{10,... | collective-permute-start | bytes 2949128 | tf_op jit(solution)/shard_map/ppermute | solution.py:17
  257.1 31.7 %collective-permute-start.32 = (bf16[320,1024]{1,0:T(8,128)(2,1)}, bf16[320,1024]{1,0:T(8,128)(2,1)}, u32[]{:S(2)}, u32[]{:S(2)}) collective-permute-start(bf16[320,1024]{1,0:T(8,128)(2,1)} %slice_bitcast_fusion.6), channel_id=1, source_target_pairs={{0,8},{4,12},{8,0},{12,4},{1,9},{5,13},{9,1},{13,5},{2,10},{6,14},... | collective-permute-start | bytes 1966088 | tf_op jit(solution)/shard_map/ppermute | solution.py:17
  293.8 31.1 %collective-permute-start.36 = (bf16[2,320,1024]{2,1,0:T(8,128)(2,1)S(1)}, bf16[2,320,1024]{2,1,0:T(8,128)(2,1)}, u32[]{:S(2)}, u32[]{:S(2)}) collective-permute-start(bf16[2,320,1024]{2,1,0:T(8,128)(2,1)S(1)} %pad_maximum_fusion.14), channel_id=1, source_target_pairs={{0,16},{16,0},{1,17},{17,1},{2,18},{18,2},{3,19},{19,3},{4,20},{20... | collective-permute-start | bytes 3932168 | tf_op jit(solution)/shard_map/ppermute | solution.py:22
  294.0 30.8 %collective-permute-start.39 = (bf16[192,2560]{1,0:T(8,128)(2,1)}, bf16[192,2560]{1,0:T(8,128)(2,1)}, u32[]{:S(2)}, u32[]{:S(2)}) collective-permute-start(bf16[192,2560]{1,0:T(8,128)(2,1)} %multiply_convert_fusion.4), channel_id=1, source_target_pairs={{0,4},{4,0},{8,12},{12,8},{1,5},{5,1},{9,13},{13,9},{2,6},{6,2},{1... | collective-permute-start | bytes 2949128 | tf_op jit(solution)/shard_map/ppermute | solution.py:17
  294.1 30.8 %collective-permute-start.38 = (bf16[192,2560]{1,0:T(8,128)(2,1)}, bf16[192,2560]{1,0:T(8,128)(2,1)}, u32[]{:S(2)}, u32[]{:S(2)}) collective-permute-start(bf16[192,2560]{1,0:T(8,128)(2,1)} %multiply_convert_fusion.4), channel_id=1, source_target_pairs={{0,2},{1,3},{2,0},{3,1},{4,6},{5,7},{6,4},{7,5},{8,10},{9,11},{10,... | collective-permute-start | bytes 2949128 | tf_op jit(solution)/shard_map/ppermute | solution.py:17
  295.6 29.3 %collective-permute-start.35 = (bf16[192,2560]{1,0:T(8,128)(2,1)}, bf16[192,2560]{1,0:T(8,128)(2,1)}, u32[]{:S(2)}, u32[]{:S(2)}) collective-permute-start(bf16[192,2560]{1,0:T(8,128)(2,1)} %multiply_convert_fusion.4), channel_id=1, source_target_pairs={{0,1},{1,0},{2,3},{3,2},{4,5},{5,4},{6,7},{7,6},{8,9},{9,8},{10,11... | collective-permute-start | bytes 2949128 | tf_op jit(solution)/shard_map/ppermute | solution.py:17
  295.6 27.1 %collective-permute-start.37 = (bf16[160,1024]{1,0:T(8,128)(2,1)}, bf16[160,1024]{1,0:T(8,128)(2,1)S(1)}, u32[]{:S(2)}, u32[]{:S(2)}) collective-permute-start(bf16[160,1024]{1,0:T(8,128)(2,1)} %get-tuple-element.1790), channel_id=1, source_target_pairs={{0,8},{4,12},{8,0},{12,4},{1,9},{5,13},{9,1},{13,5},{2,10},{6,14},... | collective-permute-start | bytes 983048 | tf_op jit(solution)/shard_map/ppermute | solution.py:17
  558.8 33.8 %collective-permute-start.66 = (bf16[320,1024]{1,0:T(8,128)(2,1)}, bf16[320,1024]{1,0:T(8,128)(2,1)}, u32[]{:S(2)}, u32[]{:S(2)}) collective-permute-start(bf16[320,1024]{1,0:T(8,128)(2,1)} %add_convert_fusion.15), channel_id=1, source_target_pairs={{0,8},{4,12},{8,0},{12,4},{1,9},{5,13},{9,1},{13,5},{2,10},{6,14},... | collective-permute-start | bytes 1966088 | tf_op jit(solution)/shard_map/ppermute | solution.py:17
  559.7 32.9 %collective-permute-start.67 = (bf16[320,1024]{1,0:T(8,128)(2,1)}, bf16[320,1024]{1,0:T(8,128)(2,1)}, u32[]{:S(2)}, u32[]{:S(2)}) collective-permute-start(bf16[320,1024]{1,0:T(8,128)(2,1)} %get-tuple-element.2284), channel_id=1, source_target_pairs={{0,16},{16,0},{1,17},{17,1},{2,18},{18,2},{3,19},{19,3},{4,20},{20... | collective-permute-start | bytes 1966088 | tf_op jit(solution)/shard_map/ppermute | solution.py:22
  561.3 31.2 %collective-permute-start.68 = (bf16[320,1024]{1,0:T(8,128)(2,1)}, bf16[320,1024]{1,0:T(8,128)(2,1)}, u32[]{:S(2)}, u32[]{:S(2)}) collective-permute-start(bf16[320,1024]{1,0:T(8,128)(2,1)} %get-tuple-element.2286), channel_id=1, source_target_pairs={{0,16},{16,0},{1,17},{17,1},{2,18},{18,2},{3,19},{19,3},{4,20},{20... | collective-permute-start | bytes 1966088 | tf_op jit(solution)/shard_map/ppermute | solution.py:22
  621.5 28.2 %collective-permute-start.77 = (bf16[320,1024]{1,0:T(8,128)(2,1)S(1)}, bf16[320,1024]{1,0:T(8,128)(2,1)S(1)}, u32[]{:S(2)}, u32[]{:S(2)}) collective-permute-start(bf16[320,1024]{1,0:T(8,128)(2,1)S(1)} %copy-done.75), channel_id=1, source_target_pairs={{0,16},{16,0},{1,17},{17,1},{2,18},{18,2},{3,19},{19,3},{4,20},{20... | collective-permute-start | bytes 1966088 | tf_op jit(solution)/shard_map/ppermute | solution.py:22
  621.8 27.9 %collective-permute-start.78 = (bf16[192,2560]{1,0:T(8,128)(2,1)S(1)}, bf16[192,2560]{1,0:T(8,128)(2,1)S(1)}, u32[]{:S(2)}, u32[]{:S(2)}) collective-permute-start(bf16[192,2560]{1,0:T(8,128)(2,1)S(1)} %pad_maximum_fusion.32), channel_id=1, source_target_pairs={{0,2},{1,3},{2,0},{3,1},{4,6},{5,7},{6,4},{7,5},{8,10},{9,11},{10,... | collective-permute-start | bytes 2949128 | tf_op jit(solution)/shard_map/ppermute | solution.py:17
  623.0 27.9 %collective-permute-start.79 = (bf16[192,2560]{1,0:T(8,128)(2,1)S(1)}, bf16[192,2560]{1,0:T(8,128)(2,1)S(1)}, u32[]{:S(2)}, u32[]{:S(2)}) collective-permute-start(bf16[192,2560]{1,0:T(8,128)(2,1)S(1)} %pad_maximum_fusion.33), channel_id=1, source_target_pairs={{0,4},{4,0},{8,12},{12,8},{1,5},{5,1},{9,13},{13,9},{2,6},{6,2},{1... | collective-permute-start | bytes 2949128 | tf_op jit(solution)/shard_map/ppermute | solution.py:17
  656.1 29.9 %collective-permute-start.82 = (bf16[192,2560]{1,0:T(8,128)(2,1)S(1)}, bf16[192,2560]{1,0:T(8,128)(2,1)}, u32[]{:S(2)}, u32[]{:S(2)}) collective-permute-start(bf16[192,2560]{1,0:T(8,128)(2,1)S(1)} %get-tuple-element.2530), channel_id=1, source_target_pairs={{0,2},{1,3},{2,0},{3,1},{4,6},{5,7},{6,4},{7,5},{8,10},{9,11},{10,... | collective-permute-start | bytes 2949128 | tf_op jit(solution)/shard_map/ppermute | solution.py:17
  657.4 28.6 %collective-permute-start.80 = (bf16[320,1024]{1,0:T(8,128)(2,1)}, bf16[320,1024]{1,0:T(8,128)(2,1)S(1)}, u32[]{:S(2)}, u32[]{:S(2)}) collective-permute-start(bf16[320,1024]{1,0:T(8,128)(2,1)} %add_convert_fusion.11), channel_id=1, source_target_pairs={{0,8},{4,12},{8,0},{12,4},{1,9},{5,13},{9,1},{13,5},{2,10},{6,14},... | collective-permute-start | bytes 1966088 | tf_op jit(solution)/shard_map/ppermute | solution.py:17
  657.9 28.1 %collective-permute-start.81 = (bf16[320,1024]{1,0:T(8,128)(2,1)}, bf16[320,1024]{1,0:T(8,128)(2,1)S(1)}, u32[]{:S(2)}, u32[]{:S(2)}) collective-permute-start(bf16[320,1024]{1,0:T(8,128)(2,1)} %get-tuple-element.2497), channel_id=1, source_target_pairs={{0,16},{16,0},{1,17},{17,1},{2,18},{18,2},{3,19},{19,3},{4,20},{20... | collective-permute-start | bytes 1966088 | tf_op jit(solution)/shard_map/ppermute | solution.py:22
  659.6 26.4 %collective-permute-start.83 = (bf16[320,1024]{1,0:T(8,128)(2,1)}, bf16[320,1024]{1,0:T(8,128)(2,1)S(1)}, u32[]{:S(2)}, u32[]{:S(2)}) collective-permute-start(bf16[320,1024]{1,0:T(8,128)(2,1)} %get-tuple-element.2508), channel_id=1, source_target_pairs={{0,16},{16,0},{1,17},{17,1},{2,18},{18,2},{3,19},{19,3},{4,20},{20... | collective-permute-start | bytes 1966088 | tf_op jit(solution)/shard_map/ppermute | solution.py:22
  694.7 44.4 %collective-permute-start.87 = (bf16[160,1024]{1,0:T(8,128)(2,1)S(1)}, bf16[160,1024]{1,0:T(8,128)(2,1)S(1)}, u32[]{:S(2)}, u32[]{:S(2)}) collective-permute-start(bf16[160,1024]{1,0:T(8,128)(2,1)S(1)} %get-tuple-element.2606), channel_id=1, source_target_pairs={{0,8},{4,12},{8,0},{12,4},{1,9},{5,13},{9,1},{13,5},{2,10},{6,14},... | collective-permute-start | bytes 983048 | tf_op jit(solution)/shard_map/ppermute | solution.py:17
  696.4 42.7 %collective-permute-start.85 = (bf16[320,1024]{1,0:T(8,128)(2,1)S(1)}, bf16[320,1024]{1,0:T(8,128)(2,1)S(1)}, u32[]{:S(2)}, u32[]{:S(2)}) collective-permute-start(bf16[320,1024]{1,0:T(8,128)(2,1)S(1)} %copy-done.82), channel_id=1, source_target_pairs={{0,4},{4,0},{8,12},{12,8},{1,5},{5,1},{9,13},{13,9},{2,6},{6,2},{1... | collective-permute-start | bytes 1966088 | tf_op jit(solution)/shard_map/ppermute | solution.py:17
  697.1 43.7 %collective-permute-start.86 = (bf16[320,1024]{1,0:T(8,128)(2,1)S(1)}, bf16[320,1024]{1,0:T(8,128)(2,1)S(1)}, u32[]{:S(2)}, u32[]{:S(2)}) collective-permute-start(bf16[320,1024]{1,0:T(8,128)(2,1)S(1)} %copy-done.83), channel_id=1, source_target_pairs={{0,8},{4,12},{8,0},{12,4},{1,9},{5,13},{9,1},{13,5},{2,10},{6,14},... | collective-permute-start | bytes 1966088 | tf_op jit(solution)/shard_map/ppermute | solution.py:17
  699.2 44.5 %collective-permute-start.88 = (bf16[3,320,1024]{2,1,0:T(8,128)(2,1)}, bf16[3,320,1024]{2,1,0:T(8,128)(2,1)S(1)}, u32[]{:S(2)}, u32[]{:S(2)}) collective-permute-start(bf16[3,320,1024]{2,1,0:T(8,128)(2,1)} %pad_maximum_fusion.8), channel_id=1, source_target_pairs={{0,16},{16,0},{1,17},{17,1},{2,18},{18,2},{3,19},{19,3},{4,20},{20... | collective-permute-start | bytes 5898248 | tf_op jit(solution)/shard_map/ppermute | solution.py:22
  759.2 30.8 %collective-permute-start.90 = (bf16[320,1024]{1,0:T(8,128)(2,1)}, bf16[320,1024]{1,0:T(8,128)(2,1)}, u32[]{:S(2)}, u32[]{:S(2)}) collective-permute-start(bf16[320,1024]{1,0:T(8,128)(2,1)} %fusion.77), channel_id=1, source_target_pairs={{0,4},{4,0},{8,12},{12,8},{1,5},{5,1},{9,13},{13,9},{2,6},{6,2},{1... | collective-permute-start | bytes 1966088 | tf_op jit(solution)/shard_map/ppermute | solution.py:17
  759.7 32.2 %collective-permute-start.93 = (bf16[320,1024]{1,0:T(8,128)(2,1)}, bf16[320,1024]{1,0:T(8,128)(2,1)}, u32[]{:S(2)}, u32[]{:S(2)}) collective-permute-start(bf16[320,1024]{1,0:T(8,128)(2,1)} %pad_maximum_fusion.38), channel_id=1, source_target_pairs={{0,8},{4,12},{8,0},{12,4},{1,9},{5,13},{9,1},{13,5},{2,10},{6,14},... | collective-permute-start | bytes 1966088 | tf_op jit(solution)/shard_map/ppermute | solution.py:17
  761.4 30.5 %collective-permute-start.91 = (bf16[3072,128]{1,0:T(8,128)(2,1)}, bf16[3072,128]{1,0:T(8,128)(2,1)}, u32[]{:S(2)}, u32[]{:S(2)}) collective-permute-start(bf16[3072,128]{1,0:T(8,128)(2,1)} %fusion.70), channel_id=1, source_target_pairs={{0,2},{1,3},{2,0},{3,1},{4,6},{5,7},{6,4},{7,5},{8,10},{9,11},{10,... | collective-permute-start | bytes 2359304 | tf_op jit(solution)/shard_map/ppermute | solution.py:17
  761.8 30.0 %collective-permute-start.92 = (bf16[2,320,768]{2,1,0:T(8,128)(2,1)}, bf16[2,320,768]{2,1,0:T(8,128)(2,1)}, u32[]{:S(2)}, u32[]{:S(2)}) collective-permute-start(bf16[2,320,768]{2,1,0:T(8,128)(2,1)} %get-tuple-element.2699), channel_id=1, source_target_pairs={{0,16},{16,0},{1,17},{17,1},{2,18},{18,2},{3,19},{19,3},{4,20},{20... | collective-permute-start | bytes 2949128 | tf_op jit(solution)/shard_map/ppermute | solution.py:22
  823.7 26.5 %collective-permute-start.100 = (bf16[160,1024]{1,0:T(8,128)(2,1)S(1)}, bf16[160,1024]{1,0:T(8,128)(2,1)S(1)}, u32[]{:S(2)}, u32[]{:S(2)}) collective-permute-start(bf16[160,1024]{1,0:T(8,128)(2,1)S(1)} %copy-done.94), channel_id=1, source_target_pairs={{0,8},{4,12},{8,0},{12,4},{1,9},{5,13},{9,1},{13,5},{2,10},{6,14},... | collective-permute-start | bytes 983048 | tf_op jit(solution)/shard_map/ppermute | solution.py:17
  (232 other events, 2457.3 us)

commit v7 on v6

--- a/solution.py
+++ b/solution.py
@@ -440,7 +440,7 @@
     at.qkv_raw = nn(at.normed, qkv_part)
     at.gate_a = over_fsdp(at.gate_pair[0])
     at.out_2 = ring(at.out_1, "ctx")
-    at.up_got = flip(at.up_sent, "ctx", 1)
+    at.far_1 = far(quarters(at.gate_pair)[:1])
     at.next()
     (qkv_raw,) = at.drop("qkv_raw")
     kv_raw = qkv_raw[:, slot_width : slot_width + kv_width]
@@ -456,10 +456,9 @@
     at.next()
     out_x = over_fsdp(at.out_near)
     at.chunks = [shifted(at.kv_own, "ctx", by) for by in range(reach_back, 0, -1)]
-    at.up_pair = paired(*at.drop("up_mine", "up_got"))
     at.next()
     at.kv_column = jnp.concatenate(at.drop("chunks")[0] + [at.kv_own], axis=0)
-    at.gate_far = jnp.concatenate(quarters(at.gate_pair)[:2], axis=0)
+    at.gate_far = jnp.concatenate(quarters(at.gate_pair)[1:3], axis=0)
     at.drop("out_0", "out_1", "out_2", "kv_own", "qkv_3")
     at.next()
     at.kv_over_y = flip(at.kv_column, "tp", 2)
@@ -471,8 +470,8 @@
     at.next()
     at.kv_other = flip(at.kv_pair, "tp", 1)
     at.down_pair = paired(*at.drop("down_mine", "down_got"))
-    at.mixed_far = jnp.concatenate(quarters(at.gate_pair)[3:] + quarters(at.up_pair)[:2], axis=0)
-    at.far_1 = far(quarters(at.gate_pair)[2:3])
+    at.down_far = jnp.concatenate(quarters(at.down_pair)[:2], axis=0)
+    at.far_0 = far(quarters(at.gate_pair)[3:])
     (out_x,) = at.drop("out_x")
     at.out_part = placed([[block[i] for block in out_x] for i in range(ctx_count)])
     at.next()
@@ -480,24 +479,25 @@
     at.keyvals = jnp.concatenate(
         swapped([kv_pair[0], kv_other[0], kv_pair[1], kv_other[1]], tp_rank), axis=1
     )
-    at.drop("up_sent", "down_sent", "gate_far", "out_near")
+    at.drop("down_sent", "gate_far", "out_near")
     at.next()
 
     queries, keyvals = at.queries, at.keyvals
     at.attended = attention_forward(queries, keyvals, live, first_key, head_size)
     blocks = low(nt(at.attended, at.out_part)).reshape(2, 2, part_rows, -1)
     at.kept, at.sent = take(blocks, core_rank, 1), take(blocks, 1 - core_rank, 1)
-    at.up_x = over_fsdp(at.up_pair)
-    at.far_3 = flip(at.mixed_far, "ctx", 2)
+    at.down_x = over_fsdp(at.down_pair)
+    at.up_got = flip(at.up_sent, "ctx", 1)
+    at.far_3 = flip(at.down_far, "ctx", 2)
+    at.gate_other = jnp.concatenate(
+        at.far_1 + [at.far_2] + at.far_0, axis=0
+    ).reshape(at.gate_pair.shape)
     at.next()
 
     out_part = at.out_part
-    quarter_rows = at.far_1[0].shape[0]
     at.got = flip(at.sent, "tp", 1)
-    at.gate_other = jnp.concatenate(
-        [at.far_2] + at.far_1 + [at.far_3[:quarter_rows]], axis=0
-    ).reshape(at.gate_pair.shape)
-    at.up_far = jnp.concatenate(quarters(at.up_pair)[2:], axis=0)
+    at.up_pair = paired(*at.drop("up_mine", "up_got"))
+    at.up_far = jnp.concatenate(quarters(at.up_pair)[:2], axis=0)
     at.next()
     summed = wide(at.kept) + wide(at.got)
     at.kept, at.sent = take(summed, y_rank), low(take(summed, 1 - y_rank))
@@ -566,22 +566,24 @@
     at.residual = residual
     at.part = low(residual * scale_two * gain_mlp)
     at.down_quarters = quarters(at.down_pair)
+    at.up_quarters = quarters(at.up_pair)
     at.next()
     residual = at.residual
     gather_sides()
-    at.down_x = over_fsdp(at.down_pair)
-    at.far_5 = flip(at.down_quarters[0], "ctx", 2)
-    at.up_a, at.up_b = at.far_3[quarter_rows:], at.far_4
+    at.up_x = over_fsdp(at.up_pair)
+    at.far_5 = flip(at.up_quarters[2], "ctx", 2)
+    at.down_a = at.far_3
     gate_a, gate_b, gate_z = at.drop("gate_a", "gate_b", "gate_z")
     at.gate_full = mlp_placed([jnp.stack(pair) for pair in zip(gate_a, gate_b)], gate_z)
     at.next()
     between_sides_and_corners()
     at.next()
     gather_corners()
-    at.up_a = over_fsdp(at.up_a)
-    at.far_6 = flip(at.down_quarters[1], "ctx", 2)
+    at.up_a = over_fsdp(at.far_4)
+    at.far_6 = flip(at.up_quarters[3], "ctx", 2)
     at.next()
     between_corners_and_core()
+    at.up_b = jnp.concatenate([at.far_5, at.far_6], axis=0)
     at.next()
     at.core_corner = flip(at.corner, "tp", 1)
     at.next()
@@ -589,7 +591,6 @@
     at.gate_proj = nn(at.normed_two, at.gate_full)
     at.up_b = over_fsdp(at.up_b)
     at.far_7 = flip(at.down_quarters[2], "ctx", 2)
-    at.down_a = jnp.concatenate([at.far_5, at.far_6], axis=0)
     at.next()
     gate_full = at.gate_full
     up_a, up_b = at.drop("up_a", "up_b")
@@ -606,7 +607,7 @@
     at.down_b = over_fsdp(at.down_b)
     at.next()
     at.drop("far_1", "far_2", "far_3", "far_4", "far_5", "far_6", "far_7", "gate_pair", "up_pair")
-    at.drop("far_8", "gate_other", "up_far", "down_quarters", "mixed_far")
+    at.drop("far_8", "gate_other", "up_far", "down_quarters", "up_quarters", "down_far", "up_sent", "far_0")
     at.drop("down_pair")
     down_x, down_a, down_b = at.drop("down_x", "down_a", "down_b")
     down_z = [jnp.stack(pair) for pair in zip(down_a, down_b)]

time: 977 us -> 979 us (level)
  waiting for transfers between devices: 400 us -> 411 us
  starting transfers between devices: 129 us -> 119 us
    unnamed x293 -> x311, local copies, waits for them, and re-layouts: 30 us -> 33 us
    ppermute x71 -> x72, starting transfers between devices: 67.2 us -> 64.8 us  [flip(): lax.ppermute(array, axis, [(i, i ^ bit) for i in range(lax.axis_size(axis...]
    ppermute x71 -> x72, waiting for transfers between devices: 269 us -> 269 us  [flip(): lax.ppermute(array, axis, [(i, i ^ bit) for i in range(lax.axis_size(axis...]
  transfers between devices with their start and end apart: 121 -> 122, of which waited for: 67 -> 68; matrix products, arithmetic and copies ran while one was open for 25% -> 24% of each run, Pallas kernels for 6% -> 6%
where the time goes in v7:
time: 979 us; the launch traced here: 967 us
  waiting for transfers between devices  411 us (42%)
  other arithmetic  142 us (15%)
  matrix products  126 us (13%)
  starting transfers between devices  119 us (12%)
  local copies, waits for them, and re-layouts  101 us (10%)
  Pallas kernels  62.3 us (6%)
    ppermute x72, waiting for transfers between devices, flip(): lax.ppermute(array, axis, [(i, i ^ bit) for i in range(lax.axis_size(axis...  269 us
    ppermute x44, waiting for transfers between devices, ring(): lax.ppermute(array, axis, [(i, (i + by) % count) for i in range(count)])  123 us
    ppermute x72, starting transfers between devices, flip(): lax.ppermute(array, axis, [(i, i ^ bit) for i in range(lax.axis_size(axis...  64.8 us
    dot_general x5, matrix products, nt(): lax.dot_general(first, second, (((1,), (1,)), ((), ())), preferred_elemen...  45.4 us
    dot_general x5, matrix products, nn(): lax.dot_general(first, second, (((1,), (0,)), ((), ())), preferred_elemen...  43.8 us
    ppermute x44, starting transfers between devices, ring(): lax.ppermute(array, axis, [(i, (i + by) % count) for i in range(count)])  40.5 us
    dot_general x6, matrix products, tn(): lax.dot_general(first, second, (((0,), (0,)), ((), ())), preferred_elemen...  37 us
    convert_element_type x26, other arithmetic, low(): return values.astype(jnp.bfloat16)  33.5 us
  transfers between devices with their start and end apart: 122, of which 68 were waited for; matrix products, arithmetic and copies ran while one was open for 24% of the time, Pallas kernels for 6%

profile of v7, /device:TPU:0, one launch (start us, length us, event | category | flops | bytes accessed | tf_op | source)
XLA Modules:
  0.0 967.4 jit_solution(11816898870816846481)
XLA Ops:
  27.5 12.0 %collective-permute-done.5.refs_1_ = bf16[320,1024]{1,0:T(8,128)(2,1)S(1)} collective-permute-done((bf16[320,1024]{1,0:T(8,128)(2,1)S(1)}, bf16[320,1024]{1,0:T(8,128)(2,1)S(1)}, u32[]{:S(2)}, u32[]{:S(2)}) %collective-permute-start.5) | collective-permute-done | bytes 655392 | tf_op jit(solution)/shard_map/ppermute | solution.py:22
  45.3 11.6 %collective-permute-done.7.refs_3_ = bf16[320,1024]{1,0:T(8,128)(2,1)S(1)} collective-permute-done((bf16[320,1024]{1,0:T(8,128)(2,1)S(1)}, bf16[320,1024]{1,0:T(8,128)(2,1)S(1)}, u32[]{:S(2)}, u32[]{:S(2)}) %collective-permute-start.7) | collective-permute-done | bytes 655392 | tf_op jit(solution)/shard_map/ppermute | solution.py:22
  154.2 23.5 %collective-permute-done.23 = bf16[320,1024]{1,0:T(8,128)(2,1)S(1)} collective-permute-done((bf16[320,1024]{1,0:T(8,128)(2,1)S(1)}, bf16[320,1024]{1,0:T(8,128)(2,1)S(1)}, u32[]{:S(2)}, u32[]{:S(2)}) %collective-permute-start.23) | collective-permute-done | bytes 655392 | tf_op jit(solution)/shard_map/ppermute | solution.py:17
  194.3 8.0 collective-permute-done.27
  212.9 18.3 %attention_forward.1 = bf16[768,768]{1,0:T(8,128)(2,1)S(1)} custom-call(s32[4]{0:T(128)S(1)} %pad_add_fusion.info_ref, bf16[768,768]{1,0:T(8,128)(2,1)S(1)} %copy.54.q_ref, bf16[3072,512]{1,0:T(8,128)(2,1)S(1)} %copy-done.7), custom_call_target="tpu_custom_call" | custom-call | flops 5435817984 | bytes 5505024 | tf_op jit(solution)/shard_map/attention_forward/pallas_call | solution.py:163
  253.7 29.7 %collective-permute-done.33 = bf16[320,1024]{1,0:T(8,128)(2,1)} collective-permute-done((bf16[320,1024]{1,0:T(8,128)(2,1)}, bf16[320,1024]{1,0:T(8,128)(2,1)}, u32[]{:S(2)}, u32[]{:S(2)}) %collective-permute-start.33) | collective-permute-done | bytes 655392 | tf_op jit(solution)/shard_map/ppermute | solution.py:17
  299.4 19.7 %collective-permute-done.37 = bf16[160,1024]{1,0:T(8,128)(2,1)S(1)} collective-permute-done((bf16[160,1024]{1,0:T(8,128)(2,1)}, bf16[160,1024]{1,0:T(8,128)(2,1)S(1)}, u32[]{:S(2)}, u32[]{:S(2)}) %collective-permute-start.37) | collective-permute-done | bytes 327712 | tf_op jit(solution)/shard_map/ppermute | solution.py:17
  329.0 15.7 %collective-permute-done.44 = bf16[160,1024]{1,0:T(8,128)(2,1)S(1)} collective-permute-done((bf16[160,1024]{1,0:T(8,128)(2,1)S(1)}, bf16[160,1024]{1,0:T(8,128)(2,1)S(1)}, u32[]{:S(2)}, u32[]{:S(2)}) %collective-permute-start.44) | collective-permute-done | bytes 327712 | tf_op jit(solution)/shard_map/ppermute | solution.py:17
  355.5 8.3 fusion.106
  373.6 12.6 %fusion.107 = f32[1536,1024]{1,0:T(8,128)S(1)} fusion(bf16[1536,2560]{1,0:T(8,128)(2,1)} %copy-done.120, bf16[2560,1024]{1,0:T(8,128)(2,1)S(1)} %bitcast.422), kind=kOutput, calls=%fused_computation.469 | convolution fusion | flops 8053063680 | bytes 19398656 | tf_op jit(solution)/shard_map/dot_general | solution.py:110
  389.2 12.2 %collective-permute-done.51 = bf16[320,1024]{1,0:T(8,128)(2,1)S(1)} collective-permute-done((bf16[320,1024]{1,0:T(8,128)(2,1)S(1)}, bf16[320,1024]{1,0:T(8,128)(2,1)S(1)}, u32[]{:S(2)}, u32[]{:S(2)}) %collective-permute-start.51) | collective-permute-done | bytes 655392 | tf_op jit(solution)/shard_map/ppermute | solution.py:22
  405.3 8.8 convolution_convert_fusion
  428.6 7.7 collective-permute-done.53
  448.9 12.5 %collective-permute-done.56 = bf16[192,2560]{1,0:T(8,128)(2,1)S(1)} collective-permute-done((bf16[192,2560]{1,0:T(8,128)(2,1)S(1)}, bf16[192,2560]{1,0:T(8,128)(2,1)S(1)}, u32[]{:S(2)}, u32[]{:S(2)}) %collective-permute-start.56) | collective-permute-done | bytes 983072 | tf_op jit(solution)/shard_map/ppermute | solution.py:17
  469.5 15.4 %collective-permute-done.60 = bf16[192,2560]{1,0:T(8,128)(2,1)S(1)} collective-permute-done((bf16[192,2560]{1,0:T(8,128)(2,1)S(1)}, bf16[192,2560]{1,0:T(8,128)(2,1)S(1)}, u32[]{:S(2)}, u32[]{:S(2)}) %collective-permute-start.60) | collective-permute-done | bytes 983072 | tf_op jit(solution)/shard_map/ppermute | solution.py:17
  488.5 12.4 %collective-permute-done.62 = bf16[96,2560]{1,0:T(8,128)(2,1)S(1)} collective-permute-done((bf16[96,2560]{1,0:T(8,128)(2,1)S(1)}, bf16[96,2560]{1,0:T(8,128)(2,1)S(1)}, u32[]{:S(2)}, u32[]{:S(2)}) %collective-permute-start.62) | collective-permute-done | bytes 491552 | tf_op jit(solution)/shard_map/ppermute | solution.py:17
  510.4 8.9 convolution_convert_fusion.3
  523.1 12.1 %multiply_convert_fusion = (bf16[1536,1024]{1,0:T(8,128)(2,1)}, bf16[1536,1024]{1,0:T(8,128)(2,1)S(1)}) fusion(bf16[1536,1024]{1,0:T(8,128)(2,1)S(1)} %copy-done.51, bf16[1536,1024]{1,0:T(8,128)(2,1)S(1)} %copy-done.50, bf16[1536,2560]{1,0:T(8,128)(2,1)} %copy-done.121, bf16[2560,1024]{1,0:T(8,128)(2,1)S(1)} %bitcast.429), kind=kOutput, calls=%fused_computation.33 | convolution fusion | flops 8062500864 | bytes 25690112 | tf_op jit(solution)/shard_map/dot_general | solution.py:110
  538.3 11.0 %convolution_convert_fusion.2 = bf16[2560,1024]{1,0:T(8,128)(2,1)S(1)} fusion(bf16[1536,2560]{1,0:T(8,128)(2,1)} %copy-done.120, bf16[1536,1024]{1,0:T(8,128)(2,1)S(1)} %get-tuple-element.2311), kind=kOutput, calls=%fused_computation.39 | convolution fusion | flops 8055685120 | bytes 16252928 | tf_op jit(solution)/shard_map/dot_general | solution.py:122
  559.3 11.0 %fusion.108 = f32[1536,2560]{1,0:T(8,128)} fusion(bf16[1536,1024]{1,0:T(8,128)(2,1)S(1)} %copy-done.134, bf16[2560,1024]{1,0:T(8,128)(2,1)S(1)} %bitcast.425), kind=kOutput, calls=%fused_computation.470 | convolution fusion | flops 8053063680 | bytes 24117248 | tf_op jit(solution)/shard_map/dot_general | solution.py:116
  570.4 15.0 %add_convert_fusion = bf16[1536,2560]{1,0:T(8,128)(2,1)} fusion(f32[1536,2560]{1,0:T(8,128)} %fusion.108, bf16[1536,1024]{1,0:T(8,128)(2,1)} %copy-done.136, bf16[2560,1024]{1,0:T(8,128)(2,1)S(1)} %bitcast.421), kind=kOutput, calls=%fused_computation | convolution fusion | flops 8060928000 | bytes 31981568 | tf_op jit(solution)/shard_map/dot_general | solution.py:116
  599.5 11.9 %collective-permute-done.73 = bf16[160,1024]{1,0:T(8,128)(2,1)S(1)} collective-permute-done((bf16[160,1024]{1,0:T(8,128)(2,1)S(1)}, bf16[160,1024]{1,0:T(8,128)(2,1)S(1)}, u32[]{:S(2)}, u32[]{:S(2)}) %collective-permute-start.73) | collective-permute-done | bytes 327712 | tf_op jit(solution)/shard_map/ppermute | solution.py:17
  622.7 9.2 convolution_convert_fusion.1
  637.9 9.5 collective-permute-done.78
  662.2 21.7 %collective-permute-done.81 = bf16[320,1024]{1,0:T(8,128)(2,1)S(1)} collective-permute-done((bf16[320,1024]{1,0:T(8,128)(2,1)}, bf16[320,1024]{1,0:T(8,128)(2,1)S(1)}, u32[]{:S(2)}, u32[]{:S(2)}) %collective-permute-start.81) | collective-permute-done | bytes 655392 | tf_op jit(solution)/shard_map/ppermute | solution.py:17
  699.9 28.3 %attention_backward.1 = (f32[768,768]{1,0:T(8,128)S(1)}, bf16[3072,512]{1,0:T(8,128)(2,1)S(1)}) custom-call(s32[1]{0:T(128)} %bitcast.info_ref, bf16[768,768]{1,0:T(8,128)(2,1)S(1)} %copy-done.12, bf16[3072,512]{1,0:T(8,128)(2,1)S(1)} %copy-done.8, bf16[768,768]{1,0:T(8,128)(2,1)S(1)} %multiply_convert_fusion.3.do_ref), custom_call_target="tpu_custom_call" | custom-call | flops 13589544960 | bytes 11010048 | tf_op jit(solution)/shard_map/attention_backward/pallas_call | solution.py:225
  778.8 7.7 collective-permute-done.91
  804.2 10.9 %collective-permute-done.96 = bf16[768,128]{1,0:T(8,128)(2,1)S(1)} collective-permute-done((bf16[768,128]{1,0:T(8,128)(2,1)}, bf16[768,128]{1,0:T(8,128)(2,1)S(1)}, u32[]{:S(2)}, u32[]{:S(2)}) %collective-permute-start.96) | collective-permute-done | bytes 196640 | tf_op jit(solution)/shard_map/ppermute | solution.py:28
  831.9 16.6 %collective-permute-done.101 = bf16[160,1024]{1,0:T(8,128)(2,1)S(1)} collective-permute-done((bf16[160,1024]{1,0:T(8,128)(2,1)S(1)}, bf16[160,1024]{1,0:T(8,128)(2,1)S(1)}, u32[]{:S(2)}, u32[]{:S(2)}) %collective-permute-start.101) | collective-permute-done | bytes 327712 | tf_op jit(solution)/shard_map/ppermute | solution.py:17
  891.0 8.7 collective-permute-done.105
  910.0 9.5 collective-permute-done.109
  932.2 8.5 collective-permute-done.111
  (812 shorter events, 532.0 us)
Async XLA Ops:
  130.2 50.9 %collective-permute-start.26 = (bf16[4,320,768]{2,1,0:T(8,128)(2,1)S(1)}, bf16[4,320,768]{2,1,0:T(8,128)(2,1)S(1)}, u32[]{:S(2)}, u32[]{:S(2)}) collective-permute-start(bf16[4,320,768]{2,1,0:T(8,128)(2,1)S(1)} %pad_maximum_fusion.5), channel_id=1, source_target_pairs={{0,16},{16,0},{1,17},{17,1},{2,18},{18,2},{3,19},{19,3},{4,20},{20... | collective-permute-start | bytes 5898248 | tf_op jit(solution)/shard_map/ppermute | solution.py:22
  145.6 35.5 %collective-permute-start.25 = (bf16[3072,128]{1,0:T(8,128)(2,1)S(1)}, bf16[3072,128]{1,0:T(8,128)(2,1)S(1)}, u32[]{:S(2)}, u32[]{:S(2)}) collective-permute-start(bf16[3072,128]{1,0:T(8,128)(2,1)S(1)} %pad_maximum_fusion.33), channel_id=1, source_target_pairs={{0,2},{1,3},{2,0},{3,1},{4,6},{5,7},{6,4},{7,5},{8,10},{9,11},{10,... | collective-permute-start | bytes 2359304 | tf_op jit(solution)/shard_map/ppermute | solution.py:17
  146.5 31.3 %collective-permute-start.23 = (bf16[320,1024]{1,0:T(8,128)(2,1)S(1)}, bf16[320,1024]{1,0:T(8,128)(2,1)S(1)}, u32[]{:S(2)}, u32[]{:S(2)}) collective-permute-start(bf16[320,1024]{1,0:T(8,128)(2,1)S(1)} %copy-done.97), channel_id=1, source_target_pairs={{0,4},{4,0},{8,12},{12,8},{1,5},{5,1},{9,13},{13,9},{2,6},{6,2},{1... | collective-permute-start | bytes 1966088 | tf_op jit(solution)/shard_map/ppermute | solution.py:17
  150.8 30.3 %collective-permute-start.24 = (bf16[320,1024]{1,0:T(8,128)(2,1)S(1)}, bf16[320,1024]{1,0:T(8,128)(2,1)S(1)}, u32[]{:S(2)}, u32[]{:S(2)}) collective-permute-start(bf16[320,1024]{1,0:T(8,128)(2,1)S(1)} %concatenate.193), channel_id=1, source_target_pairs={{0,8},{4,12},{8,0},{12,4},{1,9},{5,13},{9,1},{13,5},{2,10},{6,14},... | collective-permute-start | bytes 1966088 | tf_op jit(solution)/shard_map/ppermute | solution.py:17
  206.4 32.7 %collective-permute-start.30 = (bf16[320,1024]{1,0:T(8,128)(2,1)S(1)}, bf16[320,1024]{1,0:T(8,128)(2,1)}, u32[]{:S(2)}, u32[]{:S(2)}) collective-permute-start(bf16[320,1024]{1,0:T(8,128)(2,1)S(1)} %get-tuple-element.1730), channel_id=1, source_target_pairs={{0,8},{4,12},{8,0},{12,4},{1,9},{5,13},{9,1},{13,5},{2,10},{6,14},... | collective-permute-start | bytes 1966088 | tf_op jit(solution)/shard_map/ppermute | solution.py:17
  206.4 32.7 %collective-permute-start.31 = (bf16[320,1024]{1,0:T(8,128)(2,1)}, bf16[320,1024]{1,0:T(8,128)(2,1)}, u32[]{:S(2)}, u32[]{:S(2)}) collective-permute-start(bf16[320,1024]{1,0:T(8,128)(2,1)} %get-tuple-element.1742), channel_id=1, source_target_pairs={{0,4},{4,0},{8,12},{12,8},{1,5},{5,1},{9,13},{13,9},{2,6},{6,2},{1... | collective-permute-start | bytes 1966088 | tf_op jit(solution)/shard_map/ppermute | solution.py:17
  209.9 30.3 %collective-permute-start.29 = (bf16[2,320,1024]{2,1,0:T(8,128)(2,1)S(1)}, bf16[2,320,1024]{2,1,0:T(8,128)(2,1)S(1)}, u32[]{:S(2)}, u32[]{:S(2)}) collective-permute-start(bf16[2,320,1024]{2,1,0:T(8,128)(2,1)S(1)} %pad_maximum_fusion.13), channel_id=1, source_target_pairs={{0,16},{16,0},{1,17},{17,1},{2,18},{18,2},{3,19},{19,3},{4,20},{20... | collective-permute-start | bytes 3932168 | tf_op jit(solution)/shard_map/ppermute | solution.py:22
  250.1 33.3 %collective-permute-start.34 = (bf16[2,320,1024]{2,1,0:T(8,128)(2,1)}, bf16[2,320,1024]{2,1,0:T(8,128)(2,1)}, u32[]{:S(2)}, u32[]{:S(2)}) collective-permute-start(bf16[2,320,1024]{2,1,0:T(8,128)(2,1)} %bitcast.45), channel_id=1, source_target_pairs={{0,16},{16,0},{1,17},{17,1},{2,18},{18,2},{3,19},{19,3},{4,20},{20... | collective-permute-start | bytes 3932168 | tf_op jit(solution)/shard_map/ppermute | solution.py:22
  250.5 32.9 %collective-permute-start.35 = (bf16[192,2560]{1,0:T(8,128)(2,1)}, bf16[192,2560]{1,0:T(8,128)(2,1)}, u32[]{:S(2)}, u32[]{:S(2)}) collective-permute-start(bf16[192,2560]{1,0:T(8,128)(2,1)} %fusion.42), channel_id=1, source_target_pairs={{0,2},{1,3},{2,0},{3,1},{4,6},{5,7},{6,4},{7,5},{8,10},{9,11},{10,... | collective-permute-start | bytes 2949128 | tf_op jit(solution)/shard_map/ppermute | solution.py:17
  252.1 31.2 %collective-permute-start.33 = (bf16[320,1024]{1,0:T(8,128)(2,1)}, bf16[320,1024]{1,0:T(8,128)(2,1)}, u32[]{:S(2)}, u32[]{:S(2)}) collective-permute-start(bf16[320,1024]{1,0:T(8,128)(2,1)} %get-tuple-element.1787), channel_id=1, source_target_pairs={{0,8},{4,12},{8,0},{12,4},{1,9},{5,13},{9,1},{13,5},{2,10},{6,14},... | collective-permute-start | bytes 1966088 | tf_op jit(solution)/shard_map/ppermute | solution.py:17
  288.9 32.4 %collective-permute-start.40 = (bf16[2,320,1024]{2,1,0:T(8,128)(2,1)S(1)}, bf16[2,320,1024]{2,1,0:T(8,128)(2,1)}, u32[]{:S(2)}, u32[]{:S(2)}) collective-permute-start(bf16[2,320,1024]{2,1,0:T(8,128)(2,1)S(1)} %pad_maximum_fusion.15), channel_id=1, source_target_pairs={{0,16},{16,0},{1,17},{17,1},{2,18},{18,2},{3,19},{19,3},{4,20},{20... | collective-permute-start | bytes 3932168 | tf_op jit(solution)/shard_map/ppermute | solution.py:22
  290.6 30.7 %collective-permute-start.39 = (bf16[192,2560]{1,0:T(8,128)(2,1)}, bf16[192,2560]{1,0:T(8,128)(2,1)}, u32[]{:S(2)}, u32[]{:S(2)}) collective-permute-start(bf16[192,2560]{1,0:T(8,128)(2,1)} %multiply_convert_fusion.4), channel_id=1, source_target_pairs={{0,4},{4,0},{8,12},{12,8},{1,5},{5,1},{9,13},{13,9},{2,6},{6,2},{1... | collective-permute-start | bytes 2949128 | tf_op jit(solution)/shard_map/ppermute | solution.py:17
  290.6 30.7 %collective-permute-start.38 = (bf16[192,2560]{1,0:T(8,128)(2,1)}, bf16[192,2560]{1,0:T(8,128)(2,1)}, u32[]{:S(2)}, u32[]{:S(2)}) collective-permute-start(bf16[192,2560]{1,0:T(8,128)(2,1)} %multiply_convert_fusion.4), channel_id=1, source_target_pairs={{0,2},{1,3},{2,0},{3,1},{4,6},{5,7},{6,4},{7,5},{8,10},{9,11},{10,... | collective-permute-start | bytes 2949128 | tf_op jit(solution)/shard_map/ppermute | solution.py:17
  291.0 30.3 %collective-permute-start.36 = (bf16[192,2560]{1,0:T(8,128)(2,1)}, bf16[192,2560]{1,0:T(8,128)(2,1)}, u32[]{:S(2)}, u32[]{:S(2)}) collective-permute-start(bf16[192,2560]{1,0:T(8,128)(2,1)} %multiply_convert_fusion.4), channel_id=1, source_target_pairs={{0,1},{1,0},{2,3},{3,2},{4,5},{5,4},{6,7},{7,6},{8,9},{9,8},{10,11... | collective-permute-start | bytes 2949128 | tf_op jit(solution)/shard_map/ppermute | solution.py:17
  291.0 28.1 %collective-permute-start.37 = (bf16[160,1024]{1,0:T(8,128)(2,1)}, bf16[160,1024]{1,0:T(8,128)(2,1)S(1)}, u32[]{:S(2)}, u32[]{:S(2)}) collective-permute-start(bf16[160,1024]{1,0:T(8,128)(2,1)} %get-tuple-element.1829), channel_id=1, source_target_pairs={{0,8},{4,12},{8,0},{12,4},{1,9},{5,13},{9,1},{13,5},{2,10},{6,14},... | collective-permute-start | bytes 983048 | tf_op jit(solution)/shard_map/ppermute | solution.py:17
  556.1 34.1 %collective-permute-start.67 = (bf16[320,1024]{1,0:T(8,128)(2,1)}, bf16[320,1024]{1,0:T(8,128)(2,1)}, u32[]{:S(2)}, u32[]{:S(2)}) collective-permute-start(bf16[320,1024]{1,0:T(8,128)(2,1)} %add_convert_fusion.15), channel_id=1, source_target_pairs={{0,8},{4,12},{8,0},{12,4},{1,9},{5,13},{9,1},{13,5},{2,10},{6,14},... | collective-permute-start | bytes 1966088 | tf_op jit(solution)/shard_map/ppermute | solution.py:17
  557.3 32.9 %collective-permute-start.68 = (bf16[320,1024]{1,0:T(8,128)(2,1)}, bf16[320,1024]{1,0:T(8,128)(2,1)}, u32[]{:S(2)}, u32[]{:S(2)}) collective-permute-start(bf16[320,1024]{1,0:T(8,128)(2,1)} %get-tuple-element.2316), channel_id=1, source_target_pairs={{0,16},{16,0},{1,17},{17,1},{2,18},{18,2},{3,19},{19,3},{4,20},{20... | collective-permute-start | bytes 1966088 | tf_op jit(solution)/shard_map/ppermute | solution.py:22
  557.7 32.5 %collective-permute-start.69 = (bf16[320,1024]{1,0:T(8,128)(2,1)}, bf16[320,1024]{1,0:T(8,128)(2,1)}, u32[]{:S(2)}, u32[]{:S(2)}) collective-permute-start(bf16[320,1024]{1,0:T(8,128)(2,1)} %get-tuple-element.2318), channel_id=1, source_target_pairs={{0,16},{16,0},{1,17},{17,1},{2,18},{18,2},{3,19},{19,3},{4,20},{20... | collective-permute-start | bytes 1966088 | tf_op jit(solution)/shard_map/ppermute | solution.py:22
  618.2 29.2 %collective-permute-start.78 = (bf16[320,1024]{1,0:T(8,128)(2,1)S(1)}, bf16[320,1024]{1,0:T(8,128)(2,1)S(1)}, u32[]{:S(2)}, u32[]{:S(2)}) collective-permute-start(bf16[320,1024]{1,0:T(8,128)(2,1)S(1)} %copy-done.79), channel_id=1, source_target_pairs={{0,16},{16,0},{1,17},{17,1},{2,18},{18,2},{3,19},{19,3},{4,20},{20... | collective-permute-start | bytes 1966088 | tf_op jit(solution)/shard_map/ppermute | solution.py:22
  620.7 28.5 %collective-permute-start.80 = (bf16[192,2560]{1,0:T(8,128)(2,1)S(1)}, bf16[192,2560]{1,0:T(8,128)(2,1)S(1)}, u32[]{:S(2)}, u32[]{:S(2)}) collective-permute-start(bf16[192,2560]{1,0:T(8,128)(2,1)S(1)} %pad_maximum_fusion.32), channel_id=1, source_target_pairs={{0,4},{4,0},{8,12},{12,8},{1,5},{5,1},{9,13},{13,9},{2,6},{6,2},{1... | collective-permute-start | bytes 2949128 | tf_op jit(solution)/shard_map/ppermute | solution.py:17
  654.5 29.5 %collective-permute-start.83 = (bf16[192,2560]{1,0:T(8,128)(2,1)S(1)}, bf16[192,2560]{1,0:T(8,128)(2,1)}, u32[]{:S(2)}, u32[]{:S(2)}) collective-permute-start(bf16[192,2560]{1,0:T(8,128)(2,1)S(1)} %get-tuple-element.2562), channel_id=1, source_target_pairs={{0,2},{1,3},{2,0},{3,1},{4,6},{5,7},{6,4},{7,5},{8,10},{9,11},{10,... | collective-permute-start | bytes 2949128 | tf_op jit(solution)/shard_map/ppermute | solution.py:17
  655.4 28.5 %collective-permute-start.81 = (bf16[320,1024]{1,0:T(8,128)(2,1)}, bf16[320,1024]{1,0:T(8,128)(2,1)S(1)}, u32[]{:S(2)}, u32[]{:S(2)}) collective-permute-start(bf16[320,1024]{1,0:T(8,128)(2,1)} %add_convert_fusion.11), channel_id=1, source_target_pairs={{0,8},{4,12},{8,0},{12,4},{1,9},{5,13},{9,1},{13,5},{2,10},{6,14},... | collective-permute-start | bytes 1966088 | tf_op jit(solution)/shard_map/ppermute | solution.py:17
  655.4 28.5 %collective-permute-start.82 = (bf16[320,1024]{1,0:T(8,128)(2,1)}, bf16[320,1024]{1,0:T(8,128)(2,1)S(1)}, u32[]{:S(2)}, u32[]{:S(2)}) collective-permute-start(bf16[320,1024]{1,0:T(8,128)(2,1)} %get-tuple-element.2529), channel_id=1, source_target_pairs={{0,16},{16,0},{1,17},{17,1},{2,18},{18,2},{3,19},{19,3},{4,20},{20... | collective-permute-start | bytes 1966088 | tf_op jit(solution)/shard_map/ppermute | solution.py:22
  655.9 28.1 %collective-permute-start.84 = (bf16[320,1024]{1,0:T(8,128)(2,1)}, bf16[320,1024]{1,0:T(8,128)(2,1)S(1)}, u32[]{:S(2)}, u32[]{:S(2)}) collective-permute-start(bf16[320,1024]{1,0:T(8,128)(2,1)} %get-tuple-element.2540), channel_id=1, source_target_pairs={{0,16},{16,0},{1,17},{17,1},{2,18},{18,2},{3,19},{19,3},{4,20},{20... | collective-permute-start | bytes 1966088 | tf_op jit(solution)/shard_map/ppermute | solution.py:22
  692.6 42.3 %collective-permute-start.88 = (bf16[160,1024]{1,0:T(8,128)(2,1)S(1)}, bf16[160,1024]{1,0:T(8,128)(2,1)S(1)}, u32[]{:S(2)}, u32[]{:S(2)}) collective-permute-start(bf16[160,1024]{1,0:T(8,128)(2,1)S(1)} %get-tuple-element.2638), channel_id=1, source_target_pairs={{0,8},{4,12},{8,0},{12,4},{1,9},{5,13},{9,1},{13,5},{2,10},{6,14},... | collective-permute-start | bytes 983048 | tf_op jit(solution)/shard_map/ppermute | solution.py:17
  694.1 40.8 %collective-permute-start.86 = (bf16[320,1024]{1,0:T(8,128)(2,1)S(1)}, bf16[320,1024]{1,0:T(8,128)(2,1)S(1)}, u32[]{:S(2)}, u32[]{:S(2)}) collective-permute-start(bf16[320,1024]{1,0:T(8,128)(2,1)S(1)} %copy-done.88), channel_id=1, source_target_pairs={{0,4},{4,0},{8,12},{12,8},{1,5},{5,1},{9,13},{13,9},{2,6},{6,2},{1... | collective-permute-start | bytes 1966088 | tf_op jit(solution)/shard_map/ppermute | solution.py:17
  694.8 43.9 %collective-permute-start.87 = (bf16[320,1024]{1,0:T(8,128)(2,1)S(1)}, bf16[320,1024]{1,0:T(8,128)(2,1)S(1)}, u32[]{:S(2)}, u32[]{:S(2)}) collective-permute-start(bf16[320,1024]{1,0:T(8,128)(2,1)S(1)} %copy-done.89), channel_id=1, source_target_pairs={{0,8},{4,12},{8,0},{12,4},{1,9},{5,13},{9,1},{13,5},{2,10},{6,14},... | collective-permute-start | bytes 1966088 | tf_op jit(solution)/shard_map/ppermute | solution.py:17
  696.1 44.5 %collective-permute-start.89 = (bf16[3,320,1024]{2,1,0:T(8,128)(2,1)}, bf16[3,320,1024]{2,1,0:T(8,128)(2,1)S(1)}, u32[]{:S(2)}, u32[]{:S(2)}) collective-permute-start(bf16[3,320,1024]{2,1,0:T(8,128)(2,1)} %pad_maximum_fusion.8), channel_id=1, source_target_pairs={{0,16},{16,0},{1,17},{17,1},{2,18},{18,2},{3,19},{19,3},{4,20},{20... | collective-permute-start | bytes 5898248 | tf_op jit(solution)/shard_map/ppermute | solution.py:22
  756.1 30.4 %collective-permute-start.91 = (bf16[320,1024]{1,0:T(8,128)(2,1)}, bf16[320,1024]{1,0:T(8,128)(2,1)}, u32[]{:S(2)}, u32[]{:S(2)}) collective-permute-start(bf16[320,1024]{1,0:T(8,128)(2,1)} %fusion.77), channel_id=1, source_target_pairs={{0,4},{4,0},{8,12},{12,8},{1,5},{5,1},{9,13},{13,9},{2,6},{6,2},{1... | collective-permute-start | bytes 1966088 | tf_op jit(solution)/shard_map/ppermute | solution.py:17
  757.6 32.2 %collective-permute-start.94 = (bf16[320,1024]{1,0:T(8,128)(2,1)}, bf16[320,1024]{1,0:T(8,128)(2,1)}, u32[]{:S(2)}, u32[]{:S(2)}) collective-permute-start(bf16[320,1024]{1,0:T(8,128)(2,1)} %pad_maximum_fusion.37), channel_id=1, source_target_pairs={{0,8},{4,12},{8,0},{12,4},{1,9},{5,13},{9,1},{13,5},{2,10},{6,14},... | collective-permute-start | bytes 1966088 | tf_op jit(solution)/shard_map/ppermute | solution.py:17
  759.0 30.8 %collective-permute-start.92 = (bf16[3072,128]{1,0:T(8,128)(2,1)}, bf16[3072,128]{1,0:T(8,128)(2,1)}, u32[]{:S(2)}, u32[]{:S(2)}) collective-permute-start(bf16[3072,128]{1,0:T(8,128)(2,1)} %fusion.70), channel_id=1, source_target_pairs={{0,2},{1,3},{2,0},{3,1},{4,6},{5,7},{6,4},{7,5},{8,10},{9,11},{10,... | collective-permute-start | bytes 2359304 | tf_op jit(solution)/shard_map/ppermute | solution.py:17
  760.1 29.6 %collective-permute-start.93 = (bf16[2,320,768]{2,1,0:T(8,128)(2,1)}, bf16[2,320,768]{2,1,0:T(8,128)(2,1)}, u32[]{:S(2)}, u32[]{:S(2)}) collective-permute-start(bf16[2,320,768]{2,1,0:T(8,128)(2,1)} %get-tuple-element.2731), channel_id=1, source_target_pairs={{0,16},{16,0},{1,17},{17,1},{2,18},{18,2},{3,19},{19,3},{4,20},{20... | collective-permute-start | bytes 2949128 | tf_op jit(solution)/shard_map/ppermute | solution.py:22
  (242 other events, 2577.7 us)
